TPU v7x, 32 devices: a whole 2x2x4 slice. The times are simulated.
32 devices in a mesh: chan: 4 (over z), freq: 8 (over y, x, core).
Axes of the slice: x: 2, y: 2, z: 4, core: 2. Of those that a mesh axis runs over, the one named last changes fastest.
Arguments:
- spectra: bfloat16 [2, 32, 256, 512], P(None, None, 'freq', 'chan'), may hold values from -6 to 6
- block_position: int32 [4], replicated, may hold values from 0 to 3, each once
Outputs:
- taup: float32 [4, 256, 512], P('chan', 'freq')
Inputs may be any that keep to these rules, and one draw needn't show every extreme that they name: block_position is a permutation: every fiber position 0 to 3 holds exactly one stored block; group k of the chan axis stores block k.
All inputs are finite; a program needn't handle non-finite values.
Results may differ from a plain program's by a relative error of at most 0.0003.
Values may be sent and summed in bfloat16 or wider, within the bound.
No kernel may reach another device: no remote copies, remote signals or barrier semaphores. Data moves between devices by JAX's collectives and lax.ppermute only.
A program may use at most 64 MiB of HBM per device.

v0:
```python
import math

import jax
import jax.numpy as jnp
from jax import lax
from jax.sharding import PartitionSpec as P

SEGMENTS = 32
FREQS = 256
BLOCK = 128
SLOWNESS = 256
LAG_TIMES = 512


def passed_along(value, axis, steps):
    count = lax.axis_size(axis)
    pairs = [(source, (source + steps) % count) for source in range(count)]
    return lax.ppermute(value, axis, pairs)


def lag_sums(panel):
    leading = panel.shape[:-2]
    extent = panel.shape[-1]
    flat_panel = panel.reshape(leading + (extent * extent,))
    padded = jnp.pad(flat_panel, [(0, 0)] * len(leading) + [(0, extent)])
    skewed = padded.reshape(leading + (extent, extent + 1))
    row_index = lax.broadcasted_iota(jnp.int32, (extent, extent + 1), 0)
    col_index = lax.broadcasted_iota(jnp.int32, (extent, extent + 1), 1)
    before_wrap = row_index + col_index < extent
    forward_lags = jnp.sum(jnp.where(before_wrap, skewed, 0.0), axis=-2)
    backward_lags = jnp.sum(skewed, axis=-2) - forward_lags
    return jnp.concatenate([backward_lags[..., 1:], forward_lags[..., :extent]], axis=-1)


def angles(numerator):
    modulus = 8 * FREQS * BLOCK
    return jnp.mod(numerator, modulus).astype(jnp.float32) * (2.0 * math.pi / modulus)


def inverse_counts(delta_start, delta_count, nblocks):
    deltas = delta_start + lax.broadcasted_iota(jnp.int32, (delta_count, 2 * BLOCK), 0)
    lag_value = lax.broadcasted_iota(jnp.int32, (delta_count, 2 * BLOCK), 1) - BLOCK
    counts = SEGMENTS * (nblocks - deltas) * (BLOCK - jnp.abs(lag_value))
    usable = (lag_value > -BLOCK) & ((deltas >= 1) | (lag_value >= 1))
    inverse = jnp.where(usable, 1.0 / jnp.maximum(counts, 1).astype(jnp.float32), 0.0)
    return jnp.concatenate([inverse, inverse], axis=-1)


def slant_terms(means_block, freq_ids, delta_start, group_blocks):
    bins, delta_count = (means_block.shape[0], means_block.shape[1])
    slow_index = lax.broadcasted_iota(jnp.int32, (1, 1, SLOWNESS), 2) - SLOWNESS // 2
    lag_value = lax.broadcasted_iota(jnp.int32, (1, 2 * BLOCK, 1), 1) - BLOCK
    freq_column = freq_ids.reshape(bins, 1, 1)
    lag_angle = angles(freq_column * slow_index * lag_value)
    cosine = jnp.cos(lag_angle)
    sine_part = jnp.sin(lag_angle)
    lag_table = jnp.concatenate(
        [jnp.concatenate([cosine, sine_part], -1), jnp.concatenate([-sine_part, cosine], -1)], 1
    )
    rotated = jnp.einsum("fdk,fkp->fdp", means_block, lag_table, precision=lax.Precision.HIGHEST)
    deltas = delta_start + lax.broadcasted_iota(jnp.int32, (1, delta_count, 1), 1)
    offset_angle = angles(freq_column * slow_index * (BLOCK * deltas))
    offset_cos = jnp.cos(offset_angle)
    offset_sin = jnp.sin(offset_angle)
    real_part = rotated[..., :SLOWNESS]
    imag_part = rotated[..., SLOWNESS:]
    shifted_re = real_part * offset_cos - imag_part * offset_sin
    shifted_im = real_part * offset_sin + imag_part * offset_cos
    apertures = delta_count // group_blocks
    summed_re = shifted_re.reshape(bins, apertures, group_blocks, SLOWNESS).sum(axis=2)
    summed_im = shifted_im.reshape(bins, apertures, group_blocks, SLOWNESS).sum(axis=2)
    lag_time = lax.broadcasted_iota(jnp.int32, (1, LAG_TIMES), 1) - LAG_TIMES // 2
    time_angle = angles(freq_ids.reshape(bins, 1) * (4 * BLOCK * lag_time))
    spectrum = jnp.concatenate([summed_re, summed_im], axis=0)
    kernel = jnp.concatenate([jnp.cos(time_angle), -jnp.sin(time_angle)], axis=0)
    result = jnp.einsum("gas,gt->ast", spectrum, kernel, precision=lax.Precision.HIGHEST)
    return result.reshape(apertures * SLOWNESS, LAG_TIMES)


def slant_all(mean_stacks, freq_start, delta_start, group_blocks):
    freq_count, delta_count = (mean_stacks.shape[0], mean_stacks.shape[1])
    block_bins = 4
    block_total = freq_count // block_bins
    blocks = mean_stacks.reshape(block_total, block_bins, delta_count, 4 * BLOCK)
    freq_table = (freq_start + jnp.arange(freq_count, dtype=jnp.int32)).reshape(
        block_total, block_bins
    )

    def add_block(running, block_item):
        return (
            running + slant_terms(block_item[0], block_item[1], delta_start, group_blocks),
            None,
        )

    initial = jnp.zeros((delta_count // group_blocks * SLOWNESS, LAG_TIMES), jnp.float32)
    summed, unused = lax.scan(add_block, initial, (blocks, freq_table))
    return summed


def cross_stack(first_spec, second_spec, first_pos, second_pos, drop_backward, nblocks):
    window_rows = 2 * first_spec.shape[1]
    freq_dev = first_spec.shape[2]
    first_width, second_width = (first_spec.shape[3], second_spec.shape[3])
    first_count, second_count = (first_width // BLOCK, second_width // BLOCK)
    block_bins = 2
    block_total = freq_dev // block_bins
    left_side = jnp.concatenate([first_spec[0], first_spec[1]], axis=0)
    right_side = jnp.stack(
        [
            jnp.concatenate([second_spec[0], second_spec[1]], axis=0),
            jnp.concatenate([second_spec[1], -second_spec[0]], axis=0),
        ],
        axis=2,
    )
    left_blocks = jnp.moveaxis(
        left_side.reshape(window_rows, block_total, block_bins, first_count, BLOCK), 1, 0
    )
    right_blocks = jnp.moveaxis(
        right_side.reshape(window_rows, block_total, block_bins, 2, second_count, BLOCK), 1, 0
    )
    block_delta = second_pos[None, :] - first_pos[:, None]
    forward = (block_delta >= 0)[None, :, :, None]
    if drop_backward:
        panel_weight = (block_delta >= 0).astype(jnp.float32)
    else:
        panel_weight = jnp.ones(block_delta.shape, jnp.float32)
    targets = lax.broadcasted_iota(jnp.int32, (nblocks, 1), 0)
    selector = (jnp.abs(block_delta) == targets).astype(jnp.float32) * panel_weight

    def one_block(block_item):
        panels = jnp.einsum(
            "kfar,kfpbe->fabpre", block_item[0], block_item[1], preferred_element_type=jnp.float32
        )
        lag_block = lag_sums(panels)
        real_lags = lag_block[..., 0, :]
        imag_lags = lag_block[..., 1, :]
        flipped_re = jnp.roll(jnp.flip(real_lags, -1), 1, -1)
        flipped_im = jnp.roll(jnp.flip(imag_lags, -1), 1, -1)
        oriented = jnp.concatenate(
            [jnp.where(forward, real_lags, flipped_re), jnp.where(forward, imag_lags, -flipped_im)],
            axis=-1,
        )
        oriented = oriented.reshape(block_bins, first_count * second_count, 4 * BLOCK)
        return jnp.einsum("dp,fpk->fdk", selector, oriented, precision=lax.Precision.HIGHEST)

    block_parts = lax.map(one_block, (left_blocks, right_blocks))
    return block_parts.reshape(freq_dev, nblocks, 4 * BLOCK)


def shards(spectra, block_position):
    groups = lax.axis_size("chan")
    own_group = lax.axis_index("chan")
    freq_dev = spectra.shape[2]
    group_blocks = spectra.shape[3] // BLOCK
    nblocks = groups * group_blocks
    freq_start = lax.axis_index("freq") * freq_dev
    half_loop = groups // 2

    def positions(group_index):
        return lax.dynamic_slice_in_dim(
            block_position, jnp.mod(group_index, groups) * group_blocks, group_blocks
        )

    own_pos = positions(own_group)
    stacks = cross_stack(spectra, spectra, own_pos, own_pos, True, nblocks)
    moving = spectra
    for distance in range(1, half_loop + 1):
        moving = passed_along(moving, "chan", 1)
        if distance < half_loop:
            stacks = stacks + cross_stack(
                spectra, moving, own_pos, positions(own_group - distance), False, nblocks
            )
        else:
            second_spec = moving
            second_group = own_group - distance
            keeps_pair = jnp.mod(own_group, groups) < jnp.mod(second_group, groups)
            first_pos = positions(own_group)
            second_pos = positions(second_group)
            stacks = stacks + lax.cond(
                keeps_pair,
                lambda: cross_stack(spectra, second_spec, first_pos, second_pos, False, nblocks),
                lambda: jnp.zeros((freq_dev, nblocks, 4 * BLOCK), jnp.float32),
            )
    out_scale = math.sqrt(SEGMENTS / (FREQS * group_blocks))
    shares = lax.psum_scatter(stacks, "chan", scatter_dimension=1, tiled=True)
    delta_start = own_group * group_blocks
    mean_stacks = shares * inverse_counts(delta_start, group_blocks, nblocks)[None]
    image_term = slant_all(mean_stacks, freq_start, delta_start, group_blocks)
    summed_image = lax.psum_scatter(image_term, "freq", scatter_dimension=0, tiled=True)
    return (summed_image * out_scale).reshape(1, summed_image.shape[0], summed_image.shape[1])


def solution(mesh):
    return jax.shard_map(
        shards,
        mesh=mesh,
        in_specs=(P(None, None, "freq", "chan"), P()),
        out_specs=P("chan", "freq", None),
        check_vma=False,
    )
```

profile of v0, /device:TPU:0, one launch (start us, length us, event | category | flops | bytes accessed | tf_op | source)
XLA Modules:
  0.0 296.0 jit_solution(17180880914289304363)
XLA Ops:
  6.5 2.1 copy.28
  8.6 3.0 %collective-permute-start = (bf16[2,32,32,128]{3,1,2,0:T(8,128)(2,1)}, bf16[2,32,32,128]{3,1,2,0:T(8,128)(2,1)}, u32[]{:S(2)}, u32[]{:S(2)}) collective-permute-start(bf16[2,32,32,128]{3,1,2,0:T(8,128)(2,1)} %copy.28), channel_id=1, source_target_pairs={{0,8},{8,16},{16,24},{24,0},{1,9},{9,17},{17,25},{25,1},{2,10},{10... | collective-permute-start | bytes 1572872 | tf_op jit(solution)/shard_map/ppermute | solution.py:18
  12.3 43.0 %while.53 = (s32[]{:T(128)}, f32[16,2,4,512]{3,2,1,0:T(4,128)S(1)}, bf16[16,64,2,2,1,128]{5,1,3,2,4,0:T(8,128)(2,1)S(1)}, bf16[16,64,2,1,128]{4,1,2,3,0:T(8,128)(2,1)S(1)}, s32[]{:T(128)}, /*index=5*/f32[]{:T(128)}) while((s32[]{:T(128)}, f32[16,2,4,512]{3,2,1,0:T(4,128)S(1)}, bf16[16,64,2,2,1,128]{5,1,3,2,4,0:T(8,128)(2,1)S(1)}, ...), condition=%wide.region_3.4_spmd.clone, body=%wide.region_0.3_spmd.clone.sunk | while | flops 8625410 | bytes 3090301 | solution.py:146
  60.2 55.3 %while.54 = (s32[]{:T(128)}, f32[16,2,4,512]{3,2,1,0:T(4,128)S(1)}, pred[1,1,1,1]{3,2,1,0:T(4,128)(4,1)}, bf16[16,64,2,2,1,128]{5,1,3,2,4,0:T(8,128)(2,1)S(1)}, ...) while((s32[]{:T(128)}, f32[16,2,4,512]{3,2,1,0:T(4,128)S(1)}, ...), condition=%wide.region_7.8_spmd.clone, body=%wide.region_4.7_spmd.clone.sunk | while | flops 8627970 | bytes 3127154 | solution.py:146
  115.5 58.9 %conditional.1 = (f32[32,4,512]{2,0,1:T(8,128)S(1)}) conditional(s32[]{:T(128)} %convert_element_type.86, () %tuple.64, (bf16[2,32,32,128]{3,2,1,0:T(8,128)(2,1)S(1)}, bf16[2,32,32,128]{3,1,2,0:T(8,128)(2,1)}, s32[4]{0:T(128)S(1)}, s32[1]{0:T(128)}, s32[]{:T(128)}, /*index=5*/s32[]{:T(128)}, s32[]{:T(128)}, s32[]{:T(128)}, s32[]{:T(128)}) %tuple.180), branch_computations={%region_8.9_spmd, %region_9.14_spmd} | conditional | flops 14001928 | bytes 10205197 | solution.py:179
  119.1 55.3 %while.52 = (s32[]{:T(128)}, f32[16,2,4,512]{3,2,1,0:T(4,128)S(1)}, pred[1,1,1,1]{3,2,1,0:T(4,128)(4,1)}, bf16[16,64,2,2,1,128]{5,1,3,2,4,0:T(8,128)(2,1)S(1)}, ...) while((s32[]{:T(128)}, f32[16,2,4,512]{3,2,1,0:T(4,128)S(1)}, ...), condition=%wide.region_13.13_spmd.clone, body=%wide.region_10.12_spmd.clone.sunk | while | flops 8627970 | bytes 3127154 | solution.py:146
  175.6 18.7 %reduce-scatter.3.cloned.1.call-done = f32[32,1,512]{2,0,1:T(8,128)} async-done(((f32[32,4,512]{2,0,1:T(8,128)}), f32[32,1,512]{2,0,1:T(8,128)}) %reduce-scatter.3.cloned.1.call-update) | async-done | bytes 65552 | tf_op jit(solution)/shard_map/reduce_scatter | solution.py:185
  195.2 59.1 %while.55 = (s32[]{:T(128)}, f32[256,512]{1,0:T(8,128)S(1)}, f32[8,4,1,512]{3,2,1,0:T(1,128)S(1)}, s32[8,4]{1,0:T(8,128)S(1)}, s32[1,1,1]{2,1,0:T(1,128)}, /*index=5*/s32[]{:T(128)}, s32[]{:T(128)}) while((s32[]{:T(128)}, f32[256,512]{1,0:T(8,128)S(1)}, f32[8,4,1,512]{3,2,1,0:T(1,128)S(1)}, s32[8,4]{1,0:T(8,128)S(1)}, ...), condition=%wide.region_16.17_spmd.clone, body=%wide.region_15.16_spmd.clone.sunk | while | flops 32566532 | bytes 7446707 | solution.py:96
  195.3 4.2 %fusion.103 = (f32[4,256,256]{2,1,0:T(8,128)S(1)}, f32[4,256,256]{2,1,0:T(8,128)S(1)}, f32[4,256,256]{2,1,0:T(8,128)S(1)}) fusion(s32[256]{0:T(256)S(1)} %iota_add_fusion.2, s32[4,256]{1,0:T(4,128)S(1)} %broadcast_multiply_fusion.3), kind=kLoop, calls=%fused_computation.20.clone.2 | loop fusion | flops 3932160 | bytes 3150848 | tf_op jit(solution)/shard_map/while/body/eval_jaxpr/sin | solution.py:56
  199.5 2.1 fusion.104
  202.7 4.2 %fusion.103 = (f32[4,256,256]{2,1,0:T(8,128)S(1)}, f32[4,256,256]{2,1,0:T(8,128)S(1)}, f32[4,256,256]{2,1,0:T(8,128)S(1)}) fusion(s32[256]{0:T(256)S(1)} %iota_add_fusion.2, s32[4,256]{1,0:T(4,128)S(1)} %broadcast_multiply_fusion.3), kind=kLoop, calls=%fused_computation.20.clone.2 | loop fusion | flops 3932160 | bytes 3150848 | tf_op jit(solution)/shard_map/while/body/eval_jaxpr/sin | solution.py:56
  206.9 2.1 fusion.104
  210.1 4.2 %fusion.103 = (f32[4,256,256]{2,1,0:T(8,128)S(1)}, f32[4,256,256]{2,1,0:T(8,128)S(1)}, f32[4,256,256]{2,1,0:T(8,128)S(1)}) fusion(s32[256]{0:T(256)S(1)} %iota_add_fusion.2, s32[4,256]{1,0:T(4,128)S(1)} %broadcast_multiply_fusion.3), kind=kLoop, calls=%fused_computation.20.clone.2 | loop fusion | flops 3932160 | bytes 3150848 | tf_op jit(solution)/shard_map/while/body/eval_jaxpr/sin | solution.py:56
  214.3 2.1 fusion.104
  217.5 4.2 %fusion.103 = (f32[4,256,256]{2,1,0:T(8,128)S(1)}, f32[4,256,256]{2,1,0:T(8,128)S(1)}, f32[4,256,256]{2,1,0:T(8,128)S(1)}) fusion(s32[256]{0:T(256)S(1)} %iota_add_fusion.2, s32[4,256]{1,0:T(4,128)S(1)} %broadcast_multiply_fusion.3), kind=kLoop, calls=%fused_computation.20.clone.2 | loop fusion | flops 3932160 | bytes 3150848 | tf_op jit(solution)/shard_map/while/body/eval_jaxpr/sin | solution.py:56
  221.7 2.1 fusion.104
  224.9 4.2 %fusion.103 = (f32[4,256,256]{2,1,0:T(8,128)S(1)}, f32[4,256,256]{2,1,0:T(8,128)S(1)}, f32[4,256,256]{2,1,0:T(8,128)S(1)}) fusion(s32[256]{0:T(256)S(1)} %iota_add_fusion.2, s32[4,256]{1,0:T(4,128)S(1)} %broadcast_multiply_fusion.3), kind=kLoop, calls=%fused_computation.20.clone.2 | loop fusion | flops 3932160 | bytes 3150848 | tf_op jit(solution)/shard_map/while/body/eval_jaxpr/sin | solution.py:56
  229.1 2.1 fusion.104
  232.3 4.2 %fusion.103 = (f32[4,256,256]{2,1,0:T(8,128)S(1)}, f32[4,256,256]{2,1,0:T(8,128)S(1)}, f32[4,256,256]{2,1,0:T(8,128)S(1)}) fusion(s32[256]{0:T(256)S(1)} %iota_add_fusion.2, s32[4,256]{1,0:T(4,128)S(1)} %broadcast_multiply_fusion.3), kind=kLoop, calls=%fused_computation.20.clone.2 | loop fusion | flops 3932160 | bytes 3150848 | tf_op jit(solution)/shard_map/while/body/eval_jaxpr/sin | solution.py:56
  236.4 2.1 fusion.104
  239.7 4.2 %fusion.103 = (f32[4,256,256]{2,1,0:T(8,128)S(1)}, f32[4,256,256]{2,1,0:T(8,128)S(1)}, f32[4,256,256]{2,1,0:T(8,128)S(1)}) fusion(s32[256]{0:T(256)S(1)} %iota_add_fusion.2, s32[4,256]{1,0:T(4,128)S(1)} %broadcast_multiply_fusion.3), kind=kLoop, calls=%fused_computation.20.clone.2 | loop fusion | flops 3932160 | bytes 3150848 | tf_op jit(solution)/shard_map/while/body/eval_jaxpr/sin | solution.py:56
  243.8 2.1 fusion.104
  247.0 4.2 %fusion.103 = (f32[4,256,256]{2,1,0:T(8,128)S(1)}, f32[4,256,256]{2,1,0:T(8,128)S(1)}, f32[4,256,256]{2,1,0:T(8,128)S(1)}) fusion(s32[256]{0:T(256)S(1)} %iota_add_fusion.2, s32[4,256]{1,0:T(4,128)S(1)} %broadcast_multiply_fusion.3), kind=kLoop, calls=%fused_computation.20.clone.2 | loop fusion | flops 3932160 | bytes 3150848 | tf_op jit(solution)/shard_map/while/body/eval_jaxpr/sin | solution.py:56
  255.1 32.5 %reduce-scatter.5.cloned.1.call-done = f32[32,512]{1,0:T(8,128)} async-done(((f32[256,512]{1,0:T(8,128)}), f32[32,512]{1,0:T(8,128)}) %reduce-scatter.5.cloned.1.call-update) | async-done | bytes 65552 | tf_op jit(solution)/shard_map/reduce_scatter | solution.py:189
  (1068 shorter events, 171.0 us)
Async XLA Ops:
  6.5 5.1 %copy-start.1 = (bf16[2,32,32,128]{3,2,1,0:T(8,128)(2,1)S(1)}, bf16[2,32,32,128]{3,2,1,0:T(8,128)(2,1)}, u32[]{:S(2)}) copy-start(bf16[2,32,32,128]{3,2,1,0:T(8,128)(2,1)} %param.12) | copy-start | bytes 1572868
  6.5 187.8 %reduce-scatter.3.cloned.1.call-start = ((), (), s32[]{:S(2)}) async-start(), calls=%async_computation.2 | async-start | bytes 327680 | tf_op jit(solution)/shard_map/reduce_scatter | solution.py:185
  8.6 48.6 %collective-permute-start = (bf16[2,32,32,128]{3,1,2,0:T(8,128)(2,1)}, bf16[2,32,32,128]{3,1,2,0:T(8,128)(2,1)}, u32[]{:S(2)}, u32[]{:S(2)}) collective-permute-start(bf16[2,32,32,128]{3,1,2,0:T(8,128)(2,1)} %copy.28), channel_id=1, source_target_pairs={{0,8},{8,16},{16,24},{24,0},{1,9},{9,17},{17,25},{25,1},{2,10},{10... | collective-permute-start | bytes 1572872 | tf_op jit(solution)/shard_map/ppermute | solution.py:18
  12.3 43.0 %copy-start.2 = (s32[4]{0:T(128)S(1)}, s32[4]{0:T(128)}, u32[]{:S(2)}) copy-start(s32[4]{0:T(128)} %param.13) | copy-start | bytes 52
  58.5 57.0 %collective-permute-start.1 = (bf16[2,32,32,128]{3,1,2,0:T(8,128)(2,1)}, bf16[2,32,32,128]{3,1,2,0:T(8,128)(2,1)}, u32[]{:S(2)}, u32[]{:S(2)}) collective-permute-start(bf16[2,32,32,128]{3,1,2,0:T(8,128)(2,1)} %collective-permute-done), channel_id=1, source_target_pairs={{0,8},{8,16},{16,24},{24,0},{1,9},{9,17},{17,25},{25,1},{2,10},{10... | collective-permute-start | bytes 1572872 | tf_op jit(solution)/shard_map/ppermute | solution.py:18
  175.3 112.4 %reduce-scatter.5.cloned.1.call-start = ((), (), s32[]{:S(2)}) async-start(), calls=%async_computation.3 | async-start | bytes 589824 | tf_op jit(solution)/shard_map/reduce_scatter | solution.py:189
  254.3 0.8 copy-start
Sparse Core Ops, SparseCore 0:
  175.4 18.8 reduce-scatter.2
  255.3 32.3 reduce-scatter.4
where the time goes:
time: 296 us
  local copies, waits for them, and re-layouts  128 us (43%)
  other arithmetic  58.3 us (20%)
  waiting for transfers between devices  51.3 us (17%)
  matrix products  33.3 us (11%)
  between operations  14.9 us (5%)
  loops' own time  5.78 us (2%)
  starting transfers between devices  4.88 us (2%)
    reshape x96, local copies, waits for them, and re-layouts, lag_sums(): skewed = padded.reshape(leading + (extent, extent + 1))  55.5 us
    pad x48, local copies, waits for them, and re-layouts, lag_sums(): padded = jnp.pad(flat_panel, [(0, 0)] * len(leading) + [(0, extent)])  37.3 us
    sin x8, other arithmetic, slant_terms(): sine_part = jnp.sin(lag_angle)  33.4 us
    reduce_scatter x1, waiting for transfers between devices, shards(): lax.psum_scatter(image_term, 'freq', scatter_dimension=0, tiled=True)  32.5 us
    reduce_scatter x1, waiting for transfers between devices, shards(): shares = lax.psum_scatter(stacks, 'chan', scatter_dimension=1, tiled=True)  18.7 us
    while x176, local copies, waits for them, and re-layouts  16.7 us
    dot_general x8, matrix products, slant_terms(): jnp.einsum('fdk,fkp->fdp', means_block, lag_table, precision=lax.Precisio...  16.7 us
    dot_general x48, matrix products, one_block(): jnp.einsum('kfar,kfpbe->fabpre', block_item[0], block_item[1], preferred_...  11.1 us
  transfers between devices with their start and end apart: 4, of which 2 were waited for; matrix products, arithmetic and copies ran while one was open for 33% of the time, Pallas kernels for 0%

commit v1 on v0

v1 whole, which is shorter than its diff:
```python
import functools
import math

import jax
import jax.numpy as jnp
import numpy as np
from jax import lax
from jax.experimental import pallas as pl
from jax.experimental.pallas import tpu as pltpu
from jax.sharding import PartitionSpec as P

SEGMENTS = 32
FREQS = 256
BLOCK = 128
SLOWNESS = 256
LAG_TIMES = 512
MODULUS = 8 * FREQS * BLOCK


def unit_phase(numerator):
    quarter = MODULUS // 4
    turn = numerator & (MODULUS - 1)
    quadrant = lax.shift_right_logical(turn + quarter // 2, quarter.bit_length() - 1)
    x = (turn - quadrant * quarter).astype(jnp.float32) * (2.0 * math.pi / MODULUS)
    y = x * x
    sine = x * (1.0 + y * (-1.0 / 6 + y * (1.0 / 120 + y * (-1.0 / 5040 + y * (1.0 / 362880)))))
    cosine = 1.0 + y * (-0.5 + y * (1.0 / 24 + y * (-1.0 / 720 + y * (1.0 / 40320))))
    odd = (quadrant & 1) == 1
    first = jnp.where(odd, sine, cosine)
    second = jnp.where(odd, cosine, sine)
    first = jnp.where(((quadrant + 1) & 2) == 2, -first, first)
    second = jnp.where((quadrant & 2) == 2, -second, second)
    return first, second


def halves(value):
    high = value.astype(jnp.bfloat16)
    return high, (value - high.astype(jnp.float32)).astype(jnp.bfloat16)


def stack_kernel(groups, bins, spec_ref, position_ref, start_ref, weight_ref, out_ref, wide_ref):
    rows = spec_ref.shape[1] // bins
    windows = rows // 2
    for place in range(groups):
        block = jnp.int32(0)
        for group in range(groups):
            block = jnp.where(position_ref[group] == place, group, block)
        wide_ref[place] = spec_ref[block].astype(jnp.float32)

    row_index = lax.broadcasted_iota(jnp.int32, (BLOCK, BLOCK), 0)
    lag_index = lax.broadcasted_iota(jnp.int32, (BLOCK, BLOCK), 1)
    mirror = jnp.where(row_index + lag_index == BLOCK - 1, 1.0, 0.0).astype(jnp.bfloat16)
    ahead = lag_index <= row_index
    ahead = jnp.concatenate([ahead, ahead], axis=1)
    low_rows = lax.broadcasted_iota(jnp.int32, (8, SLOWNESS), 0)
    high_rows = lax.broadcasted_iota(jnp.int32, (16, SLOWNESS), 0) * 8
    shift_rows = lax.broadcasted_iota(jnp.int32, (2 * groups, SLOWNESS), 0)
    shift_rows = jnp.where(shift_rows < groups, shift_rows, shift_rows - groups - 1) * BLOCK

    def slow(shape):
        return lax.broadcasted_iota(jnp.int32, shape, 1) - SLOWNESS // 2

    for f in range(bins):
        left, right = [], []
        for place in range(groups):
            value = wide_ref[place, pl.ds(f, rows, stride=bins), :]
            real, imag = value[:windows], value[windows:]
            left.append(value)
            right.append(
                jnp.concatenate(
                    [jnp.concatenate([real, imag], 1), jnp.concatenate([imag, -real], 1)], 0
                )
            )
        left = lax.dot_general(
            mirror,
            jnp.concatenate(left, 0).astype(jnp.bfloat16),
            (((1,), (1,)), ((), ())),
            preferred_element_type=jnp.float32,
        ).astype(jnp.bfloat16)
        right = jnp.concatenate(right, 0).astype(jnp.bfloat16)
        forward, backward = [], []
        for delta in range(groups):
            panel = jnp.dot(
                left[:, : rows * (groups - delta)],
                right[rows * delta :],
                preferred_element_type=jnp.float32,
            )
            skewed = jnp.concatenate(
                [
                    pltpu.roll(panel[:, :BLOCK], 1, 1, stride=1, stride_axis=0),
                    pltpu.roll(panel[:, BLOCK:], 1, 1, stride=1, stride_axis=0),
                ],
                axis=1,
            )
            forward.append(jnp.sum(jnp.where(ahead, skewed, 0.0), 0, keepdims=True))
            backward.append(jnp.sum(jnp.where(ahead, 0.0, skewed), 0, keepdims=True))
        lags = jnp.concatenate(forward + backward, 0)
        weight = weight_ref[...]
        means = jnp.concatenate([lags[:, :BLOCK] * weight, lags[:, BLOCK:] * weight], 0)
        mean_high, mean_low = halves(means)
        spread = jnp.concatenate(
            [
                jnp.concatenate([mean_high, mean_high], 1),
                jnp.concatenate([mean_low, jnp.zeros_like(mean_low)], 1),
            ],
            0,
        )
        freq = start_ref[0] + f
        low_cos, low_sin = unit_phase(freq * slow(low_rows.shape) * low_rows)
        high_cos, high_sin = unit_phase(freq * slow(high_rows.shape) * high_rows)
        low_cos, low_sin = low_cos[None], low_sin[None]
        high_cos, high_sin = high_cos[:, None], high_sin[:, None]
        lag_cos = (high_cos * low_cos - high_sin * low_sin).reshape(BLOCK, SLOWNESS)
        lag_sin = (high_sin * low_cos + high_cos * low_sin).reshape(BLOCK, SLOWNESS)
        cos_high, cos_low = halves(lag_cos)
        sin_high, sin_low = halves(lag_sin)
        by_cos = jnp.dot(
            spread, jnp.concatenate([cos_high, cos_low], 0), preferred_element_type=jnp.float32
        )
        by_sin = jnp.dot(
            spread, jnp.concatenate([sin_high, sin_low], 0), preferred_element_type=jnp.float32
        )
        by_cos = by_cos[: 4 * groups] + by_cos[4 * groups :]
        by_sin = by_sin[: 4 * groups] + by_sin[4 * groups :]
        real = by_cos[: 2 * groups] - by_sin[2 * groups :]
        imag = by_sin[: 2 * groups] + by_cos[2 * groups :]
        shift_cos, shift_sin = unit_phase(freq * slow(shift_rows.shape) * shift_rows)
        turned_re = real * shift_cos - imag * shift_sin
        turned_im = real * shift_sin + imag * shift_cos
        out_ref[f, 0] = turned_re[:groups] + turned_re[groups:]
        out_ref[f, 1] = turned_im[:groups] + turned_im[groups:]


def inverse_counts(nblocks):
    delta = np.arange(nblocks)[:, None]
    lag = np.arange(BLOCK)[None, :]
    rows = []
    for lags in (lag, lag - BLOCK):
        usable = (lags > -BLOCK) & ((delta >= 1) | (lags >= 1))
        count = SEGMENTS * (nblocks - delta) * (BLOCK - np.abs(lags))
        rows.append(np.where(usable, 1.0 / np.maximum(count, 1), 0.0))
    return np.concatenate(rows, 0) * math.sqrt(SEGMENTS / FREQS)


def time_table(groups, parts):
    bins = FREQS // parts // groups
    group, part, f = np.meshgrid(
        np.arange(groups), np.arange(parts), np.arange(bins), indexing="ij"
    )
    freq = (part * groups + group) * bins + f
    lag_time = np.arange(LAG_TIMES) - LAG_TIMES // 2
    angle = 2.0 * math.pi / LAG_TIMES * ((freq[..., None] * lag_time) % LAG_TIMES)
    table = np.stack([np.cos(angle), -np.sin(angle)], axis=3)
    return table.reshape(groups * parts, bins, 2, LAG_TIMES).astype(np.float32)


def shards(spectra, block_position):
    groups = lax.axis_size("chan")
    parts = lax.axis_size("freq")
    rows = spectra.shape[0] * spectra.shape[1]
    freq_dev = spectra.shape[2]
    bins = freq_dev // groups
    first_bin = lax.axis_index("freq") * freq_dev + lax.axis_index("chan") * bins

    chunks = spectra.reshape(rows, groups, bins, BLOCK)
    gathered = lax.all_to_all(chunks, "chan", split_axis=1, concat_axis=0, tiled=False)
    gathered = gathered.reshape(groups, rows * bins, BLOCK)
    terms = pl.pallas_call(
        functools.partial(stack_kernel, groups, bins),
        out_shape=jax.ShapeDtypeStruct((bins, 2, groups, SLOWNESS), jnp.float32),
        in_specs=[
            pl.BlockSpec(memory_space=pltpu.VMEM),
            pl.BlockSpec(memory_space=pltpu.SMEM),
            pl.BlockSpec(memory_space=pltpu.SMEM),
            pl.BlockSpec(memory_space=pltpu.VMEM),
        ],
        out_specs=pl.BlockSpec(memory_space=pltpu.VMEM),
        scratch_shapes=[pltpu.VMEM((groups, rows * bins, BLOCK), jnp.float32)],
        compiler_params=pltpu.CompilerParams(vmem_limit_bytes=32 * 1024 * 1024),
        name="stack_and_slant",
    )(
        gathered,
        block_position,
        first_bin.astype(jnp.int32).reshape(1),
        jnp.asarray(inverse_counts(groups), jnp.float32),
    )
    slow_dev = SLOWNESS // parts
    terms = terms.reshape(bins, 2, groups, parts, slow_dev).transpose(2, 3, 0, 1, 4)
    terms = terms.reshape(groups * parts, bins, 2, slow_dev)
    arrived = lax.all_to_all(terms, ("chan", "freq"), split_axis=0, concat_axis=0, tiled=True)
    image = jnp.einsum(
        "gfcs,gfct->st",
        arrived,
        jnp.asarray(time_table(groups, parts)),
        precision=lax.Precision.HIGHEST,
    )
    return image[None]


def solution(mesh):
    return jax.shard_map(
        shards,
        mesh=mesh,
        in_specs=(P(None, None, "freq", "chan"), P()),
        out_specs=P("chan", "freq", None),
        check_vma=False,
    )
```

time: 296 us -> 43.1 us (0.15)
  local copies, waits for them, and re-layouts: 128 us -> 3.66 us
  other arithmetic: 58.3 us -> 0.8 us
  waiting for transfers between devices: 51.3 us -> 14.5 us
  matrix products: 33.3 us -> 1.42 us
  between operations: 14.9 us -> 0.06 us
  blocking collectives: 0 us -> 10.9 us
  loops' own time: 5.78 us -> 0 us
  Pallas kernels: 0 us -> 5.17 us
    reshape x97 -> x2, local copies, waits for them, and re-layouts: 55.6 us -> 0.29 us  [shards(): terms.reshape(bins, 2, groups, parts, slow_dev).transpose(2, 3, 0, 1, 4)]
    reduce_scatter x2 -> x0, waiting for transfers between devices: 51.2 us -> none  [the longest x1 32.5 us: shards(): lax.psum_scatter(image_term, 'freq', scatter_dimension=0, tiled=True)]
    pad x48 -> x0, local copies, waits for them, and re-layouts: 37.3 us -> none  [lag_sums(): padded = jnp.pad(flat_panel, [(0, 0)] * len(leading) + [(0, extent)])]
    sin x8 -> x0, other arithmetic: 33.4 us -> none  [slant_terms(): sine_part = jnp.sin(lag_angle)]
    dot_general x64 -> x1, matrix products: 33.3 us -> 1.42 us  [shards(): jnp.einsum('gfcs,gfct->st', arrived, jnp.asarray(time_table(groups, parts...]
    while x176 -> x0, local copies, waits for them, and re-layouts: 16.7 us -> none
    all_to_all x0 -> x1, waiting for transfers between devices: none -> 14.5 us  [shards(): lax.all_to_all(chunks, 'chan', split_axis=1, concat_axis=0, tiled=False)]
    all_to_all x0 -> x1, blocking collectives: none -> 10.9 us  [shards(): lax.all_to_all(terms, ('chan', 'freq'), split_axis=0, concat_axis=0, tile...]
  transfers between devices with their start and end apart: 4 -> 1, of which waited for: 2 -> 1; matrix products, arithmetic and copies ran while one was open for 33% -> 0% of each run, Pallas kernels for 0% -> 0%
where the time goes in v1:
time: 43.1 us; the launch traced here: 42.8 us
  waiting for transfers between devices  14.5 us (34%)
  blocking collectives  10.9 us (25%)
  starting transfers between devices  6.32 us (15%)
  Pallas kernels  5.17 us (12%)
  local copies, waits for them, and re-layouts  3.66 us (8%)
  matrix products  1.42 us (3%)
  other arithmetic  0.8 us (2%)
    all_to_all x1, waiting for transfers between devices, shards(): lax.all_to_all(chunks, 'chan', split_axis=1, concat_axis=0, tiled=False)  14.5 us
    all_to_all x1, blocking collectives, shards(): lax.all_to_all(terms, ('chan', 'freq'), split_axis=0, concat_axis=0, tile...  10.9 us
    all_to_all x1, starting transfers between devices, shards(): lax.all_to_all(chunks, 'chan', split_axis=1, concat_axis=0, tiled=False)  6.32 us
    pallas_call x1, Pallas kernels, shards(): pl.pallas_call(functools.partial(stack_kernel, groups, bins), out_shape=j...  5.17 us
    another operation x1, local copies, waits for them, and re-layouts, shards(): lax.all_to_all(chunks, 'chan', split_axis=1, concat_axis=0, tiled=False)  1.92 us
    dot_general x1, matrix products, shards(): jnp.einsum('gfcs,gfct->st', arrived, jnp.asarray(time_table(groups, parts...  1.42 us
    unnamed x8, local copies, waits for them, and re-layouts  0.93 us
  transfers between devices with their start and end apart: 1, of which 1 were waited for; matrix products, arithmetic and copies ran while one was open for 0% of the time, Pallas kernels for 0%

profile of v1, /device:TPU:0, one launch (start us, length us, event | category | flops | bytes accessed | tf_op | source)
XLA Modules:
  0.0 42.8 jit_solution(10999673614995200218)
XLA Ops:
  0.0 1.9 %copy.12 = bf16[1,64,4,8,128]{4,3,1,0,2:T(8,128)(2,1)} copy(bf16[1,64,4,8,128]{4,3,2,1,0:T(8,128)(2,1)} %bitcast.22) | data formatting | bytes 1048576 | tf_op jit(solution)/shard_map/broadcast_in_dim;reshape | solution.py:166
  1.9 6.3 %all-to-all-start = ((bf16[1,64,4,8,128]{4,3,1,0,2:T(8,128)(2,1)}), bf16[1,64,4,8,128]{4,3,1,0,2:T(8,128)(2,1)S(1)}, u32[]{:S(2)}, u32[]{:S(2)}) async-start(bf16[1,64,4,8,128]{4,3,1,0,2:T(8,128)(2,1)} %copy.12), calls=%async_computation | async-start | bytes 1048576 | tf_op jit(solution)/shard_map/all_to_all | solution.py:166
  8.2 0.0 copy-start
  8.2 14.5 %all-to-all-done = bf16[1,64,4,8,128]{4,3,1,0,2:T(8,128)(2,1)S(1)} async-done(((bf16[1,64,4,8,128]{4,3,1,0,2:T(8,128)(2,1)}), bf16[1,64,4,8,128]{4,3,1,0,2:T(8,128)(2,1)S(1)}, u32[]{:S(2)}, u32[]{:S(2)}) %all-to-all-start) | async-done | bytes 524320 | tf_op jit(solution)/shard_map/all_to_all | solution.py:166
  22.7 0.0 copy-start.1
  22.7 0.0 copy-done
  22.7 0.7 %copy-done.1 = s32[4]{0:T(128)S(1)} copy-done((s32[4]{0:T(128)S(1)}, s32[4]{0:T(128)}, u32[]{:S(2)}) %copy-start.1) | copy-done | bytes 40
  23.4 0.0 copy-start.2
  23.4 5.2 %stack_and_slant.1 = f32[8,2,4,256]{3,2,1,0:T(4,128)S(1)} custom-call(bf16[4,512,128]{2,1,0:T(8,128)(2,1)S(1)} %bitcast.19, s32[4]{0:T(128)S(1)} %copy-done.1, s32[1]{0:T(128)} %bitcast.4.start_ref, f32[8,128]{1,0:T(8,128)S(1)} %copy-done), custom_call_target="tpu_custom_call" | custom-call | tf_op jit(solution)/shard_map/stack_and_slant/pallas_call | solution.py:168
  28.6 0.1 reshape.11
  28.7 0.2 copy.13
  28.9 0.2 reshape.14
  29.0 10.9 %all_to_all.20 = f32[32,1,512]{2,1,0:T(1,128)S(1)} all-to-all(f32[32,1,512]{2,1,0:T(1,128)S(1)} %reshape.14), channel_id=1, replica_groups=mesh['chan'=4,'freq'=8] {'chan','freq'}, dimensions={0} | all-to-all | bytes 131072 | tf_op jit(solution)/shard_map/all_to_all | solution.py:190
  40.0 0.5 %broadcast = f32[]{:T(128)} broadcast(f32[]{:T(128)} %constant.18), dimensions={} | broadcast | bytes 8 | tf_op jit(solution)/shard_map/all_to_all | solution.py:190
  40.5 0.8 %reduce = f32[32,512]{1,0:T(8,128)S(1)} reduce(f32[32,1,512]{2,1,0:T(1,128)S(1)} %all_to_all.20, f32[]{:T(128)} %broadcast), dimensions={1}, to_apply=%all_to_all.17.reduce_sub_computation | reduce | bytes 131076 | tf_op jit(solution)/shard_map/all_to_all | solution.py:190
  41.3 0.1 reshape.15
  41.4 0.0 copy-done.2
  41.4 1.4 %convolution_bitcast_fusion = f32[1,32,512]{2,1,0:T(8,128)} fusion(f32[32,8,2,512]{3,0,1,2:T(8,128)S(1)} %copy-done.2, f32[32,8,2,32]{3,1,2,0:T(8,128)S(1)} %bitcast.21), kind=kOutput, calls=%fused_computation | convolution fusion | flops 100663296 | bytes 1179648 | tf_op jit(solution)/shard_map/gfcs,gfct->st/dot_general | solution.py:191
Async XLA Ops:
  1.9 20.8 %all-to-all-start = ((bf16[1,64,4,8,128]{4,3,1,0,2:T(8,128)(2,1)}), bf16[1,64,4,8,128]{4,3,1,0,2:T(8,128)(2,1)S(1)}, u32[]{:S(2)}, u32[]{:S(2)}) async-start(bf16[1,64,4,8,128]{4,3,1,0,2:T(8,128)(2,1)} %copy.12), calls=%async_computation | async-start | bytes 1048576 | tf_op jit(solution)/shard_map/all_to_all | solution.py:166
  8.2 14.5 %copy-start = (f32[8,128]{1,0:T(8,128)S(1)}, f32[8,128]{1,0:T(8,128)}, u32[]{:S(2)}) copy-start(f32[8,128]{1,0:T(8,128)} %constant.16.clone.weight_ref) | copy-start | bytes 12292
  22.7 0.7 %copy-start.1 = (s32[4]{0:T(128)S(1)}, s32[4]{0:T(128)}, u32[]{:S(2)}) copy-start(s32[4]{0:T(128)} %position_ref.1) | copy-start | bytes 52
  23.4 18.0 %copy-start.2 = (f32[32,8,2,512]{3,0,1,2:T(8,128)S(1)}, f32[32,8,2,512]{3,0,1,2:T(8,128)}, u32[]{:S(2)}) copy-start(f32[32,8,2,512]{3,0,1,2:T(8,128)} %constant.17.clone) | copy-start | bytes 3145732

commit v2 on v1

--- a/solution.py
+++ b/solution.py
@@ -38,7 +38,41 @@
     return high, (value - high.astype(jnp.float32)).astype(jnp.bfloat16)
 
 
-def stack_kernel(groups, bins, spec_ref, position_ref, start_ref, weight_ref, out_ref, wide_ref):
+def table_kernel(groups, bins, freq_dev, lag_ref, shift_ref):
+    low_rows = lax.broadcasted_iota(jnp.int32, (8, SLOWNESS), 0)
+    high_rows = lax.broadcasted_iota(jnp.int32, (BLOCK // 8, SLOWNESS), 0) * 8
+    shift_rows = lax.broadcasted_iota(jnp.int32, (2 * groups, SLOWNESS), 0)
+    shift_rows = jnp.where(shift_rows < groups, shift_rows, shift_rows - groups - 1) * BLOCK
+    first_bin = lax.axis_index("freq") * freq_dev + lax.axis_index("chan") * bins
+
+    def one_bin(f, carry):
+        def phases(rows):
+            slow = lax.broadcasted_iota(jnp.int32, rows.shape, 1) - SLOWNESS // 2
+            return unit_phase((first_bin + f) * slow * rows)
+
+        low_cos, low_sin = phases(low_rows)
+        high_cos, high_sin = phases(high_rows)
+        low_cos, low_sin = low_cos[None], low_sin[None]
+        high_cos, high_sin = high_cos[:, None], high_sin[:, None]
+        lag_cos = (high_cos * low_cos - high_sin * low_sin).reshape(BLOCK, SLOWNESS)
+        lag_sin = (high_sin * low_cos + high_cos * low_sin).reshape(BLOCK, SLOWNESS)
+        cos_high, cos_low = halves(lag_cos)
+        sin_high, sin_low = halves(lag_sin)
+        lag_ref[f, :BLOCK, :SLOWNESS] = cos_high
+        lag_ref[f, BLOCK:, :SLOWNESS] = cos_low
+        lag_ref[f, :BLOCK, SLOWNESS:] = sin_high
+        lag_ref[f, BLOCK:, SLOWNESS:] = sin_low
+        shift_cos, shift_sin = phases(shift_rows)
+        shift_ref[f, 0] = shift_cos
+        shift_ref[f, 1] = shift_sin
+        return carry
+
+    lax.fori_loop(0, bins, one_bin, 0)
+
+
+def stack_kernel(
+    groups, bins, parts, spec_ref, position_ref, weight_ref, lag_ref, shift_ref, out_ref, wide_ref
+):
     rows = spec_ref.shape[1] // bins
     windows = rows // 2
     for place in range(groups):
@@ -52,14 +86,8 @@
     mirror = jnp.where(row_index + lag_index == BLOCK - 1, 1.0, 0.0).astype(jnp.bfloat16)
     ahead = lag_index <= row_index
     ahead = jnp.concatenate([ahead, ahead], axis=1)
-    low_rows = lax.broadcasted_iota(jnp.int32, (8, SLOWNESS), 0)
-    high_rows = lax.broadcasted_iota(jnp.int32, (16, SLOWNESS), 0) * 8
-    shift_rows = lax.broadcasted_iota(jnp.int32, (2 * groups, SLOWNESS), 0)
-    shift_rows = jnp.where(shift_rows < groups, shift_rows, shift_rows - groups - 1) * BLOCK
-
-    def slow(shape):
-        return lax.broadcasted_iota(jnp.int32, shape, 1) - SLOWNESS // 2
-
+
+    terms = []
     for f in range(bins):
         left, right = [], []
         for place in range(groups):
@@ -105,30 +133,43 @@
             ],
             0,
         )
-        freq = start_ref[0] + f
-        low_cos, low_sin = unit_phase(freq * slow(low_rows.shape) * low_rows)
-        high_cos, high_sin = unit_phase(freq * slow(high_rows.shape) * high_rows)
-        low_cos, low_sin = low_cos[None], low_sin[None]
-        high_cos, high_sin = high_cos[:, None], high_sin[:, None]
-        lag_cos = (high_cos * low_cos - high_sin * low_sin).reshape(BLOCK, SLOWNESS)
-        lag_sin = (high_sin * low_cos + high_cos * low_sin).reshape(BLOCK, SLOWNESS)
-        cos_high, cos_low = halves(lag_cos)
-        sin_high, sin_low = halves(lag_sin)
-        by_cos = jnp.dot(
-            spread, jnp.concatenate([cos_high, cos_low], 0), preferred_element_type=jnp.float32
-        )
-        by_sin = jnp.dot(
-            spread, jnp.concatenate([sin_high, sin_low], 0), preferred_element_type=jnp.float32
-        )
-        by_cos = by_cos[: 4 * groups] + by_cos[4 * groups :]
-        by_sin = by_sin[: 4 * groups] + by_sin[4 * groups :]
+        product = jnp.dot(spread, lag_ref[f], preferred_element_type=jnp.float32)
+        product = product[: 4 * groups] + product[4 * groups :]
+        by_cos, by_sin = product[:, :SLOWNESS], product[:, SLOWNESS:]
         real = by_cos[: 2 * groups] - by_sin[2 * groups :]
         imag = by_sin[: 2 * groups] + by_cos[2 * groups :]
-        shift_cos, shift_sin = unit_phase(freq * slow(shift_rows.shape) * shift_rows)
+        shift_cos, shift_sin = shift_ref[f, 0], shift_ref[f, 1]
         turned_re = real * shift_cos - imag * shift_sin
         turned_im = real * shift_sin + imag * shift_cos
-        out_ref[f, 0] = turned_re[:groups] + turned_re[groups:]
-        out_ref[f, 1] = turned_im[:groups] + turned_im[groups:]
+        terms.append(turned_re[:groups] + turned_re[groups:])
+        terms.append(turned_im[:groups] + turned_im[groups:])
+
+    slow_dev = SLOWNESS // parts
+    spans = BLOCK // slow_dev
+    span_index = lax.broadcasted_iota(jnp.int32, (groups, BLOCK), 1) // slow_dev
+    for part in range(parts):
+        source = (part % spans) * slow_dev
+        lanes = slice(part // spans * BLOCK, (part // spans + 1) * BLOCK)
+        for row in range(out_ref.shape[2]):
+            packed = jnp.zeros((groups, BLOCK), jnp.float32)
+            for span, term in enumerate(terms[row * spans : (row + 1) * spans]):
+                moved = pltpu.roll(term[:, lanes], (span * slow_dev - source) % BLOCK, 1)
+                packed = jnp.where(span_index == span, moved, packed)
+            out_ref[:, part, row, :] = packed
+
+
+def image_kernel(slow_dev, spans, term_ref, table_ref, out_ref):
+    arrived = term_ref[...]
+    turned = arrived.reshape(-1, BLOCK).T
+    turned = jnp.concatenate(
+        [turned[span * slow_dev : (span + 1) * slow_dev] for span in range(spans)], 1
+    )
+    high, low = halves(turned)
+    by_high = jnp.dot(
+        jnp.concatenate([high, low], 0), table_ref[0], preferred_element_type=jnp.float32
+    )
+    by_low = jnp.dot(high, table_ref[1], preferred_element_type=jnp.float32)
+    out_ref[0] = by_high[:slow_dev] + by_high[slow_dev:] + by_low
 
 
 def inverse_counts(nblocks):
@@ -142,16 +183,20 @@
     return np.concatenate(rows, 0) * math.sqrt(SEGMENTS / FREQS)
 
 
-def time_table(groups, parts):
-    bins = FREQS // parts // groups
-    group, part, f = np.meshgrid(
-        np.arange(groups), np.arange(parts), np.arange(bins), indexing="ij"
-    )
-    freq = (part * groups + group) * bins + f
+def time_table(groups, parts, bins, slow_dev, message_rows):
+    spans = min(BLOCK // slow_dev, 2 * bins)
+    span, group, part, row = np.meshgrid(
+        np.arange(spans), np.arange(groups), np.arange(parts), np.arange(message_rows), indexing="ij"
+    )
+    entry = row * spans + span
+    freq = (part * groups + group) * bins + entry // 2
     lag_time = np.arange(LAG_TIMES) - LAG_TIMES // 2
     angle = 2.0 * math.pi / LAG_TIMES * ((freq[..., None] * lag_time) % LAG_TIMES)
-    table = np.stack([np.cos(angle), -np.sin(angle)], axis=3)
-    return table.reshape(groups * parts, bins, 2, LAG_TIMES).astype(np.float32)
+    table = np.where((entry % 2 == 0)[..., None], np.cos(angle), -np.sin(angle))
+    table = table.reshape(-1, LAG_TIMES).astype(np.float32)
+    high = table.astype(jnp.bfloat16)
+    low = (table - high.astype(np.float32)).astype(jnp.bfloat16)
+    return spans, np.stack([high, low])
 
 
 def shards(spectra, block_position):
@@ -160,41 +205,52 @@
     rows = spectra.shape[0] * spectra.shape[1]
     freq_dev = spectra.shape[2]
     bins = freq_dev // groups
-    first_bin = lax.axis_index("freq") * freq_dev + lax.axis_index("chan") * bins
+    slow_dev = SLOWNESS // parts
+    message_rows = -(-2 * bins * slow_dev // BLOCK)
+    vmem = pl.BlockSpec(memory_space=pltpu.VMEM)
+    smem = pl.BlockSpec(memory_space=pltpu.SMEM)
+    params = pltpu.CompilerParams(vmem_limit_bytes=32 * 1024 * 1024)
 
     chunks = spectra.reshape(rows, groups, bins, BLOCK)
     gathered = lax.all_to_all(chunks, "chan", split_axis=1, concat_axis=0, tiled=False)
     gathered = gathered.reshape(groups, rows * bins, BLOCK)
+    lag_table, shift_table = pl.pallas_call(
+        functools.partial(table_kernel, groups, bins, freq_dev),
+        out_shape=(
+            jax.ShapeDtypeStruct((bins, 2 * BLOCK, 2 * SLOWNESS), jnp.bfloat16),
+            jax.ShapeDtypeStruct((bins, 2, 2 * groups, SLOWNESS), jnp.float32),
+        ),
+        out_specs=(vmem, vmem),
+        compiler_params=params,
+        cost_estimate=pl.CostEstimate(flops=10**7, bytes_accessed=4 * 10**6, transcendentals=0),
+        name="slant_tables",
+    )()
     terms = pl.pallas_call(
-        functools.partial(stack_kernel, groups, bins),
-        out_shape=jax.ShapeDtypeStruct((bins, 2, groups, SLOWNESS), jnp.float32),
-        in_specs=[
-            pl.BlockSpec(memory_space=pltpu.VMEM),
-            pl.BlockSpec(memory_space=pltpu.SMEM),
-            pl.BlockSpec(memory_space=pltpu.SMEM),
-            pl.BlockSpec(memory_space=pltpu.VMEM),
-        ],
-        out_specs=pl.BlockSpec(memory_space=pltpu.VMEM),
+        functools.partial(stack_kernel, groups, bins, parts),
+        out_shape=jax.ShapeDtypeStruct((groups, parts, message_rows, BLOCK), jnp.float32),
+        in_specs=[vmem, smem, vmem, vmem, vmem],
+        out_specs=vmem,
         scratch_shapes=[pltpu.VMEM((groups, rows * bins, BLOCK), jnp.float32)],
-        compiler_params=pltpu.CompilerParams(vmem_limit_bytes=32 * 1024 * 1024),
+        compiler_params=params,
         name="stack_and_slant",
     )(
         gathered,
         block_position,
-        first_bin.astype(jnp.int32).reshape(1),
         jnp.asarray(inverse_counts(groups), jnp.float32),
-    )
-    slow_dev = SLOWNESS // parts
-    terms = terms.reshape(bins, 2, groups, parts, slow_dev).transpose(2, 3, 0, 1, 4)
-    terms = terms.reshape(groups * parts, bins, 2, slow_dev)
+        lag_table,
+        shift_table,
+    )
+    terms = terms.reshape(groups * parts, message_rows, BLOCK)
     arrived = lax.all_to_all(terms, ("chan", "freq"), split_axis=0, concat_axis=0, tiled=True)
-    image = jnp.einsum(
-        "gfcs,gfct->st",
-        arrived,
-        jnp.asarray(time_table(groups, parts)),
-        precision=lax.Precision.HIGHEST,
-    )
-    return image[None]
+    spans, table = time_table(groups, parts, bins, slow_dev, message_rows)
+    return pl.pallas_call(
+        functools.partial(image_kernel, slow_dev, spans),
+        out_shape=jax.ShapeDtypeStruct((1, slow_dev, LAG_TIMES), jnp.float32),
+        in_specs=[vmem, vmem],
+        out_specs=vmem,
+        compiler_params=params,
+        name="sum_of_bins",
+    )(arrived, jnp.asarray(table))
 
 
 def solution(mesh):

time: 43.1 us -> 39.7 us (0.921)
  Pallas kernels: 5.17 us -> 6.94 us
  local copies, waits for them, and re-layouts: 3.66 us -> 1.96 us
  matrix products: 1.42 us -> 0 us
  waiting for transfers between devices: 14.5 us -> 13.4 us
  other arithmetic: 0.8 us -> 0 us
    pallas_call x1 -> x3, Pallas kernels: 5.17 us -> 6.94 us  [the longest x1 4.86 us: shards(): pl.pallas_call(functools.partial(stack_kernel, groups, bins, parts), out_...]
    dot_general x1 -> x0, matrix products: 1.42 us -> none  [shards(): jnp.einsum('gfcs,gfct->st', arrived, jnp.asarray(time_table(groups, parts...]
    all_to_all x1, waiting for transfers between devices: 14.5 us -> 13.4 us  [shards(): lax.all_to_all(chunks, 'chan', split_axis=1, concat_axis=0, tiled=False)]
    unnamed x8 -> x6, local copies, waits for them, and re-layouts: 0.93 us -> 0.01 us
    all_to_all x1 -> x0, other arithmetic: 0.8 us -> none  [shards(): lax.all_to_all(terms, ('chan', 'freq'), split_axis=0, concat_axis=0, tile...]
    all_to_all x1 -> x0, local copies, waits for them, and re-layouts: 0.51 us -> none  [shards(): lax.all_to_all(terms, ('chan', 'freq'), split_axis=0, concat_axis=0, tile...]
  transfers between devices with their start and end apart: 1 -> 1, of which waited for: 1 -> 1; matrix products, arithmetic and copies ran while one was open for 0% -> 0% of each run, Pallas kernels for 0% -> 3%
where the time goes in v2:
time: 39.7 us; the launch traced here: 39.5 us
  waiting for transfers between devices  13.4 us (34%)
  blocking collectives  10.9 us (27%)
  Pallas kernels  6.94 us (17%)
  starting transfers between devices  6.32 us (16%)
  local copies, waits for them, and re-layouts  1.96 us (5%)
    all_to_all x1, waiting for transfers between devices, shards(): lax.all_to_all(chunks, 'chan', split_axis=1, concat_axis=0, tiled=False)  13.4 us
    all_to_all x1, blocking collectives, shards(): lax.all_to_all(terms, ('chan', 'freq'), split_axis=0, concat_axis=0, tile...  10.9 us
    all_to_all x1, starting transfers between devices, shards(): lax.all_to_all(chunks, 'chan', split_axis=1, concat_axis=0, tiled=False)  6.32 us
    pallas_call x1, Pallas kernels, shards(): pl.pallas_call(functools.partial(stack_kernel, groups, bins, parts), out_...  4.86 us
    another operation x1, local copies, waits for them, and re-layouts, shards(): lax.all_to_all(chunks, 'chan', split_axis=1, concat_axis=0, tiled=False)  1.94 us
    pallas_call x1, Pallas kernels, shards(): pl.pallas_call(functools.partial(table_kernel, groups, bins, freq_dev), o...  1.11 us
    pallas_call x1, Pallas kernels, shards(): pl.pallas_call(functools.partial(image_kernel, slow_dev, spans), out_shap...  0.97 us
  transfers between devices with their start and end apart: 1, of which 1 were waited for; matrix products, arithmetic and copies ran while one was open for 0% of the time, Pallas kernels for 3%

profile of v2, /device:TPU:0, one launch (start us, length us, event | category | flops | bytes accessed | tf_op | source)
XLA Modules:
  0.0 39.5 jit_solution(4939788656814167366)
XLA Ops:
  0.0 0.0 copy-start.1
  0.0 0.0 copy-start.2
  0.0 1.9 %copy.6 = bf16[1,64,4,8,128]{4,3,1,0,2:T(8,128)(2,1)} copy(bf16[1,64,4,8,128]{4,3,2,1,0:T(8,128)(2,1)} %bitcast.9) | data formatting | bytes 1048576 | tf_op jit(solution)/shard_map/broadcast_in_dim;reshape | solution.py:215
  1.9 6.3 %all-to-all-start = ((bf16[1,64,4,8,128]{4,3,1,0,2:T(8,128)(2,1)}), bf16[1,64,4,8,128]{4,3,1,0,2:T(8,128)(2,1)S(1)}, u32[]{:S(2)}, u32[]{:S(2)}) async-start(bf16[1,64,4,8,128]{4,3,1,0,2:T(8,128)(2,1)} %copy.6), calls=%async_computation | async-start | bytes 1048576 | tf_op jit(solution)/shard_map/all_to_all | solution.py:215
  8.3 1.1 %slant_tables.1 = (bf16[8,256,512]{2,1,0:T(8,128)(2,1)S(1)}, f32[8,2,8,256]{3,2,1,0:T(8,128)S(1)}) custom-call(), custom_call_target="tpu_custom_call" | custom-call | flops 10000000 | bytes 4000000 | tf_op jit(solution)/shard_map/slant_tables/pallas_call | solution.py:217
  9.4 13.4 %all-to-all-done = bf16[1,64,4,8,128]{4,3,1,0,2:T(8,128)(2,1)S(1)} async-done(((bf16[1,64,4,8,128]{4,3,1,0,2:T(8,128)(2,1)}), bf16[1,64,4,8,128]{4,3,1,0,2:T(8,128)(2,1)S(1)}, u32[]{:S(2)}, u32[]{:S(2)}) %all-to-all-start) | async-done | bytes 524320 | tf_op jit(solution)/shard_map/all_to_all | solution.py:215
  22.8 0.0 copy-start
  22.8 0.0 copy-done.1
  22.8 0.0 copy-done.2
  22.8 4.9 %stack_and_slant.1 = f32[4,8,4,128]{3,2,1,0:T(4,128)S(1)} custom-call(bf16[4,512,128]{2,1,0:T(8,128)(2,1)S(1)} %bitcast.7, s32[4]{0:T(128)S(1)} %copy-done.2, f32[8,128]{1,0:T(8,128)S(1)} %copy-done.1, bf16[8,256,512]{2,1,0:T(8,128)(2,1)S(1)} %get-tuple-element.7.lag_ref, f32[8,2,8,256]{3,2,1,0:T(8,128)S(1)} %get-tuple-element.8.shift_ref), custom_call_target="tpu_custom_call" | custom-call | tf_op jit(solution)/shard_map/stack_and_slant/pallas_call | solution.py:228
  27.6 10.9 %all_to_all.20.term_ref = f32[32,4,128]{2,1,0:T(4,128)S(1)} all-to-all(f32[32,4,128]{2,1,0:T(4,128)S(1)} %bitcast.8), channel_id=1, replica_groups=mesh['chan'=4,'freq'=8] {'chan','freq'}, dimensions={0} | all-to-all | bytes 131072 | tf_op jit(solution)/shard_map/all_to_all | solution.py:244
  38.6 0.0 copy-done
  38.6 1.0 %sum_of_bins.1 = f32[1,32,512]{2,1,0:T(8,128)} custom-call(f32[32,4,128]{2,1,0:T(4,128)S(1)} %all_to_all.20.term_ref, bf16[2,512,512]{2,1,0:T(8,128)(2,1)S(1)} %copy-done), custom_call_target="tpu_custom_call" | custom-call | tf_op jit(solution)/shard_map/sum_of_bins/pallas_call | solution.py:246
Async XLA Ops:
  0.0 22.8 %copy-start.1 = (f32[8,128]{1,0:T(8,128)S(1)}, f32[8,128]{1,0:T(8,128)}, u32[]{:S(2)}) copy-start(f32[8,128]{1,0:T(8,128)} %constant.4.clone.weight_ref) | copy-start | bytes 12292
  0.0 22.8 %copy-start.2 = (s32[4]{0:T(128)S(1)}, s32[4]{0:T(128)}, u32[]{:S(2)}) copy-start(s32[4]{0:T(128)} %position_ref.1) | copy-start | bytes 52
  1.9 20.8 %all-to-all-start = ((bf16[1,64,4,8,128]{4,3,1,0,2:T(8,128)(2,1)}), bf16[1,64,4,8,128]{4,3,1,0,2:T(8,128)(2,1)S(1)}, u32[]{:S(2)}, u32[]{:S(2)}) async-start(bf16[1,64,4,8,128]{4,3,1,0,2:T(8,128)(2,1)} %copy.6), calls=%async_computation | async-start | bytes 1048576 | tf_op jit(solution)/shard_map/all_to_all | solution.py:215
  22.8 15.8 %copy-start = (bf16[2,512,512]{2,1,0:T(8,128)(2,1)S(1)}, bf16[2,512,512]{2,1,0:T(8,128)(2,1)}, u32[]{:S(2)}) copy-start(bf16[2,512,512]{2,1,0:T(8,128)(2,1)} %constant.5.clone.table_ref) | copy-start | bytes 3145732

commit v3 on v2

--- a/solution.py
+++ b/solution.py
@@ -70,16 +70,28 @@
     lax.fori_loop(0, bins, one_bin, 0)
 
 
-def stack_kernel(
-    groups, bins, parts, spec_ref, position_ref, weight_ref, lag_ref, shift_ref, out_ref, wide_ref
-):
-    rows = spec_ref.shape[1] // bins
+def chunk_kernel(groups, bins, spec_ref, *refs):
+    out_refs, wide_ref = refs[:-1], refs[-1]
+    wide_ref[...] = spec_ref[...].astype(jnp.float32)
+    freq_dev = groups * bins
+    rows = spec_ref.shape[0] // freq_dev
+    own_group = lax.axis_index("chan")
+    for distance, out_ref in enumerate(out_refs):
+        first = lax.rem(own_group + distance, groups) * bins
+        for f in range(bins):
+            value = wide_ref[pl.ds(first + f, rows, stride=freq_dev), :]
+            out_ref[f] = value.astype(jnp.bfloat16)
+
+
+def stack_kernel(groups, bins, parts, *refs):
+    chunk_refs = refs[:groups]
+    position_ref, weight_ref, lag_ref, shift_ref, out_ref, placed_ref = refs[groups:]
+    rows = placed_ref.shape[2]
     windows = rows // 2
-    for place in range(groups):
-        block = jnp.int32(0)
-        for group in range(groups):
-            block = jnp.where(position_ref[group] == place, group, block)
-        wide_ref[place] = spec_ref[block].astype(jnp.float32)
+    own_group = lax.axis_index("chan")
+    for distance, chunk_ref in enumerate(chunk_refs):
+        place = position_ref[lax.rem(own_group + (groups - distance), groups)]
+        placed_ref[place] = chunk_ref[...]
 
     row_index = lax.broadcasted_iota(jnp.int32, (BLOCK, BLOCK), 0)
     lag_index = lax.broadcasted_iota(jnp.int32, (BLOCK, BLOCK), 1)
@@ -91,7 +103,7 @@
     for f in range(bins):
         left, right = [], []
         for place in range(groups):
-            value = wide_ref[place, pl.ds(f, rows, stride=bins), :]
+            value = placed_ref[place, f]
             real, imag = value[:windows], value[windows:]
             left.append(value)
             right.append(
@@ -101,11 +113,11 @@
             )
         left = lax.dot_general(
             mirror,
-            jnp.concatenate(left, 0).astype(jnp.bfloat16),
+            jnp.concatenate(left, 0),
             (((1,), (1,)), ((), ())),
             preferred_element_type=jnp.float32,
         ).astype(jnp.bfloat16)
-        right = jnp.concatenate(right, 0).astype(jnp.bfloat16)
+        right = jnp.concatenate(right, 0)
         forward, backward = [], []
         for delta in range(groups):
             panel = jnp.dot(
@@ -211,9 +223,20 @@
     smem = pl.BlockSpec(memory_space=pltpu.SMEM)
     params = pltpu.CompilerParams(vmem_limit_bytes=32 * 1024 * 1024)
 
-    chunks = spectra.reshape(rows, groups, bins, BLOCK)
-    gathered = lax.all_to_all(chunks, "chan", split_axis=1, concat_axis=0, tiled=False)
-    gathered = gathered.reshape(groups, rows * bins, BLOCK)
+    chunk = jax.ShapeDtypeStruct((bins, rows, BLOCK), jnp.bfloat16)
+    chunks = pl.pallas_call(
+        functools.partial(chunk_kernel, groups, bins),
+        out_shape=(chunk,) * groups,
+        in_specs=[vmem],
+        out_specs=(vmem,) * groups,
+        scratch_shapes=[pltpu.VMEM((rows * freq_dev, BLOCK), jnp.float32)],
+        compiler_params=params,
+        name="chunks_of_bins",
+    )(spectra.reshape(rows * freq_dev, BLOCK))
+    arrived_chunks = list(chunks)
+    for distance in sorted(range(1, groups), key=lambda steps: abs(2 * steps - groups)):
+        pairs = [(source, (source + distance) % groups) for source in range(groups)]
+        arrived_chunks[distance] = lax.ppermute(chunks[distance], "chan", pairs)
     lag_table, shift_table = pl.pallas_call(
         functools.partial(table_kernel, groups, bins, freq_dev),
         out_shape=(
@@ -228,13 +251,13 @@
     terms = pl.pallas_call(
         functools.partial(stack_kernel, groups, bins, parts),
         out_shape=jax.ShapeDtypeStruct((groups, parts, message_rows, BLOCK), jnp.float32),
-        in_specs=[vmem, smem, vmem, vmem, vmem],
+        in_specs=[vmem] * groups + [smem, vmem, vmem, vmem],
         out_specs=vmem,
-        scratch_shapes=[pltpu.VMEM((groups, rows * bins, BLOCK), jnp.float32)],
+        scratch_shapes=[pltpu.VMEM((groups, bins, rows, BLOCK), jnp.bfloat16)],
         compiler_params=params,
         name="stack_and_slant",
     )(
-        gathered,
+        *arrived_chunks,
         block_position,
         jnp.asarray(inverse_counts(groups), jnp.float32),
         lag_table,

time: 39.7 us -> 37.3 us (0.940)
  waiting for transfers between devices: 13.4 us -> 6.18 us
  blocking collectives: 10.9 us -> 13.8 us
  starting transfers between devices: 6.32 us -> 7.01 us
  Pallas kernels: 6.94 us -> 7.58 us
  local copies, waits for them, and re-layouts: 1.96 us -> 2.48 us
    all_to_all x1 -> x0, waiting for transfers between devices: 13.4 us -> none  [shards(): lax.all_to_all(chunks, 'chan', split_axis=1, concat_axis=0, tiled=False)]
    ppermute x0 -> x3, starting transfers between devices: none -> 7.01 us  [shards(): arrived_chunks[distance] = lax.ppermute(chunks[distance], 'chan', pairs)]
    all_to_all x1 -> x0, starting transfers between devices: 6.32 us -> none  [shards(): lax.all_to_all(chunks, 'chan', split_axis=1, concat_axis=0, tiled=False)]
    ppermute x0 -> x3, waiting for transfers between devices: none -> 6.18 us  [shards(): arrived_chunks[distance] = lax.ppermute(chunks[distance], 'chan', pairs)]
    all_to_all x1, blocking collectives: 10.9 us -> 13.8 us  [shards(): lax.all_to_all(terms, ('chan', 'freq'), split_axis=0, concat_axis=0, tile...]
    unnamed x6 -> x8, local copies, waits for them, and re-layouts: 0.01 us -> 2.48 us
    another operation x1 -> x0, local copies, waits for them, and re-layouts: 1.94 us -> none  [shards(): lax.all_to_all(chunks, 'chan', split_axis=1, concat_axis=0, tiled=False)]
    pallas_call x0 -> x1, Pallas kernels: none -> 0.66 us  [shards(): pl.pallas_call(functools.partial(chunk_kernel, groups, bins), out_shape=(...]
  transfers between devices with their start and end apart: 1 -> 3, of which waited for: 1 -> 2; matrix products, arithmetic and copies ran while one was open for 0% -> 0% of each run, Pallas kernels for 3% -> 3%
where the time goes in v3:
time: 37.3 us; the launch traced here: 37.1 us
  blocking collectives  13.8 us (37%)
  Pallas kernels  7.58 us (20%)
  starting transfers between devices  7.01 us (19%)
  waiting for transfers between devices  6.18 us (17%)
  local copies, waits for them, and re-layouts  2.48 us (7%)
    all_to_all x1, blocking collectives, shards(): lax.all_to_all(terms, ('chan', 'freq'), split_axis=0, concat_axis=0, tile...  13.8 us
    ppermute x3, starting transfers between devices, shards(): arrived_chunks[distance] = lax.ppermute(chunks[distance], 'chan', pairs)  7.01 us
    ppermute x3, waiting for transfers between devices, shards(): arrived_chunks[distance] = lax.ppermute(chunks[distance], 'chan', pairs)  6.18 us
    pallas_call x1, Pallas kernels, shards(): pl.pallas_call(functools.partial(stack_kernel, groups, bins, parts), out_...  4.83 us
    unnamed x8, local copies, waits for them, and re-layouts  2.48 us
    pallas_call x1, Pallas kernels, shards(): pl.pallas_call(functools.partial(table_kernel, groups, bins, freq_dev), o...  1.11 us
    pallas_call x1, Pallas kernels, shards(): pl.pallas_call(functools.partial(image_kernel, slow_dev, spans), out_shap...  0.97 us
  transfers between devices with their start and end apart: 3, of which 2 were waited for; matrix products, arithmetic and copies ran while one was open for 0% of the time, Pallas kernels for 3%

profile of v3, /device:TPU:0, one launch (start us, length us, event | category | flops | bytes accessed | tf_op | source)
XLA Modules:
  0.0 37.1 jit_solution(10591763468802802533)
XLA Ops:
  0.0 0.0 copy-start
  0.0 0.0 copy-start.1
  0.0 1.1 %copy-done.1 = bf16[2,32,32,128]{3,2,1,0:T(8,128)(2,1)S(1)} copy-done((bf16[2,32,32,128]{3,2,1,0:T(8,128)(2,1)S(1)}, bf16[2,32,32,128]{3,2,1,0:T(8,128)(2,1)}, u32[]{:S(2)}) %copy-start.1) | copy-done | bytes 524312
  1.1 0.7 %chunks_of_bins.1 = (bf16[8,64,128]{2,1,0:T(8,128)(2,1)S(1)}, bf16[8,64,128]{2,1,0:T(8,128)(2,1)S(1)}, bf16[8,64,128]{2,1,0:T(8,128)(2,1)S(1)}, bf16[8,64,128]{2,1,0:T(8,128)(2,1)S(1)}) custom-call(bf16[2048,128]{1,0:T(8,128)(2,1)S(1)} %bitcast.2), custom_call_target="tpu_custom_call" | custom-call | tf_op jit(solution)/shard_map/chunks_of_bins/pallas_call | solution.py:227
  1.8 3.1 %collective-permute-start = (bf16[8,64,128]{2,1,0:T(8,128)(2,1)S(1)}, bf16[8,64,128]{2,1,0:T(8,128)(2,1)S(1)}, u32[]{:S(2)}, u32[]{:S(2)}) collective-permute-start(bf16[8,64,128]{2,1,0:T(8,128)(2,1)S(1)} %get-tuple-element.12), channel_id=1, source_target_pairs={{0,8},{8,16},{16,24},{24,0},{1,9},{9,17},{17,25},{25,1},{2,10},{10... | collective-permute-start | bytes 393224 | tf_op jit(solution)/shard_map/ppermute | solution.py:239
  4.9 2.6 %collective-permute-start.1 = (bf16[8,64,128]{2,1,0:T(8,128)(2,1)S(1)}, bf16[8,64,128]{2,1,0:T(8,128)(2,1)S(1)}, u32[]{:S(2)}, u32[]{:S(2)}) collective-permute-start(bf16[8,64,128]{2,1,0:T(8,128)(2,1)S(1)} %get-tuple-element.13), channel_id=1, source_target_pairs={{0,16},{8,24},{16,0},{24,8},{1,17},{9,25},{17,1},{25,9},{2,18},{10... | collective-permute-start | bytes 393224 | tf_op jit(solution)/shard_map/ppermute | solution.py:239
  7.5 1.3 %collective-permute-start.2 = (bf16[8,64,128]{2,1,0:T(8,128)(2,1)S(1)}, bf16[8,64,128]{2,1,0:T(8,128)(2,1)S(1)}, u32[]{:S(2)}, u32[]{:S(2)}) collective-permute-start(bf16[8,64,128]{2,1,0:T(8,128)(2,1)S(1)} %get-tuple-element.14), channel_id=1, source_target_pairs={{0,24},{8,0},{16,8},{24,16},{1,25},{9,1},{17,9},{25,17},{2,26},{10... | collective-permute-start | bytes 393224 | tf_op jit(solution)/shard_map/ppermute | solution.py:239
  8.8 1.1 %slant_tables.1 = (bf16[8,256,512]{2,1,0:T(8,128)(2,1)S(1)}, f32[8,2,8,256]{3,2,1,0:T(8,128)S(1)}) custom-call(), custom_call_target="tpu_custom_call" | custom-call | flops 10000000 | bytes 4000000 | tf_op jit(solution)/shard_map/slant_tables/pallas_call | solution.py:240
  9.9 1.4 %collective-permute-done.refs_1_ = bf16[8,64,128]{2,1,0:T(8,128)(2,1)S(1)} collective-permute-done((bf16[8,64,128]{2,1,0:T(8,128)(2,1)S(1)}, bf16[8,64,128]{2,1,0:T(8,128)(2,1)S(1)}, u32[]{:S(2)}, u32[]{:S(2)}) %collective-permute-start) | collective-permute-done | bytes 131104 | tf_op jit(solution)/shard_map/ppermute | solution.py:239
  11.3 4.8 %collective-permute-done.1.refs_2_ = bf16[8,64,128]{2,1,0:T(8,128)(2,1)S(1)} collective-permute-done((bf16[8,64,128]{2,1,0:T(8,128)(2,1)S(1)}, bf16[8,64,128]{2,1,0:T(8,128)(2,1)S(1)}, u32[]{:S(2)}, u32[]{:S(2)}) %collective-permute-start.1) | collective-permute-done | bytes 131104 | tf_op jit(solution)/shard_map/ppermute | solution.py:239
  16.1 0.0 collective-permute-done.2.refs_3_
  16.1 0.0 copy-start.2
  16.1 0.7 %copy-done.2 = f32[8,128]{1,0:T(8,128)S(1)} copy-done((f32[8,128]{1,0:T(8,128)S(1)}, f32[8,128]{1,0:T(8,128)}, u32[]{:S(2)}) %copy-start.2) | copy-done | bytes 4120
  16.8 0.0 copy-start.3
  16.8 0.7 %copy-done.3 = s32[4]{0:T(128)S(1)} copy-done((s32[4]{0:T(128)S(1)}, s32[4]{0:T(128)}, u32[]{:S(2)}) %copy-start.3) | copy-done | bytes 40
  17.5 4.8 %stack_and_slant.1 = f32[4,8,4,128]{3,2,1,0:T(4,128)S(1)} custom-call(bf16[8,64,128]{2,1,0:T(8,128)(2,1)S(1)} %get-tuple-element.11.refs_0_, bf16[8,64,128]{2,1,0:T(8,128)(2,1)S(1)} %collective-permute-done.refs_1_, bf16[8,64,128]{2,1,0:T(8,128)(2,1)S(1)} %collective-permute-done.1.refs_2_, bf16[8,64,128]{2,1,0:T(8,128)(2,1)S(1)} %collective-permute-done.2.refs_3_, ...), custom_call_target="tpu_custom_call" | custom-call | tf_op jit(solution)/shard_map/stack_and_slant/pallas_call | solution.py:251
  22.3 13.8 %all_to_all.5.term_ref = f32[32,4,128]{2,1,0:T(4,128)S(1)} all-to-all(f32[32,4,128]{2,1,0:T(4,128)S(1)} %bitcast.3), channel_id=1, replica_groups=mesh['chan'=4,'freq'=8] {'chan','freq'}, dimensions={0} | all-to-all | bytes 131072 | tf_op jit(solution)/shard_map/all_to_all | solution.py:267
  36.1 0.0 copy-done
  36.1 1.0 %sum_of_bins.1 = f32[1,32,512]{2,1,0:T(8,128)} custom-call(f32[32,4,128]{2,1,0:T(4,128)S(1)} %all_to_all.5.term_ref, bf16[2,512,512]{2,1,0:T(8,128)(2,1)S(1)} %copy-done), custom_call_target="tpu_custom_call" | custom-call | tf_op jit(solution)/shard_map/sum_of_bins/pallas_call | solution.py:269
Async XLA Ops:
  0.0 36.1 %copy-start = (bf16[2,512,512]{2,1,0:T(8,128)(2,1)S(1)}, bf16[2,512,512]{2,1,0:T(8,128)(2,1)}, u32[]{:S(2)}) copy-start(bf16[2,512,512]{2,1,0:T(8,128)(2,1)} %constant.5.clone.table_ref) | copy-start | bytes 3145732
  0.0 1.1 %copy-start.1 = (bf16[2,32,32,128]{3,2,1,0:T(8,128)(2,1)S(1)}, bf16[2,32,32,128]{3,2,1,0:T(8,128)(2,1)}, u32[]{:S(2)}) copy-start(bf16[2,32,32,128]{3,2,1,0:T(8,128)(2,1)} %param.4) | copy-start | bytes 1572868
  1.8 9.5 %collective-permute-start = (bf16[8,64,128]{2,1,0:T(8,128)(2,1)S(1)}, bf16[8,64,128]{2,1,0:T(8,128)(2,1)S(1)}, u32[]{:S(2)}, u32[]{:S(2)}) collective-permute-start(bf16[8,64,128]{2,1,0:T(8,128)(2,1)S(1)} %get-tuple-element.12), channel_id=1, source_target_pairs={{0,8},{8,16},{16,24},{24,0},{1,9},{9,17},{17,25},{25,1},{2,10},{10... | collective-permute-start | bytes 393224 | tf_op jit(solution)/shard_map/ppermute | solution.py:239
  4.9 11.2 %collective-permute-start.1 = (bf16[8,64,128]{2,1,0:T(8,128)(2,1)S(1)}, bf16[8,64,128]{2,1,0:T(8,128)(2,1)S(1)}, u32[]{:S(2)}, u32[]{:S(2)}) collective-permute-start(bf16[8,64,128]{2,1,0:T(8,128)(2,1)S(1)} %get-tuple-element.13), channel_id=1, source_target_pairs={{0,16},{8,24},{16,0},{24,8},{1,17},{9,25},{17,1},{25,9},{2,18},{10... | collective-permute-start | bytes 393224 | tf_op jit(solution)/shard_map/ppermute | solution.py:239
  7.5 8.6 %collective-permute-start.2 = (bf16[8,64,128]{2,1,0:T(8,128)(2,1)S(1)}, bf16[8,64,128]{2,1,0:T(8,128)(2,1)S(1)}, u32[]{:S(2)}, u32[]{:S(2)}) collective-permute-start(bf16[8,64,128]{2,1,0:T(8,128)(2,1)S(1)} %get-tuple-element.14), channel_id=1, source_target_pairs={{0,24},{8,0},{16,8},{24,16},{1,25},{9,1},{17,9},{25,17},{2,26},{10... | collective-permute-start | bytes 393224 | tf_op jit(solution)/shard_map/ppermute | solution.py:239
  16.1 0.7 %copy-start.2 = (f32[8,128]{1,0:T(8,128)S(1)}, f32[8,128]{1,0:T(8,128)}, u32[]{:S(2)}) copy-start(f32[8,128]{1,0:T(8,128)} %constant.4.clone.refs_5_) | copy-start | bytes 12292
  16.8 0.7 %copy-start.3 = (s32[4]{0:T(128)S(1)}, s32[4]{0:T(128)}, u32[]{:S(2)}) copy-start(s32[4]{0:T(128)} %refs_4_.1) | copy-start | bytes 52

commit v4 on v3

--- a/solution.py
+++ b/solution.py
@@ -38,12 +38,15 @@
     return high, (value - high.astype(jnp.float32)).astype(jnp.bfloat16)
 
 
-def table_kernel(groups, bins, freq_dev, lag_ref, shift_ref):
+def table_kernel(groups, bins, freq_dev, position_ref, place_ref, lag_ref, shift_ref):
     low_rows = lax.broadcasted_iota(jnp.int32, (8, SLOWNESS), 0)
     high_rows = lax.broadcasted_iota(jnp.int32, (BLOCK // 8, SLOWNESS), 0) * 8
     shift_rows = lax.broadcasted_iota(jnp.int32, (2 * groups, SLOWNESS), 0)
     shift_rows = jnp.where(shift_rows < groups, shift_rows, shift_rows - groups - 1) * BLOCK
-    first_bin = lax.axis_index("freq") * freq_dev + lax.axis_index("chan") * bins
+    own_group = lax.axis_index("chan")
+    first_bin = lax.axis_index("freq") * freq_dev + own_group * bins
+    for distance in range(groups):
+        place_ref[distance] = position_ref[lax.rem(own_group + (groups - distance), groups)]
 
     def one_bin(f, carry):
         def phases(rows):
@@ -83,60 +86,76 @@
             out_ref[f] = value.astype(jnp.bfloat16)
 
 
+def stack_weights(groups):
+    row = lax.broadcasted_iota(jnp.int32, (2 * groups, BLOCK), 0)
+    lag = lax.broadcasted_iota(jnp.int32, (2 * groups, BLOCK), 1)
+    delta = jnp.where(row < groups, row, row - groups)
+    lag = jnp.where(row < groups, lag, lag - BLOCK)
+    usable = (lag > -BLOCK) & ((delta >= 1) | (lag >= 1))
+    count = SEGMENTS * (groups - delta) * (BLOCK - jnp.abs(lag))
+    scale = math.sqrt(SEGMENTS / FREQS)
+    return jnp.where(usable, scale / jnp.maximum(count, 1).astype(jnp.float32), 0.0)
+
+
 def stack_kernel(groups, bins, parts, *refs):
     chunk_refs = refs[:groups]
-    position_ref, weight_ref, lag_ref, shift_ref, out_ref, placed_ref = refs[groups:]
+    place_ref, lag_ref, shift_ref, out_ref, placed_ref, left_ref, part_ref = refs[groups:]
     rows = placed_ref.shape[2]
     windows = rows // 2
-    own_group = lax.axis_index("chan")
     for distance, chunk_ref in enumerate(chunk_refs):
-        place = position_ref[lax.rem(own_group + (groups - distance), groups)]
-        placed_ref[place] = chunk_ref[...]
+        placed_ref[place_ref[distance]] = chunk_ref[...]
 
     row_index = lax.broadcasted_iota(jnp.int32, (BLOCK, BLOCK), 0)
     lag_index = lax.broadcasted_iota(jnp.int32, (BLOCK, BLOCK), 1)
     mirror = jnp.where(row_index + lag_index == BLOCK - 1, 1.0, 0.0).astype(jnp.bfloat16)
     ahead = lag_index <= row_index
-    ahead = jnp.concatenate([ahead, ahead], axis=1)
-
-    terms = []
+
     for f in range(bins):
-        left, right = [], []
+        left_ref[f] = lax.dot_general(
+            mirror,
+            placed_ref[:, f].reshape(groups * rows, BLOCK),
+            (((1,), (1,)), ((), ())),
+            preferred_element_type=jnp.float32,
+        ).astype(jnp.bfloat16)
+
+    for f in range(bins):
+        right = []
         for place in range(groups):
             value = placed_ref[place, f]
             real, imag = value[:windows], value[windows:]
-            left.append(value)
             right.append(
                 jnp.concatenate(
                     [jnp.concatenate([real, imag], 1), jnp.concatenate([imag, -real], 1)], 0
                 )
             )
-        left = lax.dot_general(
-            mirror,
-            jnp.concatenate(left, 0),
-            (((1,), (1,)), ((), ())),
-            preferred_element_type=jnp.float32,
-        ).astype(jnp.bfloat16)
         right = jnp.concatenate(right, 0)
-        forward, backward = [], []
         for delta in range(groups):
             panel = jnp.dot(
-                left[:, : rows * (groups - delta)],
+                left_ref[f, :, : rows * (groups - delta)],
                 right[rows * delta :],
                 preferred_element_type=jnp.float32,
             )
-            skewed = jnp.concatenate(
-                [
-                    pltpu.roll(panel[:, :BLOCK], 1, 1, stride=1, stride_axis=0),
-                    pltpu.roll(panel[:, BLOCK:], 1, 1, stride=1, stride_axis=0),
-                ],
-                axis=1,
-            )
-            forward.append(jnp.sum(jnp.where(ahead, skewed, 0.0), 0, keepdims=True))
-            backward.append(jnp.sum(jnp.where(ahead, 0.0, skewed), 0, keepdims=True))
-        lags = jnp.concatenate(forward + backward, 0)
-        weight = weight_ref[...]
-        means = jnp.concatenate([lags[:, :BLOCK] * weight, lags[:, BLOCK:] * weight], 0)
+            for half in range(2):
+                lanes = slice(half * BLOCK, (half + 1) * BLOCK)
+                skewed = pltpu.roll(panel[:, lanes], 1, 1, stride=1, stride_axis=0)
+                forward = jnp.where(ahead, skewed, 0.0).reshape(-1, 8, BLOCK).sum(0)
+                backward = jnp.where(ahead, 0.0, skewed).reshape(-1, 8, BLOCK).sum(0)
+                first = (f * 2 * groups + delta) * 8
+                part_ref[half, first : first + 8] = forward
+                part_ref[half, first + groups * 8 : first + groups * 8 + 8] = backward
+
+    lags = []
+    for half in range(2):
+        summed = part_ref[half, pl.ds(0, bins * 2 * groups, stride=8), :]
+        for sublane in range(1, 8):
+            summed = summed + part_ref[half, pl.ds(sublane, bins * 2 * groups, stride=8), :]
+        lags.append(summed)
+    weight = stack_weights(groups)
+
+    terms = []
+    for f in range(bins):
+        lag_rows = slice(f * 2 * groups, (f + 1) * 2 * groups)
+        means = jnp.concatenate([half[lag_rows] * weight for half in lags], 0)
         mean_high, mean_low = halves(means)
         spread = jnp.concatenate(
             [
@@ -184,17 +203,6 @@
     out_ref[0] = by_high[:slow_dev] + by_high[slow_dev:] + by_low
 
 
-def inverse_counts(nblocks):
-    delta = np.arange(nblocks)[:, None]
-    lag = np.arange(BLOCK)[None, :]
-    rows = []
-    for lags in (lag, lag - BLOCK):
-        usable = (lags > -BLOCK) & ((delta >= 1) | (lags >= 1))
-        count = SEGMENTS * (nblocks - delta) * (BLOCK - np.abs(lags))
-        rows.append(np.where(usable, 1.0 / np.maximum(count, 1), 0.0))
-    return np.concatenate(rows, 0) * math.sqrt(SEGMENTS / FREQS)
-
-
 def time_table(groups, parts, bins, slow_dev, message_rows):
     spans = min(BLOCK // slow_dev, 2 * bins)
     span, group, part, row = np.meshgrid(
@@ -237,29 +245,34 @@
     for distance in sorted(range(1, groups), key=lambda steps: abs(2 * steps - groups)):
         pairs = [(source, (source + distance) % groups) for source in range(groups)]
         arrived_chunks[distance] = lax.ppermute(chunks[distance], "chan", pairs)
-    lag_table, shift_table = pl.pallas_call(
+    places, lag_table, shift_table = pl.pallas_call(
         functools.partial(table_kernel, groups, bins, freq_dev),
         out_shape=(
+            jax.ShapeDtypeStruct((groups,), jnp.int32),
             jax.ShapeDtypeStruct((bins, 2 * BLOCK, 2 * SLOWNESS), jnp.bfloat16),
             jax.ShapeDtypeStruct((bins, 2, 2 * groups, SLOWNESS), jnp.float32),
         ),
-        out_specs=(vmem, vmem),
+        in_specs=[smem],
+        out_specs=(smem, vmem, vmem),
         compiler_params=params,
         cost_estimate=pl.CostEstimate(flops=10**7, bytes_accessed=4 * 10**6, transcendentals=0),
         name="slant_tables",
-    )()
+    )(block_position)
     terms = pl.pallas_call(
         functools.partial(stack_kernel, groups, bins, parts),
         out_shape=jax.ShapeDtypeStruct((groups, parts, message_rows, BLOCK), jnp.float32),
-        in_specs=[vmem] * groups + [smem, vmem, vmem, vmem],
+        in_specs=[vmem] * groups + [smem, vmem, vmem],
         out_specs=vmem,
-        scratch_shapes=[pltpu.VMEM((groups, bins, rows, BLOCK), jnp.bfloat16)],
+        scratch_shapes=[
+            pltpu.VMEM((groups, bins, rows, BLOCK), jnp.bfloat16),
+            pltpu.VMEM((bins, BLOCK, groups * rows), jnp.bfloat16),
+            pltpu.VMEM((2, bins * 2 * groups * 8, BLOCK), jnp.float32),
+        ],
         compiler_params=params,
         name="stack_and_slant",
     )(
         *arrived_chunks,
-        block_position,
-        jnp.asarray(inverse_counts(groups), jnp.float32),
+        places,
         lag_table,
         shift_table,
     )

time: 37.3 us -> 33.6 us (0.901)
  waiting for transfers between devices: 6.18 us -> 4.5 us
  Pallas kernels: 7.58 us -> 6.25 us
  local copies, waits for them, and re-layouts: 2.48 us -> 1.79 us
    pallas_call x1, Pallas kernels: 4.83 us -> 2.5 us  [shards(): pl.pallas_call(functools.partial(stack_kernel, groups, bins, parts), out_...]
    ppermute x3, waiting for transfers between devices: 6.18 us -> 4.5 us  [shards(): arrived_chunks[distance] = lax.ppermute(chunks[distance], 'chan', pairs)]
    pallas_call x1, Pallas kernels: 1.11 us -> 2.12 us  [shards(): pl.pallas_call(functools.partial(table_kernel, groups, bins, freq_dev), o...]
    unnamed x8 -> x6, local copies, waits for them, and re-layouts: 2.48 us -> 1.79 us
  transfers between devices with their start and end apart: 3 -> 3, of which waited for: 2 -> 1; matrix products, arithmetic and copies ran while one was open for 0% -> 0% of each run, Pallas kernels for 3% -> 6%
where the time goes in v4:
time: 33.6 us; the launch traced here: 33.4 us
  blocking collectives  13.8 us (41%)
  starting transfers between devices  7.01 us (21%)
  Pallas kernels  6.25 us (19%)
  waiting for transfers between devices  4.5 us (13%)
  local copies, waits for them, and re-layouts  1.79 us (5%)
    all_to_all x1, blocking collectives, shards(): lax.all_to_all(terms, ('chan', 'freq'), split_axis=0, concat_axis=0, tile...  13.8 us
    ppermute x3, starting transfers between devices, shards(): arrived_chunks[distance] = lax.ppermute(chunks[distance], 'chan', pairs)  7.01 us
    ppermute x3, waiting for transfers between devices, shards(): arrived_chunks[distance] = lax.ppermute(chunks[distance], 'chan', pairs)  4.5 us
    pallas_call x1, Pallas kernels, shards(): pl.pallas_call(functools.partial(stack_kernel, groups, bins, parts), out_...  2.5 us
    pallas_call x1, Pallas kernels, shards(): pl.pallas_call(functools.partial(table_kernel, groups, bins, freq_dev), o...  2.12 us
    unnamed x6, local copies, waits for them, and re-layouts  1.79 us
    pallas_call x1, Pallas kernels, shards(): pl.pallas_call(functools.partial(image_kernel, slow_dev, spans), out_shap...  0.97 us
  transfers between devices with their start and end apart: 3, of which 1 were waited for; matrix products, arithmetic and copies ran while one was open for 0% of the time, Pallas kernels for 6%

profile of v4, /device:TPU:0, one launch (start us, length us, event | category | flops | bytes accessed | tf_op | source)
XLA Modules:
  0.0 33.4 jit_solution(8509174466873413175)
XLA Ops:
  0.0 0.0 copy-start
  0.0 0.0 copy-start.1
  0.0 1.1 %copy-done.1 = bf16[2,32,32,128]{3,2,1,0:T(8,128)(2,1)S(1)} copy-done((bf16[2,32,32,128]{3,2,1,0:T(8,128)(2,1)S(1)}, bf16[2,32,32,128]{3,2,1,0:T(8,128)(2,1)}, u32[]{:S(2)}) %copy-start.1) | copy-done | bytes 524312
  1.1 0.7 %chunks_of_bins.1 = (bf16[8,64,128]{2,1,0:T(8,128)(2,1)S(1)}, bf16[8,64,128]{2,1,0:T(8,128)(2,1)S(1)}, bf16[8,64,128]{2,1,0:T(8,128)(2,1)S(1)}, bf16[8,64,128]{2,1,0:T(8,128)(2,1)S(1)}) custom-call(bf16[2048,128]{1,0:T(8,128)(2,1)S(1)} %bitcast.2), custom_call_target="tpu_custom_call" | custom-call | tf_op jit(solution)/shard_map/chunks_of_bins/pallas_call | solution.py:235
  1.8 3.1 %collective-permute-start = (bf16[8,64,128]{2,1,0:T(8,128)(2,1)S(1)}, bf16[8,64,128]{2,1,0:T(8,128)(2,1)S(1)}, u32[]{:S(2)}, u32[]{:S(2)}) collective-permute-start(bf16[8,64,128]{2,1,0:T(8,128)(2,1)S(1)} %get-tuple-element.13), channel_id=1, source_target_pairs={{0,8},{8,16},{16,24},{24,0},{1,9},{9,17},{17,25},{25,1},{2,10},{10... | collective-permute-start | bytes 393224 | tf_op jit(solution)/shard_map/ppermute | solution.py:247
  4.9 2.6 %collective-permute-start.1 = (bf16[8,64,128]{2,1,0:T(8,128)(2,1)S(1)}, bf16[8,64,128]{2,1,0:T(8,128)(2,1)S(1)}, u32[]{:S(2)}, u32[]{:S(2)}) collective-permute-start(bf16[8,64,128]{2,1,0:T(8,128)(2,1)S(1)} %get-tuple-element.14), channel_id=1, source_target_pairs={{0,16},{8,24},{16,0},{24,8},{1,17},{9,25},{17,1},{25,9},{2,18},{10... | collective-permute-start | bytes 393224 | tf_op jit(solution)/shard_map/ppermute | solution.py:247
  7.5 1.3 %collective-permute-start.2 = (bf16[8,64,128]{2,1,0:T(8,128)(2,1)S(1)}, bf16[8,64,128]{2,1,0:T(8,128)(2,1)S(1)}, u32[]{:S(2)}, u32[]{:S(2)}) collective-permute-start(bf16[8,64,128]{2,1,0:T(8,128)(2,1)S(1)} %get-tuple-element.15), channel_id=1, source_target_pairs={{0,24},{8,0},{16,8},{24,16},{1,25},{9,1},{17,9},{25,17},{2,26},{10... | collective-permute-start | bytes 393224 | tf_op jit(solution)/shard_map/ppermute | solution.py:247
  8.8 0.0 copy-start.2
  8.8 0.7 %copy-done.2 = s32[4]{0:T(128)S(1)} copy-done((s32[4]{0:T(128)S(1)}, s32[4]{0:T(128)}, u32[]{:S(2)}) %copy-start.2) | copy-done | bytes 40
  9.5 2.1 %slant_tables.1 = (s32[4]{0:T(128)S(1)}, bf16[8,256,512]{2,1,0:T(8,128)(2,1)S(1)}, f32[8,2,8,256]{3,2,1,0:T(8,128)S(1)}) custom-call(s32[4]{0:T(128)S(1)} %copy-done.2), custom_call_target="tpu_custom_call" | custom-call | flops 10000000 | bytes 4000000 | tf_op jit(solution)/shard_map/slant_tables/pallas_call | solution.py:248
  11.6 0.0 collective-permute-done.refs_1_
  11.6 4.5 %collective-permute-done.1.refs_2_ = bf16[8,64,128]{2,1,0:T(8,128)(2,1)S(1)} collective-permute-done((bf16[8,64,128]{2,1,0:T(8,128)(2,1)S(1)}, bf16[8,64,128]{2,1,0:T(8,128)(2,1)S(1)}, u32[]{:S(2)}, u32[]{:S(2)}) %collective-permute-start.1) | collective-permute-done | bytes 131104 | tf_op jit(solution)/shard_map/ppermute | solution.py:247
  16.1 0.0 collective-permute-done.2.refs_3_
  16.1 2.5 %stack_and_slant.1 = f32[4,8,4,128]{3,2,1,0:T(4,128)S(1)} custom-call(bf16[8,64,128]{2,1,0:T(8,128)(2,1)S(1)} %get-tuple-element.12.refs_0_, bf16[8,64,128]{2,1,0:T(8,128)(2,1)S(1)} %collective-permute-done.refs_1_, bf16[8,64,128]{2,1,0:T(8,128)(2,1)S(1)} %collective-permute-done.1.refs_2_, bf16[8,64,128]{2,1,0:T(8,128)(2,1)S(1)} %collective-permute-done.2.refs_3_, ...), custom_call_target="tpu_custom_call" | custom-call | tf_op jit(solution)/shard_map/stack_and_slant/pallas_call | solution.py:261
  18.6 13.8 %all_to_all.5.term_ref = f32[32,4,128]{2,1,0:T(4,128)S(1)} all-to-all(f32[32,4,128]{2,1,0:T(4,128)S(1)} %bitcast.3), channel_id=1, replica_groups=mesh['chan'=4,'freq'=8] {'chan','freq'}, dimensions={0} | all-to-all | bytes 131072 | tf_op jit(solution)/shard_map/all_to_all | solution.py:280
  32.4 0.0 copy-done
  32.4 1.0 %sum_of_bins.1 = f32[1,32,512]{2,1,0:T(8,128)} custom-call(f32[32,4,128]{2,1,0:T(4,128)S(1)} %all_to_all.5.term_ref, bf16[2,512,512]{2,1,0:T(8,128)(2,1)S(1)} %copy-done), custom_call_target="tpu_custom_call" | custom-call | tf_op jit(solution)/shard_map/sum_of_bins/pallas_call | solution.py:282
Async XLA Ops:
  0.0 32.4 %copy-start = (bf16[2,512,512]{2,1,0:T(8,128)(2,1)S(1)}, bf16[2,512,512]{2,1,0:T(8,128)(2,1)}, u32[]{:S(2)}) copy-start(bf16[2,512,512]{2,1,0:T(8,128)(2,1)} %constant.2.clone.table_ref) | copy-start | bytes 3145732
  0.0 1.1 %copy-start.1 = (bf16[2,32,32,128]{3,2,1,0:T(8,128)(2,1)S(1)}, bf16[2,32,32,128]{3,2,1,0:T(8,128)(2,1)}, u32[]{:S(2)}) copy-start(bf16[2,32,32,128]{3,2,1,0:T(8,128)(2,1)} %param.3) | copy-start | bytes 1572868
  1.8 9.8 %collective-permute-start = (bf16[8,64,128]{2,1,0:T(8,128)(2,1)S(1)}, bf16[8,64,128]{2,1,0:T(8,128)(2,1)S(1)}, u32[]{:S(2)}, u32[]{:S(2)}) collective-permute-start(bf16[8,64,128]{2,1,0:T(8,128)(2,1)S(1)} %get-tuple-element.13), channel_id=1, source_target_pairs={{0,8},{8,16},{16,24},{24,0},{1,9},{9,17},{17,25},{25,1},{2,10},{10... | collective-permute-start | bytes 393224 | tf_op jit(solution)/shard_map/ppermute | solution.py:247
  4.9 11.2 %collective-permute-start.1 = (bf16[8,64,128]{2,1,0:T(8,128)(2,1)S(1)}, bf16[8,64,128]{2,1,0:T(8,128)(2,1)S(1)}, u32[]{:S(2)}, u32[]{:S(2)}) collective-permute-start(bf16[8,64,128]{2,1,0:T(8,128)(2,1)S(1)} %get-tuple-element.14), channel_id=1, source_target_pairs={{0,16},{8,24},{16,0},{24,8},{1,17},{9,25},{17,1},{25,9},{2,18},{10... | collective-permute-start | bytes 393224 | tf_op jit(solution)/shard_map/ppermute | solution.py:247
  7.5 8.6 %collective-permute-start.2 = (bf16[8,64,128]{2,1,0:T(8,128)(2,1)S(1)}, bf16[8,64,128]{2,1,0:T(8,128)(2,1)S(1)}, u32[]{:S(2)}, u32[]{:S(2)}) collective-permute-start(bf16[8,64,128]{2,1,0:T(8,128)(2,1)S(1)} %get-tuple-element.15), channel_id=1, source_target_pairs={{0,24},{8,0},{16,8},{24,16},{1,25},{9,1},{17,9},{25,17},{2,26},{10... | collective-permute-start | bytes 393224 | tf_op jit(solution)/shard_map/ppermute | solution.py:247
  8.8 0.7 %copy-start.2 = (s32[4]{0:T(128)S(1)}, s32[4]{0:T(128)}, u32[]{:S(2)}) copy-start(s32[4]{0:T(128)} %position_ref.1) | copy-start | bytes 52

commit v5 on v4

--- a/solution.py
+++ b/solution.py
@@ -276,8 +276,9 @@
         lag_table,
         shift_table,
     )
-    terms = terms.reshape(groups * parts, message_rows, BLOCK)
-    arrived = lax.all_to_all(terms, ("chan", "freq"), split_axis=0, concat_axis=0, tiled=True)
+    terms = lax.all_to_all(terms, "chan", split_axis=0, concat_axis=0, tiled=True)
+    arrived = lax.all_to_all(terms, "freq", split_axis=1, concat_axis=1, tiled=True)
+    arrived = arrived.reshape(groups * parts, message_rows, BLOCK)
     spans, table = time_table(groups, parts, bins, slow_dev, message_rows)
     return pl.pallas_call(
         functools.partial(image_kernel, slow_dev, spans),

time: 33.6 us -> 39.5 us (1.18)
  blocking collectives: 13.8 us -> 19.7 us
    all_to_all x1 -> x2, blocking collectives: 13.8 us -> 19.7 us  [the longest x1 11.2 us: shards(): lax.all_to_all(terms, 'chan', split_axis=0, concat_axis=0, tiled=True)]
  transfers between devices with their start and end apart: 3 -> 3, of which waited for: 1 -> 1; matrix products, arithmetic and copies ran while one was open for 0% -> 0% of each run, Pallas kernels for 6% -> 5%
where the time goes in v5:
time: 39.5 us; the launch traced here: 39.3 us
  blocking collectives  19.7 us (50%)
  starting transfers between devices  7.01 us (18%)
  Pallas kernels  6.25 us (16%)
  waiting for transfers between devices  4.5 us (11%)
  local copies, waits for them, and re-layouts  1.81 us (5%)
    all_to_all x1, blocking collectives, shards(): lax.all_to_all(terms, 'chan', split_axis=0, concat_axis=0, tiled=True)  11.2 us
    all_to_all x1, blocking collectives, shards(): lax.all_to_all(terms, 'freq', split_axis=1, concat_axis=1, tiled=True)  8.54 us
    ppermute x3, starting transfers between devices, shards(): arrived_chunks[distance] = lax.ppermute(chunks[distance], 'chan', pairs)  7.01 us
    ppermute x3, waiting for transfers between devices, shards(): arrived_chunks[distance] = lax.ppermute(chunks[distance], 'chan', pairs)  4.5 us
    pallas_call x1, Pallas kernels, shards(): pl.pallas_call(functools.partial(stack_kernel, groups, bins, parts), out_...  2.5 us
    pallas_call x1, Pallas kernels, shards(): pl.pallas_call(functools.partial(table_kernel, groups, bins, freq_dev), o...  2.12 us
    unnamed x6, local copies, waits for them, and re-layouts  1.79 us
    pallas_call x1, Pallas kernels, shards(): pl.pallas_call(functools.partial(image_kernel, slow_dev, spans), out_shap...  0.97 us
  transfers between devices with their start and end apart: 3, of which 1 were waited for; matrix products, arithmetic and copies ran while one was open for 0% of the time, Pallas kernels for 5%

profile of v5, /device:TPU:0, one launch (start us, length us, event | category | flops | bytes accessed | tf_op | source)
XLA Modules:
  0.0 39.3 jit_solution(4770702157102242273)
XLA Ops:
  0.0 0.0 copy-start
  0.0 0.0 copy-start.1
  0.0 1.1 %copy-done.1 = bf16[2,32,32,128]{3,2,1,0:T(8,128)(2,1)S(1)} copy-done((bf16[2,32,32,128]{3,2,1,0:T(8,128)(2,1)S(1)}, bf16[2,32,32,128]{3,2,1,0:T(8,128)(2,1)}, u32[]{:S(2)}) %copy-start.1) | copy-done | bytes 524312
  1.1 0.7 %chunks_of_bins.1 = (bf16[8,64,128]{2,1,0:T(8,128)(2,1)S(1)}, bf16[8,64,128]{2,1,0:T(8,128)(2,1)S(1)}, bf16[8,64,128]{2,1,0:T(8,128)(2,1)S(1)}, bf16[8,64,128]{2,1,0:T(8,128)(2,1)S(1)}) custom-call(bf16[2048,128]{1,0:T(8,128)(2,1)S(1)} %bitcast.2), custom_call_target="tpu_custom_call" | custom-call | tf_op jit(solution)/shard_map/chunks_of_bins/pallas_call | solution.py:235
  1.8 3.1 %collective-permute-start = (bf16[8,64,128]{2,1,0:T(8,128)(2,1)S(1)}, bf16[8,64,128]{2,1,0:T(8,128)(2,1)S(1)}, u32[]{:S(2)}, u32[]{:S(2)}) collective-permute-start(bf16[8,64,128]{2,1,0:T(8,128)(2,1)S(1)} %get-tuple-element.13), channel_id=1, source_target_pairs={{0,8},{8,16},{16,24},{24,0},{1,9},{9,17},{17,25},{25,1},{2,10},{10... | collective-permute-start | bytes 393224 | tf_op jit(solution)/shard_map/ppermute | solution.py:247
  4.9 2.6 %collective-permute-start.1 = (bf16[8,64,128]{2,1,0:T(8,128)(2,1)S(1)}, bf16[8,64,128]{2,1,0:T(8,128)(2,1)S(1)}, u32[]{:S(2)}, u32[]{:S(2)}) collective-permute-start(bf16[8,64,128]{2,1,0:T(8,128)(2,1)S(1)} %get-tuple-element.14), channel_id=1, source_target_pairs={{0,16},{8,24},{16,0},{24,8},{1,17},{9,25},{17,1},{25,9},{2,18},{10... | collective-permute-start | bytes 393224 | tf_op jit(solution)/shard_map/ppermute | solution.py:247
  7.5 1.3 %collective-permute-start.2 = (bf16[8,64,128]{2,1,0:T(8,128)(2,1)S(1)}, bf16[8,64,128]{2,1,0:T(8,128)(2,1)S(1)}, u32[]{:S(2)}, u32[]{:S(2)}) collective-permute-start(bf16[8,64,128]{2,1,0:T(8,128)(2,1)S(1)} %get-tuple-element.15), channel_id=1, source_target_pairs={{0,24},{8,0},{16,8},{24,16},{1,25},{9,1},{17,9},{25,17},{2,26},{10... | collective-permute-start | bytes 393224 | tf_op jit(solution)/shard_map/ppermute | solution.py:247
  8.8 0.0 copy-start.2
  8.8 0.7 %copy-done.2 = s32[4]{0:T(128)S(1)} copy-done((s32[4]{0:T(128)S(1)}, s32[4]{0:T(128)}, u32[]{:S(2)}) %copy-start.2) | copy-done | bytes 40
  9.5 2.1 %slant_tables.1 = (s32[4]{0:T(128)S(1)}, bf16[8,256,512]{2,1,0:T(8,128)(2,1)S(1)}, f32[8,2,8,256]{3,2,1,0:T(8,128)S(1)}) custom-call(s32[4]{0:T(128)S(1)} %copy-done.2), custom_call_target="tpu_custom_call" | custom-call | flops 10000000 | bytes 4000000 | tf_op jit(solution)/shard_map/slant_tables/pallas_call | solution.py:248
  11.6 0.0 collective-permute-done.refs_1_
  11.6 4.5 %collective-permute-done.1.refs_2_ = bf16[8,64,128]{2,1,0:T(8,128)(2,1)S(1)} collective-permute-done((bf16[8,64,128]{2,1,0:T(8,128)(2,1)S(1)}, bf16[8,64,128]{2,1,0:T(8,128)(2,1)S(1)}, u32[]{:S(2)}, u32[]{:S(2)}) %collective-permute-start.1) | collective-permute-done | bytes 131104 | tf_op jit(solution)/shard_map/ppermute | solution.py:247
  16.1 0.0 collective-permute-done.2.refs_3_
  16.1 2.5 %stack_and_slant.1 = f32[4,8,4,128]{3,2,1,0:T(4,128)S(1)} custom-call(bf16[8,64,128]{2,1,0:T(8,128)(2,1)S(1)} %get-tuple-element.12.refs_0_, bf16[8,64,128]{2,1,0:T(8,128)(2,1)S(1)} %collective-permute-done.refs_1_, bf16[8,64,128]{2,1,0:T(8,128)(2,1)S(1)} %collective-permute-done.1.refs_2_, bf16[8,64,128]{2,1,0:T(8,128)(2,1)S(1)} %collective-permute-done.2.refs_3_, ...), custom_call_target="tpu_custom_call" | custom-call | tf_op jit(solution)/shard_map/stack_and_slant/pallas_call | solution.py:261
  18.6 11.2 %all_to_all.10 = f32[4,8,4,128]{3,2,1,0:T(4,128)S(1)} all-to-all(f32[4,8,4,128]{3,2,1,0:T(4,128)S(1)} %stack_and_slant.1), channel_id=1, replica_groups=mesh['chan'=4,'freq'=8] {'chan'}, dimensions={0} | all-to-all | bytes 131072 | tf_op jit(solution)/shard_map/all_to_all | solution.py:279
  29.8 8.5 %all_to_all.11 = f32[4,8,4,128]{3,2,0,1:T(4,128)S(1)} all-to-all(f32[4,8,4,128]{3,2,0,1:T(4,128)S(1)} %copy.4), channel_id=1, replica_groups=mesh['chan'=4,'freq'=8] {'freq'}, dimensions={1} | all-to-all | bytes 131072 | tf_op jit(solution)/shard_map/all_to_all | solution.py:280
  38.3 0.0 copy-done
  38.4 1.0 %sum_of_bins.1 = f32[1,32,512]{2,1,0:T(8,128)} custom-call(f32[32,4,128]{2,1,0:T(4,128)S(1)} %bitcast.3, bf16[2,512,512]{2,1,0:T(8,128)(2,1)S(1)} %copy-done), custom_call_target="tpu_custom_call" | custom-call | tf_op jit(solution)/shard_map/sum_of_bins/pallas_call | solution.py:283
  (2 shorter events, 0.0 us)
Async XLA Ops:
  0.0 38.3 %copy-start = (bf16[2,512,512]{2,1,0:T(8,128)(2,1)S(1)}, bf16[2,512,512]{2,1,0:T(8,128)(2,1)}, u32[]{:S(2)}) copy-start(bf16[2,512,512]{2,1,0:T(8,128)(2,1)} %constant.2.clone.table_ref) | copy-start | bytes 3145732
  0.0 1.1 %copy-start.1 = (bf16[2,32,32,128]{3,2,1,0:T(8,128)(2,1)S(1)}, bf16[2,32,32,128]{3,2,1,0:T(8,128)(2,1)}, u32[]{:S(2)}) copy-start(bf16[2,32,32,128]{3,2,1,0:T(8,128)(2,1)} %param.3) | copy-start | bytes 1572868
  1.8 9.8 %collective-permute-start = (bf16[8,64,128]{2,1,0:T(8,128)(2,1)S(1)}, bf16[8,64,128]{2,1,0:T(8,128)(2,1)S(1)}, u32[]{:S(2)}, u32[]{:S(2)}) collective-permute-start(bf16[8,64,128]{2,1,0:T(8,128)(2,1)S(1)} %get-tuple-element.13), channel_id=1, source_target_pairs={{0,8},{8,16},{16,24},{24,0},{1,9},{9,17},{17,25},{25,1},{2,10},{10... | collective-permute-start | bytes 393224 | tf_op jit(solution)/shard_map/ppermute | solution.py:247
  4.9 11.2 %collective-permute-start.1 = (bf16[8,64,128]{2,1,0:T(8,128)(2,1)S(1)}, bf16[8,64,128]{2,1,0:T(8,128)(2,1)S(1)}, u32[]{:S(2)}, u32[]{:S(2)}) collective-permute-start(bf16[8,64,128]{2,1,0:T(8,128)(2,1)S(1)} %get-tuple-element.14), channel_id=1, source_target_pairs={{0,16},{8,24},{16,0},{24,8},{1,17},{9,25},{17,1},{25,9},{2,18},{10... | collective-permute-start | bytes 393224 | tf_op jit(solution)/shard_map/ppermute | solution.py:247
  7.5 8.6 %collective-permute-start.2 = (bf16[8,64,128]{2,1,0:T(8,128)(2,1)S(1)}, bf16[8,64,128]{2,1,0:T(8,128)(2,1)S(1)}, u32[]{:S(2)}, u32[]{:S(2)}) collective-permute-start(bf16[8,64,128]{2,1,0:T(8,128)(2,1)S(1)} %get-tuple-element.15), channel_id=1, source_target_pairs={{0,24},{8,0},{16,8},{24,16},{1,25},{9,1},{17,9},{25,17},{2,26},{10... | collective-permute-start | bytes 393224 | tf_op jit(solution)/shard_map/ppermute | solution.py:247
  8.8 0.7 %copy-start.2 = (s32[4]{0:T(128)S(1)}, s32[4]{0:T(128)}, u32[]{:S(2)}) copy-start(s32[4]{0:T(128)} %position_ref.1) | copy-start | bytes 52

commit v6 on v4

--- a/solution.py
+++ b/solution.py
@@ -73,15 +73,17 @@
     lax.fori_loop(0, bins, one_bin, 0)
 
 
-def chunk_kernel(groups, bins, spec_ref, *refs):
+def chunk_kernel(groups, pieces, spec_ref, *refs):
     out_refs, wide_ref = refs[:-1], refs[-1]
     wide_ref[...] = spec_ref[...].astype(jnp.float32)
+    bins = sum(size for _, size in pieces)
     freq_dev = groups * bins
     rows = spec_ref.shape[0] // freq_dev
     own_group = lax.axis_index("chan")
-    for distance, out_ref in enumerate(out_refs):
-        first = lax.rem(own_group + distance, groups) * bins
-        for f in range(bins):
+    for index, out_ref in enumerate(out_refs):
+        start, size = pieces[index // groups]
+        first = lax.rem(own_group + index % groups, groups) * bins + start
+        for f in range(size):
             value = wide_ref[pl.ds(first + f, rows, stride=freq_dev), :]
             out_ref[f] = value.astype(jnp.bfloat16)
 
@@ -97,9 +99,11 @@
     return jnp.where(usable, scale / jnp.maximum(count, 1).astype(jnp.float32), 0.0)
 
 
-def stack_kernel(groups, bins, parts, *refs):
+def stack_kernel(groups, start, bins, parts, *refs):
     chunk_refs = refs[:groups]
-    place_ref, lag_ref, shift_ref, out_ref, placed_ref, left_ref, part_ref = refs[groups:]
+    place_ref, lag_ref, shift_ref = refs[groups : groups + 3]
+    earlier_refs = refs[groups + 3 : -4]
+    out_ref, placed_ref, left_ref, part_ref = refs[-4:]
     rows = placed_ref.shape[2]
     windows = rows // 2
     for distance, chunk_ref in enumerate(chunk_refs):
@@ -164,17 +168,23 @@
             ],
             0,
         )
-        product = jnp.dot(spread, lag_ref[f], preferred_element_type=jnp.float32)
+        product = jnp.dot(spread, lag_ref[start + f], preferred_element_type=jnp.float32)
         product = product[: 4 * groups] + product[4 * groups :]
         by_cos, by_sin = product[:, :SLOWNESS], product[:, SLOWNESS:]
         real = by_cos[: 2 * groups] - by_sin[2 * groups :]
         imag = by_sin[: 2 * groups] + by_cos[2 * groups :]
-        shift_cos, shift_sin = shift_ref[f, 0], shift_ref[f, 1]
+        shift_cos, shift_sin = shift_ref[start + f, 0], shift_ref[start + f, 1]
         turned_re = real * shift_cos - imag * shift_sin
         turned_im = real * shift_sin + imag * shift_cos
         terms.append(turned_re[:groups] + turned_re[groups:])
         terms.append(turned_im[:groups] + turned_im[groups:])
 
+    if parts is None:
+        for entry, term in enumerate(terms):
+            out_ref[entry] = term
+        return
+    for earlier_ref in reversed(earlier_refs):
+        terms = [earlier_ref[entry] for entry in range(earlier_ref.shape[0])] + terms
     slow_dev = SLOWNESS // parts
     spans = BLOCK // slow_dev
     span_index = lax.broadcasted_iota(jnp.int32, (groups, BLOCK), 1) // slow_dev
@@ -231,20 +241,25 @@
     smem = pl.BlockSpec(memory_space=pltpu.SMEM)
     params = pltpu.CompilerParams(vmem_limit_bytes=32 * 1024 * 1024)
 
-    chunk = jax.ShapeDtypeStruct((bins, rows, BLOCK), jnp.bfloat16)
+    pieces = [(0, bins - bins // 2), (bins - bins // 2, bins // 2)] if bins > 1 else [(0, 1)]
     chunks = pl.pallas_call(
-        functools.partial(chunk_kernel, groups, bins),
-        out_shape=(chunk,) * groups,
+        functools.partial(chunk_kernel, groups, pieces),
+        out_shape=tuple(
+            jax.ShapeDtypeStruct((size, rows, BLOCK), jnp.bfloat16)
+            for _, size in pieces
+            for _ in range(groups)
+        ),
         in_specs=[vmem],
-        out_specs=(vmem,) * groups,
+        out_specs=(vmem,) * (groups * len(pieces)),
         scratch_shapes=[pltpu.VMEM((rows * freq_dev, BLOCK), jnp.float32)],
         compiler_params=params,
         name="chunks_of_bins",
     )(spectra.reshape(rows * freq_dev, BLOCK))
-    arrived_chunks = list(chunks)
-    for distance in sorted(range(1, groups), key=lambda steps: abs(2 * steps - groups)):
-        pairs = [(source, (source + distance) % groups) for source in range(groups)]
-        arrived_chunks[distance] = lax.ppermute(chunks[distance], "chan", pairs)
+    chunks = [list(chunks[index * groups : (index + 1) * groups]) for index in range(len(pieces))]
+    for piece in chunks:
+        for distance in sorted(range(1, groups), key=lambda steps: abs(2 * steps - groups)):
+            pairs = [(source, (source + distance) % groups) for source in range(groups)]
+            piece[distance] = lax.ppermute(piece[distance], "chan", pairs)
     places, lag_table, shift_table = pl.pallas_call(
         functools.partial(table_kernel, groups, bins, freq_dev),
         out_shape=(
@@ -258,24 +273,30 @@
         cost_estimate=pl.CostEstimate(flops=10**7, bytes_accessed=4 * 10**6, transcendentals=0),
         name="slant_tables",
     )(block_position)
-    terms = pl.pallas_call(
-        functools.partial(stack_kernel, groups, bins, parts),
-        out_shape=jax.ShapeDtypeStruct((groups, parts, message_rows, BLOCK), jnp.float32),
-        in_specs=[vmem] * groups + [smem, vmem, vmem],
-        out_specs=vmem,
-        scratch_shapes=[
-            pltpu.VMEM((groups, bins, rows, BLOCK), jnp.bfloat16),
-            pltpu.VMEM((bins, BLOCK, groups * rows), jnp.bfloat16),
-            pltpu.VMEM((2, bins * 2 * groups * 8, BLOCK), jnp.float32),
-        ],
-        compiler_params=params,
-        name="stack_and_slant",
-    )(
-        *arrived_chunks,
-        places,
-        lag_table,
-        shift_table,
-    )
+    earlier = []
+    for index, (start, size) in enumerate(pieces):
+        last = index == len(pieces) - 1
+        if last:
+            shape = (groups, parts, message_rows, BLOCK)
+        else:
+            shape = (2 * size, groups, SLOWNESS)
+        terms = pl.pallas_call(
+            functools.partial(stack_kernel, groups, start, size, parts if last else None),
+            out_shape=jax.ShapeDtypeStruct(shape, jnp.float32),
+            in_specs=[vmem] * groups + [smem, vmem, vmem] + [vmem] * len(earlier),
+            out_specs=vmem,
+            scratch_shapes=[
+                pltpu.VMEM((groups, size, rows, BLOCK), jnp.bfloat16),
+                pltpu.VMEM((size, BLOCK, groups * rows), jnp.bfloat16),
+                pltpu.VMEM((2, size * 2 * groups * 8, BLOCK), jnp.float32),
+            ],
+            compiler_params=params,
+            cost_estimate=pl.CostEstimate(
+                flops=2 * 10**8, bytes_accessed=4 * 10**6, transcendentals=0
+            ),
+            name="stack_and_slant",
+        )(*chunks[index], places, lag_table, shift_table, *earlier)
+        earlier.append(terms)
     terms = terms.reshape(groups * parts, message_rows, BLOCK)
     arrived = lax.all_to_all(terms, ("chan", "freq"), split_axis=0, concat_axis=0, tiled=True)
     spans, table = time_table(groups, parts, bins, slow_dev, message_rows)

time: 33.6 us -> 33.2 us (0.988)
  waiting for transfers between devices: 4.5 us -> 0.42 us
  starting transfers between devices: 7.01 us -> 10.8 us
  blocking collectives: 13.8 us -> 12.7 us
  Pallas kernels: 6.25 us -> 7.22 us
    ppermute x3 -> x6, waiting for transfers between devices: 4.5 us -> 0.42 us  [shards(): piece[distance] = lax.ppermute(piece[distance], 'chan', pairs)]
    ppermute x3 -> x6, starting transfers between devices: 7.01 us -> 10.8 us  [shards(): piece[distance] = lax.ppermute(piece[distance], 'chan', pairs)]
    all_to_all x1, blocking collectives: 13.8 us -> 12.7 us  [shards(): lax.all_to_all(terms, ('chan', 'freq'), split_axis=0, concat_axis=0, tile...]
    pallas_call x2 -> x3, Pallas kernels: 3.16 us -> 4.13 us  [the longest x2 3.47 us: shards(): pl.pallas_call(functools.partial(stack_kernel, groups, start, size, parts...]
  transfers between devices with their start and end apart: 3 -> 6, of which waited for: 1 -> 1; matrix products, arithmetic and copies ran while one was open for 0% -> 0% of each run, Pallas kernels for 6% -> 12%
where the time goes in v6:
time: 33.2 us; the launch traced here: 33 us
  blocking collectives  12.7 us (38%)
  starting transfers between devices  10.8 us (33%)
  Pallas kernels  7.22 us (22%)
  local copies, waits for them, and re-layouts  1.7 us (5%)
  waiting for transfers between devices  0.42 us (1%)
    all_to_all x1, blocking collectives, shards(): lax.all_to_all(terms, ('chan', 'freq'), split_axis=0, concat_axis=0, tile...  12.7 us
    ppermute x6, starting transfers between devices, shards(): piece[distance] = lax.ppermute(piece[distance], 'chan', pairs)  10.8 us
    pallas_call x2, Pallas kernels, shards(): pl.pallas_call(functools.partial(stack_kernel, groups, start, size, parts...  3.47 us
    pallas_call x1, Pallas kernels, shards(): pl.pallas_call(functools.partial(table_kernel, groups, bins, freq_dev), o...  2.12 us
    unnamed x6, local copies, waits for them, and re-layouts  1.7 us
    pallas_call x1, Pallas kernels, shards(): pl.pallas_call(functools.partial(image_kernel, slow_dev, spans), out_shap...  0.97 us
  transfers between devices with their start and end apart: 6, of which 1 were waited for; matrix products, arithmetic and copies ran while one was open for 0% of the time, Pallas kernels for 12%

profile of v6, /device:TPU:0, one launch (start us, length us, event | category | flops | bytes accessed | tf_op | source)
XLA Modules:
  0.0 33.0 jit_solution(4120211159751810495)
XLA Ops:
  0.0 0.0 copy-start.1
  0.0 1.0 %copy-done.1 = bf16[2,32,32,128]{3,2,1,0:T(8,128)(2,1)S(1)} copy-done((bf16[2,32,32,128]{3,2,1,0:T(8,128)(2,1)S(1)}, bf16[2,32,32,128]{3,2,1,0:T(8,128)(2,1)}, u32[]{:S(2)}) %copy-start.1) | copy-done | bytes 524312
  1.0 0.7 %chunks_of_bins.1 = (bf16[4,64,128]{2,1,0:T(8,128)(2,1)S(1)}, bf16[4,64,128]{2,1,0:T(8,128)(2,1)S(1)}, bf16[4,64,128]{2,1,0:T(8,128)(2,1)S(1)}, bf16[4,64,128]{2...) custom-call(bf16[2048,128]{1,0:T(8,128)(2,1)S(1)} %bitcast.2), custom_call_target="tpu_custom_call" | custom-call | tf_op jit(solution)/shard_map/chunks_of_bins/pallas_call | solution.py:245
  1.7 3.1 %collective-permute-start.3 = (bf16[4,64,128]{2,1,0:T(8,128)(2,1)S(1)}, bf16[4,64,128]{2,1,0:T(8,128)(2,1)S(1)}, u32[]{:S(2)}, u32[]{:S(2)}) collective-permute-start(bf16[4,64,128]{2,1,0:T(8,128)(2,1)S(1)} %get-tuple-element.24), channel_id=1, source_target_pairs={{0,8},{8,16},{16,24},{24,0},{1,9},{9,17},{17,25},{25,1},{2,10},{10... | collective-permute-start | bytes 196616 | tf_op jit(solution)/shard_map/ppermute | solution.py:262
  4.8 2.6 %collective-permute-start.4 = (bf16[4,64,128]{2,1,0:T(8,128)(2,1)S(1)}, bf16[4,64,128]{2,1,0:T(8,128)(2,1)S(1)}, u32[]{:S(2)}, u32[]{:S(2)}) collective-permute-start(bf16[4,64,128]{2,1,0:T(8,128)(2,1)S(1)} %get-tuple-element.25), channel_id=1, source_target_pairs={{0,16},{8,24},{16,0},{24,8},{1,17},{9,25},{17,1},{25,9},{2,18},{10... | collective-permute-start | bytes 196616 | tf_op jit(solution)/shard_map/ppermute | solution.py:262
  7.4 1.3 %collective-permute-start.5 = (bf16[4,64,128]{2,1,0:T(8,128)(2,1)S(1)}, bf16[4,64,128]{2,1,0:T(8,128)(2,1)S(1)}, u32[]{:S(2)}, u32[]{:S(2)}) collective-permute-start(bf16[4,64,128]{2,1,0:T(8,128)(2,1)S(1)} %get-tuple-element.26), channel_id=1, source_target_pairs={{0,24},{8,0},{16,8},{24,16},{1,25},{9,1},{17,9},{25,17},{2,26},{10... | collective-permute-start | bytes 196616 | tf_op jit(solution)/shard_map/ppermute | solution.py:262
  8.7 0.7 %collective-permute-start = (bf16[4,64,128]{2,1,0:T(8,128)(2,1)S(1)}, bf16[4,64,128]{2,1,0:T(8,128)(2,1)S(1)}, u32[]{:S(2)}, u32[]{:S(2)}) collective-permute-start(bf16[4,64,128]{2,1,0:T(8,128)(2,1)S(1)} %get-tuple-element.17), channel_id=1, source_target_pairs={{0,8},{8,16},{16,24},{24,0},{1,9},{9,17},{17,25},{25,1},{2,10},{10... | collective-permute-start | bytes 196616 | tf_op jit(solution)/shard_map/ppermute | solution.py:262
  9.4 0.3 %collective-permute-start.1 = (bf16[4,64,128]{2,1,0:T(8,128)(2,1)S(1)}, bf16[4,64,128]{2,1,0:T(8,128)(2,1)S(1)}, u32[]{:S(2)}, u32[]{:S(2)}) collective-permute-start(bf16[4,64,128]{2,1,0:T(8,128)(2,1)S(1)} %get-tuple-element.18), channel_id=1, source_target_pairs={{0,16},{8,24},{16,0},{24,8},{1,17},{9,25},{17,1},{25,9},{2,18},{10... | collective-permute-start | bytes 196616 | tf_op jit(solution)/shard_map/ppermute | solution.py:262
  9.7 0.0 collective-permute-done.3.refs_1_
  9.7 2.8 %collective-permute-start.2 = (bf16[4,64,128]{2,1,0:T(8,128)(2,1)S(1)}, bf16[4,64,128]{2,1,0:T(8,128)(2,1)S(1)}, u32[]{:S(2)}, u32[]{:S(2)}) collective-permute-start(bf16[4,64,128]{2,1,0:T(8,128)(2,1)S(1)} %get-tuple-element.19), channel_id=1, source_target_pairs={{0,24},{8,0},{16,8},{24,16},{1,25},{9,1},{17,9},{25,17},{2,26},{10... | collective-permute-start | bytes 196616 | tf_op jit(solution)/shard_map/ppermute | solution.py:262
  12.6 0.0 copy-start.2
  12.6 0.7 %copy-done.2 = s32[4]{0:T(128)S(1)} copy-done((s32[4]{0:T(128)S(1)}, s32[4]{0:T(128)}, u32[]{:S(2)}) %copy-start.2) | copy-done | bytes 40
  13.2 2.1 %slant_tables.1 = (s32[4]{0:T(128)S(1)}, bf16[8,256,512]{2,1,0:T(8,128)(2,1)S(1)}, f32[8,2,8,256]{3,2,1,0:T(8,128)S(1)}) custom-call(s32[4]{0:T(128)S(1)} %copy-done.2), custom_call_target="tpu_custom_call" | custom-call | flops 10000000 | bytes 4000000 | tf_op jit(solution)/shard_map/slant_tables/pallas_call | solution.py:263
  15.3 0.0 collective-permute-done.4.refs_2_
  15.3 0.0 collective-permute-done.5.refs_3_
  15.4 0.0 copy-start
  15.4 1.7 %stack_and_slant.2.refs_7_ = f32[8,4,256]{2,1,0:T(4,128)S(1)} custom-call(bf16[4,64,128]{2,1,0:T(8,128)(2,1)S(1)} %get-tuple-element.23.refs_0_, bf16[4,64,128]{2,1,0:T(8,128)(2,1)S(1)} %collective-permute-done.3.refs_1_, bf16[4,64,128]{2,1,0:T(8,128)(2,1)S(1)} %collective-permute-done.4.refs_2_, bf16[4,64,128]{2,1,0:T(8,128)(2,1)S(1)} %collective-permute-done.5.refs_3_, ...), custom_call_target="tpu_custom_call" | custom-call | flops 200000000 | bytes 4000000 | tf_op jit(solution)/shard_map/stack_and_slant/pallas_call | solution.py:283
  17.1 0.0 collective-permute-done.refs_1_
  17.1 0.4 %collective-permute-done.1.refs_2_ = bf16[4,64,128]{2,1,0:T(8,128)(2,1)S(1)} collective-permute-done((bf16[4,64,128]{2,1,0:T(8,128)(2,1)S(1)}, bf16[4,64,128]{2,1,0:T(8,128)(2,1)S(1)}, u32[]{:S(2)}, u32[]{:S(2)}) %collective-permute-start.1) | collective-permute-done | bytes 65568 | tf_op jit(solution)/shard_map/ppermute | solution.py:262
  17.5 0.0 collective-permute-done.2.refs_3_
  17.5 1.8 %stack_and_slant.3 = f32[4,8,4,128]{3,2,1,0:T(4,128)S(1)} custom-call(bf16[4,64,128]{2,1,0:T(8,128)(2,1)S(1)} %get-tuple-element.16.refs_0_, bf16[4,64,128]{2,1,0:T(8,128)(2,1)S(1)} %collective-permute-done.refs_1_, bf16[4,64,128]{2,1,0:T(8,128)(2,1)S(1)} %collective-permute-done.1.refs_2_, bf16[4,64,128]{2,1,0:T(8,128)(2,1)S(1)} %collective-permute-done.2.refs_3_, ...), custom_call_target="tpu_custom_call" | custom-call | flops 200000000 | bytes 4000000 | tf_op jit(solution)/shard_map/stack_and_slant/pallas_call | solution.py:283
  19.3 12.7 %all_to_all.5.term_ref = f32[32,4,128]{2,1,0:T(4,128)S(1)} all-to-all(f32[32,4,128]{2,1,0:T(4,128)S(1)} %bitcast.3), channel_id=1, replica_groups=mesh['chan'=4,'freq'=8] {'chan','freq'}, dimensions={0} | all-to-all | bytes 131072 | tf_op jit(solution)/shard_map/all_to_all | solution.py:301
  32.0 0.0 copy-done
  32.0 1.0 %sum_of_bins.1 = f32[1,32,512]{2,1,0:T(8,128)} custom-call(f32[32,4,128]{2,1,0:T(4,128)S(1)} %all_to_all.5.term_ref, bf16[2,512,512]{2,1,0:T(8,128)(2,1)S(1)} %copy-done), custom_call_target="tpu_custom_call" | custom-call | tf_op jit(solution)/shard_map/sum_of_bins/pallas_call | solution.py:303
Async XLA Ops:
  0.0 1.0 %copy-start.1 = (bf16[2,32,32,128]{3,2,1,0:T(8,128)(2,1)S(1)}, bf16[2,32,32,128]{3,2,1,0:T(8,128)(2,1)}, u32[]{:S(2)}) copy-start(bf16[2,32,32,128]{3,2,1,0:T(8,128)(2,1)} %param.3) | copy-start | bytes 1572868
  1.7 8.0 %collective-permute-start.3 = (bf16[4,64,128]{2,1,0:T(8,128)(2,1)S(1)}, bf16[4,64,128]{2,1,0:T(8,128)(2,1)S(1)}, u32[]{:S(2)}, u32[]{:S(2)}) collective-permute-start(bf16[4,64,128]{2,1,0:T(8,128)(2,1)S(1)} %get-tuple-element.24), channel_id=1, source_target_pairs={{0,8},{8,16},{16,24},{24,0},{1,9},{9,17},{17,25},{25,1},{2,10},{10... | collective-permute-start | bytes 196616 | tf_op jit(solution)/shard_map/ppermute | solution.py:262
  4.8 10.6 %collective-permute-start.4 = (bf16[4,64,128]{2,1,0:T(8,128)(2,1)S(1)}, bf16[4,64,128]{2,1,0:T(8,128)(2,1)S(1)}, u32[]{:S(2)}, u32[]{:S(2)}) collective-permute-start(bf16[4,64,128]{2,1,0:T(8,128)(2,1)S(1)} %get-tuple-element.25), channel_id=1, source_target_pairs={{0,16},{8,24},{16,0},{24,8},{1,17},{9,25},{17,1},{25,9},{2,18},{10... | collective-permute-start | bytes 196616 | tf_op jit(solution)/shard_map/ppermute | solution.py:262
  7.4 8.0 %collective-permute-start.5 = (bf16[4,64,128]{2,1,0:T(8,128)(2,1)S(1)}, bf16[4,64,128]{2,1,0:T(8,128)(2,1)S(1)}, u32[]{:S(2)}, u32[]{:S(2)}) collective-permute-start(bf16[4,64,128]{2,1,0:T(8,128)(2,1)S(1)} %get-tuple-element.26), channel_id=1, source_target_pairs={{0,24},{8,0},{16,8},{24,16},{1,25},{9,1},{17,9},{25,17},{2,26},{10... | collective-permute-start | bytes 196616 | tf_op jit(solution)/shard_map/ppermute | solution.py:262
  8.7 8.3 %collective-permute-start = (bf16[4,64,128]{2,1,0:T(8,128)(2,1)S(1)}, bf16[4,64,128]{2,1,0:T(8,128)(2,1)S(1)}, u32[]{:S(2)}, u32[]{:S(2)}) collective-permute-start(bf16[4,64,128]{2,1,0:T(8,128)(2,1)S(1)} %get-tuple-element.17), channel_id=1, source_target_pairs={{0,8},{8,16},{16,24},{24,0},{1,9},{9,17},{17,25},{25,1},{2,10},{10... | collective-permute-start | bytes 196616 | tf_op jit(solution)/shard_map/ppermute | solution.py:262
  9.4 8.1 %collective-permute-start.1 = (bf16[4,64,128]{2,1,0:T(8,128)(2,1)S(1)}, bf16[4,64,128]{2,1,0:T(8,128)(2,1)S(1)}, u32[]{:S(2)}, u32[]{:S(2)}) collective-permute-start(bf16[4,64,128]{2,1,0:T(8,128)(2,1)S(1)} %get-tuple-element.18), channel_id=1, source_target_pairs={{0,16},{8,24},{16,0},{24,8},{1,17},{9,25},{17,1},{25,9},{2,18},{10... | collective-permute-start | bytes 196616 | tf_op jit(solution)/shard_map/ppermute | solution.py:262
  9.7 7.7 %collective-permute-start.2 = (bf16[4,64,128]{2,1,0:T(8,128)(2,1)S(1)}, bf16[4,64,128]{2,1,0:T(8,128)(2,1)S(1)}, u32[]{:S(2)}, u32[]{:S(2)}) collective-permute-start(bf16[4,64,128]{2,1,0:T(8,128)(2,1)S(1)} %get-tuple-element.19), channel_id=1, source_target_pairs={{0,24},{8,0},{16,8},{24,16},{1,25},{9,1},{17,9},{25,17},{2,26},{10... | collective-permute-start | bytes 196616 | tf_op jit(solution)/shard_map/ppermute | solution.py:262
  12.6 0.7 %copy-start.2 = (s32[4]{0:T(128)S(1)}, s32[4]{0:T(128)}, u32[]{:S(2)}) copy-start(s32[4]{0:T(128)} %position_ref.1) | copy-start | bytes 52
  15.4 16.6 %copy-start = (bf16[2,512,512]{2,1,0:T(8,128)(2,1)S(1)}, bf16[2,512,512]{2,1,0:T(8,128)(2,1)}, u32[]{:S(2)}) copy-start(bf16[2,512,512]{2,1,0:T(8,128)(2,1)} %constant.2.clone.table_ref) | copy-start | bytes 3145732

commit v7 on v4

--- a/solution.py
+++ b/solution.py
@@ -45,8 +45,11 @@
     shift_rows = jnp.where(shift_rows < groups, shift_rows, shift_rows - groups - 1) * BLOCK
     own_group = lax.axis_index("chan")
     first_bin = lax.axis_index("freq") * freq_dev + own_group * bins
-    for distance in range(groups):
-        place_ref[distance] = position_ref[lax.rem(own_group + (groups - distance), groups)]
+    sender = lax.broadcasted_iota(jnp.int32, (groups, groups), 1)
+    distance = lax.broadcasted_iota(jnp.int32, (groups, groups), 0)
+    sends = lax.rem(own_group + groups - distance, groups) == sender
+    places = jnp.sum(jnp.where(sends, position_ref[...], 0), axis=1, keepdims=True)
+    place_ref[...] = jnp.broadcast_to(places, place_ref.shape)
 
     def one_bin(f, carry):
         def phases(rows):
@@ -102,8 +105,9 @@
     place_ref, lag_ref, shift_ref, out_ref, placed_ref, left_ref, part_ref = refs[groups:]
     rows = placed_ref.shape[2]
     windows = rows // 2
+    places = place_ref[...]
     for distance, chunk_ref in enumerate(chunk_refs):
-        placed_ref[place_ref[distance]] = chunk_ref[...]
+        placed_ref[places[distance, 0]] = chunk_ref[...]
 
     row_index = lax.broadcasted_iota(jnp.int32, (BLOCK, BLOCK), 0)
     lag_index = lax.broadcasted_iota(jnp.int32, (BLOCK, BLOCK), 1)
@@ -228,7 +232,6 @@
     slow_dev = SLOWNESS // parts
     message_rows = -(-2 * bins * slow_dev // BLOCK)
     vmem = pl.BlockSpec(memory_space=pltpu.VMEM)
-    smem = pl.BlockSpec(memory_space=pltpu.SMEM)
     params = pltpu.CompilerParams(vmem_limit_bytes=32 * 1024 * 1024)
 
     chunk = jax.ShapeDtypeStruct((bins, rows, BLOCK), jnp.bfloat16)
@@ -248,20 +251,20 @@
     places, lag_table, shift_table = pl.pallas_call(
         functools.partial(table_kernel, groups, bins, freq_dev),
         out_shape=(
-            jax.ShapeDtypeStruct((groups,), jnp.int32),
+            jax.ShapeDtypeStruct((groups, BLOCK), jnp.int32),
             jax.ShapeDtypeStruct((bins, 2 * BLOCK, 2 * SLOWNESS), jnp.bfloat16),
             jax.ShapeDtypeStruct((bins, 2, 2 * groups, SLOWNESS), jnp.float32),
         ),
-        in_specs=[smem],
-        out_specs=(smem, vmem, vmem),
+        in_specs=[vmem],
+        out_specs=(vmem, vmem, vmem),
         compiler_params=params,
         cost_estimate=pl.CostEstimate(flops=10**7, bytes_accessed=4 * 10**6, transcendentals=0),
         name="slant_tables",
-    )(block_position)
+    )(block_position.reshape(1, groups))
     terms = pl.pallas_call(
         functools.partial(stack_kernel, groups, bins, parts),
         out_shape=jax.ShapeDtypeStruct((groups, parts, message_rows, BLOCK), jnp.float32),
-        in_specs=[vmem] * groups + [smem, vmem, vmem],
+        in_specs=[vmem] * (groups + 3),
         out_specs=vmem,
         scratch_shapes=[
             pltpu.VMEM((groups, bins, rows, BLOCK), jnp.bfloat16),

time: 33.6 us -> 33 us (0.982)
  Pallas kernels: 6.25 us -> 4.8 us
  waiting for transfers between devices: 4.5 us -> 5.45 us
    ppermute x3, waiting for transfers between devices: 4.5 us -> 5.45 us  [shards(): arrived_chunks[distance] = lax.ppermute(chunks[distance], 'chan', pairs)]
    pallas_call x1, Pallas kernels: 2.12 us -> 1.19 us  [shards(): pl.pallas_call(functools.partial(table_kernel, groups, bins, freq_dev), o...]
    pallas_call x1, Pallas kernels: 2.5 us -> 1.98 us  [shards(): pl.pallas_call(functools.partial(stack_kernel, groups, bins, parts), out_...]
  transfers between devices with their start and end apart: 3 -> 3, of which waited for: 1 -> 2; matrix products, arithmetic and copies ran while one was open for 0% -> 0% of each run, Pallas kernels for 6% -> 4%
where the time goes in v7:
time: 33 us; the launch traced here: 32.9 us
  blocking collectives  13.8 us (42%)
  starting transfers between devices  7.01 us (21%)
  waiting for transfers between devices  5.45 us (17%)
  Pallas kernels  4.8 us (15%)
  local copies, waits for them, and re-layouts  1.79 us (5%)
    all_to_all x1, blocking collectives, shards(): lax.all_to_all(terms, ('chan', 'freq'), split_axis=0, concat_axis=0, tile...  13.8 us
    ppermute x3, starting transfers between devices, shards(): arrived_chunks[distance] = lax.ppermute(chunks[distance], 'chan', pairs)  7.01 us
    ppermute x3, waiting for transfers between devices, shards(): arrived_chunks[distance] = lax.ppermute(chunks[distance], 'chan', pairs)  5.45 us
    pallas_call x1, Pallas kernels, shards(): pl.pallas_call(functools.partial(stack_kernel, groups, bins, parts), out_...  1.98 us
    unnamed x6, local copies, waits for them, and re-layouts  1.79 us
    pallas_call x1, Pallas kernels, shards(): pl.pallas_call(functools.partial(table_kernel, groups, bins, freq_dev), o...  1.19 us
    pallas_call x1, Pallas kernels, shards(): pl.pallas_call(functools.partial(image_kernel, slow_dev, spans), out_shap...  0.96 us
    pallas_call x1, Pallas kernels, shards(): pl.pallas_call(functools.partial(chunk_kernel, groups, bins), out_shape=(...  0.66 us
  transfers between devices with their start and end apart: 3, of which 2 were waited for; matrix products, arithmetic and copies ran while one was open for 0% of the time, Pallas kernels for 4%

profile of v7, /device:TPU:0, one launch (start us, length us, event | category | flops | bytes accessed | tf_op | source)
XLA Modules:
  0.0 32.9 jit_solution(1651063140752331132)
XLA Ops:
  0.0 0.0 copy-start
  0.0 0.0 copy-start.1
  0.0 1.1 %copy-done.1 = bf16[2,32,32,128]{3,2,1,0:T(8,128)(2,1)S(1)} copy-done((bf16[2,32,32,128]{3,2,1,0:T(8,128)(2,1)S(1)}, bf16[2,32,32,128]{3,2,1,0:T(8,128)(2,1)}, u32[]{:S(2)}) %copy-start.1) | copy-done | bytes 524312
  1.1 0.7 %chunks_of_bins.1 = (bf16[8,64,128]{2,1,0:T(8,128)(2,1)S(1)}, bf16[8,64,128]{2,1,0:T(8,128)(2,1)S(1)}, bf16[8,64,128]{2,1,0:T(8,128)(2,1)S(1)}, bf16[8,64,128]{2,1,0:T(8,128)(2,1)S(1)}) custom-call(bf16[2048,128]{1,0:T(8,128)(2,1)S(1)} %bitcast.3), custom_call_target="tpu_custom_call" | custom-call | tf_op jit(solution)/shard_map/chunks_of_bins/pallas_call | solution.py:238
  1.8 3.1 %collective-permute-start = (bf16[8,64,128]{2,1,0:T(8,128)(2,1)S(1)}, bf16[8,64,128]{2,1,0:T(8,128)(2,1)S(1)}, u32[]{:S(2)}, u32[]{:S(2)}) collective-permute-start(bf16[8,64,128]{2,1,0:T(8,128)(2,1)S(1)} %get-tuple-element.13), channel_id=1, source_target_pairs={{0,8},{8,16},{16,24},{24,0},{1,9},{9,17},{17,25},{25,1},{2,10},{10... | collective-permute-start | bytes 393224 | tf_op jit(solution)/shard_map/ppermute | solution.py:250
  4.9 2.6 %collective-permute-start.1 = (bf16[8,64,128]{2,1,0:T(8,128)(2,1)S(1)}, bf16[8,64,128]{2,1,0:T(8,128)(2,1)S(1)}, u32[]{:S(2)}, u32[]{:S(2)}) collective-permute-start(bf16[8,64,128]{2,1,0:T(8,128)(2,1)S(1)} %get-tuple-element.14), channel_id=1, source_target_pairs={{0,16},{8,24},{16,0},{24,8},{1,17},{9,25},{17,1},{25,9},{2,18},{10... | collective-permute-start | bytes 393224 | tf_op jit(solution)/shard_map/ppermute | solution.py:250
  7.5 1.3 %collective-permute-start.2 = (bf16[8,64,128]{2,1,0:T(8,128)(2,1)S(1)}, bf16[8,64,128]{2,1,0:T(8,128)(2,1)S(1)}, u32[]{:S(2)}, u32[]{:S(2)}) collective-permute-start(bf16[8,64,128]{2,1,0:T(8,128)(2,1)S(1)} %get-tuple-element.15), channel_id=1, source_target_pairs={{0,24},{8,0},{16,8},{24,16},{1,25},{9,1},{17,9},{25,17},{2,26},{10... | collective-permute-start | bytes 393224 | tf_op jit(solution)/shard_map/ppermute | solution.py:250
  8.8 0.0 copy-start.2
  8.8 0.7 %copy-done.2 = s32[4]{0:T(128)S(1)} copy-done((s32[4]{0:T(128)S(1)}, s32[4]{0:T(128)}, u32[]{:S(2)}) %copy-start.2) | copy-done | bytes 40
  9.5 1.2 %slant_tables.1 = (s32[4,128]{1,0:T(4,128)S(1)}, bf16[8,256,512]{2,1,0:T(8,128)(2,1)S(1)}, f32[8,2,8,256]{3,2,1,0:T(8,128)S(1)}) custom-call(s32[1,4]{1,0:T(1,128)S(1)} %bitcast.5), custom_call_target="tpu_custom_call" | custom-call | flops 10000000 | bytes 4000000 | tf_op jit(solution)/shard_map/slant_tables/pallas_call | solution.py:251
  10.7 0.7 %collective-permute-done.refs_1_ = bf16[8,64,128]{2,1,0:T(8,128)(2,1)S(1)} collective-permute-done((bf16[8,64,128]{2,1,0:T(8,128)(2,1)S(1)}, bf16[8,64,128]{2,1,0:T(8,128)(2,1)S(1)}, u32[]{:S(2)}, u32[]{:S(2)}) %collective-permute-start) | collective-permute-done | bytes 131104 | tf_op jit(solution)/shard_map/ppermute | solution.py:250
  11.3 4.8 %collective-permute-done.1.refs_2_ = bf16[8,64,128]{2,1,0:T(8,128)(2,1)S(1)} collective-permute-done((bf16[8,64,128]{2,1,0:T(8,128)(2,1)S(1)}, bf16[8,64,128]{2,1,0:T(8,128)(2,1)S(1)}, u32[]{:S(2)}, u32[]{:S(2)}) %collective-permute-start.1) | collective-permute-done | bytes 131104 | tf_op jit(solution)/shard_map/ppermute | solution.py:250
  16.1 0.0 collective-permute-done.2.refs_3_
  16.1 2.0 %stack_and_slant.1 = f32[4,8,4,128]{3,2,1,0:T(4,128)S(1)} custom-call(bf16[8,64,128]{2,1,0:T(8,128)(2,1)S(1)} %get-tuple-element.12.refs_0_, bf16[8,64,128]{2,1,0:T(8,128)(2,1)S(1)} %collective-permute-done.refs_1_, bf16[8,64,128]{2,1,0:T(8,128)(2,1)S(1)} %collective-permute-done.1.refs_2_, bf16[8,64,128]{2,1,0:T(8,128)(2,1)S(1)} %collective-permute-done.2.refs_3_, ...), custom_call_target="tpu_custom_call" | custom-call | tf_op jit(solution)/shard_map/stack_and_slant/pallas_call | solution.py:264
  18.1 13.8 %all_to_all.5.term_ref = f32[32,4,128]{2,1,0:T(4,128)S(1)} all-to-all(f32[32,4,128]{2,1,0:T(4,128)S(1)} %bitcast.4), channel_id=1, replica_groups=mesh['chan'=4,'freq'=8] {'chan','freq'}, dimensions={0} | all-to-all | bytes 131072 | tf_op jit(solution)/shard_map/all_to_all | solution.py:283
  31.9 0.0 copy-done
  31.9 1.0 %sum_of_bins.1 = f32[1,32,512]{2,1,0:T(8,128)} custom-call(f32[32,4,128]{2,1,0:T(4,128)S(1)} %all_to_all.5.term_ref, bf16[2,512,512]{2,1,0:T(8,128)(2,1)S(1)} %copy-done), custom_call_target="tpu_custom_call" | custom-call | tf_op jit(solution)/shard_map/sum_of_bins/pallas_call | solution.py:285
Async XLA Ops:
  0.0 31.9 %copy-start = (bf16[2,512,512]{2,1,0:T(8,128)(2,1)S(1)}, bf16[2,512,512]{2,1,0:T(8,128)(2,1)}, u32[]{:S(2)}) copy-start(bf16[2,512,512]{2,1,0:T(8,128)(2,1)} %constant.2.clone.table_ref) | copy-start | bytes 3145732
  0.0 1.1 %copy-start.1 = (bf16[2,32,32,128]{3,2,1,0:T(8,128)(2,1)S(1)}, bf16[2,32,32,128]{3,2,1,0:T(8,128)(2,1)}, u32[]{:S(2)}) copy-start(bf16[2,32,32,128]{3,2,1,0:T(8,128)(2,1)} %param.3) | copy-start | bytes 1572868
  1.8 9.5 %collective-permute-start = (bf16[8,64,128]{2,1,0:T(8,128)(2,1)S(1)}, bf16[8,64,128]{2,1,0:T(8,128)(2,1)S(1)}, u32[]{:S(2)}, u32[]{:S(2)}) collective-permute-start(bf16[8,64,128]{2,1,0:T(8,128)(2,1)S(1)} %get-tuple-element.13), channel_id=1, source_target_pairs={{0,8},{8,16},{16,24},{24,0},{1,9},{9,17},{17,25},{25,1},{2,10},{10... | collective-permute-start | bytes 393224 | tf_op jit(solution)/shard_map/ppermute | solution.py:250
  4.9 11.2 %collective-permute-start.1 = (bf16[8,64,128]{2,1,0:T(8,128)(2,1)S(1)}, bf16[8,64,128]{2,1,0:T(8,128)(2,1)S(1)}, u32[]{:S(2)}, u32[]{:S(2)}) collective-permute-start(bf16[8,64,128]{2,1,0:T(8,128)(2,1)S(1)} %get-tuple-element.14), channel_id=1, source_target_pairs={{0,16},{8,24},{16,0},{24,8},{1,17},{9,25},{17,1},{25,9},{2,18},{10... | collective-permute-start | bytes 393224 | tf_op jit(solution)/shard_map/ppermute | solution.py:250
  7.5 8.6 %collective-permute-start.2 = (bf16[8,64,128]{2,1,0:T(8,128)(2,1)S(1)}, bf16[8,64,128]{2,1,0:T(8,128)(2,1)S(1)}, u32[]{:S(2)}, u32[]{:S(2)}) collective-permute-start(bf16[8,64,128]{2,1,0:T(8,128)(2,1)S(1)} %get-tuple-element.15), channel_id=1, source_target_pairs={{0,24},{8,0},{16,8},{24,16},{1,25},{9,1},{17,9},{25,17},{2,26},{10... | collective-permute-start | bytes 393224 | tf_op jit(solution)/shard_map/ppermute | solution.py:250
  8.8 0.7 %copy-start.2 = (s32[4]{0:T(128)S(1)}, s32[4]{0:T(128)}, u32[]{:S(2)}) copy-start(s32[4]{0:T(128)} %param.4) | copy-start | bytes 52

commit v8 on v7

--- a/solution.py
+++ b/solution.py
@@ -46,8 +46,8 @@
     own_group = lax.axis_index("chan")
     first_bin = lax.axis_index("freq") * freq_dev + own_group * bins
     sender = lax.broadcasted_iota(jnp.int32, (groups, groups), 1)
-    distance = lax.broadcasted_iota(jnp.int32, (groups, groups), 0)
-    sends = lax.rem(own_group + groups - distance, groups) == sender
+    mask = lax.broadcasted_iota(jnp.int32, (groups, groups), 0)
+    sends = lax.bitwise_xor(own_group, mask) == sender
     places = jnp.sum(jnp.where(sends, position_ref[...], 0), axis=1, keepdims=True)
     place_ref[...] = jnp.broadcast_to(places, place_ref.shape)
 
@@ -82,8 +82,8 @@
     freq_dev = groups * bins
     rows = spec_ref.shape[0] // freq_dev
     own_group = lax.axis_index("chan")
-    for distance, out_ref in enumerate(out_refs):
-        first = lax.rem(own_group + distance, groups) * bins
+    for mask, out_ref in enumerate(out_refs):
+        first = lax.bitwise_xor(own_group, mask) * bins
         for f in range(bins):
             value = wide_ref[pl.ds(first + f, rows, stride=freq_dev), :]
             out_ref[f] = value.astype(jnp.bfloat16)
@@ -106,13 +106,13 @@
     rows = placed_ref.shape[2]
     windows = rows // 2
     places = place_ref[...]
-    for distance, chunk_ref in enumerate(chunk_refs):
-        placed_ref[places[distance, 0]] = chunk_ref[...]
+    for mask, chunk_ref in enumerate(chunk_refs):
+        placed_ref[places[mask, 0]] = chunk_ref[...]
 
     row_index = lax.broadcasted_iota(jnp.int32, (BLOCK, BLOCK), 0)
     lag_index = lax.broadcasted_iota(jnp.int32, (BLOCK, BLOCK), 1)
     mirror = jnp.where(row_index + lag_index == BLOCK - 1, 1.0, 0.0).astype(jnp.bfloat16)
-    ahead = lag_index <= row_index
+    behind = (lag_index - row_index)[:8]
 
     for f in range(bins):
         left_ref[f] = lax.dot_general(
@@ -142,10 +142,13 @@
             for half in range(2):
                 lanes = slice(half * BLOCK, (half + 1) * BLOCK)
                 skewed = pltpu.roll(panel[:, lanes], 1, 1, stride=1, stride_axis=0)
-                forward = jnp.where(ahead, skewed, 0.0).reshape(-1, 8, BLOCK).sum(0)
-                backward = jnp.where(ahead, 0.0, skewed).reshape(-1, 8, BLOCK).sum(0)
+                total = skewed[:8]
+                backward = jnp.where(behind > 0, total, 0.0)
+                for row in range(8, BLOCK, 8):
+                    total = total + skewed[row : row + 8]
+                    backward = jnp.where(behind > row, total, backward)
                 first = (f * 2 * groups + delta) * 8
-                part_ref[half, first : first + 8] = forward
+                part_ref[half, first : first + 8] = total - backward
                 part_ref[half, first + groups * 8 : first + groups * 8 + 8] = backward
 
     lags = []
@@ -245,9 +248,9 @@
         name="chunks_of_bins",
     )(spectra.reshape(rows * freq_dev, BLOCK))
     arrived_chunks = list(chunks)
-    for distance in sorted(range(1, groups), key=lambda steps: abs(2 * steps - groups)):
-        pairs = [(source, (source + distance) % groups) for source in range(groups)]
-        arrived_chunks[distance] = lax.ppermute(chunks[distance], "chan", pairs)
+    for mask in list(range(groups // 2, groups)) + list(range(groups // 2 - 1, 0, -1)):
+        pairs = [(source, source ^ mask) for source in range(groups)]
+        arrived_chunks[mask] = lax.ppermute(chunks[mask], "chan", pairs)
     places, lag_table, shift_table = pl.pallas_call(
         functools.partial(table_kernel, groups, bins, freq_dev),
         out_shape=(

time: 33 us -> 33.4 us (1.012)
  waiting for transfers between devices: 5.45 us -> 8.49 us
  blocking collectives: 13.8 us -> 12.4 us
  starting transfers between devices: 7.01 us -> 5.68 us
    ppermute x3, waiting for transfers between devices: 5.45 us -> 8.49 us  [shards(): arrived_chunks[mask] = lax.ppermute(chunks[mask], 'chan', pairs)]
    all_to_all x1, blocking collectives: 13.8 us -> 12.4 us  [shards(): lax.all_to_all(terms, ('chan', 'freq'), split_axis=0, concat_axis=0, tile...]
    ppermute x3, starting transfers between devices: 7.01 us -> 5.68 us  [shards(): arrived_chunks[mask] = lax.ppermute(chunks[mask], 'chan', pairs)]
where the time goes in v8:
time: 33.4 us; the launch traced here: 33.2 us
  blocking collectives  12.4 us (37%)
  waiting for transfers between devices  8.49 us (25%)
  starting transfers between devices  5.68 us (17%)
  Pallas kernels  4.78 us (14%)
  local copies, waits for them, and re-layouts  1.79 us (5%)
    all_to_all x1, blocking collectives, shards(): lax.all_to_all(terms, ('chan', 'freq'), split_axis=0, concat_axis=0, tile...  12.4 us
    ppermute x3, waiting for transfers between devices, shards(): arrived_chunks[mask] = lax.ppermute(chunks[mask], 'chan', pairs)  8.49 us
    ppermute x3, starting transfers between devices, shards(): arrived_chunks[mask] = lax.ppermute(chunks[mask], 'chan', pairs)  5.68 us
    pallas_call x1, Pallas kernels, shards(): pl.pallas_call(functools.partial(stack_kernel, groups, bins, parts), out_...  1.97 us
    unnamed x6, local copies, waits for them, and re-layouts  1.79 us
    pallas_call x1, Pallas kernels, shards(): pl.pallas_call(functools.partial(table_kernel, groups, bins, freq_dev), o...  1.18 us
    pallas_call x1, Pallas kernels, shards(): pl.pallas_call(functools.partial(image_kernel, slow_dev, spans), out_shap...  0.96 us
  transfers between devices with their start and end apart: 3, of which 2 were waited for; matrix products, arithmetic and copies ran while one was open for 0% of the time, Pallas kernels for 4%

profile of v8, /device:TPU:0, one launch (start us, length us, event | category | flops | bytes accessed | tf_op | source)
XLA Modules:
  0.0 33.2 jit_solution(12284817738961519569)
XLA Ops:
  0.0 0.0 copy-start
  0.0 0.0 copy-start.1
  0.0 1.1 %copy-done.1 = bf16[2,32,32,128]{3,2,1,0:T(8,128)(2,1)S(1)} copy-done((bf16[2,32,32,128]{3,2,1,0:T(8,128)(2,1)S(1)}, bf16[2,32,32,128]{3,2,1,0:T(8,128)(2,1)}, u32[]{:S(2)}) %copy-start.1) | copy-done | bytes 524312
  1.1 0.7 %chunks_of_bins.1 = (bf16[8,64,128]{2,1,0:T(8,128)(2,1)S(1)}, bf16[8,64,128]{2,1,0:T(8,128)(2,1)S(1)}, bf16[8,64,128]{2,1,0:T(8,128)(2,1)S(1)}, bf16[8,64,128]{2,1,0:T(8,128)(2,1)S(1)}) custom-call(bf16[2048,128]{1,0:T(8,128)(2,1)S(1)} %bitcast.3), custom_call_target="tpu_custom_call" | custom-call | tf_op jit(solution)/shard_map/chunks_of_bins/pallas_call | solution.py:241
  1.8 3.1 %collective-permute-start = (bf16[8,64,128]{2,1,0:T(8,128)(2,1)S(1)}, bf16[8,64,128]{2,1,0:T(8,128)(2,1)S(1)}, u32[]{:S(2)}, u32[]{:S(2)}) collective-permute-start(bf16[8,64,128]{2,1,0:T(8,128)(2,1)S(1)} %get-tuple-element.13), channel_id=1, source_target_pairs={{0,8},{8,0},{16,24},{24,16},{1,9},{9,1},{17,25},{25,17},{2,10},{10... | collective-permute-start | bytes 393224 | tf_op jit(solution)/shard_map/ppermute | solution.py:253
  4.9 2.6 %collective-permute-start.1 = (bf16[8,64,128]{2,1,0:T(8,128)(2,1)S(1)}, bf16[8,64,128]{2,1,0:T(8,128)(2,1)S(1)}, u32[]{:S(2)}, u32[]{:S(2)}) collective-permute-start(bf16[8,64,128]{2,1,0:T(8,128)(2,1)S(1)} %get-tuple-element.14), channel_id=1, source_target_pairs={{0,16},{8,24},{16,0},{24,8},{1,17},{9,25},{17,1},{25,9},{2,18},{10... | collective-permute-start | bytes 393224 | tf_op jit(solution)/shard_map/ppermute | solution.py:253
  7.5 0.0 collective-permute-start.2
  7.5 0.0 copy-start.2
  7.5 0.7 %copy-done.2 = s32[4]{0:T(128)S(1)} copy-done((s32[4]{0:T(128)S(1)}, s32[4]{0:T(128)}, u32[]{:S(2)}) %copy-start.2) | copy-done | bytes 40
  8.1 1.2 %slant_tables.1 = (s32[4,128]{1,0:T(4,128)S(1)}, bf16[8,256,512]{2,1,0:T(8,128)(2,1)S(1)}, f32[8,2,8,256]{3,2,1,0:T(8,128)S(1)}) custom-call(s32[1,4]{1,0:T(1,128)S(1)} %bitcast.5), custom_call_target="tpu_custom_call" | custom-call | flops 10000000 | bytes 4000000 | tf_op jit(solution)/shard_map/slant_tables/pallas_call | solution.py:254
  9.3 0.6 %collective-permute-done.refs_1_ = bf16[8,64,128]{2,1,0:T(8,128)(2,1)S(1)} collective-permute-done((bf16[8,64,128]{2,1,0:T(8,128)(2,1)S(1)}, bf16[8,64,128]{2,1,0:T(8,128)(2,1)S(1)}, u32[]{:S(2)}, u32[]{:S(2)}) %collective-permute-start) | collective-permute-done | bytes 131104 | tf_op jit(solution)/shard_map/ppermute | solution.py:253
  9.9 7.9 %collective-permute-done.1.refs_2_ = bf16[8,64,128]{2,1,0:T(8,128)(2,1)S(1)} collective-permute-done((bf16[8,64,128]{2,1,0:T(8,128)(2,1)S(1)}, bf16[8,64,128]{2,1,0:T(8,128)(2,1)S(1)}, u32[]{:S(2)}, u32[]{:S(2)}) %collective-permute-start.1) | collective-permute-done | bytes 131104 | tf_op jit(solution)/shard_map/ppermute | solution.py:253
  17.8 0.0 collective-permute-done.2.refs_3_
  17.8 2.0 %stack_and_slant.1 = f32[4,8,4,128]{3,2,1,0:T(4,128)S(1)} custom-call(bf16[8,64,128]{2,1,0:T(8,128)(2,1)S(1)} %get-tuple-element.12.refs_0_, bf16[8,64,128]{2,1,0:T(8,128)(2,1)S(1)} %collective-permute-done.refs_1_, bf16[8,64,128]{2,1,0:T(8,128)(2,1)S(1)} %collective-permute-done.1.refs_2_, bf16[8,64,128]{2,1,0:T(8,128)(2,1)S(1)} %collective-permute-done.2.refs_3_, ...), custom_call_target="tpu_custom_call" | custom-call | tf_op jit(solution)/shard_map/stack_and_slant/pallas_call | solution.py:267
  19.8 12.4 %all_to_all.5.term_ref = f32[32,4,128]{2,1,0:T(4,128)S(1)} all-to-all(f32[32,4,128]{2,1,0:T(4,128)S(1)} %bitcast.4), channel_id=1, replica_groups=mesh['chan'=4,'freq'=8] {'chan','freq'}, dimensions={0} | all-to-all | bytes 131072 | tf_op jit(solution)/shard_map/all_to_all | solution.py:286
  32.2 0.0 copy-done
  32.2 1.0 %sum_of_bins.1 = f32[1,32,512]{2,1,0:T(8,128)} custom-call(f32[32,4,128]{2,1,0:T(4,128)S(1)} %all_to_all.5.term_ref, bf16[2,512,512]{2,1,0:T(8,128)(2,1)S(1)} %copy-done), custom_call_target="tpu_custom_call" | custom-call | tf_op jit(solution)/shard_map/sum_of_bins/pallas_call | solution.py:288
Async XLA Ops:
  0.0 32.2 %copy-start = (bf16[2,512,512]{2,1,0:T(8,128)(2,1)S(1)}, bf16[2,512,512]{2,1,0:T(8,128)(2,1)}, u32[]{:S(2)}) copy-start(bf16[2,512,512]{2,1,0:T(8,128)(2,1)} %constant.2.clone.table_ref) | copy-start | bytes 3145732
  0.0 1.1 %copy-start.1 = (bf16[2,32,32,128]{3,2,1,0:T(8,128)(2,1)S(1)}, bf16[2,32,32,128]{3,2,1,0:T(8,128)(2,1)}, u32[]{:S(2)}) copy-start(bf16[2,32,32,128]{3,2,1,0:T(8,128)(2,1)} %param.3) | copy-start | bytes 1572868
  1.8 8.1 %collective-permute-start = (bf16[8,64,128]{2,1,0:T(8,128)(2,1)S(1)}, bf16[8,64,128]{2,1,0:T(8,128)(2,1)S(1)}, u32[]{:S(2)}, u32[]{:S(2)}) collective-permute-start(bf16[8,64,128]{2,1,0:T(8,128)(2,1)S(1)} %get-tuple-element.13), channel_id=1, source_target_pairs={{0,8},{8,0},{16,24},{24,16},{1,9},{9,1},{17,25},{25,17},{2,10},{10... | collective-permute-start | bytes 393224 | tf_op jit(solution)/shard_map/ppermute | solution.py:253
  4.9 12.9 %collective-permute-start.1 = (bf16[8,64,128]{2,1,0:T(8,128)(2,1)S(1)}, bf16[8,64,128]{2,1,0:T(8,128)(2,1)S(1)}, u32[]{:S(2)}, u32[]{:S(2)}) collective-permute-start(bf16[8,64,128]{2,1,0:T(8,128)(2,1)S(1)} %get-tuple-element.14), channel_id=1, source_target_pairs={{0,16},{8,24},{16,0},{24,8},{1,17},{9,25},{17,1},{25,9},{2,18},{10... | collective-permute-start | bytes 393224 | tf_op jit(solution)/shard_map/ppermute | solution.py:253
  7.5 10.3 %collective-permute-start.2 = (bf16[8,64,128]{2,1,0:T(8,128)(2,1)S(1)}, bf16[8,64,128]{2,1,0:T(8,128)(2,1)S(1)}, u32[]{:S(2)}, u32[]{:S(2)}) collective-permute-start(bf16[8,64,128]{2,1,0:T(8,128)(2,1)S(1)} %get-tuple-element.15), channel_id=1, source_target_pairs={{0,24},{8,16},{16,8},{24,0},{1,25},{9,17},{17,9},{25,1},{2,26},{10... | collective-permute-start | bytes 393224 | tf_op jit(solution)/shard_map/ppermute | solution.py:253
  7.5 0.7 %copy-start.2 = (s32[4]{0:T(128)S(1)}, s32[4]{0:T(128)}, u32[]{:S(2)}) copy-start(s32[4]{0:T(128)} %param.4) | copy-start | bytes 52

commit v9 on v8

--- a/solution.py
+++ b/solution.py
@@ -76,6 +76,10 @@
     lax.fori_loop(0, bins, one_bin, 0)
 
 
+def partner_order(groups):
+    return list(range(groups // 2, groups)) + list(range(groups // 2 - 1, -1, -1))
+
+
 def chunk_kernel(groups, bins, spec_ref, *refs):
     out_refs, wide_ref = refs[:-1], refs[-1]
     wide_ref[...] = spec_ref[...].astype(jnp.float32)
@@ -106,7 +110,7 @@
     rows = placed_ref.shape[2]
     windows = rows // 2
     places = place_ref[...]
-    for mask, chunk_ref in enumerate(chunk_refs):
+    for mask, chunk_ref in zip(partner_order(groups), chunk_refs):
         placed_ref[places[mask, 0]] = chunk_ref[...]
 
     row_index = lax.broadcasted_iota(jnp.int32, (BLOCK, BLOCK), 0)
@@ -248,7 +252,8 @@
         name="chunks_of_bins",
     )(spectra.reshape(rows * freq_dev, BLOCK))
     arrived_chunks = list(chunks)
-    for mask in list(range(groups // 2, groups)) + list(range(groups // 2 - 1, 0, -1)):
+    order = partner_order(groups)
+    for mask in order[:-1]:
         pairs = [(source, source ^ mask) for source in range(groups)]
         arrived_chunks[mask] = lax.ppermute(chunks[mask], "chan", pairs)
     places, lag_table, shift_table = pl.pallas_call(
@@ -277,7 +282,7 @@
         compiler_params=params,
         name="stack_and_slant",
     )(
-        *arrived_chunks,
+        *[arrived_chunks[mask] for mask in order],
         places,
         lag_table,
         shift_table,

time: 33.4 us -> 33.1 us (level)
  waiting for transfers between devices: 8.49 us -> 7.08 us
  blocking collectives: 12.4 us -> 13.6 us
    ppermute x3, waiting for transfers between devices: 8.49 us -> 7.08 us  [shards(): arrived_chunks[mask] = lax.ppermute(chunks[mask], 'chan', pairs)]
    all_to_all x1, blocking collectives: 12.4 us -> 13.6 us  [shards(): lax.all_to_all(terms, ('chan', 'freq'), split_axis=0, concat_axis=0, tile...]
where the time goes in v9:
time: 33.1 us; the launch traced here: 32.9 us
  blocking collectives  13.6 us (41%)
  waiting for transfers between devices  7.08 us (21%)
  starting transfers between devices  5.68 us (17%)
  Pallas kernels  4.78 us (14%)
  local copies, waits for them, and re-layouts  1.79 us (5%)
    all_to_all x1, blocking collectives, shards(): lax.all_to_all(terms, ('chan', 'freq'), split_axis=0, concat_axis=0, tile...  13.6 us
    ppermute x3, waiting for transfers between devices, shards(): arrived_chunks[mask] = lax.ppermute(chunks[mask], 'chan', pairs)  7.08 us
    ppermute x3, starting transfers between devices, shards(): arrived_chunks[mask] = lax.ppermute(chunks[mask], 'chan', pairs)  5.68 us
    pallas_call x1, Pallas kernels, shards(): pl.pallas_call(functools.partial(stack_kernel, groups, bins, parts), out_...  1.97 us
    unnamed x6, local copies, waits for them, and re-layouts  1.79 us
    pallas_call x1, Pallas kernels, shards(): pl.pallas_call(functools.partial(table_kernel, groups, bins, freq_dev), o...  1.18 us
    pallas_call x1, Pallas kernels, shards(): pl.pallas_call(functools.partial(image_kernel, slow_dev, spans), out_shap...  0.97 us
  transfers between devices with their start and end apart: 3, of which 2 were waited for; matrix products, arithmetic and copies ran while one was open for 0% of the time, Pallas kernels for 4%

profile of v9, /device:TPU:0, one launch (start us, length us, event | category | flops | bytes accessed | tf_op | source)
XLA Modules:
  0.0 32.9 jit_solution(1728358953269950797)
XLA Ops:
  0.0 0.0 copy-start
  0.0 0.0 copy-start.1
  0.0 1.1 %copy-done.1 = bf16[2,32,32,128]{3,2,1,0:T(8,128)(2,1)S(1)} copy-done((bf16[2,32,32,128]{3,2,1,0:T(8,128)(2,1)S(1)}, bf16[2,32,32,128]{3,2,1,0:T(8,128)(2,1)}, u32[]{:S(2)}) %copy-start.1) | copy-done | bytes 524312
  1.1 0.7 %chunks_of_bins.1 = (bf16[8,64,128]{2,1,0:T(8,128)(2,1)S(1)}, bf16[8,64,128]{2,1,0:T(8,128)(2,1)S(1)}, bf16[8,64,128]{2,1,0:T(8,128)(2,1)S(1)}, bf16[8,64,128]{2,1,0:T(8,128)(2,1)S(1)}) custom-call(bf16[2048,128]{1,0:T(8,128)(2,1)S(1)} %bitcast.3), custom_call_target="tpu_custom_call" | custom-call | tf_op jit(solution)/shard_map/chunks_of_bins/pallas_call | solution.py:245
  1.8 4.1 %collective-permute-start = (bf16[8,64,128]{2,1,0:T(8,128)(2,1)S(1)}, bf16[8,64,128]{2,1,0:T(8,128)(2,1)S(1)}, u32[]{:S(2)}, u32[]{:S(2)}) collective-permute-start(bf16[8,64,128]{2,1,0:T(8,128)(2,1)S(1)} %get-tuple-element.12), channel_id=1, source_target_pairs={{0,16},{8,24},{16,0},{24,8},{1,17},{9,25},{17,1},{25,9},{2,18},{10... | collective-permute-start | bytes 393224 | tf_op jit(solution)/shard_map/ppermute | solution.py:258
  5.9 1.3 %collective-permute-start.1 = (bf16[8,64,128]{2,1,0:T(8,128)(2,1)S(1)}, bf16[8,64,128]{2,1,0:T(8,128)(2,1)S(1)}, u32[]{:S(2)}, u32[]{:S(2)}) collective-permute-start(bf16[8,64,128]{2,1,0:T(8,128)(2,1)S(1)} %get-tuple-element.13), channel_id=1, source_target_pairs={{0,24},{8,16},{16,8},{24,0},{1,25},{9,17},{17,9},{25,1},{2,26},{10... | collective-permute-start | bytes 393224 | tf_op jit(solution)/shard_map/ppermute | solution.py:258
  7.2 0.2 collective-permute-start.2
  7.5 0.0 copy-start.2
  7.5 0.7 %copy-done.2 = s32[4]{0:T(128)S(1)} copy-done((s32[4]{0:T(128)S(1)}, s32[4]{0:T(128)}, u32[]{:S(2)}) %copy-start.2) | copy-done | bytes 40
  8.1 1.2 %slant_tables.1 = (s32[4,128]{1,0:T(4,128)S(1)}, bf16[8,256,512]{2,1,0:T(8,128)(2,1)S(1)}, f32[8,2,8,256]{3,2,1,0:T(8,128)S(1)}) custom-call(s32[1,4]{1,0:T(1,128)S(1)} %bitcast.5), custom_call_target="tpu_custom_call" | custom-call | flops 10000000 | bytes 4000000 | tf_op jit(solution)/shard_map/slant_tables/pallas_call | solution.py:259
  9.3 6.6 %collective-permute-done.refs_0_ = bf16[8,64,128]{2,1,0:T(8,128)(2,1)S(1)} collective-permute-done((bf16[8,64,128]{2,1,0:T(8,128)(2,1)S(1)}, bf16[8,64,128]{2,1,0:T(8,128)(2,1)S(1)}, u32[]{:S(2)}, u32[]{:S(2)}) %collective-permute-start) | collective-permute-done | bytes 131104 | tf_op jit(solution)/shard_map/ppermute | solution.py:258
  15.9 0.0 collective-permute-done.1.refs_1_
  15.9 0.5 %collective-permute-done.2.refs_2_ = bf16[8,64,128]{2,1,0:T(8,128)(2,1)S(1)} collective-permute-done((bf16[8,64,128]{2,1,0:T(8,128)(2,1)S(1)}, bf16[8,64,128]{2,1,0:T(8,128)(2,1)S(1)}, u32[]{:S(2)}, u32[]{:S(2)}) %collective-permute-start.2) | collective-permute-done | bytes 131104 | tf_op jit(solution)/shard_map/ppermute | solution.py:258
  16.4 2.0 %stack_and_slant.1 = f32[4,8,4,128]{3,2,1,0:T(4,128)S(1)} custom-call(bf16[8,64,128]{2,1,0:T(8,128)(2,1)S(1)} %collective-permute-done.refs_0_, bf16[8,64,128]{2,1,0:T(8,128)(2,1)S(1)} %collective-permute-done.1.refs_1_, bf16[8,64,128]{2,1,0:T(8,128)(2,1)S(1)} %collective-permute-done.2.refs_2_, bf16[8,64,128]{2,1,0:T(8,128)(2,1)S(1)} %get-tuple-element.15.refs_3_, ...), custom_call_target="tpu_custom_call" | custom-call | tf_op jit(solution)/shard_map/stack_and_slant/pallas_call | solution.py:272
  18.4 13.6 %all_to_all.5.term_ref = f32[32,4,128]{2,1,0:T(4,128)S(1)} all-to-all(f32[32,4,128]{2,1,0:T(4,128)S(1)} %bitcast.4), channel_id=1, replica_groups=mesh['chan'=4,'freq'=8] {'chan','freq'}, dimensions={0} | all-to-all | bytes 131072 | tf_op jit(solution)/shard_map/all_to_all | solution.py:291
  32.0 0.0 copy-done
  32.0 1.0 %sum_of_bins.1 = f32[1,32,512]{2,1,0:T(8,128)} custom-call(f32[32,4,128]{2,1,0:T(4,128)S(1)} %all_to_all.5.term_ref, bf16[2,512,512]{2,1,0:T(8,128)(2,1)S(1)} %copy-done), custom_call_target="tpu_custom_call" | custom-call | tf_op jit(solution)/shard_map/sum_of_bins/pallas_call | solution.py:293
Async XLA Ops:
  0.0 32.0 %copy-start = (bf16[2,512,512]{2,1,0:T(8,128)(2,1)S(1)}, bf16[2,512,512]{2,1,0:T(8,128)(2,1)}, u32[]{:S(2)}) copy-start(bf16[2,512,512]{2,1,0:T(8,128)(2,1)} %constant.2.clone.table_ref) | copy-start | bytes 3145732
  0.0 1.1 %copy-start.1 = (bf16[2,32,32,128]{3,2,1,0:T(8,128)(2,1)S(1)}, bf16[2,32,32,128]{3,2,1,0:T(8,128)(2,1)}, u32[]{:S(2)}) copy-start(bf16[2,32,32,128]{3,2,1,0:T(8,128)(2,1)} %param.3) | copy-start | bytes 1572868
  1.8 14.1 %collective-permute-start = (bf16[8,64,128]{2,1,0:T(8,128)(2,1)S(1)}, bf16[8,64,128]{2,1,0:T(8,128)(2,1)S(1)}, u32[]{:S(2)}, u32[]{:S(2)}) collective-permute-start(bf16[8,64,128]{2,1,0:T(8,128)(2,1)S(1)} %get-tuple-element.12), channel_id=1, source_target_pairs={{0,16},{8,24},{16,0},{24,8},{1,17},{9,25},{17,1},{25,9},{2,18},{10... | collective-permute-start | bytes 393224 | tf_op jit(solution)/shard_map/ppermute | solution.py:258
  5.9 10.0 %collective-permute-start.1 = (bf16[8,64,128]{2,1,0:T(8,128)(2,1)S(1)}, bf16[8,64,128]{2,1,0:T(8,128)(2,1)S(1)}, u32[]{:S(2)}, u32[]{:S(2)}) collective-permute-start(bf16[8,64,128]{2,1,0:T(8,128)(2,1)S(1)} %get-tuple-element.13), channel_id=1, source_target_pairs={{0,24},{8,16},{16,8},{24,0},{1,25},{9,17},{17,9},{25,1},{2,26},{10... | collective-permute-start | bytes 393224 | tf_op jit(solution)/shard_map/ppermute | solution.py:258
  7.2 9.2 %collective-permute-start.2 = (bf16[8,64,128]{2,1,0:T(8,128)(2,1)S(1)}, bf16[8,64,128]{2,1,0:T(8,128)(2,1)S(1)}, u32[]{:S(2)}, u32[]{:S(2)}) collective-permute-start(bf16[8,64,128]{2,1,0:T(8,128)(2,1)S(1)} %get-tuple-element.14), channel_id=1, source_target_pairs={{0,8},{8,0},{16,24},{24,16},{1,9},{9,1},{17,25},{25,17},{2,10},{10... | collective-permute-start | bytes 393224 | tf_op jit(solution)/shard_map/ppermute | solution.py:258
  7.5 0.7 %copy-start.2 = (s32[4]{0:T(128)S(1)}, s32[4]{0:T(128)}, u32[]{:S(2)}) copy-start(s32[4]{0:T(128)} %param.4) | copy-start | bytes 52

commit v10 on v9

--- a/solution.py
+++ b/solution.py
@@ -38,7 +38,13 @@
     return high, (value - high.astype(jnp.float32)).astype(jnp.bfloat16)
 
 
-def table_kernel(groups, bins, freq_dev, position_ref, place_ref, lag_ref, shift_ref):
+def table_kernel(
+    groups, bins, freq_dev, position_ref, far_ref, place_ref, ordered_ref, lag_ref, shift_ref, wide_ref
+):
+    rows = far_ref.shape[0] // bins
+    wide_ref[...] = far_ref[...].astype(jnp.float32)
+    for f in range(bins):
+        ordered_ref[f] = wide_ref[pl.ds(f, rows, stride=bins), :].astype(jnp.bfloat16)
     low_rows = lax.broadcasted_iota(jnp.int32, (8, SLOWNESS), 0)
     high_rows = lax.broadcasted_iota(jnp.int32, (BLOCK // 8, SLOWNESS), 0) * 8
     shift_rows = lax.broadcasted_iota(jnp.int32, (2 * groups, SLOWNESS), 0)
@@ -80,13 +86,13 @@
     return list(range(groups // 2, groups)) + list(range(groups // 2 - 1, -1, -1))
 
 
-def chunk_kernel(groups, bins, spec_ref, *refs):
+def chunk_kernel(groups, bins, masks, spec_ref, far_ref, *refs):
     out_refs, wide_ref = refs[:-1], refs[-1]
     wide_ref[...] = spec_ref[...].astype(jnp.float32)
     freq_dev = groups * bins
     rows = spec_ref.shape[0] // freq_dev
     own_group = lax.axis_index("chan")
-    for mask, out_ref in enumerate(out_refs):
+    for mask, out_ref in zip(masks, out_refs):
         first = lax.bitwise_xor(own_group, mask) * bins
         for f in range(bins):
             value = wide_ref[pl.ds(first + f, rows, stride=freq_dev), :]
@@ -241,34 +247,40 @@
     vmem = pl.BlockSpec(memory_space=pltpu.VMEM)
     params = pltpu.CompilerParams(vmem_limit_bytes=32 * 1024 * 1024)
 
-    chunk = jax.ShapeDtypeStruct((bins, rows, BLOCK), jnp.bfloat16)
-    chunks = pl.pallas_call(
-        functools.partial(chunk_kernel, groups, bins),
-        out_shape=(chunk,) * groups,
-        in_specs=[vmem],
-        out_specs=(vmem,) * groups,
+    order = partner_order(groups)
+    far, others = order[0], order[1:]
+    group = lax.bitwise_xor(lax.axis_index("chan"), far)
+    by_group = spectra.reshape(rows, groups, bins, BLOCK)
+    far_chunk = lax.dynamic_index_in_dim(by_group, group, 1, False).reshape(rows * bins, BLOCK)
+    other_chunks = pl.pallas_call(
+        functools.partial(chunk_kernel, groups, bins, others),
+        out_shape=(jax.ShapeDtypeStruct((bins, rows, BLOCK), jnp.bfloat16),) * len(others),
+        in_specs=[vmem, pl.BlockSpec(memory_space=pl.ANY)],
+        out_specs=(vmem,) * len(others),
         scratch_shapes=[pltpu.VMEM((rows * freq_dev, BLOCK), jnp.float32)],
         compiler_params=params,
+        cost_estimate=pl.CostEstimate(flops=10**7, bytes_accessed=4 * 10**6, transcendentals=0),
         name="chunks_of_bins",
-    )(spectra.reshape(rows * freq_dev, BLOCK))
-    arrived_chunks = list(chunks)
-    order = partner_order(groups)
+    )(spectra.reshape(rows * freq_dev, BLOCK), far_chunk)
+    chunks = dict(zip(order, (far_chunk, *other_chunks)))
     for mask in order[:-1]:
         pairs = [(source, source ^ mask) for source in range(groups)]
-        arrived_chunks[mask] = lax.ppermute(chunks[mask], "chan", pairs)
-    places, lag_table, shift_table = pl.pallas_call(
+        chunks[mask] = lax.ppermute(chunks[mask], "chan", pairs)
+    places, chunks[far], lag_table, shift_table = pl.pallas_call(
         functools.partial(table_kernel, groups, bins, freq_dev),
         out_shape=(
             jax.ShapeDtypeStruct((groups, BLOCK), jnp.int32),
+            jax.ShapeDtypeStruct((bins, rows, BLOCK), jnp.bfloat16),
             jax.ShapeDtypeStruct((bins, 2 * BLOCK, 2 * SLOWNESS), jnp.bfloat16),
             jax.ShapeDtypeStruct((bins, 2, 2 * groups, SLOWNESS), jnp.float32),
         ),
-        in_specs=[vmem],
-        out_specs=(vmem, vmem, vmem),
+        in_specs=[vmem, vmem],
+        out_specs=(vmem,) * 4,
+        scratch_shapes=[pltpu.VMEM((rows * bins, BLOCK), jnp.float32)],
         compiler_params=params,
         cost_estimate=pl.CostEstimate(flops=10**7, bytes_accessed=4 * 10**6, transcendentals=0),
         name="slant_tables",
-    )(block_position.reshape(1, groups))
+    )(block_position.reshape(1, groups), chunks[far])
     terms = pl.pallas_call(
         functools.partial(stack_kernel, groups, bins, parts),
         out_shape=jax.ShapeDtypeStruct((groups, parts, message_rows, BLOCK), jnp.float32),
@@ -282,7 +294,7 @@
         compiler_params=params,
         name="stack_and_slant",
     )(
-        *[arrived_chunks[mask] for mask in order],
+        *[chunks[mask] for mask in order],
         places,
         lag_table,
         shift_table,

time: 33.1 us -> 33.2 us (level)
  local copies, waits for them, and re-layouts: 1.79 us -> 2.7 us
  blocking collectives: 13.6 us -> 13 us
    reshape x0 -> x1, local copies, waits for them, and re-layouts: none -> 1 us  [shards(): lax.dynamic_index_in_dim(by_group, group, 1, False)]
    all_to_all x1, blocking collectives: 13.6 us -> 13 us  [shards(): lax.all_to_all(terms, ('chan', 'freq'), split_axis=0, concat_axis=0, tile...]
  transfers between devices with their start and end apart: 3 -> 3, of which waited for: 2 -> 2; matrix products, arithmetic and copies ran while one was open for 0% -> 0% of each run, Pallas kernels for 4% -> 5%
where the time goes in v10:
time: 33.2 us; the launch traced here: 33 us
  blocking collectives  13 us (39%)
  waiting for transfers between devices  6.78 us (20%)
  starting transfers between devices  5.82 us (18%)
  Pallas kernels  4.64 us (14%)
  local copies, waits for them, and re-layouts  2.7 us (8%)
    all_to_all x1, blocking collectives, shards(): lax.all_to_all(terms, ('chan', 'freq'), split_axis=0, concat_axis=0, tile...  13 us
    ppermute x3, waiting for transfers between devices, shards(): chunks[mask] = lax.ppermute(chunks[mask], 'chan', pairs)  6.78 us
    ppermute x3, starting transfers between devices, shards(): chunks[mask] = lax.ppermute(chunks[mask], 'chan', pairs)  5.82 us
    pallas_call x1, Pallas kernels, shards(): pl.pallas_call(functools.partial(stack_kernel, groups, bins, parts), out_...  1.97 us
    unnamed x6, local copies, waits for them, and re-layouts  1.7 us
    pallas_call x1, Pallas kernels, shards(): pl.pallas_call(functools.partial(table_kernel, groups, bins, freq_dev), o...  1.19 us
    reshape x1, local copies, waits for them, and re-layouts, shards(): lax.dynamic_index_in_dim(by_group, group, 1, False)  1 us
    pallas_call x1, Pallas kernels, shards(): pl.pallas_call(functools.partial(image_kernel, slow_dev, spans), out_shap...  0.97 us
  transfers between devices with their start and end apart: 3, of which 2 were waited for; matrix products, arithmetic and copies ran while one was open for 0% of the time, Pallas kernels for 5%

profile of v10, /device:TPU:0, one launch (start us, length us, event | category | flops | bytes accessed | tf_op | source)
XLA Modules:
  0.0 33.0 jit_solution(4446669653440311771)
XLA Ops:
  0.0 0.0 copy-start
  0.0 1.0 %dynamic-slice_bitcast_fusion.far_ref = bf16[512,128]{1,0:T(8,128)(2,1)S(1)} fusion(bf16[64,4,8,128]{3,2,1,0:T(8,128)(2,1)} %bitcast.8, s32[]{:T(128)S(6)} %select_n.4), kind=kLoop, calls=%fused_computation | loop fusion | bytes 262148 | tf_op jit(solution)/shard_map/reshape | solution.py:254
  1.0 4.1 %collective-permute-start = (bf16[512,128]{1,0:T(8,128)(2,1)S(1)}, bf16[512,128]{1,0:T(8,128)(2,1)S(1)}, u32[]{:S(2)}, u32[]{:S(2)}) collective-permute-start(bf16[512,128]{1,0:T(8,128)(2,1)S(1)} %dynamic-slice_bitcast_fusion.far_ref), channel_id=1, source_target_pairs={{0,16},{8,24},{16,0},{24,8},{1,17},{9,25},{17,1},{25,9},{2,18},{10... | collective-permute-start | bytes 393224 | tf_op jit(solution)/shard_map/ppermute | solution.py:268
  5.1 0.0 copy-start.1
  5.1 1.0 %copy-done.1 = bf16[2,32,32,128]{3,2,1,0:T(8,128)(2,1)S(1)} copy-done((bf16[2,32,32,128]{3,2,1,0:T(8,128)(2,1)S(1)}, bf16[2,32,32,128]{3,2,1,0:T(8,128)(2,1)}, u32[]{:S(2)}) %copy-start.1) | copy-done | bytes 524312
  6.2 0.5 %chunks_of_bins.1 = (bf16[8,64,128]{2,1,0:T(8,128)(2,1)S(1)}, bf16[8,64,128]{2,1,0:T(8,128)(2,1)S(1)}, bf16[8,64,128]{2,1,0:T(8,128)(2,1)S(1)}) custom-call(bf16[2048,128]{1,0:T(8,128)(2,1)S(1)} %bitcast.9, bf16[512,128]{1,0:T(8,128)(2,1)S(1)} %dynamic-slice_bitcast_fusion.far_ref), custom_call_target="tpu_custom_call" | custom-call | flops 10000000 | bytes 4000000 | tf_op jit(solution)/shard_map/chunks_of_bins/pallas_call | solution.py:255
  6.7 1.4 %collective-permute-start.1 = (bf16[8,64,128]{2,1,0:T(8,128)(2,1)S(1)}, bf16[8,64,128]{2,1,0:T(8,128)(2,1)S(1)}, u32[]{:S(2)}, u32[]{:S(2)}) collective-permute-start(bf16[8,64,128]{2,1,0:T(8,128)(2,1)S(1)} %get-tuple-element.13), channel_id=1, source_target_pairs={{0,24},{8,16},{16,8},{24,0},{1,25},{9,17},{17,9},{25,1},{2,26},{10... | collective-permute-start | bytes 393224 | tf_op jit(solution)/shard_map/ppermute | solution.py:268
  8.1 0.3 collective-permute-start.2
  8.4 6.7 %collective-permute-done.far_ref = bf16[512,128]{1,0:T(8,128)(2,1)S(1)} collective-permute-done((bf16[512,128]{1,0:T(8,128)(2,1)S(1)}, bf16[512,128]{1,0:T(8,128)(2,1)S(1)}, u32[]{:S(2)}, u32[]{:S(2)}) %collective-permute-start) | collective-permute-done | bytes 131104 | tf_op jit(solution)/shard_map/ppermute | solution.py:268
  15.1 0.0 copy-start.2
  15.1 0.7 %copy-done.2 = s32[4]{0:T(128)S(1)} copy-done((s32[4]{0:T(128)S(1)}, s32[4]{0:T(128)}, u32[]{:S(2)}) %copy-start.2) | copy-done | bytes 40
  15.7 1.2 %slant_tables.1 = (s32[4,128]{1,0:T(4,128)S(1)}, bf16[8,64,128]{2,1,0:T(8,128)(2,1)S(1)}, bf16[8,256,512]{2,1,0:T(8,128)(2,1)S(1)}, f32[8,2,8,256]{3,2,1,0:T(8,128)S(1)}) custom-call(s32[1,4]{1,0:T(1,128)S(1)} %bitcast.11, bf16[512,128]{1,0:T(8,128)(2,1)S(1)} %collective-permute-done.far_ref), custom_call_target="tpu_custom_call" | custom-call | flops 10000000 | bytes 4000000 | tf_op jit(solution)/shard_map/slant_tables/pallas_call | solution.py:269
  16.9 0.0 collective-permute-done.1.refs_1_
  16.9 0.1 collective-permute-done.2.refs_2_
  17.0 2.0 %stack_and_slant.1 = f32[4,8,4,128]{3,2,1,0:T(4,128)S(1)} custom-call(bf16[8,64,128]{2,1,0:T(8,128)(2,1)S(1)} %get-tuple-element.12.refs_0_, bf16[8,64,128]{2,1,0:T(8,128)(2,1)S(1)} %collective-permute-done.1.refs_1_, bf16[8,64,128]{2,1,0:T(8,128)(2,1)S(1)} %collective-permute-done.2.refs_2_, bf16[8,64,128]{2,1,0:T(8,128)(2,1)S(1)} %get-tuple-element.15.refs_3_, ...), custom_call_target="tpu_custom_call" | custom-call | tf_op jit(solution)/shard_map/stack_and_slant/pallas_call | solution.py:284
  19.0 13.0 %all_to_all.5.term_ref = f32[32,4,128]{2,1,0:T(4,128)S(1)} all-to-all(f32[32,4,128]{2,1,0:T(4,128)S(1)} %bitcast.10), channel_id=1, replica_groups=mesh['chan'=4,'freq'=8] {'chan','freq'}, dimensions={0} | all-to-all | bytes 131072 | tf_op jit(solution)/shard_map/all_to_all | solution.py:303
  32.0 0.0 copy-done
  32.0 1.0 %sum_of_bins.1 = f32[1,32,512]{2,1,0:T(8,128)} custom-call(f32[32,4,128]{2,1,0:T(4,128)S(1)} %all_to_all.5.term_ref, bf16[2,512,512]{2,1,0:T(8,128)(2,1)S(1)} %copy-done), custom_call_target="tpu_custom_call" | custom-call | tf_op jit(solution)/shard_map/sum_of_bins/pallas_call | solution.py:305
Async XLA Ops:
  0.0 32.0 %copy-start = (bf16[2,512,512]{2,1,0:T(8,128)(2,1)S(1)}, bf16[2,512,512]{2,1,0:T(8,128)(2,1)}, u32[]{:S(2)}) copy-start(bf16[2,512,512]{2,1,0:T(8,128)(2,1)} %constant.15.clone.table_ref) | copy-start | bytes 3145732
  1.0 14.0 %collective-permute-start = (bf16[512,128]{1,0:T(8,128)(2,1)S(1)}, bf16[512,128]{1,0:T(8,128)(2,1)S(1)}, u32[]{:S(2)}, u32[]{:S(2)}) collective-permute-start(bf16[512,128]{1,0:T(8,128)(2,1)S(1)} %dynamic-slice_bitcast_fusion.far_ref), channel_id=1, source_target_pairs={{0,16},{8,24},{16,0},{24,8},{1,17},{9,25},{17,1},{25,9},{2,18},{10... | collective-permute-start | bytes 393224 | tf_op jit(solution)/shard_map/ppermute | solution.py:268
  5.1 1.0 %copy-start.1 = (bf16[2,32,32,128]{3,2,1,0:T(8,128)(2,1)S(1)}, bf16[2,32,32,128]{3,2,1,0:T(8,128)(2,1)}, u32[]{:S(2)}) copy-start(bf16[2,32,32,128]{3,2,1,0:T(8,128)(2,1)} %param.3) | copy-start | bytes 1572868
  6.7 10.2 %collective-permute-start.1 = (bf16[8,64,128]{2,1,0:T(8,128)(2,1)S(1)}, bf16[8,64,128]{2,1,0:T(8,128)(2,1)S(1)}, u32[]{:S(2)}, u32[]{:S(2)}) collective-permute-start(bf16[8,64,128]{2,1,0:T(8,128)(2,1)S(1)} %get-tuple-element.13), channel_id=1, source_target_pairs={{0,24},{8,16},{16,8},{24,0},{1,25},{9,17},{17,9},{25,1},{2,26},{10... | collective-permute-start | bytes 393224 | tf_op jit(solution)/shard_map/ppermute | solution.py:268
  8.1 8.9 %collective-permute-start.2 = (bf16[8,64,128]{2,1,0:T(8,128)(2,1)S(1)}, bf16[8,64,128]{2,1,0:T(8,128)(2,1)S(1)}, u32[]{:S(2)}, u32[]{:S(2)}) collective-permute-start(bf16[8,64,128]{2,1,0:T(8,128)(2,1)S(1)} %get-tuple-element.14), channel_id=1, source_target_pairs={{0,8},{8,0},{16,24},{24,16},{1,9},{9,1},{17,25},{25,17},{2,10},{10... | collective-permute-start | bytes 393224 | tf_op jit(solution)/shard_map/ppermute | solution.py:268
  15.1 0.7 %copy-start.2 = (s32[4]{0:T(128)S(1)}, s32[4]{0:T(128)}, u32[]{:S(2)}) copy-start(s32[4]{0:T(128)} %param.4) | copy-start | bytes 52

commit v11 on v7

--- a/solution.py
+++ b/solution.py
@@ -112,15 +112,21 @@
     row_index = lax.broadcasted_iota(jnp.int32, (BLOCK, BLOCK), 0)
     lag_index = lax.broadcasted_iota(jnp.int32, (BLOCK, BLOCK), 1)
     mirror = jnp.where(row_index + lag_index == BLOCK - 1, 1.0, 0.0).astype(jnp.bfloat16)
-    ahead = lag_index <= row_index
+    behind = (lag_index - row_index)[:8]
 
     for f in range(bins):
-        left_ref[f] = lax.dot_general(
+        left = lax.dot_general(
             mirror,
             placed_ref[:, f].reshape(groups * rows, BLOCK),
             (((1,), (1,)), ((), ())),
             preferred_element_type=jnp.float32,
-        ).astype(jnp.bfloat16)
+        )
+        for delta in range(groups):
+            shifted = left
+            if delta:
+                ahead = jnp.zeros((BLOCK, rows * delta), jnp.float32)
+                shifted = jnp.concatenate([ahead, left[:, : rows * (groups - delta)]], 1)
+            left_ref[f, delta * BLOCK : (delta + 1) * BLOCK] = shifted.astype(jnp.bfloat16)
 
     for f in range(bins):
         right = []
@@ -133,19 +139,19 @@
                 )
             )
         right = jnp.concatenate(right, 0)
+        panels = jnp.dot(left_ref[f], right, preferred_element_type=jnp.float32)
         for delta in range(groups):
-            panel = jnp.dot(
-                left_ref[f, :, : rows * (groups - delta)],
-                right[rows * delta :],
-                preferred_element_type=jnp.float32,
-            )
+            panel = panels[delta * BLOCK : (delta + 1) * BLOCK]
             for half in range(2):
                 lanes = slice(half * BLOCK, (half + 1) * BLOCK)
                 skewed = pltpu.roll(panel[:, lanes], 1, 1, stride=1, stride_axis=0)
-                forward = jnp.where(ahead, skewed, 0.0).reshape(-1, 8, BLOCK).sum(0)
-                backward = jnp.where(ahead, 0.0, skewed).reshape(-1, 8, BLOCK).sum(0)
+                total = skewed[:8]
+                backward = jnp.where(behind > 0, total, 0.0)
+                for row in range(8, BLOCK, 8):
+                    total = total + skewed[row : row + 8]
+                    backward = jnp.where(behind > row, total, backward)
                 first = (f * 2 * groups + delta) * 8
-                part_ref[half, first : first + 8] = forward
+                part_ref[half, first : first + 8] = total - backward
                 part_ref[half, first + groups * 8 : first + groups * 8 + 8] = backward
 
     lags = []
@@ -268,7 +274,7 @@
         out_specs=vmem,
         scratch_shapes=[
             pltpu.VMEM((groups, bins, rows, BLOCK), jnp.bfloat16),
-            pltpu.VMEM((bins, BLOCK, groups * rows), jnp.bfloat16),
+            pltpu.VMEM((bins, groups * BLOCK, groups * rows), jnp.bfloat16),
             pltpu.VMEM((2, bins * 2 * groups * 8, BLOCK), jnp.float32),
         ],
         compiler_params=params,

time: 33 us -> 33.1 us (level)
  no operation moved by 1% of the time
where the time goes in v11:
time: 33.1 us; the launch traced here: 32.9 us
  blocking collectives  13.8 us (42%)
  starting transfers between devices  7.01 us (21%)
  waiting for transfers between devices  5.45 us (16%)
  Pallas kernels  4.83 us (15%)
  local copies, waits for them, and re-layouts  1.79 us (5%)
    all_to_all x1, blocking collectives, shards(): lax.all_to_all(terms, ('chan', 'freq'), split_axis=0, concat_axis=0, tile...  13.8 us
    ppermute x3, starting transfers between devices, shards(): arrived_chunks[distance] = lax.ppermute(chunks[distance], 'chan', pairs)  7.01 us
    ppermute x3, waiting for transfers between devices, shards(): arrived_chunks[distance] = lax.ppermute(chunks[distance], 'chan', pairs)  5.45 us
    pallas_call x1, Pallas kernels, shards(): pl.pallas_call(functools.partial(stack_kernel, groups, bins, parts), out_...  2.01 us
    unnamed x6, local copies, waits for them, and re-layouts  1.79 us
    pallas_call x1, Pallas kernels, shards(): pl.pallas_call(functools.partial(table_kernel, groups, bins, freq_dev), o...  1.19 us
    pallas_call x1, Pallas kernels, shards(): pl.pallas_call(functools.partial(image_kernel, slow_dev, spans), out_shap...  0.96 us
    pallas_call x1, Pallas kernels, shards(): pl.pallas_call(functools.partial(chunk_kernel, groups, bins), out_shape=(...  0.66 us
  transfers between devices with their start and end apart: 3, of which 2 were waited for; matrix products, arithmetic and copies ran while one was open for 0% of the time, Pallas kernels for 4%

profile of v11, /device:TPU:0, one launch (start us, length us, event | category | flops | bytes accessed | tf_op | source)
XLA Modules:
  0.0 32.9 jit_solution(8673739287470056012)
XLA Ops:
  0.0 0.0 copy-start
  0.0 0.0 copy-start.1
  0.0 1.1 %copy-done.1 = bf16[2,32,32,128]{3,2,1,0:T(8,128)(2,1)S(1)} copy-done((bf16[2,32,32,128]{3,2,1,0:T(8,128)(2,1)S(1)}, bf16[2,32,32,128]{3,2,1,0:T(8,128)(2,1)}, u32[]{:S(2)}) %copy-start.1) | copy-done | bytes 524312
  1.1 0.7 %chunks_of_bins.1 = (bf16[8,64,128]{2,1,0:T(8,128)(2,1)S(1)}, bf16[8,64,128]{2,1,0:T(8,128)(2,1)S(1)}, bf16[8,64,128]{2,1,0:T(8,128)(2,1)S(1)}, bf16[8,64,128]{2,1,0:T(8,128)(2,1)S(1)}) custom-call(bf16[2048,128]{1,0:T(8,128)(2,1)S(1)} %bitcast.3), custom_call_target="tpu_custom_call" | custom-call | tf_op jit(solution)/shard_map/chunks_of_bins/pallas_call | solution.py:244
  1.8 3.1 %collective-permute-start = (bf16[8,64,128]{2,1,0:T(8,128)(2,1)S(1)}, bf16[8,64,128]{2,1,0:T(8,128)(2,1)S(1)}, u32[]{:S(2)}, u32[]{:S(2)}) collective-permute-start(bf16[8,64,128]{2,1,0:T(8,128)(2,1)S(1)} %get-tuple-element.13), channel_id=1, source_target_pairs={{0,8},{8,16},{16,24},{24,0},{1,9},{9,17},{17,25},{25,1},{2,10},{10... | collective-permute-start | bytes 393224 | tf_op jit(solution)/shard_map/ppermute | solution.py:256
  4.9 2.6 %collective-permute-start.1 = (bf16[8,64,128]{2,1,0:T(8,128)(2,1)S(1)}, bf16[8,64,128]{2,1,0:T(8,128)(2,1)S(1)}, u32[]{:S(2)}, u32[]{:S(2)}) collective-permute-start(bf16[8,64,128]{2,1,0:T(8,128)(2,1)S(1)} %get-tuple-element.14), channel_id=1, source_target_pairs={{0,16},{8,24},{16,0},{24,8},{1,17},{9,25},{17,1},{25,9},{2,18},{10... | collective-permute-start | bytes 393224 | tf_op jit(solution)/shard_map/ppermute | solution.py:256
  7.5 1.3 %collective-permute-start.2 = (bf16[8,64,128]{2,1,0:T(8,128)(2,1)S(1)}, bf16[8,64,128]{2,1,0:T(8,128)(2,1)S(1)}, u32[]{:S(2)}, u32[]{:S(2)}) collective-permute-start(bf16[8,64,128]{2,1,0:T(8,128)(2,1)S(1)} %get-tuple-element.15), channel_id=1, source_target_pairs={{0,24},{8,0},{16,8},{24,16},{1,25},{9,1},{17,9},{25,17},{2,26},{10... | collective-permute-start | bytes 393224 | tf_op jit(solution)/shard_map/ppermute | solution.py:256
  8.8 0.0 copy-start.2
  8.8 0.7 %copy-done.2 = s32[4]{0:T(128)S(1)} copy-done((s32[4]{0:T(128)S(1)}, s32[4]{0:T(128)}, u32[]{:S(2)}) %copy-start.2) | copy-done | bytes 40
  9.5 1.2 %slant_tables.1 = (s32[4,128]{1,0:T(4,128)S(1)}, bf16[8,256,512]{2,1,0:T(8,128)(2,1)S(1)}, f32[8,2,8,256]{3,2,1,0:T(8,128)S(1)}) custom-call(s32[1,4]{1,0:T(1,128)S(1)} %bitcast.5), custom_call_target="tpu_custom_call" | custom-call | flops 10000000 | bytes 4000000 | tf_op jit(solution)/shard_map/slant_tables/pallas_call | solution.py:257
  10.7 0.7 %collective-permute-done.refs_1_ = bf16[8,64,128]{2,1,0:T(8,128)(2,1)S(1)} collective-permute-done((bf16[8,64,128]{2,1,0:T(8,128)(2,1)S(1)}, bf16[8,64,128]{2,1,0:T(8,128)(2,1)S(1)}, u32[]{:S(2)}, u32[]{:S(2)}) %collective-permute-start) | collective-permute-done | bytes 131104 | tf_op jit(solution)/shard_map/ppermute | solution.py:256
  11.3 4.8 %collective-permute-done.1.refs_2_ = bf16[8,64,128]{2,1,0:T(8,128)(2,1)S(1)} collective-permute-done((bf16[8,64,128]{2,1,0:T(8,128)(2,1)S(1)}, bf16[8,64,128]{2,1,0:T(8,128)(2,1)S(1)}, u32[]{:S(2)}, u32[]{:S(2)}) %collective-permute-start.1) | collective-permute-done | bytes 131104 | tf_op jit(solution)/shard_map/ppermute | solution.py:256
  16.1 0.0 collective-permute-done.2.refs_3_
  16.1 2.0 %stack_and_slant.1 = f32[4,8,4,128]{3,2,1,0:T(4,128)S(1)} custom-call(bf16[8,64,128]{2,1,0:T(8,128)(2,1)S(1)} %get-tuple-element.12.refs_0_, bf16[8,64,128]{2,1,0:T(8,128)(2,1)S(1)} %collective-permute-done.refs_1_, bf16[8,64,128]{2,1,0:T(8,128)(2,1)S(1)} %collective-permute-done.1.refs_2_, bf16[8,64,128]{2,1,0:T(8,128)(2,1)S(1)} %collective-permute-done.2.refs_3_, ...), custom_call_target="tpu_custom_call" | custom-call | tf_op jit(solution)/shard_map/stack_and_slant/pallas_call | solution.py:270
  18.1 13.8 %all_to_all.5.term_ref = f32[32,4,128]{2,1,0:T(4,128)S(1)} all-to-all(f32[32,4,128]{2,1,0:T(4,128)S(1)} %bitcast.4), channel_id=1, replica_groups=mesh['chan'=4,'freq'=8] {'chan','freq'}, dimensions={0} | all-to-all | bytes 131072 | tf_op jit(solution)/shard_map/all_to_all | solution.py:289
  31.9 0.0 copy-done
  31.9 1.0 %sum_of_bins.1 = f32[1,32,512]{2,1,0:T(8,128)} custom-call(f32[32,4,128]{2,1,0:T(4,128)S(1)} %all_to_all.5.term_ref, bf16[2,512,512]{2,1,0:T(8,128)(2,1)S(1)} %copy-done), custom_call_target="tpu_custom_call" | custom-call | tf_op jit(solution)/shard_map/sum_of_bins/pallas_call | solution.py:291
Async XLA Ops:
  0.0 31.9 %copy-start = (bf16[2,512,512]{2,1,0:T(8,128)(2,1)S(1)}, bf16[2,512,512]{2,1,0:T(8,128)(2,1)}, u32[]{:S(2)}) copy-start(bf16[2,512,512]{2,1,0:T(8,128)(2,1)} %constant.2.clone.table_ref) | copy-start | bytes 3145732
  0.0 1.1 %copy-start.1 = (bf16[2,32,32,128]{3,2,1,0:T(8,128)(2,1)S(1)}, bf16[2,32,32,128]{3,2,1,0:T(8,128)(2,1)}, u32[]{:S(2)}) copy-start(bf16[2,32,32,128]{3,2,1,0:T(8,128)(2,1)} %param.3) | copy-start | bytes 1572868
  1.8 9.5 %collective-permute-start = (bf16[8,64,128]{2,1,0:T(8,128)(2,1)S(1)}, bf16[8,64,128]{2,1,0:T(8,128)(2,1)S(1)}, u32[]{:S(2)}, u32[]{:S(2)}) collective-permute-start(bf16[8,64,128]{2,1,0:T(8,128)(2,1)S(1)} %get-tuple-element.13), channel_id=1, source_target_pairs={{0,8},{8,16},{16,24},{24,0},{1,9},{9,17},{17,25},{25,1},{2,10},{10... | collective-permute-start | bytes 393224 | tf_op jit(solution)/shard_map/ppermute | solution.py:256
  4.9 11.2 %collective-permute-start.1 = (bf16[8,64,128]{2,1,0:T(8,128)(2,1)S(1)}, bf16[8,64,128]{2,1,0:T(8,128)(2,1)S(1)}, u32[]{:S(2)}, u32[]{:S(2)}) collective-permute-start(bf16[8,64,128]{2,1,0:T(8,128)(2,1)S(1)} %get-tuple-element.14), channel_id=1, source_target_pairs={{0,16},{8,24},{16,0},{24,8},{1,17},{9,25},{17,1},{25,9},{2,18},{10... | collective-permute-start | bytes 393224 | tf_op jit(solution)/shard_map/ppermute | solution.py:256
  7.5 8.6 %collective-permute-start.2 = (bf16[8,64,128]{2,1,0:T(8,128)(2,1)S(1)}, bf16[8,64,128]{2,1,0:T(8,128)(2,1)S(1)}, u32[]{:S(2)}, u32[]{:S(2)}) collective-permute-start(bf16[8,64,128]{2,1,0:T(8,128)(2,1)S(1)} %get-tuple-element.15), channel_id=1, source_target_pairs={{0,24},{8,0},{16,8},{24,16},{1,25},{9,1},{17,9},{25,17},{2,26},{10... | collective-permute-start | bytes 393224 | tf_op jit(solution)/shard_map/ppermute | solution.py:256
  8.8 0.7 %copy-start.2 = (s32[4]{0:T(128)S(1)}, s32[4]{0:T(128)}, u32[]{:S(2)}) copy-start(s32[4]{0:T(128)} %param.4) | copy-start | bytes 52

commit v12 on v7

--- a/solution.py
+++ b/solution.py
@@ -84,9 +84,13 @@
     own_group = lax.axis_index("chan")
     for distance, out_ref in enumerate(out_refs):
         first = lax.rem(own_group + distance, groups) * bins
-        for f in range(bins):
+
+        def one_bin(f, carry, first=first, out_ref=out_ref):
             value = wide_ref[pl.ds(first + f, rows, stride=freq_dev), :]
             out_ref[f] = value.astype(jnp.bfloat16)
+            return carry
+
+        lax.fori_loop(0, bins, one_bin, 0, unroll=min(bins, 2))
 
 
 def stack_weights(groups):
@@ -102,7 +106,7 @@
 
 def stack_kernel(groups, bins, parts, *refs):
     chunk_refs = refs[:groups]
-    place_ref, lag_ref, shift_ref, out_ref, placed_ref, left_ref, part_ref = refs[groups:]
+    place_ref, lag_ref, shift_ref, out_ref, placed_ref, part_ref = refs[groups:]
     rows = placed_ref.shape[2]
     windows = rows // 2
     places = place_ref[...]
@@ -112,17 +116,15 @@
     row_index = lax.broadcasted_iota(jnp.int32, (BLOCK, BLOCK), 0)
     lag_index = lax.broadcasted_iota(jnp.int32, (BLOCK, BLOCK), 1)
     mirror = jnp.where(row_index + lag_index == BLOCK - 1, 1.0, 0.0).astype(jnp.bfloat16)
-    ahead = lag_index <= row_index
-
-    for f in range(bins):
-        left_ref[f] = lax.dot_general(
+    behind = (lag_index - row_index)[:8]
+
+    def one_bin(f, carry):
+        left = lax.dot_general(
             mirror,
             placed_ref[:, f].reshape(groups * rows, BLOCK),
             (((1,), (1,)), ((), ())),
             preferred_element_type=jnp.float32,
         ).astype(jnp.bfloat16)
-
-    for f in range(bins):
         right = []
         for place in range(groups):
             value = placed_ref[place, f]
@@ -135,18 +137,25 @@
         right = jnp.concatenate(right, 0)
         for delta in range(groups):
             panel = jnp.dot(
-                left_ref[f, :, : rows * (groups - delta)],
+                left[:, : rows * (groups - delta)],
                 right[rows * delta :],
                 preferred_element_type=jnp.float32,
             )
             for half in range(2):
                 lanes = slice(half * BLOCK, (half + 1) * BLOCK)
                 skewed = pltpu.roll(panel[:, lanes], 1, 1, stride=1, stride_axis=0)
-                forward = jnp.where(ahead, skewed, 0.0).reshape(-1, 8, BLOCK).sum(0)
-                backward = jnp.where(ahead, 0.0, skewed).reshape(-1, 8, BLOCK).sum(0)
+                total = skewed[:8]
+                backward = jnp.where(behind > 0, total, 0.0)
+                for row in range(8, BLOCK, 8):
+                    total = total + skewed[row : row + 8]
+                    backward = jnp.where(behind > row, total, backward)
                 first = (f * 2 * groups + delta) * 8
-                part_ref[half, first : first + 8] = forward
-                part_ref[half, first + groups * 8 : first + groups * 8 + 8] = backward
+                part_ref[half, pl.ds(pl.multiple_of(first, 8), 8)] = total - backward
+                first = first + groups * 8
+                part_ref[half, pl.ds(pl.multiple_of(first, 8), 8)] = backward
+        return carry
+
+    lax.fori_loop(0, bins, one_bin, 0, unroll=min(bins, 2))
 
     lags = []
     for half in range(2):
@@ -268,7 +277,6 @@
         out_specs=vmem,
         scratch_shapes=[
             pltpu.VMEM((groups, bins, rows, BLOCK), jnp.bfloat16),
-            pltpu.VMEM((bins, BLOCK, groups * rows), jnp.bfloat16),
             pltpu.VMEM((2, bins * 2 * groups * 8, BLOCK), jnp.float32),
         ],
         compiler_params=params,

time: 33 us -> 34.8 us (1.055)
  Pallas kernels: 4.8 us -> 6.54 us
    pallas_call x1, Pallas kernels: 1.98 us -> 3.43 us  [shards(): pl.pallas_call(functools.partial(stack_kernel, groups, bins, parts), out_...]
  transfers between devices with their start and end apart: 3 -> 3, of which waited for: 2 -> 2; matrix products, arithmetic and copies ran while one was open for 0% -> 0% of each run, Pallas kernels for 4% -> 3%
where the time goes in v12:
time: 34.8 us; the launch traced here: 34.6 us
  blocking collectives  13.8 us (40%)
  starting transfers between devices  7.01 us (20%)
  Pallas kernels  6.54 us (19%)
  waiting for transfers between devices  5.45 us (16%)
  local copies, waits for them, and re-layouts  1.79 us (5%)
    all_to_all x1, blocking collectives, shards(): lax.all_to_all(terms, ('chan', 'freq'), split_axis=0, concat_axis=0, tile...  13.8 us
    ppermute x3, starting transfers between devices, shards(): arrived_chunks[distance] = lax.ppermute(chunks[distance], 'chan', pairs)  7.01 us
    ppermute x3, waiting for transfers between devices, shards(): arrived_chunks[distance] = lax.ppermute(chunks[distance], 'chan', pairs)  5.45 us
    pallas_call x1, Pallas kernels, shards(): pl.pallas_call(functools.partial(stack_kernel, groups, bins, parts), out_...  3.43 us
    unnamed x6, local copies, waits for them, and re-layouts  1.79 us
    pallas_call x1, Pallas kernels, shards(): pl.pallas_call(functools.partial(table_kernel, groups, bins, freq_dev), o...  1.19 us
    pallas_call x1, Pallas kernels, shards(): pl.pallas_call(functools.partial(image_kernel, slow_dev, spans), out_shap...  0.96 us
    pallas_call x1, Pallas kernels, shards(): pl.pallas_call(functools.partial(chunk_kernel, groups, bins), out_shape=(...  0.96 us
  transfers between devices with their start and end apart: 3, of which 2 were waited for; matrix products, arithmetic and copies ran while one was open for 0% of the time, Pallas kernels for 3%

profile of v12, /device:TPU:0, one launch (start us, length us, event | category | flops | bytes accessed | tf_op | source)
XLA Modules:
  0.0 34.6 jit_solution(10017314033254257698)
XLA Ops:
  0.0 0.0 copy-start
  0.0 0.0 copy-start.1
  0.0 1.1 %copy-done.1 = bf16[2,32,32,128]{3,2,1,0:T(8,128)(2,1)S(1)} copy-done((bf16[2,32,32,128]{3,2,1,0:T(8,128)(2,1)S(1)}, bf16[2,32,32,128]{3,2,1,0:T(8,128)(2,1)}, u32[]{:S(2)}) %copy-start.1) | copy-done | bytes 524312
  1.1 1.0 %chunks_of_bins.1 = (bf16[8,64,128]{2,1,0:T(8,128)(2,1)S(1)}, bf16[8,64,128]{2,1,0:T(8,128)(2,1)S(1)}, bf16[8,64,128]{2,1,0:T(8,128)(2,1)S(1)}, bf16[8,64,128]{2,1,0:T(8,128)(2,1)S(1)}) custom-call(bf16[2048,128]{1,0:T(8,128)(2,1)S(1)} %bitcast.3), custom_call_target="tpu_custom_call" | custom-call | tf_op jit(solution)/shard_map/chunks_of_bins/pallas_call | solution.py:247
  2.1 3.1 %collective-permute-start = (bf16[8,64,128]{2,1,0:T(8,128)(2,1)S(1)}, bf16[8,64,128]{2,1,0:T(8,128)(2,1)S(1)}, u32[]{:S(2)}, u32[]{:S(2)}) collective-permute-start(bf16[8,64,128]{2,1,0:T(8,128)(2,1)S(1)} %get-tuple-element.13), channel_id=1, source_target_pairs={{0,8},{8,16},{16,24},{24,0},{1,9},{9,17},{17,25},{25,1},{2,10},{10... | collective-permute-start | bytes 393224 | tf_op jit(solution)/shard_map/ppermute | solution.py:259
  5.2 2.6 %collective-permute-start.1 = (bf16[8,64,128]{2,1,0:T(8,128)(2,1)S(1)}, bf16[8,64,128]{2,1,0:T(8,128)(2,1)S(1)}, u32[]{:S(2)}, u32[]{:S(2)}) collective-permute-start(bf16[8,64,128]{2,1,0:T(8,128)(2,1)S(1)} %get-tuple-element.14), channel_id=1, source_target_pairs={{0,16},{8,24},{16,0},{24,8},{1,17},{9,25},{17,1},{25,9},{2,18},{10... | collective-permute-start | bytes 393224 | tf_op jit(solution)/shard_map/ppermute | solution.py:259
  7.8 1.3 %collective-permute-start.2 = (bf16[8,64,128]{2,1,0:T(8,128)(2,1)S(1)}, bf16[8,64,128]{2,1,0:T(8,128)(2,1)S(1)}, u32[]{:S(2)}, u32[]{:S(2)}) collective-permute-start(bf16[8,64,128]{2,1,0:T(8,128)(2,1)S(1)} %get-tuple-element.15), channel_id=1, source_target_pairs={{0,24},{8,0},{16,8},{24,16},{1,25},{9,1},{17,9},{25,17},{2,26},{10... | collective-permute-start | bytes 393224 | tf_op jit(solution)/shard_map/ppermute | solution.py:259
  9.1 0.0 copy-start.2
  9.1 0.7 %copy-done.2 = s32[4]{0:T(128)S(1)} copy-done((s32[4]{0:T(128)S(1)}, s32[4]{0:T(128)}, u32[]{:S(2)}) %copy-start.2) | copy-done | bytes 40
  9.8 1.2 %slant_tables.1 = (s32[4,128]{1,0:T(4,128)S(1)}, bf16[8,256,512]{2,1,0:T(8,128)(2,1)S(1)}, f32[8,2,8,256]{3,2,1,0:T(8,128)S(1)}) custom-call(s32[1,4]{1,0:T(1,128)S(1)} %bitcast.5), custom_call_target="tpu_custom_call" | custom-call | flops 10000000 | bytes 4000000 | tf_op jit(solution)/shard_map/slant_tables/pallas_call | solution.py:260
  11.0 0.7 %collective-permute-done.refs_1_ = bf16[8,64,128]{2,1,0:T(8,128)(2,1)S(1)} collective-permute-done((bf16[8,64,128]{2,1,0:T(8,128)(2,1)S(1)}, bf16[8,64,128]{2,1,0:T(8,128)(2,1)S(1)}, u32[]{:S(2)}, u32[]{:S(2)}) %collective-permute-start) | collective-permute-done | bytes 131104 | tf_op jit(solution)/shard_map/ppermute | solution.py:259
  11.6 4.8 %collective-permute-done.1.refs_2_ = bf16[8,64,128]{2,1,0:T(8,128)(2,1)S(1)} collective-permute-done((bf16[8,64,128]{2,1,0:T(8,128)(2,1)S(1)}, bf16[8,64,128]{2,1,0:T(8,128)(2,1)S(1)}, u32[]{:S(2)}, u32[]{:S(2)}) %collective-permute-start.1) | collective-permute-done | bytes 131104 | tf_op jit(solution)/shard_map/ppermute | solution.py:259
  16.4 0.0 collective-permute-done.2.refs_3_
  16.4 3.4 %stack_and_slant.1 = f32[4,8,4,128]{3,2,1,0:T(4,128)S(1)} custom-call(bf16[8,64,128]{2,1,0:T(8,128)(2,1)S(1)} %get-tuple-element.12.refs_0_, bf16[8,64,128]{2,1,0:T(8,128)(2,1)S(1)} %collective-permute-done.refs_1_, bf16[8,64,128]{2,1,0:T(8,128)(2,1)S(1)} %collective-permute-done.1.refs_2_, bf16[8,64,128]{2,1,0:T(8,128)(2,1)S(1)} %collective-permute-done.2.refs_3_, ...), custom_call_target="tpu_custom_call" | custom-call | tf_op jit(solution)/shard_map/stack_and_slant/pallas_call | solution.py:273
  19.9 13.8 %all_to_all.5.term_ref = f32[32,4,128]{2,1,0:T(4,128)S(1)} all-to-all(f32[32,4,128]{2,1,0:T(4,128)S(1)} %bitcast.4), channel_id=1, replica_groups=mesh['chan'=4,'freq'=8] {'chan','freq'}, dimensions={0} | all-to-all | bytes 131072 | tf_op jit(solution)/shard_map/all_to_all | solution.py:291
  33.7 0.0 copy-done
  33.7 1.0 %sum_of_bins.1 = f32[1,32,512]{2,1,0:T(8,128)} custom-call(f32[32,4,128]{2,1,0:T(4,128)S(1)} %all_to_all.5.term_ref, bf16[2,512,512]{2,1,0:T(8,128)(2,1)S(1)} %copy-done), custom_call_target="tpu_custom_call" | custom-call | tf_op jit(solution)/shard_map/sum_of_bins/pallas_call | solution.py:293
Async XLA Ops:
  0.0 33.7 %copy-start = (bf16[2,512,512]{2,1,0:T(8,128)(2,1)S(1)}, bf16[2,512,512]{2,1,0:T(8,128)(2,1)}, u32[]{:S(2)}) copy-start(bf16[2,512,512]{2,1,0:T(8,128)(2,1)} %constant.2.clone.table_ref) | copy-start | bytes 3145732
  0.0 1.1 %copy-start.1 = (bf16[2,32,32,128]{3,2,1,0:T(8,128)(2,1)S(1)}, bf16[2,32,32,128]{3,2,1,0:T(8,128)(2,1)}, u32[]{:S(2)}) copy-start(bf16[2,32,32,128]{3,2,1,0:T(8,128)(2,1)} %param.3) | copy-start | bytes 1572868
  2.1 9.5 %collective-permute-start = (bf16[8,64,128]{2,1,0:T(8,128)(2,1)S(1)}, bf16[8,64,128]{2,1,0:T(8,128)(2,1)S(1)}, u32[]{:S(2)}, u32[]{:S(2)}) collective-permute-start(bf16[8,64,128]{2,1,0:T(8,128)(2,1)S(1)} %get-tuple-element.13), channel_id=1, source_target_pairs={{0,8},{8,16},{16,24},{24,0},{1,9},{9,17},{17,25},{25,1},{2,10},{10... | collective-permute-start | bytes 393224 | tf_op jit(solution)/shard_map/ppermute | solution.py:259
  5.2 11.2 %collective-permute-start.1 = (bf16[8,64,128]{2,1,0:T(8,128)(2,1)S(1)}, bf16[8,64,128]{2,1,0:T(8,128)(2,1)S(1)}, u32[]{:S(2)}, u32[]{:S(2)}) collective-permute-start(bf16[8,64,128]{2,1,0:T(8,128)(2,1)S(1)} %get-tuple-element.14), channel_id=1, source_target_pairs={{0,16},{8,24},{16,0},{24,8},{1,17},{9,25},{17,1},{25,9},{2,18},{10... | collective-permute-start | bytes 393224 | tf_op jit(solution)/shard_map/ppermute | solution.py:259
  7.8 8.6 %collective-permute-start.2 = (bf16[8,64,128]{2,1,0:T(8,128)(2,1)S(1)}, bf16[8,64,128]{2,1,0:T(8,128)(2,1)S(1)}, u32[]{:S(2)}, u32[]{:S(2)}) collective-permute-start(bf16[8,64,128]{2,1,0:T(8,128)(2,1)S(1)} %get-tuple-element.15), channel_id=1, source_target_pairs={{0,24},{8,0},{16,8},{24,16},{1,25},{9,1},{17,9},{25,17},{2,26},{10... | collective-permute-start | bytes 393224 | tf_op jit(solution)/shard_map/ppermute | solution.py:259
  9.1 0.7 %copy-start.2 = (s32[4]{0:T(128)S(1)}, s32[4]{0:T(128)}, u32[]{:S(2)}) copy-start(s32[4]{0:T(128)} %param.4) | copy-start | bytes 52

commit v13 on v7

--- a/solution.py
+++ b/solution.py
@@ -193,6 +193,10 @@
             out_ref[:, part, row, :] = packed
 
 
+def split_kernel(table_ref, term_ref, out_ref):
+    out_ref[0], out_ref[1] = halves(table_ref[...])
+
+
 def image_kernel(slow_dev, spans, term_ref, table_ref, out_ref):
     arrived = term_ref[...]
     turned = arrived.reshape(-1, BLOCK).T
@@ -217,10 +221,7 @@
     lag_time = np.arange(LAG_TIMES) - LAG_TIMES // 2
     angle = 2.0 * math.pi / LAG_TIMES * ((freq[..., None] * lag_time) % LAG_TIMES)
     table = np.where((entry % 2 == 0)[..., None], np.cos(angle), -np.sin(angle))
-    table = table.reshape(-1, LAG_TIMES).astype(np.float32)
-    high = table.astype(jnp.bfloat16)
-    low = (table - high.astype(np.float32)).astype(jnp.bfloat16)
-    return spans, np.stack([high, low])
+    return spans, table.reshape(-1, LAG_TIMES).astype(np.float32)
 
 
 def shards(spectra, block_position):
@@ -282,6 +283,15 @@
     terms = terms.reshape(groups * parts, message_rows, BLOCK)
     arrived = lax.all_to_all(terms, ("chan", "freq"), split_axis=0, concat_axis=0, tiled=True)
     spans, table = time_table(groups, parts, bins, slow_dev, message_rows)
+    table = pl.pallas_call(
+        split_kernel,
+        out_shape=jax.ShapeDtypeStruct((2,) + table.shape, jnp.bfloat16),
+        in_specs=[vmem, pl.BlockSpec(memory_space=pl.ANY)],
+        out_specs=vmem,
+        compiler_params=params,
+        cost_estimate=pl.CostEstimate(flops=10**7, bytes_accessed=4 * 10**6, transcendentals=0),
+        name="table_halves",
+    )(jnp.asarray(table), terms)
     return pl.pallas_call(
         functools.partial(image_kernel, slow_dev, spans),
         out_shape=jax.ShapeDtypeStruct((1, slow_dev, LAG_TIMES), jnp.float32),
@@ -289,7 +299,7 @@
         out_specs=vmem,
         compiler_params=params,
         name="sum_of_bins",
-    )(arrived, jnp.asarray(table))
+    )(arrived, table)
 
 
 def solution(mesh):

time: 33 us -> 33.9 us (1.027)
  blocking collectives: 13.8 us -> 0 us
  waiting for transfers between devices: 5.45 us -> 12.7 us
  starting transfers between devices: 7.01 us -> 13.6 us
  Pallas kernels: 4.8 us -> 5.57 us
    all_to_all x1 -> x0, blocking collectives: 13.8 us -> none  [shards(): lax.all_to_all(terms, ('chan', 'freq'), split_axis=0, concat_axis=0, tile...]
    all_to_all x0 -> x1, waiting for transfers between devices: none -> 7.25 us  [shards(): lax.all_to_all(terms, ('chan', 'freq'), split_axis=0, concat_axis=0, tile...]
    all_to_all x0 -> x1, starting transfers between devices: none -> 6.59 us  [shards(): lax.all_to_all(terms, ('chan', 'freq'), split_axis=0, concat_axis=0, tile...]
    pallas_call x1, Pallas kernels: 1.98 us -> 2.61 us  [shards(): pl.pallas_call(functools.partial(stack_kernel, groups, bins, parts), out_...]
  transfers between devices with their start and end apart: 3 -> 4, of which waited for: 2 -> 3; matrix products, arithmetic and copies ran while one was open for 0% -> 0% of each run, Pallas kernels for 4% -> 4%
where the time goes in v13:
time: 33.9 us; the launch traced here: 33.7 us
  starting transfers between devices  13.6 us (40%)
  waiting for transfers between devices  12.7 us (37%)
  Pallas kernels  5.57 us (16%)
  local copies, waits for them, and re-layouts  1.79 us (5%)
    all_to_all x1, waiting for transfers between devices, shards(): lax.all_to_all(terms, ('chan', 'freq'), split_axis=0, concat_axis=0, tile...  7.25 us
    ppermute x3, starting transfers between devices, shards(): arrived_chunks[distance] = lax.ppermute(chunks[distance], 'chan', pairs)  7.01 us
    all_to_all x1, starting transfers between devices, shards(): lax.all_to_all(terms, ('chan', 'freq'), split_axis=0, concat_axis=0, tile...  6.59 us
    ppermute x3, waiting for transfers between devices, shards(): arrived_chunks[distance] = lax.ppermute(chunks[distance], 'chan', pairs)  5.45 us
    pallas_call x1, Pallas kernels, shards(): pl.pallas_call(functools.partial(stack_kernel, groups, bins, parts), out_...  2.61 us
    unnamed x6, local copies, waits for them, and re-layouts  1.79 us
    pallas_call x1, Pallas kernels, shards(): pl.pallas_call(functools.partial(table_kernel, groups, bins, freq_dev), o...  1.19 us
    pallas_call x1, Pallas kernels, shards(): pl.pallas_call(functools.partial(image_kernel, slow_dev, spans), out_shap...  0.97 us
  transfers between devices with their start and end apart: 4, of which 3 were waited for; matrix products, arithmetic and copies ran while one was open for 0% of the time, Pallas kernels for 4%

profile of v13, /device:TPU:0, one launch (start us, length us, event | category | flops | bytes accessed | tf_op | source)
XLA Modules:
  0.0 33.7 jit_solution(13930470072460354599)
XLA Ops:
  0.0 0.0 copy-start
  0.0 0.0 copy-start.1
  0.0 1.1 %copy-done.1 = bf16[2,32,32,128]{3,2,1,0:T(8,128)(2,1)S(1)} copy-done((bf16[2,32,32,128]{3,2,1,0:T(8,128)(2,1)S(1)}, bf16[2,32,32,128]{3,2,1,0:T(8,128)(2,1)}, u32[]{:S(2)}) %copy-start.1) | copy-done | bytes 524312
  1.1 0.7 %chunks_of_bins.1 = (bf16[8,64,128]{2,1,0:T(8,128)(2,1)S(1)}, bf16[8,64,128]{2,1,0:T(8,128)(2,1)S(1)}, bf16[8,64,128]{2,1,0:T(8,128)(2,1)S(1)}, bf16[8,64,128]{2,1,0:T(8,128)(2,1)S(1)}) custom-call(bf16[2048,128]{1,0:T(8,128)(2,1)S(1)} %bitcast.3), custom_call_target="tpu_custom_call" | custom-call | tf_op jit(solution)/shard_map/chunks_of_bins/pallas_call | solution.py:239
  1.8 3.1 %collective-permute-start = (bf16[8,64,128]{2,1,0:T(8,128)(2,1)S(1)}, bf16[8,64,128]{2,1,0:T(8,128)(2,1)S(1)}, u32[]{:S(2)}, u32[]{:S(2)}) collective-permute-start(bf16[8,64,128]{2,1,0:T(8,128)(2,1)S(1)} %get-tuple-element.13), channel_id=1, source_target_pairs={{0,8},{8,16},{16,24},{24,0},{1,9},{9,17},{17,25},{25,1},{2,10},{10... | collective-permute-start | bytes 393224 | tf_op jit(solution)/shard_map/ppermute | solution.py:251
  4.9 2.6 %collective-permute-start.1 = (bf16[8,64,128]{2,1,0:T(8,128)(2,1)S(1)}, bf16[8,64,128]{2,1,0:T(8,128)(2,1)S(1)}, u32[]{:S(2)}, u32[]{:S(2)}) collective-permute-start(bf16[8,64,128]{2,1,0:T(8,128)(2,1)S(1)} %get-tuple-element.14), channel_id=1, source_target_pairs={{0,16},{8,24},{16,0},{24,8},{1,17},{9,25},{17,1},{25,9},{2,18},{10... | collective-permute-start | bytes 393224 | tf_op jit(solution)/shard_map/ppermute | solution.py:251
  7.5 1.3 %collective-permute-start.2 = (bf16[8,64,128]{2,1,0:T(8,128)(2,1)S(1)}, bf16[8,64,128]{2,1,0:T(8,128)(2,1)S(1)}, u32[]{:S(2)}, u32[]{:S(2)}) collective-permute-start(bf16[8,64,128]{2,1,0:T(8,128)(2,1)S(1)} %get-tuple-element.15), channel_id=1, source_target_pairs={{0,24},{8,0},{16,8},{24,16},{1,25},{9,1},{17,9},{25,17},{2,26},{10... | collective-permute-start | bytes 393224 | tf_op jit(solution)/shard_map/ppermute | solution.py:251
  8.8 0.0 copy-start.2
  8.8 0.7 %copy-done.2 = s32[4]{0:T(128)S(1)} copy-done((s32[4]{0:T(128)S(1)}, s32[4]{0:T(128)}, u32[]{:S(2)}) %copy-start.2) | copy-done | bytes 40
  9.5 1.2 %slant_tables.1 = (s32[4,128]{1,0:T(4,128)S(1)}, bf16[8,256,512]{2,1,0:T(8,128)(2,1)S(1)}, f32[8,2,8,256]{3,2,1,0:T(8,128)S(1)}) custom-call(s32[1,4]{1,0:T(1,128)S(1)} %bitcast.4), custom_call_target="tpu_custom_call" | custom-call | flops 10000000 | bytes 4000000 | tf_op jit(solution)/shard_map/slant_tables/pallas_call | solution.py:252
  10.7 0.7 %collective-permute-done.refs_1_ = bf16[8,64,128]{2,1,0:T(8,128)(2,1)S(1)} collective-permute-done((bf16[8,64,128]{2,1,0:T(8,128)(2,1)S(1)}, bf16[8,64,128]{2,1,0:T(8,128)(2,1)S(1)}, u32[]{:S(2)}, u32[]{:S(2)}) %collective-permute-start) | collective-permute-done | bytes 131104 | tf_op jit(solution)/shard_map/ppermute | solution.py:251
  11.3 4.8 %collective-permute-done.1.refs_2_ = bf16[8,64,128]{2,1,0:T(8,128)(2,1)S(1)} collective-permute-done((bf16[8,64,128]{2,1,0:T(8,128)(2,1)S(1)}, bf16[8,64,128]{2,1,0:T(8,128)(2,1)S(1)}, u32[]{:S(2)}, u32[]{:S(2)}) %collective-permute-start.1) | collective-permute-done | bytes 131104 | tf_op jit(solution)/shard_map/ppermute | solution.py:251
  16.1 0.0 collective-permute-done.2.refs_3_
  16.1 2.6 %stack_and_slant.1 = f32[4,8,4,128]{3,2,1,0:T(4,128)} custom-call(bf16[8,64,128]{2,1,0:T(8,128)(2,1)S(1)} %get-tuple-element.12.refs_0_, bf16[8,64,128]{2,1,0:T(8,128)(2,1)S(1)} %collective-permute-done.refs_1_, bf16[8,64,128]{2,1,0:T(8,128)(2,1)S(1)} %collective-permute-done.1.refs_2_, bf16[8,64,128]{2,1,0:T(8,128)(2,1)S(1)} %collective-permute-done.2.refs_3_, ...), custom_call_target="tpu_custom_call" | custom-call | tf_op jit(solution)/shard_map/stack_and_slant/pallas_call | solution.py:265
  18.7 6.6 %all-to-all-start = ((f32[32,4,128]{2,1,0:T(4,128)}), f32[32,4,128]{2,1,0:T(4,128)S(1)}, u32[]{:S(2)}, u32[]{:S(2)}) async-start(f32[32,4,128]{2,1,0:T(4,128)} %bitcast.2.term_ref), calls=%async_computation | async-start | bytes 131072 | tf_op jit(solution)/shard_map/all_to_all | solution.py:284
  25.3 0.0 copy-done
  25.3 0.1 table_halves.1.table_ref
  25.5 7.3 %all-to-all-done.term_ref = f32[32,4,128]{2,1,0:T(4,128)S(1)} async-done(((f32[32,4,128]{2,1,0:T(4,128)}), f32[32,4,128]{2,1,0:T(4,128)S(1)}, u32[]{:S(2)}, u32[]{:S(2)}) %all-to-all-start) | async-done | bytes 65568 | tf_op jit(solution)/shard_map/all_to_all | solution.py:284
  32.7 1.0 %sum_of_bins.1 = f32[1,32,512]{2,1,0:T(8,128)} custom-call(f32[32,4,128]{2,1,0:T(4,128)S(1)} %all-to-all-done.term_ref, bf16[2,512,512]{2,1,0:T(8,128)(2,1)S(1)} %table_halves.1.table_ref), custom_call_target="tpu_custom_call" | custom-call | tf_op jit(solution)/shard_map/sum_of_bins/pallas_call | solution.py:295
Async XLA Ops:
  0.0 25.3 %copy-start = (f32[512,512]{1,0:T(8,128)S(1)}, f32[512,512]{1,0:T(8,128)}, u32[]{:S(2)}) copy-start(f32[512,512]{1,0:T(8,128)} %constant.2.clone.table_ref) | copy-start | bytes 3145732
  0.0 1.1 %copy-start.1 = (bf16[2,32,32,128]{3,2,1,0:T(8,128)(2,1)S(1)}, bf16[2,32,32,128]{3,2,1,0:T(8,128)(2,1)}, u32[]{:S(2)}) copy-start(bf16[2,32,32,128]{3,2,1,0:T(8,128)(2,1)} %param.3) | copy-start | bytes 1572868
  1.8 9.5 %collective-permute-start = (bf16[8,64,128]{2,1,0:T(8,128)(2,1)S(1)}, bf16[8,64,128]{2,1,0:T(8,128)(2,1)S(1)}, u32[]{:S(2)}, u32[]{:S(2)}) collective-permute-start(bf16[8,64,128]{2,1,0:T(8,128)(2,1)S(1)} %get-tuple-element.13), channel_id=1, source_target_pairs={{0,8},{8,16},{16,24},{24,0},{1,9},{9,17},{17,25},{25,1},{2,10},{10... | collective-permute-start | bytes 393224 | tf_op jit(solution)/shard_map/ppermute | solution.py:251
  4.9 11.2 %collective-permute-start.1 = (bf16[8,64,128]{2,1,0:T(8,128)(2,1)S(1)}, bf16[8,64,128]{2,1,0:T(8,128)(2,1)S(1)}, u32[]{:S(2)}, u32[]{:S(2)}) collective-permute-start(bf16[8,64,128]{2,1,0:T(8,128)(2,1)S(1)} %get-tuple-element.14), channel_id=1, source_target_pairs={{0,16},{8,24},{16,0},{24,8},{1,17},{9,25},{17,1},{25,9},{2,18},{10... | collective-permute-start | bytes 393224 | tf_op jit(solution)/shard_map/ppermute | solution.py:251
  7.5 8.6 %collective-permute-start.2 = (bf16[8,64,128]{2,1,0:T(8,128)(2,1)S(1)}, bf16[8,64,128]{2,1,0:T(8,128)(2,1)S(1)}, u32[]{:S(2)}, u32[]{:S(2)}) collective-permute-start(bf16[8,64,128]{2,1,0:T(8,128)(2,1)S(1)} %get-tuple-element.15), channel_id=1, source_target_pairs={{0,24},{8,0},{16,8},{24,16},{1,25},{9,1},{17,9},{25,17},{2,26},{10... | collective-permute-start | bytes 393224 | tf_op jit(solution)/shard_map/ppermute | solution.py:251
  8.8 0.7 %copy-start.2 = (s32[4]{0:T(128)S(1)}, s32[4]{0:T(128)}, u32[]{:S(2)}) copy-start(s32[4]{0:T(128)} %param.4) | copy-start | bytes 52
  18.7 14.0 %all-to-all-start = ((f32[32,4,128]{2,1,0:T(4,128)}), f32[32,4,128]{2,1,0:T(4,128)S(1)}, u32[]{:S(2)}, u32[]{:S(2)}) async-start(f32[32,4,128]{2,1,0:T(4,128)} %bitcast.2.term_ref), calls=%async_computation | async-start | bytes 131072 | tf_op jit(solution)/shard_map/all_to_all | solution.py:284

commit v14 on v6

--- a/solution.py
+++ b/solution.py
@@ -45,8 +45,11 @@
     shift_rows = jnp.where(shift_rows < groups, shift_rows, shift_rows - groups - 1) * BLOCK
     own_group = lax.axis_index("chan")
     first_bin = lax.axis_index("freq") * freq_dev + own_group * bins
-    for distance in range(groups):
-        place_ref[distance] = position_ref[lax.rem(own_group + (groups - distance), groups)]
+    sender = lax.broadcasted_iota(jnp.int32, (groups, groups), 1)
+    distance = lax.broadcasted_iota(jnp.int32, (groups, groups), 0)
+    sends = lax.rem(own_group + groups - distance, groups) == sender
+    places = jnp.sum(jnp.where(sends, position_ref[...], 0), axis=1, keepdims=True)
+    place_ref[...] = jnp.broadcast_to(places, place_ref.shape)
 
     def one_bin(f, carry):
         def phases(rows):
@@ -106,8 +109,9 @@
     out_ref, placed_ref, left_ref, part_ref = refs[-4:]
     rows = placed_ref.shape[2]
     windows = rows // 2
+    places = place_ref[...]
     for distance, chunk_ref in enumerate(chunk_refs):
-        placed_ref[place_ref[distance]] = chunk_ref[...]
+        placed_ref[places[distance, 0]] = chunk_ref[...]
 
     row_index = lax.broadcasted_iota(jnp.int32, (BLOCK, BLOCK), 0)
     lag_index = lax.broadcasted_iota(jnp.int32, (BLOCK, BLOCK), 1)
@@ -238,10 +242,10 @@
     slow_dev = SLOWNESS // parts
     message_rows = -(-2 * bins * slow_dev // BLOCK)
     vmem = pl.BlockSpec(memory_space=pltpu.VMEM)
-    smem = pl.BlockSpec(memory_space=pltpu.SMEM)
     params = pltpu.CompilerParams(vmem_limit_bytes=32 * 1024 * 1024)
 
-    pieces = [(0, bins - bins // 2), (bins - bins // 2, bins // 2)] if bins > 1 else [(0, 1)]
+    late = max(1, bins // 4)
+    pieces = [(0, bins - late), (bins - late, late)] if bins > 1 else [(0, 1)]
     chunks = pl.pallas_call(
         functools.partial(chunk_kernel, groups, pieces),
         out_shape=tuple(
@@ -263,16 +267,16 @@
     places, lag_table, shift_table = pl.pallas_call(
         functools.partial(table_kernel, groups, bins, freq_dev),
         out_shape=(
-            jax.ShapeDtypeStruct((groups,), jnp.int32),
+            jax.ShapeDtypeStruct((groups, BLOCK), jnp.int32),
             jax.ShapeDtypeStruct((bins, 2 * BLOCK, 2 * SLOWNESS), jnp.bfloat16),
             jax.ShapeDtypeStruct((bins, 2, 2 * groups, SLOWNESS), jnp.float32),
         ),
-        in_specs=[smem],
-        out_specs=(smem, vmem, vmem),
+        in_specs=[vmem],
+        out_specs=(vmem, vmem, vmem),
         compiler_params=params,
         cost_estimate=pl.CostEstimate(flops=10**7, bytes_accessed=4 * 10**6, transcendentals=0),
         name="slant_tables",
-    )(block_position)
+    )(block_position.reshape(1, groups))
     earlier = []
     for index, (start, size) in enumerate(pieces):
         last = index == len(pieces) - 1
@@ -283,7 +287,7 @@
         terms = pl.pallas_call(
             functools.partial(stack_kernel, groups, start, size, parts if last else None),
             out_shape=jax.ShapeDtypeStruct(shape, jnp.float32),
-            in_specs=[vmem] * groups + [smem, vmem, vmem] + [vmem] * len(earlier),
+            in_specs=[vmem] * (groups + 3 + len(earlier)),
             out_specs=vmem,
             scratch_shapes=[
                 pltpu.VMEM((groups, size, rows, BLOCK), jnp.bfloat16),

time: 33.2 us -> 33.2 us (level)
  waiting for transfers between devices: 0.42 us -> 3 us
  Pallas kernels: 7.22 us -> 5.24 us
  starting transfers between devices: 10.8 us -> 10.1 us
    ppermute x6, waiting for transfers between devices: 0.42 us -> 3 us  [shards(): piece[distance] = lax.ppermute(piece[distance], 'chan', pairs)]
    pallas_call x2, Pallas kernels: 3.47 us -> 2.42 us  [shards(): pl.pallas_call(functools.partial(stack_kernel, groups, start, size, parts...]
    pallas_call x1, Pallas kernels: 2.12 us -> 1.19 us  [shards(): pl.pallas_call(functools.partial(table_kernel, groups, bins, freq_dev), o...]
    ppermute x6, starting transfers between devices: 10.8 us -> 10.1 us  [shards(): piece[distance] = lax.ppermute(piece[distance], 'chan', pairs)]
  transfers between devices with their start and end apart: 6 -> 6, of which waited for: 1 -> 3; matrix products, arithmetic and copies ran while one was open for 0% -> 0% of each run, Pallas kernels for 12% -> 8%
where the time goes in v14:
time: 33.2 us; the launch traced here: 33 us
  blocking collectives  12.9 us (39%)
  starting transfers between devices  10.1 us (30%)
  Pallas kernels  5.24 us (16%)
  waiting for transfers between devices  3 us (9%)
  local copies, waits for them, and re-layouts  1.7 us (5%)
    all_to_all x1, blocking collectives, shards(): lax.all_to_all(terms, ('chan', 'freq'), split_axis=0, concat_axis=0, tile...  12.9 us
    ppermute x6, starting transfers between devices, shards(): piece[distance] = lax.ppermute(piece[distance], 'chan', pairs)  10.1 us
    ppermute x6, waiting for transfers between devices, shards(): piece[distance] = lax.ppermute(piece[distance], 'chan', pairs)  3 us
    pallas_call x2, Pallas kernels, shards(): pl.pallas_call(functools.partial(stack_kernel, groups, start, size, parts...  2.42 us
    unnamed x6, local copies, waits for them, and re-layouts  1.7 us
    pallas_call x1, Pallas kernels, shards(): pl.pallas_call(functools.partial(table_kernel, groups, bins, freq_dev), o...  1.19 us
    pallas_call x1, Pallas kernels, shards(): pl.pallas_call(functools.partial(image_kernel, slow_dev, spans), out_shap...  0.97 us
  transfers between devices with their start and end apart: 6, of which 3 were waited for; matrix products, arithmetic and copies ran while one was open for 0% of the time, Pallas kernels for 8%

profile of v14, /device:TPU:0, one launch (start us, length us, event | category | flops | bytes accessed | tf_op | source)
XLA Modules:
  0.0 33.0 jit_solution(9715747620748762557)
XLA Ops:
  0.0 0.0 copy-start.1
  0.0 1.0 %copy-done.1 = bf16[2,32,32,128]{3,2,1,0:T(8,128)(2,1)S(1)} copy-done((bf16[2,32,32,128]{3,2,1,0:T(8,128)(2,1)S(1)}, bf16[2,32,32,128]{3,2,1,0:T(8,128)(2,1)}, u32[]{:S(2)}) %copy-start.1) | copy-done | bytes 524312
  1.0 0.7 %chunks_of_bins.1 = (bf16[6,64,128]{2,1,0:T(8,128)(2,1)S(1)}, bf16[6,64,128]{2,1,0:T(8,128)(2,1)S(1)}, bf16[6,64,128]{2,1,0:T(8,128)(2,1)S(1)}, bf16[6,64,128]{2...) custom-call(bf16[2048,128]{1,0:T(8,128)(2,1)S(1)} %bitcast.3), custom_call_target="tpu_custom_call" | custom-call | tf_op jit(solution)/shard_map/chunks_of_bins/pallas_call | solution.py:249
  1.7 3.1 %collective-permute-start.3 = (bf16[6,64,128]{2,1,0:T(8,128)(2,1)S(1)}, bf16[6,64,128]{2,1,0:T(8,128)(2,1)S(1)}, u32[]{:S(2)}, u32[]{:S(2)}) collective-permute-start(bf16[6,64,128]{2,1,0:T(8,128)(2,1)S(1)} %get-tuple-element.24), channel_id=1, source_target_pairs={{0,8},{8,16},{16,24},{24,0},{1,9},{9,17},{17,25},{25,1},{2,10},{10... | collective-permute-start | bytes 294920 | tf_op jit(solution)/shard_map/ppermute | solution.py:266
  4.8 2.6 %collective-permute-start.4 = (bf16[6,64,128]{2,1,0:T(8,128)(2,1)S(1)}, bf16[6,64,128]{2,1,0:T(8,128)(2,1)S(1)}, u32[]{:S(2)}, u32[]{:S(2)}) collective-permute-start(bf16[6,64,128]{2,1,0:T(8,128)(2,1)S(1)} %get-tuple-element.25), channel_id=1, source_target_pairs={{0,16},{8,24},{16,0},{24,8},{1,17},{9,25},{17,1},{25,9},{2,18},{10... | collective-permute-start | bytes 294920 | tf_op jit(solution)/shard_map/ppermute | solution.py:266
  7.4 1.3 %collective-permute-start.5 = (bf16[6,64,128]{2,1,0:T(8,128)(2,1)S(1)}, bf16[6,64,128]{2,1,0:T(8,128)(2,1)S(1)}, u32[]{:S(2)}, u32[]{:S(2)}) collective-permute-start(bf16[6,64,128]{2,1,0:T(8,128)(2,1)S(1)} %get-tuple-element.26), channel_id=1, source_target_pairs={{0,24},{8,0},{16,8},{24,16},{1,25},{9,1},{17,9},{25,17},{2,26},{10... | collective-permute-start | bytes 294920 | tf_op jit(solution)/shard_map/ppermute | solution.py:266
  8.7 0.7 %collective-permute-start = (bf16[2,64,128]{2,1,0:T(8,128)(2,1)S(1)}, bf16[2,64,128]{2,1,0:T(8,128)(2,1)S(1)}, u32[]{:S(2)}, u32[]{:S(2)}) collective-permute-start(bf16[2,64,128]{2,1,0:T(8,128)(2,1)S(1)} %get-tuple-element.17), channel_id=1, source_target_pairs={{0,8},{8,16},{16,24},{24,0},{1,9},{9,17},{17,25},{25,1},{2,10},{10... | collective-permute-start | bytes 98312 | tf_op jit(solution)/shard_map/ppermute | solution.py:266
  9.4 0.3 %collective-permute-start.1 = (bf16[2,64,128]{2,1,0:T(8,128)(2,1)S(1)}, bf16[2,64,128]{2,1,0:T(8,128)(2,1)S(1)}, u32[]{:S(2)}, u32[]{:S(2)}) collective-permute-start(bf16[2,64,128]{2,1,0:T(8,128)(2,1)S(1)} %get-tuple-element.18), channel_id=1, source_target_pairs={{0,16},{8,24},{16,0},{24,8},{1,17},{9,25},{17,1},{25,9},{2,18},{10... | collective-permute-start | bytes 98312 | tf_op jit(solution)/shard_map/ppermute | solution.py:266
  9.7 0.7 %collective-permute-done.3.refs_1_ = bf16[6,64,128]{2,1,0:T(8,128)(2,1)S(1)} collective-permute-done((bf16[6,64,128]{2,1,0:T(8,128)(2,1)S(1)}, bf16[6,64,128]{2,1,0:T(8,128)(2,1)S(1)}, u32[]{:S(2)}, u32[]{:S(2)}) %collective-permute-start.3) | collective-permute-done | bytes 98336 | tf_op jit(solution)/shard_map/ppermute | solution.py:266
  10.5 2.1 %collective-permute-start.2 = (bf16[2,64,128]{2,1,0:T(8,128)(2,1)S(1)}, bf16[2,64,128]{2,1,0:T(8,128)(2,1)S(1)}, u32[]{:S(2)}, u32[]{:S(2)}) collective-permute-start(bf16[2,64,128]{2,1,0:T(8,128)(2,1)S(1)} %get-tuple-element.19), channel_id=1, source_target_pairs={{0,24},{8,0},{16,8},{24,16},{1,25},{9,1},{17,9},{25,17},{2,26},{10... | collective-permute-start | bytes 98312 | tf_op jit(solution)/shard_map/ppermute | solution.py:266
  12.6 0.0 copy-start.2
  12.6 0.7 %copy-done.2 = s32[4]{0:T(128)S(1)} copy-done((s32[4]{0:T(128)S(1)}, s32[4]{0:T(128)}, u32[]{:S(2)}) %copy-start.2) | copy-done | bytes 40
  13.2 1.2 %slant_tables.1 = (s32[4,128]{1,0:T(4,128)S(1)}, bf16[8,256,512]{2,1,0:T(8,128)(2,1)S(1)}, f32[8,2,8,256]{3,2,1,0:T(8,128)S(1)}) custom-call(s32[1,4]{1,0:T(1,128)S(1)} %bitcast.5), custom_call_target="tpu_custom_call" | custom-call | flops 10000000 | bytes 4000000 | tf_op jit(solution)/shard_map/slant_tables/pallas_call | solution.py:267
  14.4 0.3 collective-permute-done.4.refs_2_
  14.7 0.0 collective-permute-done.5.refs_3_
  14.7 0.0 copy-start
  14.7 1.5 %stack_and_slant.2.refs_7_ = f32[12,4,256]{2,1,0:T(4,128)S(1)} custom-call(bf16[6,64,128]{2,1,0:T(8,128)(2,1)S(1)} %get-tuple-element.23.refs_0_, bf16[6,64,128]{2,1,0:T(8,128)(2,1)S(1)} %collective-permute-done.3.refs_1_, bf16[6,64,128]{2,1,0:T(8,128)(2,1)S(1)} %collective-permute-done.4.refs_2_, bf16[6,64,128]{2,1,0:T(8,128)(2,1)S(1)} %collective-permute-done.5.refs_3_, ...), custom_call_target="tpu_custom_call" | custom-call | flops 200000000 | bytes 4000000 | tf_op jit(solution)/shard_map/stack_and_slant/pallas_call | solution.py:287
  16.2 0.0 collective-permute-done.refs_1_
  16.2 2.0 %collective-permute-done.1.refs_2_ = bf16[2,64,128]{2,1,0:T(8,128)(2,1)S(1)} collective-permute-done((bf16[2,64,128]{2,1,0:T(8,128)(2,1)S(1)}, bf16[2,64,128]{2,1,0:T(8,128)(2,1)S(1)}, u32[]{:S(2)}, u32[]{:S(2)}) %collective-permute-start.1) | collective-permute-done | bytes 32800 | tf_op jit(solution)/shard_map/ppermute | solution.py:266
  18.2 0.0 collective-permute-done.2.refs_3_
  18.2 0.9 %stack_and_slant.3 = f32[4,8,4,128]{3,2,1,0:T(4,128)S(1)} custom-call(bf16[2,64,128]{2,1,0:T(8,128)(2,1)S(1)} %get-tuple-element.16.refs_0_, bf16[2,64,128]{2,1,0:T(8,128)(2,1)S(1)} %collective-permute-done.refs_1_, bf16[2,64,128]{2,1,0:T(8,128)(2,1)S(1)} %collective-permute-done.1.refs_2_, bf16[2,64,128]{2,1,0:T(8,128)(2,1)S(1)} %collective-permute-done.2.refs_3_, ...), custom_call_target="tpu_custom_call" | custom-call | flops 200000000 | bytes 4000000 | tf_op jit(solution)/shard_map/stack_and_slant/pallas_call | solution.py:287
  19.1 12.9 %all_to_all.5.term_ref = f32[32,4,128]{2,1,0:T(4,128)S(1)} all-to-all(f32[32,4,128]{2,1,0:T(4,128)S(1)} %bitcast.4), channel_id=1, replica_groups=mesh['chan'=4,'freq'=8] {'chan','freq'}, dimensions={0} | all-to-all | bytes 131072 | tf_op jit(solution)/shard_map/all_to_all | solution.py:305
  32.0 0.0 copy-done
  32.0 1.0 %sum_of_bins.1 = f32[1,32,512]{2,1,0:T(8,128)} custom-call(f32[32,4,128]{2,1,0:T(4,128)S(1)} %all_to_all.5.term_ref, bf16[2,512,512]{2,1,0:T(8,128)(2,1)S(1)} %copy-done), custom_call_target="tpu_custom_call" | custom-call | tf_op jit(solution)/shard_map/sum_of_bins/pallas_call | solution.py:307
Async XLA Ops:
  0.0 1.0 %copy-start.1 = (bf16[2,32,32,128]{3,2,1,0:T(8,128)(2,1)S(1)}, bf16[2,32,32,128]{3,2,1,0:T(8,128)(2,1)}, u32[]{:S(2)}) copy-start(bf16[2,32,32,128]{3,2,1,0:T(8,128)(2,1)} %param.3) | copy-start | bytes 1572868
  1.7 8.8 %collective-permute-start.3 = (bf16[6,64,128]{2,1,0:T(8,128)(2,1)S(1)}, bf16[6,64,128]{2,1,0:T(8,128)(2,1)S(1)}, u32[]{:S(2)}, u32[]{:S(2)}) collective-permute-start(bf16[6,64,128]{2,1,0:T(8,128)(2,1)S(1)} %get-tuple-element.24), channel_id=1, source_target_pairs={{0,8},{8,16},{16,24},{24,0},{1,9},{9,17},{17,25},{25,1},{2,10},{10... | collective-permute-start | bytes 294920 | tf_op jit(solution)/shard_map/ppermute | solution.py:266
  4.8 9.9 %collective-permute-start.4 = (bf16[6,64,128]{2,1,0:T(8,128)(2,1)S(1)}, bf16[6,64,128]{2,1,0:T(8,128)(2,1)S(1)}, u32[]{:S(2)}, u32[]{:S(2)}) collective-permute-start(bf16[6,64,128]{2,1,0:T(8,128)(2,1)S(1)} %get-tuple-element.25), channel_id=1, source_target_pairs={{0,16},{8,24},{16,0},{24,8},{1,17},{9,25},{17,1},{25,9},{2,18},{10... | collective-permute-start | bytes 294920 | tf_op jit(solution)/shard_map/ppermute | solution.py:266
  7.4 7.3 %collective-permute-start.5 = (bf16[6,64,128]{2,1,0:T(8,128)(2,1)S(1)}, bf16[6,64,128]{2,1,0:T(8,128)(2,1)S(1)}, u32[]{:S(2)}, u32[]{:S(2)}) collective-permute-start(bf16[6,64,128]{2,1,0:T(8,128)(2,1)S(1)} %get-tuple-element.26), channel_id=1, source_target_pairs={{0,24},{8,0},{16,8},{24,16},{1,25},{9,1},{17,9},{25,17},{2,26},{10... | collective-permute-start | bytes 294920 | tf_op jit(solution)/shard_map/ppermute | solution.py:266
  8.7 7.5 %collective-permute-start = (bf16[2,64,128]{2,1,0:T(8,128)(2,1)S(1)}, bf16[2,64,128]{2,1,0:T(8,128)(2,1)S(1)}, u32[]{:S(2)}, u32[]{:S(2)}) collective-permute-start(bf16[2,64,128]{2,1,0:T(8,128)(2,1)S(1)} %get-tuple-element.17), channel_id=1, source_target_pairs={{0,8},{8,16},{16,24},{24,0},{1,9},{9,17},{17,25},{25,1},{2,10},{10... | collective-permute-start | bytes 98312 | tf_op jit(solution)/shard_map/ppermute | solution.py:266
  9.4 8.8 %collective-permute-start.1 = (bf16[2,64,128]{2,1,0:T(8,128)(2,1)S(1)}, bf16[2,64,128]{2,1,0:T(8,128)(2,1)S(1)}, u32[]{:S(2)}, u32[]{:S(2)}) collective-permute-start(bf16[2,64,128]{2,1,0:T(8,128)(2,1)S(1)} %get-tuple-element.18), channel_id=1, source_target_pairs={{0,16},{8,24},{16,0},{24,8},{1,17},{9,25},{17,1},{25,9},{2,18},{10... | collective-permute-start | bytes 98312 | tf_op jit(solution)/shard_map/ppermute | solution.py:266
  10.5 7.7 %collective-permute-start.2 = (bf16[2,64,128]{2,1,0:T(8,128)(2,1)S(1)}, bf16[2,64,128]{2,1,0:T(8,128)(2,1)S(1)}, u32[]{:S(2)}, u32[]{:S(2)}) collective-permute-start(bf16[2,64,128]{2,1,0:T(8,128)(2,1)S(1)} %get-tuple-element.19), channel_id=1, source_target_pairs={{0,24},{8,0},{16,8},{24,16},{1,25},{9,1},{17,9},{25,17},{2,26},{10... | collective-permute-start | bytes 98312 | tf_op jit(solution)/shard_map/ppermute | solution.py:266
  12.6 0.7 %copy-start.2 = (s32[4]{0:T(128)S(1)}, s32[4]{0:T(128)}, u32[]{:S(2)}) copy-start(s32[4]{0:T(128)} %param.4) | copy-start | bytes 52
  14.7 17.3 %copy-start = (bf16[2,512,512]{2,1,0:T(8,128)(2,1)S(1)}, bf16[2,512,512]{2,1,0:T(8,128)(2,1)}, u32[]{:S(2)}) copy-start(bf16[2,512,512]{2,1,0:T(8,128)(2,1)} %constant.2.clone.table_ref) | copy-start | bytes 3145732

commit v15 on v7

--- a/solution.py
+++ b/solution.py
@@ -38,7 +38,7 @@
     return high, (value - high.astype(jnp.float32)).astype(jnp.bfloat16)
 
 
-def table_kernel(groups, bins, freq_dev, position_ref, place_ref, lag_ref, shift_ref):
+def table_kernel(groups, bins, freq_dev, position_ref, far_ref, place_ref, lag_ref, shift_ref):
     low_rows = lax.broadcasted_iota(jnp.int32, (8, SLOWNESS), 0)
     high_rows = lax.broadcasted_iota(jnp.int32, (BLOCK // 8, SLOWNESS), 0) * 8
     shift_rows = lax.broadcasted_iota(jnp.int32, (2 * groups, SLOWNESS), 0)
@@ -76,16 +76,15 @@
     lax.fori_loop(0, bins, one_bin, 0)
 
 
-def chunk_kernel(groups, bins, spec_ref, *refs):
-    out_refs, wide_ref = refs[:-1], refs[-1]
-    wide_ref[...] = spec_ref[...].astype(jnp.float32)
-    freq_dev = groups * bins
-    rows = spec_ref.shape[0] // freq_dev
+def chunk_kernel(distances, spec_ref, *refs):
+    rows, groups, bins, _ = spec_ref.shape
+    out_refs, wide_ref = refs[-1 - len(distances) : -1], refs[-1]
     own_group = lax.axis_index("chan")
-    for distance, out_ref in enumerate(out_refs):
-        first = lax.rem(own_group + distance, groups) * bins
+    for index, (distance, out_ref) in enumerate(zip(distances, out_refs)):
+        group = lax.rem(own_group + distance, groups)
+        wide_ref[index] = spec_ref[:, group].astype(jnp.float32).reshape(rows * bins, BLOCK)
         for f in range(bins):
-            value = wide_ref[pl.ds(first + f, rows, stride=freq_dev), :]
+            value = wide_ref[index, pl.ds(f, rows, stride=bins), :]
             out_ref[f] = value.astype(jnp.bfloat16)
 
 
@@ -232,22 +231,30 @@
     slow_dev = SLOWNESS // parts
     message_rows = -(-2 * bins * slow_dev // BLOCK)
     vmem = pl.BlockSpec(memory_space=pltpu.VMEM)
+    anywhere = pl.BlockSpec(memory_space=pl.ANY)
     params = pltpu.CompilerParams(vmem_limit_bytes=32 * 1024 * 1024)
 
-    chunk = jax.ShapeDtypeStruct((bins, rows, BLOCK), jnp.bfloat16)
-    chunks = pl.pallas_call(
-        functools.partial(chunk_kernel, groups, bins),
-        out_shape=(chunk,) * groups,
-        in_specs=[vmem],
-        out_specs=(vmem,) * groups,
-        scratch_shapes=[pltpu.VMEM((rows * freq_dev, BLOCK), jnp.float32)],
-        compiler_params=params,
-        name="chunks_of_bins",
-    )(spectra.reshape(rows * freq_dev, BLOCK))
-    arrived_chunks = list(chunks)
-    for distance in sorted(range(1, groups), key=lambda steps: abs(2 * steps - groups)):
+    whole = spectra.reshape(rows, groups, bins, BLOCK)
+
+    def cut(distances, *earlier):
+        return pl.pallas_call(
+            functools.partial(chunk_kernel, distances),
+            out_shape=(jax.ShapeDtypeStruct((bins, rows, BLOCK), jnp.bfloat16),) * len(distances),
+            in_specs=[vmem] + [anywhere] * len(earlier),
+            out_specs=(vmem,) * len(distances),
+            scratch_shapes=[pltpu.VMEM((len(distances), rows * bins, BLOCK), jnp.float32)],
+            compiler_params=params,
+            cost_estimate=pl.CostEstimate(flops=10**7, bytes_accessed=10**6, transcendentals=0),
+            name="chunks_of_bins",
+        )(whole, *earlier)
+
+    far = groups // 2
+    order = [far] + [distance for distance in range(1, groups) if distance != far] + [0]
+    (far_chunk,) = cut(order[:1])
+    chunks = dict(zip(order, (far_chunk, *cut(order[1:], far_chunk))))
+    for distance in order[:-1]:
         pairs = [(source, (source + distance) % groups) for source in range(groups)]
-        arrived_chunks[distance] = lax.ppermute(chunks[distance], "chan", pairs)
+        chunks[distance] = lax.ppermute(chunks[distance], "chan", pairs)
     places, lag_table, shift_table = pl.pallas_call(
         functools.partial(table_kernel, groups, bins, freq_dev),
         out_shape=(
@@ -255,12 +262,12 @@
             jax.ShapeDtypeStruct((bins, 2 * BLOCK, 2 * SLOWNESS), jnp.bfloat16),
             jax.ShapeDtypeStruct((bins, 2, 2 * groups, SLOWNESS), jnp.float32),
         ),
-        in_specs=[vmem],
+        in_specs=[vmem, anywhere],
         out_specs=(vmem, vmem, vmem),
         compiler_params=params,
         cost_estimate=pl.CostEstimate(flops=10**7, bytes_accessed=4 * 10**6, transcendentals=0),
         name="slant_tables",
-    )(block_position.reshape(1, groups))
+    )(block_position.reshape(1, groups), chunks[far])
     terms = pl.pallas_call(
         functools.partial(stack_kernel, groups, bins, parts),
         out_shape=jax.ShapeDtypeStruct((groups, parts, message_rows, BLOCK), jnp.float32),
@@ -274,7 +281,7 @@
         compiler_params=params,
         name="stack_and_slant",
     )(
-        *arrived_chunks,
+        *[chunks[distance] for distance in range(groups)],
         places,
         lag_table,
         shift_table,

time: 33 us -> 32.4 us (0.982)
  blocking collectives: 13.8 us -> 12.2 us
  starting transfers between devices: 7.01 us -> 7.98 us
  waiting for transfers between devices: 5.45 us -> 5.93 us
  Pallas kernels: 4.8 us -> 4.38 us
    all_to_all x1, blocking collectives: 13.8 us -> 12.2 us  [shards(): lax.all_to_all(terms, ('chan', 'freq'), split_axis=0, concat_axis=0, tile...]
    ppermute x3, starting transfers between devices: 7.01 us -> 7.98 us  [shards(): chunks[distance] = lax.ppermute(chunks[distance], 'chan', pairs)]
    ppermute x3, waiting for transfers between devices: 5.45 us -> 5.93 us  [shards(): chunks[distance] = lax.ppermute(chunks[distance], 'chan', pairs)]
    pallas_call x1 -> x2, Pallas kernels: 0.66 us -> 0.24 us  [cut(): pl.pallas_call(functools.partial(chunk_kernel, distances), out_shape=(jax...]
  transfers between devices with their start and end apart: 3 -> 3, of which waited for: 2 -> 1; matrix products, arithmetic and copies ran while one was open for 0% -> 0% of each run, Pallas kernels for 4% -> 4%
where the time goes in v15:
time: 32.4 us; the launch traced here: 32.2 us
  blocking collectives  12.2 us (38%)
  starting transfers between devices  7.98 us (25%)
  waiting for transfers between devices  5.93 us (18%)
  Pallas kernels  4.38 us (14%)
  local copies, waits for them, and re-layouts  1.7 us (5%)
    all_to_all x1, blocking collectives, shards(): lax.all_to_all(terms, ('chan', 'freq'), split_axis=0, concat_axis=0, tile...  12.2 us
    ppermute x3, starting transfers between devices, shards(): chunks[distance] = lax.ppermute(chunks[distance], 'chan', pairs)  7.98 us
    ppermute x3, waiting for transfers between devices, shards(): chunks[distance] = lax.ppermute(chunks[distance], 'chan', pairs)  5.93 us
    pallas_call x1, Pallas kernels, shards(): pl.pallas_call(functools.partial(stack_kernel, groups, bins, parts), out_...  1.98 us
    unnamed x6, local copies, waits for them, and re-layouts  1.7 us
    pallas_call x1, Pallas kernels, shards(): pl.pallas_call(functools.partial(table_kernel, groups, bins, freq_dev), o...  1.19 us
    pallas_call x1, Pallas kernels, shards(): pl.pallas_call(functools.partial(image_kernel, slow_dev, spans), out_shap...  0.97 us
  transfers between devices with their start and end apart: 3, of which 1 were waited for; matrix products, arithmetic and copies ran while one was open for 0% of the time, Pallas kernels for 4%

profile of v15, /device:TPU:0, one launch (start us, length us, event | category | flops | bytes accessed | tf_op | source)
XLA Modules:
  0.0 32.2 jit_solution(18256937261351092369)
XLA Ops:
  0.0 0.0 copy-start
  0.0 1.0 %copy-done = bf16[2,32,32,128]{3,2,1,0:T(8,128)(2,1)S(1)} copy-done((bf16[2,32,32,128]{3,2,1,0:T(8,128)(2,1)S(1)}, bf16[2,32,32,128]{3,2,1,0:T(8,128)(2,1)}, u32[]{:S(2)}) %copy-start) | copy-done | bytes 524312
  1.0 0.0 copy-start.1
  1.0 0.1 chunks_of_bins.2.refs_0_
  1.1 4.1 %collective-permute-start.1 = (bf16[8,64,128]{2,1,0:T(8,128)(2,1)S(1)}, bf16[8,64,128]{2,1,0:T(8,128)(2,1)S(1)}, u32[]{:S(2)}, u32[]{:S(2)}) collective-permute-start(bf16[8,64,128]{2,1,0:T(8,128)(2,1)S(1)} %chunks_of_bins.2.refs_0_), channel_id=1, source_target_pairs={{0,16},{8,24},{16,0},{24,8},{1,17},{9,25},{17,1},{25,9},{2,18},{10... | collective-permute-start | bytes 393224 | tf_op jit(solution)/shard_map/ppermute | solution.py:257
  5.2 0.2 chunks_of_bins.3
  5.4 1.6 %collective-permute-start = (bf16[8,64,128]{2,1,0:T(8,128)(2,1)S(1)}, bf16[8,64,128]{2,1,0:T(8,128)(2,1)S(1)}, u32[]{:S(2)}, u32[]{:S(2)}) collective-permute-start(bf16[8,64,128]{2,1,0:T(8,128)(2,1)S(1)} %get-tuple-element.12), channel_id=1, source_target_pairs={{0,8},{8,16},{16,24},{24,0},{1,9},{9,17},{17,25},{25,1},{2,10},{10... | collective-permute-start | bytes 393224 | tf_op jit(solution)/shard_map/ppermute | solution.py:257
  7.0 2.2 %collective-permute-start.2 = (bf16[8,64,128]{2,1,0:T(8,128)(2,1)S(1)}, bf16[8,64,128]{2,1,0:T(8,128)(2,1)S(1)}, u32[]{:S(2)}, u32[]{:S(2)}) collective-permute-start(bf16[8,64,128]{2,1,0:T(8,128)(2,1)S(1)} %get-tuple-element.13), channel_id=1, source_target_pairs={{0,24},{8,0},{16,8},{24,16},{1,25},{9,1},{17,9},{25,17},{2,26},{10... | collective-permute-start | bytes 393224 | tf_op jit(solution)/shard_map/ppermute | solution.py:257
  9.3 5.9 %collective-permute-done.1.far_ref.refs_2_ = bf16[8,64,128]{2,1,0:T(8,128)(2,1)S(1)} collective-permute-done((bf16[8,64,128]{2,1,0:T(8,128)(2,1)S(1)}, bf16[8,64,128]{2,1,0:T(8,128)(2,1)S(1)}, u32[]{:S(2)}, u32[]{:S(2)}) %collective-permute-start.1) | collective-permute-done | bytes 131104 | tf_op jit(solution)/shard_map/ppermute | solution.py:257
  15.2 0.0 copy-start.2
  15.2 0.7 %copy-done.2 = s32[4]{0:T(128)S(1)} copy-done((s32[4]{0:T(128)S(1)}, s32[4]{0:T(128)}, u32[]{:S(2)}) %copy-start.2) | copy-done | bytes 40
  15.9 1.2 %slant_tables.1 = (s32[4,128]{1,0:T(4,128)S(1)}, bf16[8,256,512]{2,1,0:T(8,128)(2,1)S(1)}, f32[8,2,8,256]{3,2,1,0:T(8,128)S(1)}) custom-call(s32[1,4]{1,0:T(1,128)S(1)} %bitcast.6, bf16[8,64,128]{2,1,0:T(8,128)(2,1)S(1)} %collective-permute-done.1.far_ref.refs_2_), custom_call_target="tpu_custom_call" | custom-call | flops 10000000 | bytes 4000000 | tf_op jit(solution)/shard_map/slant_tables/pallas_call | solution.py:258
  17.1 0.0 collective-permute-done.refs_1_
  17.1 0.0 collective-permute-done.2.refs_3_
  17.1 2.0 %stack_and_slant.1 = f32[4,8,4,128]{3,2,1,0:T(4,128)S(1)} custom-call(bf16[8,64,128]{2,1,0:T(8,128)(2,1)S(1)} %get-tuple-element.11.refs_0_, bf16[8,64,128]{2,1,0:T(8,128)(2,1)S(1)} %collective-permute-done.refs_1_, bf16[8,64,128]{2,1,0:T(8,128)(2,1)S(1)} %collective-permute-done.1.far_ref.refs_2_, bf16[8,64,128]{2,1,0:T(8,128)(2,1)S(1)} %collective-permute-done.2.refs_3_, ...), custom_call_target="tpu_custom_call" | custom-call | tf_op jit(solution)/shard_map/stack_and_slant/pallas_call | solution.py:271
  19.1 12.2 %all_to_all.5.term_ref = f32[32,4,128]{2,1,0:T(4,128)S(1)} all-to-all(f32[32,4,128]{2,1,0:T(4,128)S(1)} %bitcast.5), channel_id=1, replica_groups=mesh['chan'=4,'freq'=8] {'chan','freq'}, dimensions={0} | all-to-all | bytes 131072 | tf_op jit(solution)/shard_map/all_to_all | solution.py:290
  31.2 0.0 copy-done.1
  31.2 1.0 %sum_of_bins.1 = f32[1,32,512]{2,1,0:T(8,128)} custom-call(f32[32,4,128]{2,1,0:T(4,128)S(1)} %all_to_all.5.term_ref, bf16[2,512,512]{2,1,0:T(8,128)(2,1)S(1)} %copy-done.1), custom_call_target="tpu_custom_call" | custom-call | tf_op jit(solution)/shard_map/sum_of_bins/pallas_call | solution.py:292
Async XLA Ops:
  0.0 1.0 %copy-start = (bf16[2,32,32,128]{3,2,1,0:T(8,128)(2,1)S(1)}, bf16[2,32,32,128]{3,2,1,0:T(8,128)(2,1)}, u32[]{:S(2)}) copy-start(bf16[2,32,32,128]{3,2,1,0:T(8,128)(2,1)} %param.3) | copy-start | bytes 1572868
  1.0 30.2 %copy-start.1 = (bf16[2,512,512]{2,1,0:T(8,128)(2,1)S(1)}, bf16[2,512,512]{2,1,0:T(8,128)(2,1)}, u32[]{:S(2)}) copy-start(bf16[2,512,512]{2,1,0:T(8,128)(2,1)} %constant.2.clone.table_ref) | copy-start | bytes 3145732
  1.1 14.1 %collective-permute-start.1 = (bf16[8,64,128]{2,1,0:T(8,128)(2,1)S(1)}, bf16[8,64,128]{2,1,0:T(8,128)(2,1)S(1)}, u32[]{:S(2)}, u32[]{:S(2)}) collective-permute-start(bf16[8,64,128]{2,1,0:T(8,128)(2,1)S(1)} %chunks_of_bins.2.refs_0_), channel_id=1, source_target_pairs={{0,16},{8,24},{16,0},{24,8},{1,17},{9,25},{17,1},{25,9},{2,18},{10... | collective-permute-start | bytes 393224 | tf_op jit(solution)/shard_map/ppermute | solution.py:257
  5.4 11.7 %collective-permute-start = (bf16[8,64,128]{2,1,0:T(8,128)(2,1)S(1)}, bf16[8,64,128]{2,1,0:T(8,128)(2,1)S(1)}, u32[]{:S(2)}, u32[]{:S(2)}) collective-permute-start(bf16[8,64,128]{2,1,0:T(8,128)(2,1)S(1)} %get-tuple-element.12), channel_id=1, source_target_pairs={{0,8},{8,16},{16,24},{24,0},{1,9},{9,17},{17,25},{25,1},{2,10},{10... | collective-permute-start | bytes 393224 | tf_op jit(solution)/shard_map/ppermute | solution.py:257
  7.0 10.0 %collective-permute-start.2 = (bf16[8,64,128]{2,1,0:T(8,128)(2,1)S(1)}, bf16[8,64,128]{2,1,0:T(8,128)(2,1)S(1)}, u32[]{:S(2)}, u32[]{:S(2)}) collective-permute-start(bf16[8,64,128]{2,1,0:T(8,128)(2,1)S(1)} %get-tuple-element.13), channel_id=1, source_target_pairs={{0,24},{8,0},{16,8},{24,16},{1,25},{9,1},{17,9},{25,17},{2,26},{10... | collective-permute-start | bytes 393224 | tf_op jit(solution)/shard_map/ppermute | solution.py:257
  15.2 0.7 %copy-start.2 = (s32[4]{0:T(128)S(1)}, s32[4]{0:T(128)}, u32[]{:S(2)}) copy-start(s32[4]{0:T(128)} %param.4) | copy-start | bytes 52

commit v16 on v15

--- a/solution.py
+++ b/solution.py
@@ -195,31 +195,40 @@
 def image_kernel(slow_dev, spans, term_ref, table_ref, out_ref):
     arrived = term_ref[...]
     turned = arrived.reshape(-1, BLOCK).T
-    turned = jnp.concatenate(
-        [turned[span * slow_dev : (span + 1) * slow_dev] for span in range(spans)], 1
-    )
-    high, low = halves(turned)
-    by_high = jnp.dot(
-        jnp.concatenate([high, low], 0), table_ref[0], preferred_element_type=jnp.float32
-    )
-    by_low = jnp.dot(high, table_ref[1], preferred_element_type=jnp.float32)
-    out_ref[0] = by_high[:slow_dev] + by_high[slow_dev:] + by_low
+    sums = []
+    for odd, chosen in enumerate(spans):
+        terms = jnp.concatenate(
+            [turned[span * slow_dev : (span + 1) * slow_dev] for span in chosen], 1
+        )
+        high, low = halves(terms)
+        by_high = jnp.dot(
+            jnp.concatenate([high, low], 0), table_ref[odd, 0], preferred_element_type=jnp.float32
+        )
+        by_low = jnp.dot(high, table_ref[odd, 1], preferred_element_type=jnp.float32)
+        sums.append(by_high[:slow_dev] + by_high[slow_dev:] + by_low)
+    even, odd = sums
+    out_ref[0, :, : LAG_TIMES // 2] = even - odd
+    out_ref[0, :, LAG_TIMES // 2 :] = even + odd
 
 
 def time_table(groups, parts, bins, slow_dev, message_rows):
-    spans = min(BLOCK // slow_dev, 2 * bins)
-    span, group, part, row = np.meshgrid(
-        np.arange(spans), np.arange(groups), np.arange(parts), np.arange(message_rows), indexing="ij"
-    )
-    entry = row * spans + span
-    freq = (part * groups + group) * bins + entry // 2
-    lag_time = np.arange(LAG_TIMES) - LAG_TIMES // 2
-    angle = 2.0 * math.pi / LAG_TIMES * ((freq[..., None] * lag_time) % LAG_TIMES)
-    table = np.where((entry % 2 == 0)[..., None], np.cos(angle), -np.sin(angle))
-    table = table.reshape(-1, LAG_TIMES).astype(np.float32)
-    high = table.astype(jnp.bfloat16)
-    low = (table - high.astype(np.float32)).astype(jnp.bfloat16)
-    return spans, np.stack([high, low])
+    count = min(BLOCK // slow_dev, 2 * bins)
+    spans = [[span for span in range(count) if span // 2 % 2 == odd] for odd in range(2)]
+    tables = []
+    for chosen in spans:
+        span, group, part, row = np.meshgrid(
+            chosen, np.arange(groups), np.arange(parts), np.arange(message_rows), indexing="ij"
+        )
+        entry = row * count + span
+        freq = (part * groups + group) * bins + entry // 2
+        lag_time = np.arange(LAG_TIMES // 2)
+        angle = 2.0 * math.pi / LAG_TIMES * ((freq[..., None] * lag_time) % LAG_TIMES)
+        table = np.where((entry % 2 == 0)[..., None], np.cos(angle), -np.sin(angle))
+        table = table.reshape(-1, LAG_TIMES // 2).astype(np.float32)
+        high = table.astype(jnp.bfloat16)
+        low = (table - high.astype(np.float32)).astype(jnp.bfloat16)
+        tables.append(np.stack([high, low]))
+    return spans, np.stack(tables)
 
 
 def shards(spectra, block_position):

time: 32.4 us -> 32.3 us (level)
  no operation moved by 1% of the time
where the time goes in v16:
time: 32.3 us; the launch traced here: 32.1 us
  blocking collectives  12.2 us (38%)
  starting transfers between devices  7.98 us (25%)
  waiting for transfers between devices  5.93 us (18%)
  Pallas kernels  4.29 us (13%)
  local copies, waits for them, and re-layouts  1.7 us (5%)
    all_to_all x1, blocking collectives, shards(): lax.all_to_all(terms, ('chan', 'freq'), split_axis=0, concat_axis=0, tile...  12.2 us
    ppermute x3, starting transfers between devices, shards(): chunks[distance] = lax.ppermute(chunks[distance], 'chan', pairs)  7.98 us
    ppermute x3, waiting for transfers between devices, shards(): chunks[distance] = lax.ppermute(chunks[distance], 'chan', pairs)  5.93 us
    pallas_call x1, Pallas kernels, shards(): pl.pallas_call(functools.partial(stack_kernel, groups, bins, parts), out_...  1.98 us
    unnamed x6, local copies, waits for them, and re-layouts  1.7 us
    pallas_call x1, Pallas kernels, shards(): pl.pallas_call(functools.partial(table_kernel, groups, bins, freq_dev), o...  1.19 us
    pallas_call x1, Pallas kernels, shards(): pl.pallas_call(functools.partial(image_kernel, slow_dev, spans), out_shap...  0.88 us
  transfers between devices with their start and end apart: 3, of which 1 were waited for; matrix products, arithmetic and copies ran while one was open for 0% of the time, Pallas kernels for 4%

profile of v16, /device:TPU:0, one launch (start us, length us, event | category | flops | bytes accessed | tf_op | source)
XLA Modules:
  0.0 32.1 jit_solution(8811531122565239829)
XLA Ops:
  0.0 0.0 copy-start
  0.0 1.0 %copy-done = bf16[2,32,32,128]{3,2,1,0:T(8,128)(2,1)S(1)} copy-done((bf16[2,32,32,128]{3,2,1,0:T(8,128)(2,1)S(1)}, bf16[2,32,32,128]{3,2,1,0:T(8,128)(2,1)}, u32[]{:S(2)}) %copy-start) | copy-done | bytes 524312
  1.0 0.0 copy-start.1
  1.0 0.1 chunks_of_bins.2.refs_0_
  1.1 4.1 %collective-permute-start.1 = (bf16[8,64,128]{2,1,0:T(8,128)(2,1)S(1)}, bf16[8,64,128]{2,1,0:T(8,128)(2,1)S(1)}, u32[]{:S(2)}, u32[]{:S(2)}) collective-permute-start(bf16[8,64,128]{2,1,0:T(8,128)(2,1)S(1)} %chunks_of_bins.2.refs_0_), channel_id=1, source_target_pairs={{0,16},{8,24},{16,0},{24,8},{1,17},{9,25},{17,1},{25,9},{2,18},{10... | collective-permute-start | bytes 393224 | tf_op jit(solution)/shard_map/ppermute | solution.py:266
  5.2 0.2 chunks_of_bins.3
  5.4 1.6 %collective-permute-start = (bf16[8,64,128]{2,1,0:T(8,128)(2,1)S(1)}, bf16[8,64,128]{2,1,0:T(8,128)(2,1)S(1)}, u32[]{:S(2)}, u32[]{:S(2)}) collective-permute-start(bf16[8,64,128]{2,1,0:T(8,128)(2,1)S(1)} %get-tuple-element.12), channel_id=1, source_target_pairs={{0,8},{8,16},{16,24},{24,0},{1,9},{9,17},{17,25},{25,1},{2,10},{10... | collective-permute-start | bytes 393224 | tf_op jit(solution)/shard_map/ppermute | solution.py:266
  7.0 2.2 %collective-permute-start.2 = (bf16[8,64,128]{2,1,0:T(8,128)(2,1)S(1)}, bf16[8,64,128]{2,1,0:T(8,128)(2,1)S(1)}, u32[]{:S(2)}, u32[]{:S(2)}) collective-permute-start(bf16[8,64,128]{2,1,0:T(8,128)(2,1)S(1)} %get-tuple-element.13), channel_id=1, source_target_pairs={{0,24},{8,0},{16,8},{24,16},{1,25},{9,1},{17,9},{25,17},{2,26},{10... | collective-permute-start | bytes 393224 | tf_op jit(solution)/shard_map/ppermute | solution.py:266
  9.3 5.9 %collective-permute-done.1.far_ref.refs_2_ = bf16[8,64,128]{2,1,0:T(8,128)(2,1)S(1)} collective-permute-done((bf16[8,64,128]{2,1,0:T(8,128)(2,1)S(1)}, bf16[8,64,128]{2,1,0:T(8,128)(2,1)S(1)}, u32[]{:S(2)}, u32[]{:S(2)}) %collective-permute-start.1) | collective-permute-done | bytes 131104 | tf_op jit(solution)/shard_map/ppermute | solution.py:266
  15.2 0.0 copy-start.2
  15.2 0.7 %copy-done.2 = s32[4]{0:T(128)S(1)} copy-done((s32[4]{0:T(128)S(1)}, s32[4]{0:T(128)}, u32[]{:S(2)}) %copy-start.2) | copy-done | bytes 40
  15.9 1.2 %slant_tables.1 = (s32[4,128]{1,0:T(4,128)S(1)}, bf16[8,256,512]{2,1,0:T(8,128)(2,1)S(1)}, f32[8,2,8,256]{3,2,1,0:T(8,128)S(1)}) custom-call(s32[1,4]{1,0:T(1,128)S(1)} %bitcast.6, bf16[8,64,128]{2,1,0:T(8,128)(2,1)S(1)} %collective-permute-done.1.far_ref.refs_2_), custom_call_target="tpu_custom_call" | custom-call | flops 10000000 | bytes 4000000 | tf_op jit(solution)/shard_map/slant_tables/pallas_call | solution.py:267
  17.1 0.0 collective-permute-done.refs_1_
  17.1 0.0 collective-permute-done.2.refs_3_
  17.1 2.0 %stack_and_slant.1 = f32[4,8,4,128]{3,2,1,0:T(4,128)S(1)} custom-call(bf16[8,64,128]{2,1,0:T(8,128)(2,1)S(1)} %get-tuple-element.11.refs_0_, bf16[8,64,128]{2,1,0:T(8,128)(2,1)S(1)} %collective-permute-done.refs_1_, bf16[8,64,128]{2,1,0:T(8,128)(2,1)S(1)} %collective-permute-done.1.far_ref.refs_2_, bf16[8,64,128]{2,1,0:T(8,128)(2,1)S(1)} %collective-permute-done.2.refs_3_, ...), custom_call_target="tpu_custom_call" | custom-call | tf_op jit(solution)/shard_map/stack_and_slant/pallas_call | solution.py:280
  19.1 12.2 %all_to_all.5.term_ref = f32[32,4,128]{2,1,0:T(4,128)S(1)} all-to-all(f32[32,4,128]{2,1,0:T(4,128)S(1)} %bitcast.5), channel_id=1, replica_groups=mesh['chan'=4,'freq'=8] {'chan','freq'}, dimensions={0} | all-to-all | bytes 131072 | tf_op jit(solution)/shard_map/all_to_all | solution.py:299
  31.2 0.0 copy-done.1
  31.2 0.9 %sum_of_bins.1 = f32[1,32,512]{2,1,0:T(8,128)} custom-call(f32[32,4,128]{2,1,0:T(4,128)S(1)} %all_to_all.5.term_ref, bf16[2,2,256,256]{3,2,1,0:T(8,128)(2,1)S(1)} %copy-done.1), custom_call_target="tpu_custom_call" | custom-call | tf_op jit(solution)/shard_map/sum_of_bins/pallas_call | solution.py:301
Async XLA Ops:
  0.0 1.0 %copy-start = (bf16[2,32,32,128]{3,2,1,0:T(8,128)(2,1)S(1)}, bf16[2,32,32,128]{3,2,1,0:T(8,128)(2,1)}, u32[]{:S(2)}) copy-start(bf16[2,32,32,128]{3,2,1,0:T(8,128)(2,1)} %param.3) | copy-start | bytes 1572868
  1.0 30.2 %copy-start.1 = (bf16[2,2,256,256]{3,2,1,0:T(8,128)(2,1)S(1)}, bf16[2,2,256,256]{3,2,1,0:T(8,128)(2,1)}, u32[]{:S(2)}) copy-start(bf16[2,2,256,256]{3,2,1,0:T(8,128)(2,1)} %constant.2.clone.table_ref) | copy-start | bytes 1572868
  1.1 14.1 %collective-permute-start.1 = (bf16[8,64,128]{2,1,0:T(8,128)(2,1)S(1)}, bf16[8,64,128]{2,1,0:T(8,128)(2,1)S(1)}, u32[]{:S(2)}, u32[]{:S(2)}) collective-permute-start(bf16[8,64,128]{2,1,0:T(8,128)(2,1)S(1)} %chunks_of_bins.2.refs_0_), channel_id=1, source_target_pairs={{0,16},{8,24},{16,0},{24,8},{1,17},{9,25},{17,1},{25,9},{2,18},{10... | collective-permute-start | bytes 393224 | tf_op jit(solution)/shard_map/ppermute | solution.py:266
  5.4 11.7 %collective-permute-start = (bf16[8,64,128]{2,1,0:T(8,128)(2,1)S(1)}, bf16[8,64,128]{2,1,0:T(8,128)(2,1)S(1)}, u32[]{:S(2)}, u32[]{:S(2)}) collective-permute-start(bf16[8,64,128]{2,1,0:T(8,128)(2,1)S(1)} %get-tuple-element.12), channel_id=1, source_target_pairs={{0,8},{8,16},{16,24},{24,0},{1,9},{9,17},{17,25},{25,1},{2,10},{10... | collective-permute-start | bytes 393224 | tf_op jit(solution)/shard_map/ppermute | solution.py:266
  7.0 10.0 %collective-permute-start.2 = (bf16[8,64,128]{2,1,0:T(8,128)(2,1)S(1)}, bf16[8,64,128]{2,1,0:T(8,128)(2,1)S(1)}, u32[]{:S(2)}, u32[]{:S(2)}) collective-permute-start(bf16[8,64,128]{2,1,0:T(8,128)(2,1)S(1)} %get-tuple-element.13), channel_id=1, source_target_pairs={{0,24},{8,0},{16,8},{24,16},{1,25},{9,1},{17,9},{25,17},{2,26},{10... | collective-permute-start | bytes 393224 | tf_op jit(solution)/shard_map/ppermute | solution.py:266
  15.2 0.7 %copy-start.2 = (s32[4]{0:T(128)S(1)}, s32[4]{0:T(128)}, u32[]{:S(2)}) copy-start(s32[4]{0:T(128)} %param.4) | copy-start | bytes 52

commit v17 on v16

--- a/solution.py
+++ b/solution.py
@@ -38,7 +38,11 @@
     return high, (value - high.astype(jnp.float32)).astype(jnp.bfloat16)
 
 
-def table_kernel(groups, bins, freq_dev, position_ref, far_ref, place_ref, lag_ref, shift_ref):
+def copy_kernel(in_ref, out_ref):
+    out_ref[...] = in_ref[...]
+
+
+def table_kernel(groups, bins, freq_dev, position_ref, place_ref, lag_ref, shift_ref):
     low_rows = lax.broadcasted_iota(jnp.int32, (8, SLOWNESS), 0)
     high_rows = lax.broadcasted_iota(jnp.int32, (BLOCK // 8, SLOWNESS), 0) * 8
     shift_rows = lax.broadcasted_iota(jnp.int32, (2 * groups, SLOWNESS), 0)
@@ -257,13 +261,21 @@
             name="chunks_of_bins",
         )(whole, *earlier)
 
-    far = groups // 2
-    order = [far] + [distance for distance in range(1, groups) if distance != far] + [0]
-    (far_chunk,) = cut(order[:1])
-    chunks = dict(zip(order, (far_chunk, *cut(order[1:], far_chunk))))
+    order = list(range(1, groups)) + [0]
+    (first_chunk,) = cut(order[:1])
+    chunks = dict(zip(order, (first_chunk, *cut(order[1:], first_chunk))))
     for distance in order[:-1]:
         pairs = [(source, (source + distance) % groups) for source in range(groups)]
         chunks[distance] = lax.ppermute(chunks[distance], "chan", pairs)
+    first = order[0]
+    chunks[first] = pl.pallas_call(
+        copy_kernel,
+        out_shape=jax.ShapeDtypeStruct((bins, rows, BLOCK), jnp.bfloat16),
+        in_specs=[vmem],
+        out_specs=vmem,
+        compiler_params=params,
+        name="first_arrived",
+    )(chunks[first])
     places, lag_table, shift_table = pl.pallas_call(
         functools.partial(table_kernel, groups, bins, freq_dev),
         out_shape=(
@@ -271,12 +283,12 @@
             jax.ShapeDtypeStruct((bins, 2 * BLOCK, 2 * SLOWNESS), jnp.bfloat16),
             jax.ShapeDtypeStruct((bins, 2, 2 * groups, SLOWNESS), jnp.float32),
         ),
-        in_specs=[vmem, anywhere],
+        in_specs=[vmem],
         out_specs=(vmem, vmem, vmem),
         compiler_params=params,
         cost_estimate=pl.CostEstimate(flops=10**7, bytes_accessed=4 * 10**6, transcendentals=0),
         name="slant_tables",
-    )(block_position.reshape(1, groups), chunks[far])
+    )(block_position.reshape(1, groups))
     terms = pl.pallas_call(
         functools.partial(stack_kernel, groups, bins, parts),
         out_shape=jax.ShapeDtypeStruct((groups, parts, message_rows, BLOCK), jnp.float32),

time: 32.3 us -> 32.3 us (level)
  blocking collectives: 12.2 us -> 13.8 us
  starting transfers between devices: 7.98 us -> 7.08 us
  waiting for transfers between devices: 5.93 us -> 5.19 us
    all_to_all x1, blocking collectives: 12.2 us -> 13.8 us  [shards(): lax.all_to_all(terms, ('chan', 'freq'), split_axis=0, concat_axis=0, tile...]
    ppermute x3, starting transfers between devices: 7.98 us -> 7.08 us  [shards(): chunks[distance] = lax.ppermute(chunks[distance], 'chan', pairs)]
    ppermute x3, waiting for transfers between devices: 5.93 us -> 5.19 us  [shards(): chunks[distance] = lax.ppermute(chunks[distance], 'chan', pairs)]
  transfers between devices with their start and end apart: 3 -> 3, of which waited for: 1 -> 2; matrix products, arithmetic and copies ran while one was open for 0% -> 0% of each run, Pallas kernels for 4% -> 4%
where the time goes in v17:
time: 32.3 us; the launch traced here: 32.1 us
  blocking collectives  13.8 us (43%)
  starting transfers between devices  7.08 us (22%)
  waiting for transfers between devices  5.19 us (16%)
  Pallas kernels  4.3 us (13%)
  local copies, waits for them, and re-layouts  1.7 us (5%)
    all_to_all x1, blocking collectives, shards(): lax.all_to_all(terms, ('chan', 'freq'), split_axis=0, concat_axis=0, tile...  13.8 us
    ppermute x3, starting transfers between devices, shards(): chunks[distance] = lax.ppermute(chunks[distance], 'chan', pairs)  7.08 us
    ppermute x3, waiting for transfers between devices, shards(): chunks[distance] = lax.ppermute(chunks[distance], 'chan', pairs)  5.19 us
    pallas_call x1, Pallas kernels, shards(): pl.pallas_call(functools.partial(stack_kernel, groups, bins, parts), out_...  1.98 us
    unnamed x6, local copies, waits for them, and re-layouts  1.7 us
    pallas_call x1, Pallas kernels, shards(): pl.pallas_call(functools.partial(table_kernel, groups, bins, freq_dev), o...  1.19 us
    pallas_call x1, Pallas kernels, shards(): pl.pallas_call(functools.partial(image_kernel, slow_dev, spans), out_shap...  0.88 us
  transfers between devices with their start and end apart: 3, of which 2 were waited for; matrix products, arithmetic and copies ran while one was open for 0% of the time, Pallas kernels for 4%

profile of v17, /device:TPU:0, one launch (start us, length us, event | category | flops | bytes accessed | tf_op | source)
XLA Modules:
  0.0 32.1 jit_solution(12469630446400200746)
XLA Ops:
  0.0 0.0 copy-start
  0.0 1.0 %copy-done = bf16[2,32,32,128]{3,2,1,0:T(8,128)(2,1)S(1)} copy-done((bf16[2,32,32,128]{3,2,1,0:T(8,128)(2,1)S(1)}, bf16[2,32,32,128]{3,2,1,0:T(8,128)(2,1)}, u32[]{:S(2)}) %copy-start) | copy-done | bytes 524312
  1.0 0.1 chunks_of_bins.2.refs_0_
  1.1 0.0 copy-start.1
  1.1 3.1 %collective-permute-start = (bf16[8,64,128]{2,1,0:T(8,128)(2,1)S(1)}, bf16[8,64,128]{2,1,0:T(8,128)(2,1)S(1)}, u32[]{:S(2)}, u32[]{:S(2)}) collective-permute-start(bf16[8,64,128]{2,1,0:T(8,128)(2,1)S(1)} %chunks_of_bins.2.refs_0_), channel_id=1, source_target_pairs={{0,8},{8,16},{16,24},{24,0},{1,9},{9,17},{17,25},{25,1},{2,10},{10... | collective-permute-start | bytes 393224 | tf_op jit(solution)/shard_map/ppermute | solution.py:269
  4.2 0.2 chunks_of_bins.3
  4.4 2.7 %collective-permute-start.1 = (bf16[8,64,128]{2,1,0:T(8,128)(2,1)S(1)}, bf16[8,64,128]{2,1,0:T(8,128)(2,1)S(1)}, u32[]{:S(2)}, u32[]{:S(2)}) collective-permute-start(bf16[8,64,128]{2,1,0:T(8,128)(2,1)S(1)} %get-tuple-element.12), channel_id=1, source_target_pairs={{0,16},{8,24},{16,0},{24,8},{1,17},{9,25},{17,1},{25,9},{2,18},{10... | collective-permute-start | bytes 393224 | tf_op jit(solution)/shard_map/ppermute | solution.py:269
  7.0 1.3 %collective-permute-start.2 = (bf16[8,64,128]{2,1,0:T(8,128)(2,1)S(1)}, bf16[8,64,128]{2,1,0:T(8,128)(2,1)S(1)}, u32[]{:S(2)}, u32[]{:S(2)}) collective-permute-start(bf16[8,64,128]{2,1,0:T(8,128)(2,1)S(1)} %get-tuple-element.13), channel_id=1, source_target_pairs={{0,24},{8,0},{16,8},{24,16},{1,25},{9,1},{17,9},{25,17},{2,26},{10... | collective-permute-start | bytes 393224 | tf_op jit(solution)/shard_map/ppermute | solution.py:269
  8.4 0.0 copy-start.2
  8.4 0.7 %copy-done.2 = s32[4]{0:T(128)S(1)} copy-done((s32[4]{0:T(128)S(1)}, s32[4]{0:T(128)}, u32[]{:S(2)}) %copy-start.2) | copy-done | bytes 40
  9.0 1.2 %slant_tables.1 = (s32[4,128]{1,0:T(4,128)S(1)}, bf16[8,256,512]{2,1,0:T(8,128)(2,1)S(1)}, f32[8,2,8,256]{3,2,1,0:T(8,128)S(1)}) custom-call(s32[1,4]{1,0:T(1,128)S(1)} %bitcast.6), custom_call_target="tpu_custom_call" | custom-call | flops 10000000 | bytes 4000000 | tf_op jit(solution)/shard_map/slant_tables/pallas_call | solution.py:279
  10.2 0.4 %collective-permute-done.in_ref = bf16[8,64,128]{2,1,0:T(8,128)(2,1)S(1)} collective-permute-done((bf16[8,64,128]{2,1,0:T(8,128)(2,1)S(1)}, bf16[8,64,128]{2,1,0:T(8,128)(2,1)S(1)}, u32[]{:S(2)}, u32[]{:S(2)}) %collective-permute-start) | collective-permute-done | bytes 131104 | tf_op jit(solution)/shard_map/ppermute | solution.py:269
  10.7 4.8 %collective-permute-done.1.refs_2_ = bf16[8,64,128]{2,1,0:T(8,128)(2,1)S(1)} collective-permute-done((bf16[8,64,128]{2,1,0:T(8,128)(2,1)S(1)}, bf16[8,64,128]{2,1,0:T(8,128)(2,1)S(1)}, u32[]{:S(2)}, u32[]{:S(2)}) %collective-permute-start.1) | collective-permute-done | bytes 131104 | tf_op jit(solution)/shard_map/ppermute | solution.py:269
  15.4 0.0 collective-permute-done.2.refs_3_
  15.4 2.0 %stack_and_slant.1 = f32[4,8,4,128]{3,2,1,0:T(4,128)S(1)} custom-call(bf16[8,64,128]{2,1,0:T(8,128)(2,1)S(1)} %get-tuple-element.11.refs_0_, bf16[8,64,128]{2,1,0:T(8,128)(2,1)S(1)} %first_arrived.1.refs_1_, bf16[8,64,128]{2,1,0:T(8,128)(2,1)S(1)} %collective-permute-done.1.refs_2_, bf16[8,64,128]{2,1,0:T(8,128)(2,1)S(1)} %collective-permute-done.2.refs_3_, ...), custom_call_target="tpu_custom_call" | custom-call | tf_op jit(solution)/shard_map/stack_and_slant/pallas_call | solution.py:292
  17.4 13.8 %all_to_all.5.term_ref = f32[32,4,128]{2,1,0:T(4,128)S(1)} all-to-all(f32[32,4,128]{2,1,0:T(4,128)S(1)} %bitcast.5), channel_id=1, replica_groups=mesh['chan'=4,'freq'=8] {'chan','freq'}, dimensions={0} | all-to-all | bytes 131072 | tf_op jit(solution)/shard_map/all_to_all | solution.py:311
  31.2 0.0 copy-done.1
  31.2 0.9 %sum_of_bins.1 = f32[1,32,512]{2,1,0:T(8,128)} custom-call(f32[32,4,128]{2,1,0:T(4,128)S(1)} %all_to_all.5.term_ref, bf16[2,2,256,256]{3,2,1,0:T(8,128)(2,1)S(1)} %copy-done.1), custom_call_target="tpu_custom_call" | custom-call | tf_op jit(solution)/shard_map/sum_of_bins/pallas_call | solution.py:313
  (1 shorter events, 0.0 us)
Async XLA Ops:
  0.0 1.0 %copy-start = (bf16[2,32,32,128]{3,2,1,0:T(8,128)(2,1)S(1)}, bf16[2,32,32,128]{3,2,1,0:T(8,128)(2,1)}, u32[]{:S(2)}) copy-start(bf16[2,32,32,128]{3,2,1,0:T(8,128)(2,1)} %param.3) | copy-start | bytes 1572868
  1.1 30.1 %copy-start.1 = (bf16[2,2,256,256]{3,2,1,0:T(8,128)(2,1)S(1)}, bf16[2,2,256,256]{3,2,1,0:T(8,128)(2,1)}, u32[]{:S(2)}) copy-start(bf16[2,2,256,256]{3,2,1,0:T(8,128)(2,1)} %constant.2.clone.table_ref) | copy-start | bytes 1572868
  1.1 9.5 %collective-permute-start = (bf16[8,64,128]{2,1,0:T(8,128)(2,1)S(1)}, bf16[8,64,128]{2,1,0:T(8,128)(2,1)S(1)}, u32[]{:S(2)}, u32[]{:S(2)}) collective-permute-start(bf16[8,64,128]{2,1,0:T(8,128)(2,1)S(1)} %chunks_of_bins.2.refs_0_), channel_id=1, source_target_pairs={{0,8},{8,16},{16,24},{24,0},{1,9},{9,17},{17,25},{25,1},{2,10},{10... | collective-permute-start | bytes 393224 | tf_op jit(solution)/shard_map/ppermute | solution.py:269
  4.4 11.0 %collective-permute-start.1 = (bf16[8,64,128]{2,1,0:T(8,128)(2,1)S(1)}, bf16[8,64,128]{2,1,0:T(8,128)(2,1)S(1)}, u32[]{:S(2)}, u32[]{:S(2)}) collective-permute-start(bf16[8,64,128]{2,1,0:T(8,128)(2,1)S(1)} %get-tuple-element.12), channel_id=1, source_target_pairs={{0,16},{8,24},{16,0},{24,8},{1,17},{9,25},{17,1},{25,9},{2,18},{10... | collective-permute-start | bytes 393224 | tf_op jit(solution)/shard_map/ppermute | solution.py:269
  7.0 8.4 %collective-permute-start.2 = (bf16[8,64,128]{2,1,0:T(8,128)(2,1)S(1)}, bf16[8,64,128]{2,1,0:T(8,128)(2,1)S(1)}, u32[]{:S(2)}, u32[]{:S(2)}) collective-permute-start(bf16[8,64,128]{2,1,0:T(8,128)(2,1)S(1)} %get-tuple-element.13), channel_id=1, source_target_pairs={{0,24},{8,0},{16,8},{24,16},{1,25},{9,1},{17,9},{25,17},{2,26},{10... | collective-permute-start | bytes 393224 | tf_op jit(solution)/shard_map/ppermute | solution.py:269
  8.4 0.7 %copy-start.2 = (s32[4]{0:T(128)S(1)}, s32[4]{0:T(128)}, u32[]{:S(2)}) copy-start(s32[4]{0:T(128)} %param.4) | copy-start | bytes 52

commit v18 on v17

--- a/solution.py
+++ b/solution.py
@@ -105,7 +105,7 @@
 
 def stack_kernel(groups, bins, parts, *refs):
     chunk_refs = refs[:groups]
-    place_ref, lag_ref, shift_ref, out_ref, placed_ref, left_ref, part_ref = refs[groups:]
+    place_ref, lag_ref, shift_ref, out_ref, placed_ref, *part_refs = refs[groups:]
     rows = placed_ref.shape[2]
     windows = rows // 2
     places = place_ref[...]
@@ -115,17 +115,20 @@
     row_index = lax.broadcasted_iota(jnp.int32, (BLOCK, BLOCK), 0)
     lag_index = lax.broadcasted_iota(jnp.int32, (BLOCK, BLOCK), 1)
     mirror = jnp.where(row_index + lag_index == BLOCK - 1, 1.0, 0.0).astype(jnp.bfloat16)
-    ahead = lag_index <= row_index
-
-    for f in range(bins):
-        left_ref[f] = lax.dot_general(
+    behind = (lag_index - row_index)[:8]
+
+    weight = stack_weights(groups)
+    lefts, lags = {}, {}
+
+    def turn(f):
+        lefts[f] = lax.dot_general(
             mirror,
             placed_ref[:, f].reshape(groups * rows, BLOCK),
             (((1,), (1,)), ((), ())),
             preferred_element_type=jnp.float32,
         ).astype(jnp.bfloat16)
 
-    for f in range(bins):
+    def correlate(f):
         right = []
         for place in range(groups):
             value = placed_ref[place, f]
@@ -138,31 +141,32 @@
         right = jnp.concatenate(right, 0)
         for delta in range(groups):
             panel = jnp.dot(
-                left_ref[f, :, : rows * (groups - delta)],
+                lefts[f][:, : rows * (groups - delta)],
                 right[rows * delta :],
                 preferred_element_type=jnp.float32,
             )
             for half in range(2):
                 lanes = slice(half * BLOCK, (half + 1) * BLOCK)
                 skewed = pltpu.roll(panel[:, lanes], 1, 1, stride=1, stride_axis=0)
-                forward = jnp.where(ahead, skewed, 0.0).reshape(-1, 8, BLOCK).sum(0)
-                backward = jnp.where(ahead, 0.0, skewed).reshape(-1, 8, BLOCK).sum(0)
-                first = (f * 2 * groups + delta) * 8
-                part_ref[half, first : first + 8] = forward
-                part_ref[half, first + groups * 8 : first + groups * 8 + 8] = backward
-
-    lags = []
-    for half in range(2):
-        summed = part_ref[half, pl.ds(0, bins * 2 * groups, stride=8), :]
-        for sublane in range(1, 8):
-            summed = summed + part_ref[half, pl.ds(sublane, bins * 2 * groups, stride=8), :]
-        lags.append(summed)
-    weight = stack_weights(groups)
+                total = skewed[:8]
+                backward = jnp.where(behind > 0, total, 0.0)
+                for row in range(8, BLOCK, 8):
+                    total = total + skewed[row : row + 8]
+                    backward = jnp.where(behind > row, total, backward)
+                part_refs[f][half, delta * 8 : delta * 8 + 8] = total - backward
+                first = (groups + delta) * 8
+                part_refs[f][half, first : first + 8] = backward
+        lags[f] = []
+        for half in range(2):
+            summed = part_refs[f][half, pl.ds(0, 2 * groups, stride=8), :]
+            for sublane in range(1, 8):
+                summed = summed + part_refs[f][half, pl.ds(sublane, 2 * groups, stride=8), :]
+            lags[f].append(summed)
 
     terms = []
-    for f in range(bins):
-        lag_rows = slice(f * 2 * groups, (f + 1) * 2 * groups)
-        means = jnp.concatenate([half[lag_rows] * weight for half in lags], 0)
+
+    def slant(f):
+        means = jnp.concatenate([half * weight for half in lags[f]], 0)
         mean_high, mean_low = halves(means)
         spread = jnp.concatenate(
             [
@@ -182,23 +186,38 @@
         terms.append(turned_re[:groups] + turned_re[groups:])
         terms.append(turned_im[:groups] + turned_im[groups:])
 
+    turn(0)
+    for f in range(bins):
+        if f + 1 < bins:
+            turn(f + 1)
+        correlate(f)
+        if f:
+            slant(f - 1)
+    slant(bins - 1)
+
     slow_dev = SLOWNESS // parts
     spans = BLOCK // slow_dev
+    count = min(spans, len(terms))
     span_index = lax.broadcasted_iota(jnp.int32, (groups, BLOCK), 1) // slow_dev
-    for part in range(parts):
-        source = (part % spans) * slow_dev
-        lanes = slice(part // spans * BLOCK, (part // spans + 1) * BLOCK)
-        for row in range(out_ref.shape[2]):
-            packed = jnp.zeros((groups, BLOCK), jnp.float32)
-            for span, term in enumerate(terms[row * spans : (row + 1) * spans]):
-                moved = pltpu.roll(term[:, lanes], (span * slow_dev - source) % BLOCK, 1)
-                packed = jnp.where(span_index == span, moved, packed)
-            out_ref[:, part, row, :] = packed
+    for row in range(out_ref.shape[2]):
+        for half in range(SLOWNESS // BLOCK):
+            lanes = slice(half * BLOCK, (half + 1) * BLOCK)
+            moved = [
+                pltpu.roll(term[:, lanes], span * slow_dev, 1) if span else term[:, lanes]
+                for span, term in enumerate(terms[row * count : (row + 1) * count])
+            ]
+            for part in range(spans):
+                packed = jnp.zeros((groups, BLOCK), jnp.float32)
+                for span, value in enumerate(moved):
+                    packed = jnp.where(span_index == (span + part) % spans, value, packed)
+                out_ref[:, half * spans + part, row, :] = packed
 
 
 def image_kernel(slow_dev, spans, term_ref, table_ref, out_ref):
-    arrived = term_ref[...]
-    turned = arrived.reshape(-1, BLOCK).T
+    count = BLOCK // slow_dev
+    back = count - lax.rem(lax.axis_index("freq"), count)
+    arrived = pltpu.roll(term_ref[...].reshape(-1, BLOCK), back * slow_dev, 1)
+    turned = arrived.T
     sums = []
     for odd, chosen in enumerate(spans):
         terms = jnp.concatenate(
@@ -296,9 +315,8 @@
         out_specs=vmem,
         scratch_shapes=[
             pltpu.VMEM((groups, bins, rows, BLOCK), jnp.bfloat16),
-            pltpu.VMEM((bins, BLOCK, groups * rows), jnp.bfloat16),
-            pltpu.VMEM((2, bins * 2 * groups * 8, BLOCK), jnp.float32),
-        ],
+        ]
+        + [pltpu.VMEM((2, 2 * groups * 8, BLOCK), jnp.float32)] * bins,
         compiler_params=params,
         name="stack_and_slant",
     )(

time: 32.3 us -> 32.8 us (1.015)
  Pallas kernels: 4.3 us -> 4.77 us
    pallas_call x1, Pallas kernels: 1.98 us -> 2.37 us  [shards(): pl.pallas_call(functools.partial(stack_kernel, groups, bins, parts), out_...]
where the time goes in v18:
time: 32.8 us; the launch traced here: 32.6 us
  blocking collectives  13.8 us (42%)
  starting transfers between devices  7.08 us (22%)
  waiting for transfers between devices  5.19 us (16%)
  Pallas kernels  4.77 us (15%)
  local copies, waits for them, and re-layouts  1.7 us (5%)
    all_to_all x1, blocking collectives, shards(): lax.all_to_all(terms, ('chan', 'freq'), split_axis=0, concat_axis=0, tile...  13.8 us
    ppermute x3, starting transfers between devices, shards(): chunks[distance] = lax.ppermute(chunks[distance], 'chan', pairs)  7.08 us
    ppermute x3, waiting for transfers between devices, shards(): chunks[distance] = lax.ppermute(chunks[distance], 'chan', pairs)  5.19 us
    pallas_call x1, Pallas kernels, shards(): pl.pallas_call(functools.partial(stack_kernel, groups, bins, parts), out_...  2.37 us
    unnamed x6, local copies, waits for them, and re-layouts  1.7 us
    pallas_call x1, Pallas kernels, shards(): pl.pallas_call(functools.partial(table_kernel, groups, bins, freq_dev), o...  1.19 us
    pallas_call x1, Pallas kernels, shards(): pl.pallas_call(functools.partial(image_kernel, slow_dev, spans), out_shap...  0.95 us
  transfers between devices with their start and end apart: 3, of which 2 were waited for; matrix products, arithmetic and copies ran while one was open for 0% of the time, Pallas kernels for 4%

profile of v18, /device:TPU:0, one launch (start us, length us, event | category | flops | bytes accessed | tf_op | source)
XLA Modules:
  0.0 32.6 jit_solution(10423776372416724449)
XLA Ops:
  0.0 0.0 copy-start
  0.0 1.0 %copy-done = bf16[2,32,32,128]{3,2,1,0:T(8,128)(2,1)S(1)} copy-done((bf16[2,32,32,128]{3,2,1,0:T(8,128)(2,1)S(1)}, bf16[2,32,32,128]{3,2,1,0:T(8,128)(2,1)}, u32[]{:S(2)}) %copy-start) | copy-done | bytes 524312
  1.0 0.1 chunks_of_bins.2.refs_0_
  1.1 0.0 copy-start.1
  1.1 3.1 %collective-permute-start = (bf16[8,64,128]{2,1,0:T(8,128)(2,1)S(1)}, bf16[8,64,128]{2,1,0:T(8,128)(2,1)S(1)}, u32[]{:S(2)}, u32[]{:S(2)}) collective-permute-start(bf16[8,64,128]{2,1,0:T(8,128)(2,1)S(1)} %chunks_of_bins.2.refs_0_), channel_id=1, source_target_pairs={{0,8},{8,16},{16,24},{24,0},{1,9},{9,17},{17,25},{25,1},{2,10},{10... | collective-permute-start | bytes 393224 | tf_op jit(solution)/shard_map/ppermute | solution.py:288
  4.2 0.2 chunks_of_bins.3
  4.4 2.7 %collective-permute-start.1 = (bf16[8,64,128]{2,1,0:T(8,128)(2,1)S(1)}, bf16[8,64,128]{2,1,0:T(8,128)(2,1)S(1)}, u32[]{:S(2)}, u32[]{:S(2)}) collective-permute-start(bf16[8,64,128]{2,1,0:T(8,128)(2,1)S(1)} %get-tuple-element.12), channel_id=1, source_target_pairs={{0,16},{8,24},{16,0},{24,8},{1,17},{9,25},{17,1},{25,9},{2,18},{10... | collective-permute-start | bytes 393224 | tf_op jit(solution)/shard_map/ppermute | solution.py:288
  7.0 1.3 %collective-permute-start.2 = (bf16[8,64,128]{2,1,0:T(8,128)(2,1)S(1)}, bf16[8,64,128]{2,1,0:T(8,128)(2,1)S(1)}, u32[]{:S(2)}, u32[]{:S(2)}) collective-permute-start(bf16[8,64,128]{2,1,0:T(8,128)(2,1)S(1)} %get-tuple-element.13), channel_id=1, source_target_pairs={{0,24},{8,0},{16,8},{24,16},{1,25},{9,1},{17,9},{25,17},{2,26},{10... | collective-permute-start | bytes 393224 | tf_op jit(solution)/shard_map/ppermute | solution.py:288
  8.4 0.0 copy-start.2
  8.4 0.7 %copy-done.2 = s32[4]{0:T(128)S(1)} copy-done((s32[4]{0:T(128)S(1)}, s32[4]{0:T(128)}, u32[]{:S(2)}) %copy-start.2) | copy-done | bytes 40
  9.0 1.2 %slant_tables.1 = (s32[4,128]{1,0:T(4,128)S(1)}, bf16[8,256,512]{2,1,0:T(8,128)(2,1)S(1)}, f32[8,2,8,256]{3,2,1,0:T(8,128)S(1)}) custom-call(s32[1,4]{1,0:T(1,128)S(1)} %bitcast.6), custom_call_target="tpu_custom_call" | custom-call | flops 10000000 | bytes 4000000 | tf_op jit(solution)/shard_map/slant_tables/pallas_call | solution.py:298
  10.2 0.4 %collective-permute-done.in_ref = bf16[8,64,128]{2,1,0:T(8,128)(2,1)S(1)} collective-permute-done((bf16[8,64,128]{2,1,0:T(8,128)(2,1)S(1)}, bf16[8,64,128]{2,1,0:T(8,128)(2,1)S(1)}, u32[]{:S(2)}, u32[]{:S(2)}) %collective-permute-start) | collective-permute-done | bytes 131104 | tf_op jit(solution)/shard_map/ppermute | solution.py:288
  10.7 4.8 %collective-permute-done.1.refs_2_ = bf16[8,64,128]{2,1,0:T(8,128)(2,1)S(1)} collective-permute-done((bf16[8,64,128]{2,1,0:T(8,128)(2,1)S(1)}, bf16[8,64,128]{2,1,0:T(8,128)(2,1)S(1)}, u32[]{:S(2)}, u32[]{:S(2)}) %collective-permute-start.1) | collective-permute-done | bytes 131104 | tf_op jit(solution)/shard_map/ppermute | solution.py:288
  15.4 0.0 collective-permute-done.2.refs_3_
  15.4 2.4 %stack_and_slant.1 = f32[4,8,4,128]{3,2,1,0:T(4,128)S(1)} custom-call(bf16[8,64,128]{2,1,0:T(8,128)(2,1)S(1)} %get-tuple-element.11.refs_0_, bf16[8,64,128]{2,1,0:T(8,128)(2,1)S(1)} %first_arrived.1.refs_1_, bf16[8,64,128]{2,1,0:T(8,128)(2,1)S(1)} %collective-permute-done.1.refs_2_, bf16[8,64,128]{2,1,0:T(8,128)(2,1)S(1)} %collective-permute-done.2.refs_3_, ...), custom_call_target="tpu_custom_call" | custom-call | tf_op jit(solution)/shard_map/stack_and_slant/pallas_call | solution.py:311
  17.8 13.8 %all_to_all.5.term_ref = f32[32,4,128]{2,1,0:T(4,128)S(1)} all-to-all(f32[32,4,128]{2,1,0:T(4,128)S(1)} %bitcast.5), channel_id=1, replica_groups=mesh['chan'=4,'freq'=8] {'chan','freq'}, dimensions={0} | all-to-all | bytes 131072 | tf_op jit(solution)/shard_map/all_to_all | solution.py:329
  31.6 0.0 copy-done.1
  31.6 1.0 %sum_of_bins.1 = f32[1,32,512]{2,1,0:T(8,128)} custom-call(f32[32,4,128]{2,1,0:T(4,128)S(1)} %all_to_all.5.term_ref, bf16[2,2,256,256]{3,2,1,0:T(8,128)(2,1)S(1)} %copy-done.1), custom_call_target="tpu_custom_call" | custom-call | tf_op jit(solution)/shard_map/sum_of_bins/pallas_call | solution.py:331
  (1 shorter events, 0.0 us)
Async XLA Ops:
  0.0 1.0 %copy-start = (bf16[2,32,32,128]{3,2,1,0:T(8,128)(2,1)S(1)}, bf16[2,32,32,128]{3,2,1,0:T(8,128)(2,1)}, u32[]{:S(2)}) copy-start(bf16[2,32,32,128]{3,2,1,0:T(8,128)(2,1)} %param.3) | copy-start | bytes 1572868
  1.1 30.5 %copy-start.1 = (bf16[2,2,256,256]{3,2,1,0:T(8,128)(2,1)S(1)}, bf16[2,2,256,256]{3,2,1,0:T(8,128)(2,1)}, u32[]{:S(2)}) copy-start(bf16[2,2,256,256]{3,2,1,0:T(8,128)(2,1)} %constant.2.clone.table_ref) | copy-start | bytes 1572868
  1.1 9.5 %collective-permute-start = (bf16[8,64,128]{2,1,0:T(8,128)(2,1)S(1)}, bf16[8,64,128]{2,1,0:T(8,128)(2,1)S(1)}, u32[]{:S(2)}, u32[]{:S(2)}) collective-permute-start(bf16[8,64,128]{2,1,0:T(8,128)(2,1)S(1)} %chunks_of_bins.2.refs_0_), channel_id=1, source_target_pairs={{0,8},{8,16},{16,24},{24,0},{1,9},{9,17},{17,25},{25,1},{2,10},{10... | collective-permute-start | bytes 393224 | tf_op jit(solution)/shard_map/ppermute | solution.py:288
  4.4 11.0 %collective-permute-start.1 = (bf16[8,64,128]{2,1,0:T(8,128)(2,1)S(1)}, bf16[8,64,128]{2,1,0:T(8,128)(2,1)S(1)}, u32[]{:S(2)}, u32[]{:S(2)}) collective-permute-start(bf16[8,64,128]{2,1,0:T(8,128)(2,1)S(1)} %get-tuple-element.12), channel_id=1, source_target_pairs={{0,16},{8,24},{16,0},{24,8},{1,17},{9,25},{17,1},{25,9},{2,18},{10... | collective-permute-start | bytes 393224 | tf_op jit(solution)/shard_map/ppermute | solution.py:288
  7.0 8.4 %collective-permute-start.2 = (bf16[8,64,128]{2,1,0:T(8,128)(2,1)S(1)}, bf16[8,64,128]{2,1,0:T(8,128)(2,1)S(1)}, u32[]{:S(2)}, u32[]{:S(2)}) collective-permute-start(bf16[8,64,128]{2,1,0:T(8,128)(2,1)S(1)} %get-tuple-element.13), channel_id=1, source_target_pairs={{0,24},{8,0},{16,8},{24,16},{1,25},{9,1},{17,9},{25,17},{2,26},{10... | collective-permute-start | bytes 393224 | tf_op jit(solution)/shard_map/ppermute | solution.py:288
  8.4 0.7 %copy-start.2 = (s32[4]{0:T(128)S(1)}, s32[4]{0:T(128)}, u32[]{:S(2)}) copy-start(s32[4]{0:T(128)} %param.4) | copy-start | bytes 52

commit v19 on v17

--- a/solution.py
+++ b/solution.py
@@ -193,7 +193,8 @@
             for span, term in enumerate(terms[row * spans : (row + 1) * spans]):
                 moved = pltpu.roll(term[:, lanes], (span * slow_dev - source) % BLOCK, 1)
                 packed = jnp.where(span_index == span, moved, packed)
-            out_ref[:, part, row, :] = packed
+            for delta in range(groups):
+                out_ref[groups - 1 - delta, parts - 1 - part, row] = packed[delta]
 
 
 def image_kernel(slow_dev, spans, term_ref, table_ref, out_ref):
@@ -221,7 +222,11 @@
     tables = []
     for chosen in spans:
         span, group, part, row = np.meshgrid(
-            chosen, np.arange(groups), np.arange(parts), np.arange(message_rows), indexing="ij"
+            chosen,
+            np.arange(groups)[::-1],
+            np.arange(parts)[::-1],
+            np.arange(message_rows),
+            indexing="ij",
         )
         entry = row * count + span
         freq = (part * groups + group) * bins + entry // 2
@@ -308,7 +313,14 @@
         shift_table,
     )
     terms = terms.reshape(groups * parts, message_rows, BLOCK)
-    arrived = lax.all_to_all(terms, ("chan", "freq"), split_axis=0, concat_axis=0, tiled=True)
+    arrived = lax.all_to_all(
+        terms,
+        ("chan", "freq"),
+        split_axis=0,
+        concat_axis=0,
+        axis_index_groups=[list(range(groups * parts))[::-1]],
+        tiled=True,
+    )
     spans, table = time_table(groups, parts, bins, slow_dev, message_rows)
     return pl.pallas_call(
         functools.partial(image_kernel, slow_dev, spans),

time: 32.3 us -> 32.2 us (level)
  no operation moved by 1% of the time
where the time goes in v19:
time: 32.2 us; the launch traced here: 32 us
  blocking collectives  13.7 us (43%)
  starting transfers between devices  7.08 us (22%)
  waiting for transfers between devices  5.19 us (16%)
  Pallas kernels  4.3 us (13%)
  local copies, waits for them, and re-layouts  1.7 us (5%)
    all_to_all x1, blocking collectives, shards(): lax.all_to_all(terms, ('chan', 'freq'), split_axis=0, concat_axis=0, axis...  13.7 us
    ppermute x3, starting transfers between devices, shards(): chunks[distance] = lax.ppermute(chunks[distance], 'chan', pairs)  7.08 us
    ppermute x3, waiting for transfers between devices, shards(): chunks[distance] = lax.ppermute(chunks[distance], 'chan', pairs)  5.19 us
    pallas_call x1, Pallas kernels, shards(): pl.pallas_call(functools.partial(stack_kernel, groups, bins, parts), out_...  1.98 us
    unnamed x6, local copies, waits for them, and re-layouts  1.7 us
    pallas_call x1, Pallas kernels, shards(): pl.pallas_call(functools.partial(table_kernel, groups, bins, freq_dev), o...  1.19 us
    pallas_call x1, Pallas kernels, shards(): pl.pallas_call(functools.partial(image_kernel, slow_dev, spans), out_shap...  0.88 us
  transfers between devices with their start and end apart: 3, of which 2 were waited for; matrix products, arithmetic and copies ran while one was open for 0% of the time, Pallas kernels for 4%

profile of v19, /device:TPU:0, one launch (start us, length us, event | category | flops | bytes accessed | tf_op | source)
XLA Modules:
  0.0 32.0 jit_solution(7876336688625326175)
XLA Ops:
  0.0 0.0 copy-start
  0.0 1.0 %copy-done = bf16[2,32,32,128]{3,2,1,0:T(8,128)(2,1)S(1)} copy-done((bf16[2,32,32,128]{3,2,1,0:T(8,128)(2,1)S(1)}, bf16[2,32,32,128]{3,2,1,0:T(8,128)(2,1)}, u32[]{:S(2)}) %copy-start) | copy-done | bytes 524312
  1.0 0.1 chunks_of_bins.2.refs_0_
  1.1 0.0 copy-start.1
  1.1 3.1 %collective-permute-start = (bf16[8,64,128]{2,1,0:T(8,128)(2,1)S(1)}, bf16[8,64,128]{2,1,0:T(8,128)(2,1)S(1)}, u32[]{:S(2)}, u32[]{:S(2)}) collective-permute-start(bf16[8,64,128]{2,1,0:T(8,128)(2,1)S(1)} %chunks_of_bins.2.refs_0_), channel_id=1, source_target_pairs={{0,8},{8,16},{16,24},{24,0},{1,9},{9,17},{17,25},{25,1},{2,10},{10... | collective-permute-start | bytes 393224 | tf_op jit(solution)/shard_map/ppermute | solution.py:274
  4.2 0.2 chunks_of_bins.3
  4.4 2.7 %collective-permute-start.1 = (bf16[8,64,128]{2,1,0:T(8,128)(2,1)S(1)}, bf16[8,64,128]{2,1,0:T(8,128)(2,1)S(1)}, u32[]{:S(2)}, u32[]{:S(2)}) collective-permute-start(bf16[8,64,128]{2,1,0:T(8,128)(2,1)S(1)} %get-tuple-element.12), channel_id=1, source_target_pairs={{0,16},{8,24},{16,0},{24,8},{1,17},{9,25},{17,1},{25,9},{2,18},{10... | collective-permute-start | bytes 393224 | tf_op jit(solution)/shard_map/ppermute | solution.py:274
  7.0 1.3 %collective-permute-start.2 = (bf16[8,64,128]{2,1,0:T(8,128)(2,1)S(1)}, bf16[8,64,128]{2,1,0:T(8,128)(2,1)S(1)}, u32[]{:S(2)}, u32[]{:S(2)}) collective-permute-start(bf16[8,64,128]{2,1,0:T(8,128)(2,1)S(1)} %get-tuple-element.13), channel_id=1, source_target_pairs={{0,24},{8,0},{16,8},{24,16},{1,25},{9,1},{17,9},{25,17},{2,26},{10... | collective-permute-start | bytes 393224 | tf_op jit(solution)/shard_map/ppermute | solution.py:274
  8.4 0.0 copy-start.2
  8.4 0.7 %copy-done.2 = s32[4]{0:T(128)S(1)} copy-done((s32[4]{0:T(128)S(1)}, s32[4]{0:T(128)}, u32[]{:S(2)}) %copy-start.2) | copy-done | bytes 40
  9.0 1.2 %slant_tables.1 = (s32[4,128]{1,0:T(4,128)S(1)}, bf16[8,256,512]{2,1,0:T(8,128)(2,1)S(1)}, f32[8,2,8,256]{3,2,1,0:T(8,128)S(1)}) custom-call(s32[1,4]{1,0:T(1,128)S(1)} %bitcast.6), custom_call_target="tpu_custom_call" | custom-call | flops 10000000 | bytes 4000000 | tf_op jit(solution)/shard_map/slant_tables/pallas_call | solution.py:284
  10.2 0.4 %collective-permute-done.in_ref = bf16[8,64,128]{2,1,0:T(8,128)(2,1)S(1)} collective-permute-done((bf16[8,64,128]{2,1,0:T(8,128)(2,1)S(1)}, bf16[8,64,128]{2,1,0:T(8,128)(2,1)S(1)}, u32[]{:S(2)}, u32[]{:S(2)}) %collective-permute-start) | collective-permute-done | bytes 131104 | tf_op jit(solution)/shard_map/ppermute | solution.py:274
  10.7 4.8 %collective-permute-done.1.refs_2_ = bf16[8,64,128]{2,1,0:T(8,128)(2,1)S(1)} collective-permute-done((bf16[8,64,128]{2,1,0:T(8,128)(2,1)S(1)}, bf16[8,64,128]{2,1,0:T(8,128)(2,1)S(1)}, u32[]{:S(2)}, u32[]{:S(2)}) %collective-permute-start.1) | collective-permute-done | bytes 131104 | tf_op jit(solution)/shard_map/ppermute | solution.py:274
  15.4 0.0 collective-permute-done.2.refs_3_
  15.4 2.0 %stack_and_slant.1 = f32[4,8,4,128]{3,2,1,0:T(4,128)S(1)} custom-call(bf16[8,64,128]{2,1,0:T(8,128)(2,1)S(1)} %get-tuple-element.11.refs_0_, bf16[8,64,128]{2,1,0:T(8,128)(2,1)S(1)} %first_arrived.1.refs_1_, bf16[8,64,128]{2,1,0:T(8,128)(2,1)S(1)} %collective-permute-done.1.refs_2_, bf16[8,64,128]{2,1,0:T(8,128)(2,1)S(1)} %collective-permute-done.2.refs_3_, ...), custom_call_target="tpu_custom_call" | custom-call | tf_op jit(solution)/shard_map/stack_and_slant/pallas_call | solution.py:297
  17.4 13.7 %all_to_all.5.term_ref = f32[32,4,128]{2,1,0:T(4,128)S(1)} all-to-all(f32[32,4,128]{2,1,0:T(4,128)S(1)} %bitcast.5), channel_id=1, replica_groups={{31,30,29,28,27,26,25,24,23,22,21,20,19,18,17,16,15,14,13,12,11,10,9,8,..., dimensions={0} | all-to-all | bytes 131072 | tf_op jit(solution)/shard_map/all_to_all | solution.py:316
  31.1 0.0 copy-done.1
  31.1 0.9 %sum_of_bins.1 = f32[1,32,512]{2,1,0:T(8,128)} custom-call(f32[32,4,128]{2,1,0:T(4,128)S(1)} %all_to_all.5.term_ref, bf16[2,2,256,256]{3,2,1,0:T(8,128)(2,1)S(1)} %copy-done.1), custom_call_target="tpu_custom_call" | custom-call | tf_op jit(solution)/shard_map/sum_of_bins/pallas_call | solution.py:325
  (1 shorter events, 0.0 us)
Async XLA Ops:
  0.0 1.0 %copy-start = (bf16[2,32,32,128]{3,2,1,0:T(8,128)(2,1)S(1)}, bf16[2,32,32,128]{3,2,1,0:T(8,128)(2,1)}, u32[]{:S(2)}) copy-start(bf16[2,32,32,128]{3,2,1,0:T(8,128)(2,1)} %param.3) | copy-start | bytes 1572868
  1.1 30.0 %copy-start.1 = (bf16[2,2,256,256]{3,2,1,0:T(8,128)(2,1)S(1)}, bf16[2,2,256,256]{3,2,1,0:T(8,128)(2,1)}, u32[]{:S(2)}) copy-start(bf16[2,2,256,256]{3,2,1,0:T(8,128)(2,1)} %constant.2.clone.table_ref) | copy-start | bytes 1572868
  1.1 9.5 %collective-permute-start = (bf16[8,64,128]{2,1,0:T(8,128)(2,1)S(1)}, bf16[8,64,128]{2,1,0:T(8,128)(2,1)S(1)}, u32[]{:S(2)}, u32[]{:S(2)}) collective-permute-start(bf16[8,64,128]{2,1,0:T(8,128)(2,1)S(1)} %chunks_of_bins.2.refs_0_), channel_id=1, source_target_pairs={{0,8},{8,16},{16,24},{24,0},{1,9},{9,17},{17,25},{25,1},{2,10},{10... | collective-permute-start | bytes 393224 | tf_op jit(solution)/shard_map/ppermute | solution.py:274
  4.4 11.0 %collective-permute-start.1 = (bf16[8,64,128]{2,1,0:T(8,128)(2,1)S(1)}, bf16[8,64,128]{2,1,0:T(8,128)(2,1)S(1)}, u32[]{:S(2)}, u32[]{:S(2)}) collective-permute-start(bf16[8,64,128]{2,1,0:T(8,128)(2,1)S(1)} %get-tuple-element.12), channel_id=1, source_target_pairs={{0,16},{8,24},{16,0},{24,8},{1,17},{9,25},{17,1},{25,9},{2,18},{10... | collective-permute-start | bytes 393224 | tf_op jit(solution)/shard_map/ppermute | solution.py:274
  7.0 8.4 %collective-permute-start.2 = (bf16[8,64,128]{2,1,0:T(8,128)(2,1)S(1)}, bf16[8,64,128]{2,1,0:T(8,128)(2,1)S(1)}, u32[]{:S(2)}, u32[]{:S(2)}) collective-permute-start(bf16[8,64,128]{2,1,0:T(8,128)(2,1)S(1)} %get-tuple-element.13), channel_id=1, source_target_pairs={{0,24},{8,0},{16,8},{24,16},{1,25},{9,1},{17,9},{25,17},{2,26},{10... | collective-permute-start | bytes 393224 | tf_op jit(solution)/shard_map/ppermute | solution.py:274
  8.4 0.7 %copy-start.2 = (s32[4]{0:T(128)S(1)}, s32[4]{0:T(128)}, u32[]{:S(2)}) copy-start(s32[4]{0:T(128)} %param.4) | copy-start | bytes 52

commit v20 on v19

--- a/solution.py
+++ b/solution.py
@@ -105,50 +105,48 @@
 
 def stack_kernel(groups, bins, parts, *refs):
     chunk_refs = refs[:groups]
-    place_ref, lag_ref, shift_ref, out_ref, placed_ref, left_ref, part_ref = refs[groups:]
-    rows = placed_ref.shape[2]
+    place_ref, lag_ref, shift_ref, out_ref, right_ref, left_ref, part_ref = refs[groups:]
+    rows = right_ref.shape[1] // groups
     windows = rows // 2
     places = place_ref[...]
     for distance, chunk_ref in enumerate(chunk_refs):
-        placed_ref[places[distance, 0]] = chunk_ref[...]
+        here = pl.multiple_of(places[distance, 0] * rows, rows)
+        for f in range(bins):
+            value = chunk_ref[f]
+            right_ref[f, pl.ds(here, rows), :BLOCK] = value
+            turned = jnp.concatenate([value[windows:], -value[:windows]], 0)
+            right_ref[f, pl.ds(here, rows), BLOCK:] = turned
 
     row_index = lax.broadcasted_iota(jnp.int32, (BLOCK, BLOCK), 0)
     lag_index = lax.broadcasted_iota(jnp.int32, (BLOCK, BLOCK), 1)
     mirror = jnp.where(row_index + lag_index == BLOCK - 1, 1.0, 0.0).astype(jnp.bfloat16)
-    ahead = lag_index <= row_index
+    behind = (lag_index - row_index)[:8]
 
     for f in range(bins):
         left_ref[f] = lax.dot_general(
             mirror,
-            placed_ref[:, f].reshape(groups * rows, BLOCK),
+            right_ref[f, :, :BLOCK],
             (((1,), (1,)), ((), ())),
             preferred_element_type=jnp.float32,
         ).astype(jnp.bfloat16)
 
     for f in range(bins):
-        right = []
-        for place in range(groups):
-            value = placed_ref[place, f]
-            real, imag = value[:windows], value[windows:]
-            right.append(
-                jnp.concatenate(
-                    [jnp.concatenate([real, imag], 1), jnp.concatenate([imag, -real], 1)], 0
-                )
-            )
-        right = jnp.concatenate(right, 0)
         for delta in range(groups):
             panel = jnp.dot(
                 left_ref[f, :, : rows * (groups - delta)],
-                right[rows * delta :],
+                right_ref[f, rows * delta :],
                 preferred_element_type=jnp.float32,
             )
             for half in range(2):
                 lanes = slice(half * BLOCK, (half + 1) * BLOCK)
                 skewed = pltpu.roll(panel[:, lanes], 1, 1, stride=1, stride_axis=0)
-                forward = jnp.where(ahead, skewed, 0.0).reshape(-1, 8, BLOCK).sum(0)
-                backward = jnp.where(ahead, 0.0, skewed).reshape(-1, 8, BLOCK).sum(0)
+                total = skewed[:8]
+                backward = jnp.where(behind > 0, total, 0.0)
+                for row in range(8, BLOCK, 8):
+                    total = total + skewed[row : row + 8]
+                    backward = jnp.where(behind > row, total, backward)
                 first = (f * 2 * groups + delta) * 8
-                part_ref[half, first : first + 8] = forward
+                part_ref[half, first : first + 8] = total - backward
                 part_ref[half, first + groups * 8 : first + groups * 8 + 8] = backward
 
     lags = []
@@ -300,7 +298,7 @@
         in_specs=[vmem] * (groups + 3),
         out_specs=vmem,
         scratch_shapes=[
-            pltpu.VMEM((groups, bins, rows, BLOCK), jnp.bfloat16),
+            pltpu.VMEM((bins, groups * rows, 2 * BLOCK), jnp.bfloat16),
             pltpu.VMEM((bins, BLOCK, groups * rows), jnp.bfloat16),
             pltpu.VMEM((2, bins * 2 * groups * 8, BLOCK), jnp.float32),
         ],

time: 32.2 us -> 32.3 us (level)
  no operation moved by 1% of the time
where the time goes in v20:
time: 32.3 us; the launch traced here: 32.1 us
  blocking collectives  13.7 us (42%)
  starting transfers between devices  7.08 us (22%)
  waiting for transfers between devices  5.19 us (16%)
  Pallas kernels  4.4 us (14%)
  local copies, waits for them, and re-layouts  1.7 us (5%)
    all_to_all x1, blocking collectives, shards(): lax.all_to_all(terms, ('chan', 'freq'), split_axis=0, concat_axis=0, axis...  13.7 us
    ppermute x3, starting transfers between devices, shards(): chunks[distance] = lax.ppermute(chunks[distance], 'chan', pairs)  7.08 us
    ppermute x3, waiting for transfers between devices, shards(): chunks[distance] = lax.ppermute(chunks[distance], 'chan', pairs)  5.19 us
    pallas_call x1, Pallas kernels, shards(): pl.pallas_call(functools.partial(stack_kernel, groups, bins, parts), out_...  2.07 us
    unnamed x6, local copies, waits for them, and re-layouts  1.7 us
    pallas_call x1, Pallas kernels, shards(): pl.pallas_call(functools.partial(table_kernel, groups, bins, freq_dev), o...  1.19 us
    pallas_call x1, Pallas kernels, shards(): pl.pallas_call(functools.partial(image_kernel, slow_dev, spans), out_shap...  0.88 us
  transfers between devices with their start and end apart: 3, of which 2 were waited for; matrix products, arithmetic and copies ran while one was open for 0% of the time, Pallas kernels for 4%

profile of v20, /device:TPU:0, one launch (start us, length us, event | category | flops | bytes accessed | tf_op | source)
XLA Modules:
  0.0 32.1 jit_solution(15933689625149533926)
XLA Ops:
  0.0 0.0 copy-start
  0.0 1.0 %copy-done = bf16[2,32,32,128]{3,2,1,0:T(8,128)(2,1)S(1)} copy-done((bf16[2,32,32,128]{3,2,1,0:T(8,128)(2,1)S(1)}, bf16[2,32,32,128]{3,2,1,0:T(8,128)(2,1)}, u32[]{:S(2)}) %copy-start) | copy-done | bytes 524312
  1.0 0.1 chunks_of_bins.2.refs_0_
  1.1 0.0 copy-start.1
  1.1 3.1 %collective-permute-start = (bf16[8,64,128]{2,1,0:T(8,128)(2,1)S(1)}, bf16[8,64,128]{2,1,0:T(8,128)(2,1)S(1)}, u32[]{:S(2)}, u32[]{:S(2)}) collective-permute-start(bf16[8,64,128]{2,1,0:T(8,128)(2,1)S(1)} %chunks_of_bins.2.refs_0_), channel_id=1, source_target_pairs={{0,8},{8,16},{16,24},{24,0},{1,9},{9,17},{17,25},{25,1},{2,10},{10... | collective-permute-start | bytes 393224 | tf_op jit(solution)/shard_map/ppermute | solution.py:272
  4.2 0.2 chunks_of_bins.3
  4.4 2.7 %collective-permute-start.1 = (bf16[8,64,128]{2,1,0:T(8,128)(2,1)S(1)}, bf16[8,64,128]{2,1,0:T(8,128)(2,1)S(1)}, u32[]{:S(2)}, u32[]{:S(2)}) collective-permute-start(bf16[8,64,128]{2,1,0:T(8,128)(2,1)S(1)} %get-tuple-element.12), channel_id=1, source_target_pairs={{0,16},{8,24},{16,0},{24,8},{1,17},{9,25},{17,1},{25,9},{2,18},{10... | collective-permute-start | bytes 393224 | tf_op jit(solution)/shard_map/ppermute | solution.py:272
  7.0 1.3 %collective-permute-start.2 = (bf16[8,64,128]{2,1,0:T(8,128)(2,1)S(1)}, bf16[8,64,128]{2,1,0:T(8,128)(2,1)S(1)}, u32[]{:S(2)}, u32[]{:S(2)}) collective-permute-start(bf16[8,64,128]{2,1,0:T(8,128)(2,1)S(1)} %get-tuple-element.13), channel_id=1, source_target_pairs={{0,24},{8,0},{16,8},{24,16},{1,25},{9,1},{17,9},{25,17},{2,26},{10... | collective-permute-start | bytes 393224 | tf_op jit(solution)/shard_map/ppermute | solution.py:272
  8.4 0.0 copy-start.2
  8.4 0.7 %copy-done.2 = s32[4]{0:T(128)S(1)} copy-done((s32[4]{0:T(128)S(1)}, s32[4]{0:T(128)}, u32[]{:S(2)}) %copy-start.2) | copy-done | bytes 40
  9.0 1.2 %slant_tables.1 = (s32[4,128]{1,0:T(4,128)S(1)}, bf16[8,256,512]{2,1,0:T(8,128)(2,1)S(1)}, f32[8,2,8,256]{3,2,1,0:T(8,128)S(1)}) custom-call(s32[1,4]{1,0:T(1,128)S(1)} %bitcast.6), custom_call_target="tpu_custom_call" | custom-call | flops 10000000 | bytes 4000000 | tf_op jit(solution)/shard_map/slant_tables/pallas_call | solution.py:282
  10.2 0.4 %collective-permute-done.in_ref = bf16[8,64,128]{2,1,0:T(8,128)(2,1)S(1)} collective-permute-done((bf16[8,64,128]{2,1,0:T(8,128)(2,1)S(1)}, bf16[8,64,128]{2,1,0:T(8,128)(2,1)S(1)}, u32[]{:S(2)}, u32[]{:S(2)}) %collective-permute-start) | collective-permute-done | bytes 131104 | tf_op jit(solution)/shard_map/ppermute | solution.py:272
  10.7 4.8 %collective-permute-done.1.refs_2_ = bf16[8,64,128]{2,1,0:T(8,128)(2,1)S(1)} collective-permute-done((bf16[8,64,128]{2,1,0:T(8,128)(2,1)S(1)}, bf16[8,64,128]{2,1,0:T(8,128)(2,1)S(1)}, u32[]{:S(2)}, u32[]{:S(2)}) %collective-permute-start.1) | collective-permute-done | bytes 131104 | tf_op jit(solution)/shard_map/ppermute | solution.py:272
  15.4 0.0 collective-permute-done.2.refs_3_
  15.4 2.1 %stack_and_slant.1 = f32[4,8,4,128]{3,2,1,0:T(4,128)S(1)} custom-call(bf16[8,64,128]{2,1,0:T(8,128)(2,1)S(1)} %get-tuple-element.11.refs_0_, bf16[8,64,128]{2,1,0:T(8,128)(2,1)S(1)} %first_arrived.1.refs_1_, bf16[8,64,128]{2,1,0:T(8,128)(2,1)S(1)} %collective-permute-done.1.refs_2_, bf16[8,64,128]{2,1,0:T(8,128)(2,1)S(1)} %collective-permute-done.2.refs_3_, ...), custom_call_target="tpu_custom_call" | custom-call | tf_op jit(solution)/shard_map/stack_and_slant/pallas_call | solution.py:295
  17.5 13.7 %all_to_all.5.term_ref = f32[32,4,128]{2,1,0:T(4,128)S(1)} all-to-all(f32[32,4,128]{2,1,0:T(4,128)S(1)} %bitcast.5), channel_id=1, replica_groups={{31,30,29,28,27,26,25,24,23,22,21,20,19,18,17,16,15,14,13,12,11,10,9,8,..., dimensions={0} | all-to-all | bytes 131072 | tf_op jit(solution)/shard_map/all_to_all | solution.py:314
  31.2 0.0 copy-done.1
  31.2 0.9 %sum_of_bins.1 = f32[1,32,512]{2,1,0:T(8,128)} custom-call(f32[32,4,128]{2,1,0:T(4,128)S(1)} %all_to_all.5.term_ref, bf16[2,2,256,256]{3,2,1,0:T(8,128)(2,1)S(1)} %copy-done.1), custom_call_target="tpu_custom_call" | custom-call | tf_op jit(solution)/shard_map/sum_of_bins/pallas_call | solution.py:323
  (1 shorter events, 0.0 us)
Async XLA Ops:
  0.0 1.0 %copy-start = (bf16[2,32,32,128]{3,2,1,0:T(8,128)(2,1)S(1)}, bf16[2,32,32,128]{3,2,1,0:T(8,128)(2,1)}, u32[]{:S(2)}) copy-start(bf16[2,32,32,128]{3,2,1,0:T(8,128)(2,1)} %param.3) | copy-start | bytes 1572868
  1.1 30.1 %copy-start.1 = (bf16[2,2,256,256]{3,2,1,0:T(8,128)(2,1)S(1)}, bf16[2,2,256,256]{3,2,1,0:T(8,128)(2,1)}, u32[]{:S(2)}) copy-start(bf16[2,2,256,256]{3,2,1,0:T(8,128)(2,1)} %constant.2.clone.table_ref) | copy-start | bytes 1572868
  1.1 9.5 %collective-permute-start = (bf16[8,64,128]{2,1,0:T(8,128)(2,1)S(1)}, bf16[8,64,128]{2,1,0:T(8,128)(2,1)S(1)}, u32[]{:S(2)}, u32[]{:S(2)}) collective-permute-start(bf16[8,64,128]{2,1,0:T(8,128)(2,1)S(1)} %chunks_of_bins.2.refs_0_), channel_id=1, source_target_pairs={{0,8},{8,16},{16,24},{24,0},{1,9},{9,17},{17,25},{25,1},{2,10},{10... | collective-permute-start | bytes 393224 | tf_op jit(solution)/shard_map/ppermute | solution.py:272
  4.4 11.0 %collective-permute-start.1 = (bf16[8,64,128]{2,1,0:T(8,128)(2,1)S(1)}, bf16[8,64,128]{2,1,0:T(8,128)(2,1)S(1)}, u32[]{:S(2)}, u32[]{:S(2)}) collective-permute-start(bf16[8,64,128]{2,1,0:T(8,128)(2,1)S(1)} %get-tuple-element.12), channel_id=1, source_target_pairs={{0,16},{8,24},{16,0},{24,8},{1,17},{9,25},{17,1},{25,9},{2,18},{10... | collective-permute-start | bytes 393224 | tf_op jit(solution)/shard_map/ppermute | solution.py:272
  7.0 8.4 %collective-permute-start.2 = (bf16[8,64,128]{2,1,0:T(8,128)(2,1)S(1)}, bf16[8,64,128]{2,1,0:T(8,128)(2,1)S(1)}, u32[]{:S(2)}, u32[]{:S(2)}) collective-permute-start(bf16[8,64,128]{2,1,0:T(8,128)(2,1)S(1)} %get-tuple-element.13), channel_id=1, source_target_pairs={{0,24},{8,0},{16,8},{24,16},{1,25},{9,1},{17,9},{25,17},{2,26},{10... | collective-permute-start | bytes 393224 | tf_op jit(solution)/shard_map/ppermute | solution.py:272
  8.4 0.7 %copy-start.2 = (s32[4]{0:T(128)S(1)}, s32[4]{0:T(128)}, u32[]{:S(2)}) copy-start(s32[4]{0:T(128)} %param.4) | copy-start | bytes 52

commit v21 on v19

--- a/solution.py
+++ b/solution.py
@@ -80,15 +80,19 @@
     lax.fori_loop(0, bins, one_bin, 0)
 
 
-def chunk_kernel(distances, spec_ref, *refs):
+def chunk_kernel(cuts, spec_ref, *refs):
     rows, groups, bins, _ = spec_ref.shape
-    out_refs, wide_ref = refs[-1 - len(distances) : -1], refs[-1]
+    out_refs, wide_ref = refs[-1 - len(cuts) : -1], refs[-1]
     own_group = lax.axis_index("chan")
-    for index, (distance, out_ref) in enumerate(zip(distances, out_refs)):
-        group = lax.rem(own_group + distance, groups)
-        wide_ref[index] = spec_ref[:, group].astype(jnp.float32).reshape(rows * bins, BLOCK)
-        for f in range(bins):
-            value = wide_ref[index, pl.ds(f, rows, stride=bins), :]
+    widened = []
+    for (distance, start, size), out_ref in zip(cuts, out_refs):
+        if distance not in widened:
+            group = lax.rem(own_group + distance, groups)
+            index = len(widened)
+            wide_ref[index] = spec_ref[:, group].astype(jnp.float32).reshape(rows * bins, BLOCK)
+            widened.append(distance)
+        for f in range(size):
+            value = wide_ref[widened.index(distance), pl.ds(start + f, rows, stride=bins), :]
             out_ref[f] = value.astype(jnp.bfloat16)
 
 
@@ -103,9 +107,11 @@
     return jnp.where(usable, scale / jnp.maximum(count, 1).astype(jnp.float32), 0.0)
 
 
-def stack_kernel(groups, bins, parts, *refs):
+def stack_kernel(groups, start, bins, parts, *refs):
     chunk_refs = refs[:groups]
-    place_ref, lag_ref, shift_ref, out_ref, placed_ref, left_ref, part_ref = refs[groups:]
+    place_ref, lag_ref, shift_ref = refs[groups : groups + 3]
+    earlier_refs = refs[groups + 3 : -4]
+    out_ref, placed_ref, left_ref, part_ref = refs[-4:]
     rows = placed_ref.shape[2]
     windows = rows // 2
     places = place_ref[...]
@@ -171,17 +177,23 @@
             ],
             0,
         )
-        product = jnp.dot(spread, lag_ref[f], preferred_element_type=jnp.float32)
+        product = jnp.dot(spread, lag_ref[start + f], preferred_element_type=jnp.float32)
         product = product[: 4 * groups] + product[4 * groups :]
         by_cos, by_sin = product[:, :SLOWNESS], product[:, SLOWNESS:]
         real = by_cos[: 2 * groups] - by_sin[2 * groups :]
         imag = by_sin[: 2 * groups] + by_cos[2 * groups :]
-        shift_cos, shift_sin = shift_ref[f, 0], shift_ref[f, 1]
+        shift_cos, shift_sin = shift_ref[start + f, 0], shift_ref[start + f, 1]
         turned_re = real * shift_cos - imag * shift_sin
         turned_im = real * shift_sin + imag * shift_cos
         terms.append(turned_re[:groups] + turned_re[groups:])
         terms.append(turned_im[:groups] + turned_im[groups:])
 
+    if parts is None:
+        for entry, term in enumerate(terms):
+            out_ref[entry] = term
+        return
+    for earlier_ref in reversed(earlier_refs):
+        terms = [earlier_ref[entry] for entry in range(earlier_ref.shape[0])] + terms
     slow_dev = SLOWNESS // parts
     spans = BLOCK // slow_dev
     span_index = lax.broadcasted_iota(jnp.int32, (groups, BLOCK), 1) // slow_dev
@@ -254,33 +266,38 @@
 
     whole = spectra.reshape(rows, groups, bins, BLOCK)
 
-    def cut(distances, *earlier):
+    def cut(cuts, *earlier):
+        distances = {distance for distance, _, _ in cuts}
         return pl.pallas_call(
-            functools.partial(chunk_kernel, distances),
-            out_shape=(jax.ShapeDtypeStruct((bins, rows, BLOCK), jnp.bfloat16),) * len(distances),
+            functools.partial(chunk_kernel, cuts),
+            out_shape=tuple(
+                jax.ShapeDtypeStruct((size, rows, BLOCK), jnp.bfloat16) for _, _, size in cuts
+            ),
             in_specs=[vmem] + [anywhere] * len(earlier),
-            out_specs=(vmem,) * len(distances),
+            out_specs=(vmem,) * len(cuts),
             scratch_shapes=[pltpu.VMEM((len(distances), rows * bins, BLOCK), jnp.float32)],
             compiler_params=params,
             cost_estimate=pl.CostEstimate(flops=10**7, bytes_accessed=10**6, transcendentals=0),
             name="chunks_of_bins",
         )(whole, *earlier)
 
-    order = list(range(1, groups)) + [0]
-    (first_chunk,) = cut(order[:1])
-    chunks = dict(zip(order, (first_chunk, *cut(order[1:], first_chunk))))
-    for distance in order[:-1]:
-        pairs = [(source, (source + distance) % groups) for source in range(groups)]
-        chunks[distance] = lax.ppermute(chunks[distance], "chan", pairs)
-    first = order[0]
-    chunks[first] = pl.pallas_call(
+    late = bins // 2
+    pieces = [(0, bins - late), (bins - late, late)] if late else [(0, bins)]
+    cuts = [(distance, *piece) for piece in pieces for distance in list(range(1, groups)) + [0]]
+    (first_chunk,) = cut(cuts[:1])
+    chunks = dict(zip(cuts, (first_chunk, *cut(cuts[1:], first_chunk))))
+    for key in cuts:
+        if key[0]:
+            pairs = [(source, (source + key[0]) % groups) for source in range(groups)]
+            chunks[key] = lax.ppermute(chunks[key], "chan", pairs)
+    chunks[cuts[0]] = pl.pallas_call(
         copy_kernel,
-        out_shape=jax.ShapeDtypeStruct((bins, rows, BLOCK), jnp.bfloat16),
+        out_shape=jax.ShapeDtypeStruct(first_chunk.shape, jnp.bfloat16),
         in_specs=[vmem],
         out_specs=vmem,
         compiler_params=params,
         name="first_arrived",
-    )(chunks[first])
+    )(chunks[cuts[0]])
     places, lag_table, shift_table = pl.pallas_call(
         functools.partial(table_kernel, groups, bins, freq_dev),
         out_shape=(
@@ -294,24 +311,33 @@
         cost_estimate=pl.CostEstimate(flops=10**7, bytes_accessed=4 * 10**6, transcendentals=0),
         name="slant_tables",
     )(block_position.reshape(1, groups))
-    terms = pl.pallas_call(
-        functools.partial(stack_kernel, groups, bins, parts),
-        out_shape=jax.ShapeDtypeStruct((groups, parts, message_rows, BLOCK), jnp.float32),
-        in_specs=[vmem] * (groups + 3),
-        out_specs=vmem,
-        scratch_shapes=[
-            pltpu.VMEM((groups, bins, rows, BLOCK), jnp.bfloat16),
-            pltpu.VMEM((bins, BLOCK, groups * rows), jnp.bfloat16),
-            pltpu.VMEM((2, bins * 2 * groups * 8, BLOCK), jnp.float32),
-        ],
-        compiler_params=params,
-        name="stack_and_slant",
-    )(
-        *[chunks[distance] for distance in range(groups)],
-        places,
-        lag_table,
-        shift_table,
-    )
+    earlier = []
+    for start, size in pieces:
+        last = start + size == bins
+        shape = (groups, parts, message_rows, BLOCK) if last else (2 * size, groups, SLOWNESS)
+        terms = pl.pallas_call(
+            functools.partial(stack_kernel, groups, start, size, parts if last else None),
+            out_shape=jax.ShapeDtypeStruct(shape, jnp.float32),
+            in_specs=[vmem] * (groups + 3 + len(earlier)),
+            out_specs=vmem,
+            scratch_shapes=[
+                pltpu.VMEM((groups, size, rows, BLOCK), jnp.bfloat16),
+                pltpu.VMEM((size, BLOCK, groups * rows), jnp.bfloat16),
+                pltpu.VMEM((2, size * 2 * groups * 8, BLOCK), jnp.float32),
+            ],
+            compiler_params=params,
+            cost_estimate=pl.CostEstimate(
+                flops=2 * 10**8, bytes_accessed=4 * 10**6, transcendentals=0
+            ),
+            name="stack_and_slant",
+        )(
+            *[chunks[distance, start, size] for distance in range(groups)],
+            places,
+            lag_table,
+            shift_table,
+            *earlier,
+        )
+        earlier.append(terms)
     terms = terms.reshape(groups * parts, message_rows, BLOCK)
     arrived = lax.all_to_all(
         terms,

time: 32.2 us -> 31.9 us (level)
  starting transfers between devices: 7.08 us -> 10.9 us
  waiting for transfers between devices: 5.19 us -> 1.65 us
  blocking collectives: 13.7 us -> 12.6 us
  Pallas kernels: 4.3 us -> 4.78 us
    ppermute x3 -> x6, starting transfers between devices: 7.08 us -> 10.9 us  [shards(): chunks[key] = lax.ppermute(chunks[key], 'chan', pairs)]
    ppermute x3 -> x6, waiting for transfers between devices: 5.19 us -> 1.65 us  [shards(): chunks[key] = lax.ppermute(chunks[key], 'chan', pairs)]
    all_to_all x1, blocking collectives: 13.7 us -> 12.6 us  [shards(): lax.all_to_all(terms, ('chan', 'freq'), split_axis=0, concat_axis=0, axis...]
    pallas_call x4 -> x5, Pallas kernels: 2.23 us -> 2.71 us  [the longest x2 2.44 us: shards(): pl.pallas_call(functools.partial(stack_kernel, groups, start, size, parts...]
  transfers between devices with their start and end apart: 3 -> 6, of which waited for: 2 -> 1; matrix products, arithmetic and copies ran while one was open for 0% -> 0% of each run, Pallas kernels for 4% -> 8%
where the time goes in v21:
time: 31.9 us; the launch traced here: 31.7 us
  blocking collectives  12.6 us (39%)
  starting transfers between devices  10.9 us (34%)
  Pallas kernels  4.78 us (15%)
  local copies, waits for them, and re-layouts  1.7 us (5%)
  waiting for transfers between devices  1.65 us (5%)
    all_to_all x1, blocking collectives, shards(): lax.all_to_all(terms, ('chan', 'freq'), split_axis=0, concat_axis=0, axis...  12.6 us
    ppermute x6, starting transfers between devices, shards(): chunks[key] = lax.ppermute(chunks[key], 'chan', pairs)  10.9 us
    pallas_call x2, Pallas kernels, shards(): pl.pallas_call(functools.partial(stack_kernel, groups, start, size, parts...  2.44 us
    unnamed x6, local copies, waits for them, and re-layouts  1.7 us
    ppermute x6, waiting for transfers between devices, shards(): chunks[key] = lax.ppermute(chunks[key], 'chan', pairs)  1.65 us
    pallas_call x1, Pallas kernels, shards(): pl.pallas_call(functools.partial(table_kernel, groups, bins, freq_dev), o...  1.19 us
    pallas_call x1, Pallas kernels, shards(): pl.pallas_call(functools.partial(image_kernel, slow_dev, spans), out_shap...  0.88 us
  transfers between devices with their start and end apart: 6, of which 1 were waited for; matrix products, arithmetic and copies ran while one was open for 0% of the time, Pallas kernels for 8%

profile of v21, /device:TPU:0, one launch (start us, length us, event | category | flops | bytes accessed | tf_op | source)
XLA Modules:
  0.0 31.7 jit_solution(1829240673573257016)
XLA Ops:
  0.0 0.0 copy-start
  0.0 1.0 %copy-done = bf16[2,32,32,128]{3,2,1,0:T(8,128)(2,1)S(1)} copy-done((bf16[2,32,32,128]{3,2,1,0:T(8,128)(2,1)S(1)}, bf16[2,32,32,128]{3,2,1,0:T(8,128)(2,1)}, u32[]{:S(2)}) %copy-start) | copy-done | bytes 524312
  1.1 3.1 %collective-permute-start.3 = (bf16[4,64,128]{2,1,0:T(8,128)(2,1)S(1)}, bf16[4,64,128]{2,1,0:T(8,128)(2,1)S(1)}, u32[]{:S(2)}, u32[]{:S(2)}) collective-permute-start(bf16[4,64,128]{2,1,0:T(8,128)(2,1)S(1)} %chunks_of_bins.2.refs_0_), channel_id=1, source_target_pairs={{0,8},{8,16},{16,24},{24,0},{1,9},{9,17},{17,25},{25,1},{2,10},{10... | collective-permute-start | bytes 196616 | tf_op jit(solution)/shard_map/ppermute | solution.py:292
  4.2 0.2 chunks_of_bins.3
  4.4 2.7 %collective-permute-start.4 = (bf16[4,64,128]{2,1,0:T(8,128)(2,1)S(1)}, bf16[4,64,128]{2,1,0:T(8,128)(2,1)S(1)}, u32[]{:S(2)}, u32[]{:S(2)}) collective-permute-start(bf16[4,64,128]{2,1,0:T(8,128)(2,1)S(1)} %get-tuple-element.23), channel_id=1, source_target_pairs={{0,16},{8,24},{16,0},{24,8},{1,17},{9,25},{17,1},{25,9},{2,18},{10... | collective-permute-start | bytes 196616 | tf_op jit(solution)/shard_map/ppermute | solution.py:292
  7.0 1.3 %collective-permute-start.5 = (bf16[4,64,128]{2,1,0:T(8,128)(2,1)S(1)}, bf16[4,64,128]{2,1,0:T(8,128)(2,1)S(1)}, u32[]{:S(2)}, u32[]{:S(2)}) collective-permute-start(bf16[4,64,128]{2,1,0:T(8,128)(2,1)S(1)} %get-tuple-element.24), channel_id=1, source_target_pairs={{0,24},{8,0},{16,8},{24,16},{1,25},{9,1},{17,9},{25,17},{2,26},{10... | collective-permute-start | bytes 196616 | tf_op jit(solution)/shard_map/ppermute | solution.py:292
  8.4 0.7 %collective-permute-start = (bf16[4,64,128]{2,1,0:T(8,128)(2,1)S(1)}, bf16[4,64,128]{2,1,0:T(8,128)(2,1)S(1)}, u32[]{:S(2)}, u32[]{:S(2)}) collective-permute-start(bf16[4,64,128]{2,1,0:T(8,128)(2,1)S(1)} %get-tuple-element.16), channel_id=1, source_target_pairs={{0,8},{8,16},{16,24},{24,0},{1,9},{9,17},{17,25},{25,1},{2,10},{10... | collective-permute-start | bytes 196616 | tf_op jit(solution)/shard_map/ppermute | solution.py:292
  9.1 0.3 %collective-permute-start.1 = (bf16[4,64,128]{2,1,0:T(8,128)(2,1)S(1)}, bf16[4,64,128]{2,1,0:T(8,128)(2,1)S(1)}, u32[]{:S(2)}, u32[]{:S(2)}) collective-permute-start(bf16[4,64,128]{2,1,0:T(8,128)(2,1)S(1)} %get-tuple-element.17), channel_id=1, source_target_pairs={{0,16},{8,24},{16,0},{24,8},{1,17},{9,25},{17,1},{25,9},{2,18},{10... | collective-permute-start | bytes 196616 | tf_op jit(solution)/shard_map/ppermute | solution.py:292
  9.4 0.0 collective-permute-done.3.in_ref
  9.4 2.8 %collective-permute-start.2 = (bf16[4,64,128]{2,1,0:T(8,128)(2,1)S(1)}, bf16[4,64,128]{2,1,0:T(8,128)(2,1)S(1)}, u32[]{:S(2)}, u32[]{:S(2)}) collective-permute-start(bf16[4,64,128]{2,1,0:T(8,128)(2,1)S(1)} %get-tuple-element.18), channel_id=1, source_target_pairs={{0,24},{8,0},{16,8},{24,16},{1,25},{9,1},{17,9},{25,17},{2,26},{10... | collective-permute-start | bytes 196616 | tf_op jit(solution)/shard_map/ppermute | solution.py:292
  12.2 0.0 copy-start.2
  12.2 0.7 %copy-done.2 = s32[4]{0:T(128)S(1)} copy-done((s32[4]{0:T(128)S(1)}, s32[4]{0:T(128)}, u32[]{:S(2)}) %copy-start.2) | copy-done | bytes 40
  12.9 1.2 %slant_tables.1 = (s32[4,128]{1,0:T(4,128)S(1)}, bf16[8,256,512]{2,1,0:T(8,128)(2,1)S(1)}, f32[8,2,8,256]{3,2,1,0:T(8,128)S(1)}) custom-call(s32[1,4]{1,0:T(1,128)S(1)} %bitcast.6), custom_call_target="tpu_custom_call" | custom-call | flops 10000000 | bytes 4000000 | tf_op jit(solution)/shard_map/slant_tables/pallas_call | solution.py:301
  14.1 0.0 collective-permute-done.4.refs_2_
  14.1 0.0 collective-permute-done.5.refs_3_
  14.1 0.0 copy-start.1
  14.1 1.2 %stack_and_slant.2.refs_7_ = f32[8,4,256]{2,1,0:T(4,128)S(1)} custom-call(bf16[4,64,128]{2,1,0:T(8,128)(2,1)S(1)} %get-tuple-element.22.refs_0_, bf16[4,64,128]{2,1,0:T(8,128)(2,1)S(1)} %first_arrived.1.refs_1_, bf16[4,64,128]{2,1,0:T(8,128)(2,1)S(1)} %collective-permute-done.4.refs_2_, bf16[4,64,128]{2,1,0:T(8,128)(2,1)S(1)} %collective-permute-done.5.refs_3_, ...), custom_call_target="tpu_custom_call" | custom-call | flops 200000000 | bytes 4000000 | tf_op jit(solution)/shard_map/stack_and_slant/pallas_call | solution.py:318
  15.3 0.0 collective-permute-done.refs_1_
  15.3 1.6 %collective-permute-done.1.refs_2_ = bf16[4,64,128]{2,1,0:T(8,128)(2,1)S(1)} collective-permute-done((bf16[4,64,128]{2,1,0:T(8,128)(2,1)S(1)}, bf16[4,64,128]{2,1,0:T(8,128)(2,1)S(1)}, u32[]{:S(2)}, u32[]{:S(2)}) %collective-permute-start.1) | collective-permute-done | bytes 65568 | tf_op jit(solution)/shard_map/ppermute | solution.py:292
  16.9 0.0 collective-permute-done.2.refs_3_
  16.9 1.3 %stack_and_slant.3 = f32[4,8,4,128]{3,2,1,0:T(4,128)S(1)} custom-call(bf16[4,64,128]{2,1,0:T(8,128)(2,1)S(1)} %get-tuple-element.15.refs_0_, bf16[4,64,128]{2,1,0:T(8,128)(2,1)S(1)} %collective-permute-done.refs_1_, bf16[4,64,128]{2,1,0:T(8,128)(2,1)S(1)} %collective-permute-done.1.refs_2_, bf16[4,64,128]{2,1,0:T(8,128)(2,1)S(1)} %collective-permute-done.2.refs_3_, ...), custom_call_target="tpu_custom_call" | custom-call | flops 200000000 | bytes 4000000 | tf_op jit(solution)/shard_map/stack_and_slant/pallas_call | solution.py:318
  18.2 12.6 %all_to_all.5.term_ref = f32[32,4,128]{2,1,0:T(4,128)S(1)} all-to-all(f32[32,4,128]{2,1,0:T(4,128)S(1)} %bitcast.5), channel_id=1, replica_groups={{31,30,29,28,27,26,25,24,23,22,21,20,19,18,17,16,15,14,13,12,11,10,9,8,..., dimensions={0} | all-to-all | bytes 131072 | tf_op jit(solution)/shard_map/all_to_all | solution.py:342
  30.8 0.0 copy-done.1
  30.8 0.9 %sum_of_bins.1 = f32[1,32,512]{2,1,0:T(8,128)} custom-call(f32[32,4,128]{2,1,0:T(4,128)S(1)} %all_to_all.5.term_ref, bf16[2,2,256,256]{3,2,1,0:T(8,128)(2,1)S(1)} %copy-done.1), custom_call_target="tpu_custom_call" | custom-call | tf_op jit(solution)/shard_map/sum_of_bins/pallas_call | solution.py:351
  (2 shorter events, 0.0 us)
Async XLA Ops:
  0.0 1.0 %copy-start = (bf16[2,32,32,128]{3,2,1,0:T(8,128)(2,1)S(1)}, bf16[2,32,32,128]{3,2,1,0:T(8,128)(2,1)}, u32[]{:S(2)}) copy-start(bf16[2,32,32,128]{3,2,1,0:T(8,128)(2,1)} %param.3) | copy-start | bytes 1572868
  1.1 8.3 %collective-permute-start.3 = (bf16[4,64,128]{2,1,0:T(8,128)(2,1)S(1)}, bf16[4,64,128]{2,1,0:T(8,128)(2,1)S(1)}, u32[]{:S(2)}, u32[]{:S(2)}) collective-permute-start(bf16[4,64,128]{2,1,0:T(8,128)(2,1)S(1)} %chunks_of_bins.2.refs_0_), channel_id=1, source_target_pairs={{0,8},{8,16},{16,24},{24,0},{1,9},{9,17},{17,25},{25,1},{2,10},{10... | collective-permute-start | bytes 196616 | tf_op jit(solution)/shard_map/ppermute | solution.py:292
  4.4 9.7 %collective-permute-start.4 = (bf16[4,64,128]{2,1,0:T(8,128)(2,1)S(1)}, bf16[4,64,128]{2,1,0:T(8,128)(2,1)S(1)}, u32[]{:S(2)}, u32[]{:S(2)}) collective-permute-start(bf16[4,64,128]{2,1,0:T(8,128)(2,1)S(1)} %get-tuple-element.23), channel_id=1, source_target_pairs={{0,16},{8,24},{16,0},{24,8},{1,17},{9,25},{17,1},{25,9},{2,18},{10... | collective-permute-start | bytes 196616 | tf_op jit(solution)/shard_map/ppermute | solution.py:292
  7.0 7.1 %collective-permute-start.5 = (bf16[4,64,128]{2,1,0:T(8,128)(2,1)S(1)}, bf16[4,64,128]{2,1,0:T(8,128)(2,1)S(1)}, u32[]{:S(2)}, u32[]{:S(2)}) collective-permute-start(bf16[4,64,128]{2,1,0:T(8,128)(2,1)S(1)} %get-tuple-element.24), channel_id=1, source_target_pairs={{0,24},{8,0},{16,8},{24,16},{1,25},{9,1},{17,9},{25,17},{2,26},{10... | collective-permute-start | bytes 196616 | tf_op jit(solution)/shard_map/ppermute | solution.py:292
  8.4 6.9 %collective-permute-start = (bf16[4,64,128]{2,1,0:T(8,128)(2,1)S(1)}, bf16[4,64,128]{2,1,0:T(8,128)(2,1)S(1)}, u32[]{:S(2)}, u32[]{:S(2)}) collective-permute-start(bf16[4,64,128]{2,1,0:T(8,128)(2,1)S(1)} %get-tuple-element.16), channel_id=1, source_target_pairs={{0,8},{8,16},{16,24},{24,0},{1,9},{9,17},{17,25},{25,1},{2,10},{10... | collective-permute-start | bytes 196616 | tf_op jit(solution)/shard_map/ppermute | solution.py:292
  9.1 7.9 %collective-permute-start.1 = (bf16[4,64,128]{2,1,0:T(8,128)(2,1)S(1)}, bf16[4,64,128]{2,1,0:T(8,128)(2,1)S(1)}, u32[]{:S(2)}, u32[]{:S(2)}) collective-permute-start(bf16[4,64,128]{2,1,0:T(8,128)(2,1)S(1)} %get-tuple-element.17), channel_id=1, source_target_pairs={{0,16},{8,24},{16,0},{24,8},{1,17},{9,25},{17,1},{25,9},{2,18},{10... | collective-permute-start | bytes 196616 | tf_op jit(solution)/shard_map/ppermute | solution.py:292
  9.4 7.5 %collective-permute-start.2 = (bf16[4,64,128]{2,1,0:T(8,128)(2,1)S(1)}, bf16[4,64,128]{2,1,0:T(8,128)(2,1)S(1)}, u32[]{:S(2)}, u32[]{:S(2)}) collective-permute-start(bf16[4,64,128]{2,1,0:T(8,128)(2,1)S(1)} %get-tuple-element.18), channel_id=1, source_target_pairs={{0,24},{8,0},{16,8},{24,16},{1,25},{9,1},{17,9},{25,17},{2,26},{10... | collective-permute-start | bytes 196616 | tf_op jit(solution)/shard_map/ppermute | solution.py:292
  12.2 0.7 %copy-start.2 = (s32[4]{0:T(128)S(1)}, s32[4]{0:T(128)}, u32[]{:S(2)}) copy-start(s32[4]{0:T(128)} %param.4) | copy-start | bytes 52
  14.1 16.7 %copy-start.1 = (bf16[2,2,256,256]{3,2,1,0:T(8,128)(2,1)S(1)}, bf16[2,2,256,256]{3,2,1,0:T(8,128)(2,1)}, u32[]{:S(2)}) copy-start(bf16[2,2,256,256]{3,2,1,0:T(8,128)(2,1)} %constant.2.clone.table_ref) | copy-start | bytes 1572868

commit v22 on v21

--- a/solution.py
+++ b/solution.py
@@ -107,7 +107,8 @@
     return jnp.where(usable, scale / jnp.maximum(count, 1).astype(jnp.float32), 0.0)
 
 
-def stack_kernel(groups, start, bins, parts, *refs):
+def stack_kernel(order, start, bins, parts, *refs):
+    groups = len(order)
     chunk_refs = refs[:groups]
     place_ref, lag_ref, shift_ref = refs[groups : groups + 3]
     earlier_refs = refs[groups + 3 : -4]
@@ -115,7 +116,7 @@
     rows = placed_ref.shape[2]
     windows = rows // 2
     places = place_ref[...]
-    for distance, chunk_ref in enumerate(chunk_refs):
+    for distance, chunk_ref in zip(order, chunk_refs):
         placed_ref[places[distance, 0]] = chunk_ref[...]
 
     row_index = lax.broadcasted_iota(jnp.int32, (BLOCK, BLOCK), 0)
@@ -281,9 +282,12 @@
             name="chunks_of_bins",
         )(whole, *earlier)
 
-    late = bins // 2
+    late = max(1, 3 * bins // 8) if bins > 1 else 0
     pieces = [(0, bins - late), (bins - late, late)] if late else [(0, bins)]
-    cuts = [(distance, *piece) for piece in pieces for distance in list(range(1, groups)) + [0]]
+    near_first = list(range(1, groups)) + [0]
+    far_first = sorted(range(1, groups), key=lambda steps: abs(2 * steps - groups)) + [0]
+    orders = [near_first, far_first][: len(pieces)]
+    cuts = [(distance, *piece) for piece, order in zip(pieces, orders) for distance in order]
     (first_chunk,) = cut(cuts[:1])
     chunks = dict(zip(cuts, (first_chunk, *cut(cuts[1:], first_chunk))))
     for key in cuts:
@@ -312,11 +316,11 @@
         name="slant_tables",
     )(block_position.reshape(1, groups))
     earlier = []
-    for start, size in pieces:
+    for (start, size), order in zip(pieces, orders):
         last = start + size == bins
         shape = (groups, parts, message_rows, BLOCK) if last else (2 * size, groups, SLOWNESS)
         terms = pl.pallas_call(
-            functools.partial(stack_kernel, groups, start, size, parts if last else None),
+            functools.partial(stack_kernel, order, start, size, parts if last else None),
             out_shape=jax.ShapeDtypeStruct(shape, jnp.float32),
             in_specs=[vmem] * (groups + 3 + len(earlier)),
             out_specs=vmem,
@@ -331,7 +335,7 @@
             ),
             name="stack_and_slant",
         )(
-            *[chunks[distance, start, size] for distance in range(groups)],
+            *[chunks[distance, start, size] for distance in order],
             places,
             lag_table,
             shift_table,

time: 31.9 us -> 31.5 us (0.987)
  blocking collectives: 12.6 us -> 12.1 us
    all_to_all x1, blocking collectives: 12.6 us -> 12.1 us  [shards(): lax.all_to_all(terms, ('chan', 'freq'), split_axis=0, concat_axis=0, axis...]
  transfers between devices with their start and end apart: 6 -> 6, of which waited for: 1 -> 1; matrix products, arithmetic and copies ran while one was open for 0% -> 0% of each run, Pallas kernels for 8% -> 9%
where the time goes in v22:
time: 31.5 us; the launch traced here: 31.3 us
  blocking collectives  12.1 us (38%)
  starting transfers between devices  11 us (35%)
  Pallas kernels  4.76 us (15%)
  local copies, waits for them, and re-layouts  1.7 us (5%)
  waiting for transfers between devices  1.65 us (5%)
    all_to_all x1, blocking collectives, shards(): lax.all_to_all(terms, ('chan', 'freq'), split_axis=0, concat_axis=0, axis...  12.1 us
    ppermute x6, starting transfers between devices, shards(): chunks[key] = lax.ppermute(chunks[key], 'chan', pairs)  11 us
    pallas_call x2, Pallas kernels, shards(): pl.pallas_call(functools.partial(stack_kernel, order, start, size, parts...  2.41 us
    unnamed x6, local copies, waits for them, and re-layouts  1.7 us
    ppermute x6, waiting for transfers between devices, shards(): chunks[key] = lax.ppermute(chunks[key], 'chan', pairs)  1.65 us
    pallas_call x1, Pallas kernels, shards(): pl.pallas_call(functools.partial(table_kernel, groups, bins, freq_dev), o...  1.19 us
    pallas_call x1, Pallas kernels, shards(): pl.pallas_call(functools.partial(image_kernel, slow_dev, spans), out_shap...  0.89 us
  transfers between devices with their start and end apart: 6, of which 1 were waited for; matrix products, arithmetic and copies ran while one was open for 0% of the time, Pallas kernels for 9%

profile of v22, /device:TPU:0, one launch (start us, length us, event | category | flops | bytes accessed | tf_op | source)
XLA Modules:
  0.0 31.3 jit_solution(9721944218139048441)
XLA Ops:
  0.0 0.0 copy-start
  0.0 1.0 %copy-done = bf16[2,32,32,128]{3,2,1,0:T(8,128)(2,1)S(1)} copy-done((bf16[2,32,32,128]{3,2,1,0:T(8,128)(2,1)S(1)}, bf16[2,32,32,128]{3,2,1,0:T(8,128)(2,1)}, u32[]{:S(2)}) %copy-start) | copy-done | bytes 524312
  1.1 3.1 %collective-permute-start.3 = (bf16[5,64,128]{2,1,0:T(8,128)(2,1)S(1)}, bf16[5,64,128]{2,1,0:T(8,128)(2,1)S(1)}, u32[]{:S(2)}, u32[]{:S(2)}) collective-permute-start(bf16[5,64,128]{2,1,0:T(8,128)(2,1)S(1)} %chunks_of_bins.2.refs_0_), channel_id=1, source_target_pairs={{0,8},{8,16},{16,24},{24,0},{1,9},{9,17},{17,25},{25,1},{2,10},{10... | collective-permute-start | bytes 245768 | tf_op jit(solution)/shard_map/ppermute | solution.py:296
  4.2 0.2 chunks_of_bins.3
  4.4 2.7 %collective-permute-start.4 = (bf16[5,64,128]{2,1,0:T(8,128)(2,1)S(1)}, bf16[5,64,128]{2,1,0:T(8,128)(2,1)S(1)}, u32[]{:S(2)}, u32[]{:S(2)}) collective-permute-start(bf16[5,64,128]{2,1,0:T(8,128)(2,1)S(1)} %get-tuple-element.22), channel_id=1, source_target_pairs={{0,16},{8,24},{16,0},{24,8},{1,17},{9,25},{17,1},{25,9},{2,18},{10... | collective-permute-start | bytes 245768 | tf_op jit(solution)/shard_map/ppermute | solution.py:296
  7.0 1.3 %collective-permute-start.5 = (bf16[5,64,128]{2,1,0:T(8,128)(2,1)S(1)}, bf16[5,64,128]{2,1,0:T(8,128)(2,1)S(1)}, u32[]{:S(2)}, u32[]{:S(2)}) collective-permute-start(bf16[5,64,128]{2,1,0:T(8,128)(2,1)S(1)} %get-tuple-element.23), channel_id=1, source_target_pairs={{0,24},{8,0},{16,8},{24,16},{1,25},{9,1},{17,9},{25,17},{2,26},{10... | collective-permute-start | bytes 245768 | tf_op jit(solution)/shard_map/ppermute | solution.py:296
  8.4 0.1 collective-permute-start
  8.5 0.9 %collective-permute-start.1 = (bf16[3,64,128]{2,1,0:T(8,128)(2,1)S(1)}, bf16[3,64,128]{2,1,0:T(8,128)(2,1)S(1)}, u32[]{:S(2)}, u32[]{:S(2)}) collective-permute-start(bf16[3,64,128]{2,1,0:T(8,128)(2,1)S(1)} %get-tuple-element.16), channel_id=1, source_target_pairs={{0,8},{8,16},{16,24},{24,0},{1,9},{9,17},{17,25},{25,1},{2,10},{10... | collective-permute-start | bytes 147464 | tf_op jit(solution)/shard_map/ppermute | solution.py:296
  9.4 0.0 collective-permute-done.3.in_ref
  9.4 2.9 %collective-permute-start.2 = (bf16[3,64,128]{2,1,0:T(8,128)(2,1)S(1)}, bf16[3,64,128]{2,1,0:T(8,128)(2,1)S(1)}, u32[]{:S(2)}, u32[]{:S(2)}) collective-permute-start(bf16[3,64,128]{2,1,0:T(8,128)(2,1)S(1)} %get-tuple-element.17), channel_id=1, source_target_pairs={{0,24},{8,0},{16,8},{24,16},{1,25},{9,1},{17,9},{25,17},{2,26},{10... | collective-permute-start | bytes 147464 | tf_op jit(solution)/shard_map/ppermute | solution.py:296
  12.4 0.0 copy-start.2
  12.4 0.7 %copy-done.2 = s32[4]{0:T(128)S(1)} copy-done((s32[4]{0:T(128)S(1)}, s32[4]{0:T(128)}, u32[]{:S(2)}) %copy-start.2) | copy-done | bytes 40
  13.0 1.2 %slant_tables.1 = (s32[4,128]{1,0:T(4,128)S(1)}, bf16[8,256,512]{2,1,0:T(8,128)(2,1)S(1)}, f32[8,2,8,256]{3,2,1,0:T(8,128)S(1)}) custom-call(s32[1,4]{1,0:T(1,128)S(1)} %bitcast.6), custom_call_target="tpu_custom_call" | custom-call | flops 10000000 | bytes 4000000 | tf_op jit(solution)/shard_map/slant_tables/pallas_call | solution.py:305
  14.2 0.0 collective-permute-done.4.refs_1_
  14.2 0.0 collective-permute-done.5.refs_2_
  14.2 0.0 copy-start.1
  14.3 1.3 %stack_and_slant.2.refs_7_ = f32[10,4,256]{2,1,0:T(4,128)S(1)} custom-call(bf16[5,64,128]{2,1,0:T(8,128)(2,1)S(1)} %first_arrived.1.refs_0_, bf16[5,64,128]{2,1,0:T(8,128)(2,1)S(1)} %collective-permute-done.4.refs_1_, bf16[5,64,128]{2,1,0:T(8,128)(2,1)S(1)} %collective-permute-done.5.refs_2_, bf16[5,64,128]{2,1,0:T(8,128)(2,1)S(1)} %get-tuple-element.24.refs_3_, ...), custom_call_target="tpu_custom_call" | custom-call | flops 200000000 | bytes 4000000 | tf_op jit(solution)/shard_map/stack_and_slant/pallas_call | solution.py:322
  15.6 1.6 %collective-permute-done.refs_0_ = bf16[3,64,128]{2,1,0:T(8,128)(2,1)S(1)} collective-permute-done((bf16[3,64,128]{2,1,0:T(8,128)(2,1)S(1)}, bf16[3,64,128]{2,1,0:T(8,128)(2,1)S(1)}, u32[]{:S(2)}, u32[]{:S(2)}) %collective-permute-start) | collective-permute-done | bytes 49184 | tf_op jit(solution)/shard_map/ppermute | solution.py:296
  17.2 0.0 collective-permute-done.1.refs_1_
  17.2 0.0 collective-permute-done.2.refs_2_
  17.2 1.1 %stack_and_slant.3 = f32[4,8,4,128]{3,2,1,0:T(4,128)S(1)} custom-call(bf16[3,64,128]{2,1,0:T(8,128)(2,1)S(1)} %collective-permute-done.refs_0_, bf16[3,64,128]{2,1,0:T(8,128)(2,1)S(1)} %collective-permute-done.1.refs_1_, bf16[3,64,128]{2,1,0:T(8,128)(2,1)S(1)} %collective-permute-done.2.refs_2_, bf16[3,64,128]{2,1,0:T(8,128)(2,1)S(1)} %get-tuple-element.18.refs_3_, ...), custom_call_target="tpu_custom_call" | custom-call | flops 200000000 | bytes 4000000 | tf_op jit(solution)/shard_map/stack_and_slant/pallas_call | solution.py:322
  18.3 12.1 %all_to_all.5.term_ref = f32[32,4,128]{2,1,0:T(4,128)S(1)} all-to-all(f32[32,4,128]{2,1,0:T(4,128)S(1)} %bitcast.5), channel_id=1, replica_groups={{31,30,29,28,27,26,25,24,23,22,21,20,19,18,17,16,15,14,13,12,11,10,9,8,..., dimensions={0} | all-to-all | bytes 131072 | tf_op jit(solution)/shard_map/all_to_all | solution.py:346
  30.4 0.0 copy-done.1
  30.4 0.9 %sum_of_bins.1 = f32[1,32,512]{2,1,0:T(8,128)} custom-call(f32[32,4,128]{2,1,0:T(4,128)S(1)} %all_to_all.5.term_ref, bf16[2,2,256,256]{3,2,1,0:T(8,128)(2,1)S(1)} %copy-done.1), custom_call_target="tpu_custom_call" | custom-call | tf_op jit(solution)/shard_map/sum_of_bins/pallas_call | solution.py:355
  (2 shorter events, 0.1 us)
Async XLA Ops:
  0.0 1.0 %copy-start = (bf16[2,32,32,128]{3,2,1,0:T(8,128)(2,1)S(1)}, bf16[2,32,32,128]{3,2,1,0:T(8,128)(2,1)}, u32[]{:S(2)}) copy-start(bf16[2,32,32,128]{3,2,1,0:T(8,128)(2,1)} %param.3) | copy-start | bytes 1572868
  1.1 8.3 %collective-permute-start.3 = (bf16[5,64,128]{2,1,0:T(8,128)(2,1)S(1)}, bf16[5,64,128]{2,1,0:T(8,128)(2,1)S(1)}, u32[]{:S(2)}, u32[]{:S(2)}) collective-permute-start(bf16[5,64,128]{2,1,0:T(8,128)(2,1)S(1)} %chunks_of_bins.2.refs_0_), channel_id=1, source_target_pairs={{0,8},{8,16},{16,24},{24,0},{1,9},{9,17},{17,25},{25,1},{2,10},{10... | collective-permute-start | bytes 245768 | tf_op jit(solution)/shard_map/ppermute | solution.py:296
  4.4 9.8 %collective-permute-start.4 = (bf16[5,64,128]{2,1,0:T(8,128)(2,1)S(1)}, bf16[5,64,128]{2,1,0:T(8,128)(2,1)S(1)}, u32[]{:S(2)}, u32[]{:S(2)}) collective-permute-start(bf16[5,64,128]{2,1,0:T(8,128)(2,1)S(1)} %get-tuple-element.22), channel_id=1, source_target_pairs={{0,16},{8,24},{16,0},{24,8},{1,17},{9,25},{17,1},{25,9},{2,18},{10... | collective-permute-start | bytes 245768 | tf_op jit(solution)/shard_map/ppermute | solution.py:296
  7.0 7.2 %collective-permute-start.5 = (bf16[5,64,128]{2,1,0:T(8,128)(2,1)S(1)}, bf16[5,64,128]{2,1,0:T(8,128)(2,1)S(1)}, u32[]{:S(2)}, u32[]{:S(2)}) collective-permute-start(bf16[5,64,128]{2,1,0:T(8,128)(2,1)S(1)} %get-tuple-element.23), channel_id=1, source_target_pairs={{0,24},{8,0},{16,8},{24,16},{1,25},{9,1},{17,9},{25,17},{2,26},{10... | collective-permute-start | bytes 245768 | tf_op jit(solution)/shard_map/ppermute | solution.py:296
  8.4 8.8 %collective-permute-start = (bf16[3,64,128]{2,1,0:T(8,128)(2,1)S(1)}, bf16[3,64,128]{2,1,0:T(8,128)(2,1)S(1)}, u32[]{:S(2)}, u32[]{:S(2)}) collective-permute-start(bf16[3,64,128]{2,1,0:T(8,128)(2,1)S(1)} %get-tuple-element.15), channel_id=1, source_target_pairs={{0,16},{8,24},{16,0},{24,8},{1,17},{9,25},{17,1},{25,9},{2,18},{10... | collective-permute-start | bytes 147464 | tf_op jit(solution)/shard_map/ppermute | solution.py:296
  8.5 8.7 %collective-permute-start.1 = (bf16[3,64,128]{2,1,0:T(8,128)(2,1)S(1)}, bf16[3,64,128]{2,1,0:T(8,128)(2,1)S(1)}, u32[]{:S(2)}, u32[]{:S(2)}) collective-permute-start(bf16[3,64,128]{2,1,0:T(8,128)(2,1)S(1)} %get-tuple-element.16), channel_id=1, source_target_pairs={{0,8},{8,16},{16,24},{24,0},{1,9},{9,17},{17,25},{25,1},{2,10},{10... | collective-permute-start | bytes 147464 | tf_op jit(solution)/shard_map/ppermute | solution.py:296
  9.4 7.8 %collective-permute-start.2 = (bf16[3,64,128]{2,1,0:T(8,128)(2,1)S(1)}, bf16[3,64,128]{2,1,0:T(8,128)(2,1)S(1)}, u32[]{:S(2)}, u32[]{:S(2)}) collective-permute-start(bf16[3,64,128]{2,1,0:T(8,128)(2,1)S(1)} %get-tuple-element.17), channel_id=1, source_target_pairs={{0,24},{8,0},{16,8},{24,16},{1,25},{9,1},{17,9},{25,17},{2,26},{10... | collective-permute-start | bytes 147464 | tf_op jit(solution)/shard_map/ppermute | solution.py:296
  12.4 0.7 %copy-start.2 = (s32[4]{0:T(128)S(1)}, s32[4]{0:T(128)}, u32[]{:S(2)}) copy-start(s32[4]{0:T(128)} %param.4) | copy-start | bytes 52
  14.2 16.2 %copy-start.1 = (bf16[2,2,256,256]{3,2,1,0:T(8,128)(2,1)S(1)}, bf16[2,2,256,256]{3,2,1,0:T(8,128)(2,1)}, u32[]{:S(2)}) copy-start(bf16[2,2,256,256]{3,2,1,0:T(8,128)(2,1)} %constant.2.clone.table_ref) | copy-start | bytes 1572868

commit v23 on v22

--- a/solution.py
+++ b/solution.py
@@ -284,10 +284,8 @@
 
     late = max(1, 3 * bins // 8) if bins > 1 else 0
     pieces = [(0, bins - late), (bins - late, late)] if late else [(0, bins)]
-    near_first = list(range(1, groups)) + [0]
-    far_first = sorted(range(1, groups), key=lambda steps: abs(2 * steps - groups)) + [0]
-    orders = [near_first, far_first][: len(pieces)]
-    cuts = [(distance, *piece) for piece, order in zip(pieces, orders) for distance in order]
+    order = sorted(range(1, groups), key=lambda steps: abs(2 * steps - groups)) + [0]
+    cuts = [(distance, *piece) for piece in pieces for distance in order]
     (first_chunk,) = cut(cuts[:1])
     chunks = dict(zip(cuts, (first_chunk, *cut(cuts[1:], first_chunk))))
     for key in cuts:
@@ -316,7 +314,7 @@
         name="slant_tables",
     )(block_position.reshape(1, groups))
     earlier = []
-    for (start, size), order in zip(pieces, orders):
+    for start, size in pieces:
         last = start + size == bins
         shape = (groups, parts, message_rows, BLOCK) if last else (2 * size, groups, SLOWNESS)
         terms = pl.pallas_call(

time: 31.5 us -> 31.4 us (level)
  waiting for transfers between devices: 1.65 us -> 0.81 us
  blocking collectives: 12.1 us -> 12.5 us
  starting transfers between devices: 11 us -> 11.4 us
    ppermute x6, waiting for transfers between devices: 1.65 us -> 0.81 us  [shards(): chunks[key] = lax.ppermute(chunks[key], 'chan', pairs)]
    all_to_all x1, blocking collectives: 12.1 us -> 12.5 us  [shards(): lax.all_to_all(terms, ('chan', 'freq'), split_axis=0, concat_axis=0, axis...]
    ppermute x6, starting transfers between devices: 11 us -> 11.4 us  [shards(): chunks[key] = lax.ppermute(chunks[key], 'chan', pairs)]
where the time goes in v23:
time: 31.4 us; the launch traced here: 31.2 us
  blocking collectives  12.5 us (40%)
  starting transfers between devices  11.4 us (36%)
  Pallas kernels  4.78 us (15%)
  local copies, waits for them, and re-layouts  1.7 us (5%)
  waiting for transfers between devices  0.81 us (3%)
    all_to_all x1, blocking collectives, shards(): lax.all_to_all(terms, ('chan', 'freq'), split_axis=0, concat_axis=0, axis...  12.5 us
    ppermute x6, starting transfers between devices, shards(): chunks[key] = lax.ppermute(chunks[key], 'chan', pairs)  11.4 us
    pallas_call x2, Pallas kernels, shards(): pl.pallas_call(functools.partial(stack_kernel, order, start, size, parts...  2.43 us
    unnamed x6, local copies, waits for them, and re-layouts  1.7 us
    pallas_call x1, Pallas kernels, shards(): pl.pallas_call(functools.partial(table_kernel, groups, bins, freq_dev), o...  1.19 us
    pallas_call x1, Pallas kernels, shards(): pl.pallas_call(functools.partial(image_kernel, slow_dev, spans), out_shap...  0.89 us
    ppermute x6, waiting for transfers between devices, shards(): chunks[key] = lax.ppermute(chunks[key], 'chan', pairs)  0.81 us
  transfers between devices with their start and end apart: 6, of which 1 were waited for; matrix products, arithmetic and copies ran while one was open for 0% of the time, Pallas kernels for 9%

profile of v23, /device:TPU:0, one launch (start us, length us, event | category | flops | bytes accessed | tf_op | source)
XLA Modules:
  0.0 31.2 jit_solution(12127420396127019058)
XLA Ops:
  0.0 0.0 copy-start
  0.0 1.0 %copy-done = bf16[2,32,32,128]{3,2,1,0:T(8,128)(2,1)S(1)} copy-done((bf16[2,32,32,128]{3,2,1,0:T(8,128)(2,1)S(1)}, bf16[2,32,32,128]{3,2,1,0:T(8,128)(2,1)}, u32[]{:S(2)}) %copy-start) | copy-done | bytes 524312
  1.1 4.1 %collective-permute-start.3 = (bf16[5,64,128]{2,1,0:T(8,128)(2,1)S(1)}, bf16[5,64,128]{2,1,0:T(8,128)(2,1)S(1)}, u32[]{:S(2)}, u32[]{:S(2)}) collective-permute-start(bf16[5,64,128]{2,1,0:T(8,128)(2,1)S(1)} %chunks_of_bins.2.refs_0_), channel_id=1, source_target_pairs={{0,16},{8,24},{16,0},{24,8},{1,17},{9,25},{17,1},{25,9},{2,18},{10... | collective-permute-start | bytes 245768 | tf_op jit(solution)/shard_map/ppermute | solution.py:294
  5.2 0.2 chunks_of_bins.3
  5.4 1.6 %collective-permute-start.4 = (bf16[5,64,128]{2,1,0:T(8,128)(2,1)S(1)}, bf16[5,64,128]{2,1,0:T(8,128)(2,1)S(1)}, u32[]{:S(2)}, u32[]{:S(2)}) collective-permute-start(bf16[5,64,128]{2,1,0:T(8,128)(2,1)S(1)} %get-tuple-element.22), channel_id=1, source_target_pairs={{0,8},{8,16},{16,24},{24,0},{1,9},{9,17},{17,25},{25,1},{2,10},{10... | collective-permute-start | bytes 245768 | tf_op jit(solution)/shard_map/ppermute | solution.py:294
  7.0 2.2 %collective-permute-start.5 = (bf16[5,64,128]{2,1,0:T(8,128)(2,1)S(1)}, bf16[5,64,128]{2,1,0:T(8,128)(2,1)S(1)}, u32[]{:S(2)}, u32[]{:S(2)}) collective-permute-start(bf16[5,64,128]{2,1,0:T(8,128)(2,1)S(1)} %get-tuple-element.23), channel_id=1, source_target_pairs={{0,24},{8,0},{16,8},{24,16},{1,25},{9,1},{17,9},{25,17},{2,26},{10... | collective-permute-start | bytes 245768 | tf_op jit(solution)/shard_map/ppermute | solution.py:294
  9.3 0.0 collective-permute-start
  9.3 0.6 %collective-permute-start.1 = (bf16[3,64,128]{2,1,0:T(8,128)(2,1)S(1)}, bf16[3,64,128]{2,1,0:T(8,128)(2,1)S(1)}, u32[]{:S(2)}, u32[]{:S(2)}) collective-permute-start(bf16[3,64,128]{2,1,0:T(8,128)(2,1)S(1)} %get-tuple-element.16), channel_id=1, source_target_pairs={{0,8},{8,16},{16,24},{24,0},{1,9},{9,17},{17,25},{25,1},{2,10},{10... | collective-permute-start | bytes 147464 | tf_op jit(solution)/shard_map/ppermute | solution.py:294
  9.9 0.8 %collective-permute-done.3.in_ref = bf16[5,64,128]{2,1,0:T(8,128)(2,1)S(1)} collective-permute-done((bf16[5,64,128]{2,1,0:T(8,128)(2,1)S(1)}, bf16[5,64,128]{2,1,0:T(8,128)(2,1)S(1)}, u32[]{:S(2)}, u32[]{:S(2)}) %collective-permute-start.3) | collective-permute-done | bytes 81952 | tf_op jit(solution)/shard_map/ppermute | solution.py:294
  10.6 2.8 %collective-permute-start.2 = (bf16[3,64,128]{2,1,0:T(8,128)(2,1)S(1)}, bf16[3,64,128]{2,1,0:T(8,128)(2,1)S(1)}, u32[]{:S(2)}, u32[]{:S(2)}) collective-permute-start(bf16[3,64,128]{2,1,0:T(8,128)(2,1)S(1)} %get-tuple-element.17), channel_id=1, source_target_pairs={{0,24},{8,0},{16,8},{24,16},{1,25},{9,1},{17,9},{25,17},{2,26},{10... | collective-permute-start | bytes 147464 | tf_op jit(solution)/shard_map/ppermute | solution.py:294
  13.5 0.0 copy-start.2
  13.5 0.7 %copy-done.2 = s32[4]{0:T(128)S(1)} copy-done((s32[4]{0:T(128)S(1)}, s32[4]{0:T(128)}, u32[]{:S(2)}) %copy-start.2) | copy-done | bytes 40
  14.1 1.2 %slant_tables.1 = (s32[4,128]{1,0:T(4,128)S(1)}, bf16[8,256,512]{2,1,0:T(8,128)(2,1)S(1)}, f32[8,2,8,256]{3,2,1,0:T(8,128)S(1)}) custom-call(s32[1,4]{1,0:T(1,128)S(1)} %bitcast.6), custom_call_target="tpu_custom_call" | custom-call | flops 10000000 | bytes 4000000 | tf_op jit(solution)/shard_map/slant_tables/pallas_call | solution.py:303
  15.3 0.0 collective-permute-done.4.refs_1_
  15.4 0.0 collective-permute-done.5.refs_2_
  15.4 0.0 copy-start.1
  15.4 1.3 %stack_and_slant.2.refs_7_ = f32[10,4,256]{2,1,0:T(4,128)S(1)} custom-call(bf16[5,64,128]{2,1,0:T(8,128)(2,1)S(1)} %first_arrived.1.refs_0_, bf16[5,64,128]{2,1,0:T(8,128)(2,1)S(1)} %collective-permute-done.4.refs_1_, bf16[5,64,128]{2,1,0:T(8,128)(2,1)S(1)} %collective-permute-done.5.refs_2_, bf16[5,64,128]{2,1,0:T(8,128)(2,1)S(1)} %get-tuple-element.24.refs_3_, ...), custom_call_target="tpu_custom_call" | custom-call | flops 200000000 | bytes 4000000 | tf_op jit(solution)/shard_map/stack_and_slant/pallas_call | solution.py:320
  16.7 0.0 collective-permute-done.refs_0_
  16.7 0.0 collective-permute-done.1.refs_1_
  16.7 0.0 collective-permute-done.2.refs_2_
  16.7 1.1 %stack_and_slant.3 = f32[4,8,4,128]{3,2,1,0:T(4,128)S(1)} custom-call(bf16[3,64,128]{2,1,0:T(8,128)(2,1)S(1)} %collective-permute-done.refs_0_, bf16[3,64,128]{2,1,0:T(8,128)(2,1)S(1)} %collective-permute-done.1.refs_1_, bf16[3,64,128]{2,1,0:T(8,128)(2,1)S(1)} %collective-permute-done.2.refs_2_, bf16[3,64,128]{2,1,0:T(8,128)(2,1)S(1)} %get-tuple-element.18.refs_3_, ...), custom_call_target="tpu_custom_call" | custom-call | flops 200000000 | bytes 4000000 | tf_op jit(solution)/shard_map/stack_and_slant/pallas_call | solution.py:320
  17.9 12.5 %all_to_all.5.term_ref = f32[32,4,128]{2,1,0:T(4,128)S(1)} all-to-all(f32[32,4,128]{2,1,0:T(4,128)S(1)} %bitcast.5), channel_id=1, replica_groups={{31,30,29,28,27,26,25,24,23,22,21,20,19,18,17,16,15,14,13,12,11,10,9,8,..., dimensions={0} | all-to-all | bytes 131072 | tf_op jit(solution)/shard_map/all_to_all | solution.py:344
  30.4 0.0 copy-done.1
  30.4 0.9 %sum_of_bins.1 = f32[1,32,512]{2,1,0:T(8,128)} custom-call(f32[32,4,128]{2,1,0:T(4,128)S(1)} %all_to_all.5.term_ref, bf16[2,2,256,256]{3,2,1,0:T(8,128)(2,1)S(1)} %copy-done.1), custom_call_target="tpu_custom_call" | custom-call | tf_op jit(solution)/shard_map/sum_of_bins/pallas_call | solution.py:353
  (2 shorter events, 0.1 us)
Async XLA Ops:
  0.0 1.0 %copy-start = (bf16[2,32,32,128]{3,2,1,0:T(8,128)(2,1)S(1)}, bf16[2,32,32,128]{3,2,1,0:T(8,128)(2,1)}, u32[]{:S(2)}) copy-start(bf16[2,32,32,128]{3,2,1,0:T(8,128)(2,1)} %param.3) | copy-start | bytes 1572868
  1.1 9.5 %collective-permute-start.3 = (bf16[5,64,128]{2,1,0:T(8,128)(2,1)S(1)}, bf16[5,64,128]{2,1,0:T(8,128)(2,1)S(1)}, u32[]{:S(2)}, u32[]{:S(2)}) collective-permute-start(bf16[5,64,128]{2,1,0:T(8,128)(2,1)S(1)} %chunks_of_bins.2.refs_0_), channel_id=1, source_target_pairs={{0,16},{8,24},{16,0},{24,8},{1,17},{9,25},{17,1},{25,9},{2,18},{10... | collective-permute-start | bytes 245768 | tf_op jit(solution)/shard_map/ppermute | solution.py:294
  5.4 9.9 %collective-permute-start.4 = (bf16[5,64,128]{2,1,0:T(8,128)(2,1)S(1)}, bf16[5,64,128]{2,1,0:T(8,128)(2,1)S(1)}, u32[]{:S(2)}, u32[]{:S(2)}) collective-permute-start(bf16[5,64,128]{2,1,0:T(8,128)(2,1)S(1)} %get-tuple-element.22), channel_id=1, source_target_pairs={{0,8},{8,16},{16,24},{24,0},{1,9},{9,17},{17,25},{25,1},{2,10},{10... | collective-permute-start | bytes 245768 | tf_op jit(solution)/shard_map/ppermute | solution.py:294
  7.0 8.3 %collective-permute-start.5 = (bf16[5,64,128]{2,1,0:T(8,128)(2,1)S(1)}, bf16[5,64,128]{2,1,0:T(8,128)(2,1)S(1)}, u32[]{:S(2)}, u32[]{:S(2)}) collective-permute-start(bf16[5,64,128]{2,1,0:T(8,128)(2,1)S(1)} %get-tuple-element.23), channel_id=1, source_target_pairs={{0,24},{8,0},{16,8},{24,16},{1,25},{9,1},{17,9},{25,17},{2,26},{10... | collective-permute-start | bytes 245768 | tf_op jit(solution)/shard_map/ppermute | solution.py:294
  9.3 7.4 %collective-permute-start = (bf16[3,64,128]{2,1,0:T(8,128)(2,1)S(1)}, bf16[3,64,128]{2,1,0:T(8,128)(2,1)S(1)}, u32[]{:S(2)}, u32[]{:S(2)}) collective-permute-start(bf16[3,64,128]{2,1,0:T(8,128)(2,1)S(1)} %get-tuple-element.15), channel_id=1, source_target_pairs={{0,16},{8,24},{16,0},{24,8},{1,17},{9,25},{17,1},{25,9},{2,18},{10... | collective-permute-start | bytes 147464 | tf_op jit(solution)/shard_map/ppermute | solution.py:294
  9.3 7.4 %collective-permute-start.1 = (bf16[3,64,128]{2,1,0:T(8,128)(2,1)S(1)}, bf16[3,64,128]{2,1,0:T(8,128)(2,1)S(1)}, u32[]{:S(2)}, u32[]{:S(2)}) collective-permute-start(bf16[3,64,128]{2,1,0:T(8,128)(2,1)S(1)} %get-tuple-element.16), channel_id=1, source_target_pairs={{0,8},{8,16},{16,24},{24,0},{1,9},{9,17},{17,25},{25,1},{2,10},{10... | collective-permute-start | bytes 147464 | tf_op jit(solution)/shard_map/ppermute | solution.py:294
  10.6 6.1 %collective-permute-start.2 = (bf16[3,64,128]{2,1,0:T(8,128)(2,1)S(1)}, bf16[3,64,128]{2,1,0:T(8,128)(2,1)S(1)}, u32[]{:S(2)}, u32[]{:S(2)}) collective-permute-start(bf16[3,64,128]{2,1,0:T(8,128)(2,1)S(1)} %get-tuple-element.17), channel_id=1, source_target_pairs={{0,24},{8,0},{16,8},{24,16},{1,25},{9,1},{17,9},{25,17},{2,26},{10... | collective-permute-start | bytes 147464 | tf_op jit(solution)/shard_map/ppermute | solution.py:294
  13.5 0.7 %copy-start.2 = (s32[4]{0:T(128)S(1)}, s32[4]{0:T(128)}, u32[]{:S(2)}) copy-start(s32[4]{0:T(128)} %param.4) | copy-start | bytes 52
  15.4 15.0 %copy-start.1 = (bf16[2,2,256,256]{3,2,1,0:T(8,128)(2,1)S(1)}, bf16[2,2,256,256]{3,2,1,0:T(8,128)(2,1)}, u32[]{:S(2)}) copy-start(bf16[2,2,256,256]{3,2,1,0:T(8,128)(2,1)} %constant.2.clone.table_ref) | copy-start | bytes 1572868

commit v24 on v22

--- a/solution.py
+++ b/solution.py
@@ -282,11 +282,11 @@
             name="chunks_of_bins",
         )(whole, *earlier)
 
-    late = max(1, 3 * bins // 8) if bins > 1 else 0
+    late = max(1, bins // 4) if bins > 1 else 0
     pieces = [(0, bins - late), (bins - late, late)] if late else [(0, bins)]
+    far_first = sorted(range(1, groups), key=lambda steps: abs(2 * steps - groups)) + [0]
     near_first = list(range(1, groups)) + [0]
-    far_first = sorted(range(1, groups), key=lambda steps: abs(2 * steps - groups)) + [0]
-    orders = [near_first, far_first][: len(pieces)]
+    orders = [far_first, near_first][: len(pieces)]
     cuts = [(distance, *piece) for piece, order in zip(pieces, orders) for distance in order]
     (first_chunk,) = cut(cuts[:1])
     chunks = dict(zip(cuts, (first_chunk, *cut(cuts[1:], first_chunk))))

time: 31.5 us -> 32.1 us (1.019)
  waiting for transfers between devices: 1.65 us -> 3.49 us
  starting transfers between devices: 11 us -> 9.73 us
    ppermute x6, waiting for transfers between devices: 1.65 us -> 3.49 us  [shards(): chunks[key] = lax.ppermute(chunks[key], 'chan', pairs)]
    ppermute x6, starting transfers between devices: 11 us -> 9.73 us  [shards(): chunks[key] = lax.ppermute(chunks[key], 'chan', pairs)]
where the time goes in v24:
time: 32.1 us; the launch traced here: 31.9 us
  blocking collectives  12.1 us (38%)
  starting transfers between devices  9.73 us (30%)
  Pallas kernels  4.77 us (15%)
  waiting for transfers between devices  3.49 us (11%)
  local copies, waits for them, and re-layouts  1.7 us (5%)
    all_to_all x1, blocking collectives, shards(): lax.all_to_all(terms, ('chan', 'freq'), split_axis=0, concat_axis=0, axis...  12.1 us
    ppermute x6, starting transfers between devices, shards(): chunks[key] = lax.ppermute(chunks[key], 'chan', pairs)  9.73 us
    ppermute x6, waiting for transfers between devices, shards(): chunks[key] = lax.ppermute(chunks[key], 'chan', pairs)  3.49 us
    pallas_call x2, Pallas kernels, shards(): pl.pallas_call(functools.partial(stack_kernel, order, start, size, parts...  2.42 us
    unnamed x6, local copies, waits for them, and re-layouts  1.7 us
    pallas_call x1, Pallas kernels, shards(): pl.pallas_call(functools.partial(table_kernel, groups, bins, freq_dev), o...  1.19 us
    pallas_call x1, Pallas kernels, shards(): pl.pallas_call(functools.partial(image_kernel, slow_dev, spans), out_shap...  0.89 us
  transfers between devices with their start and end apart: 6, of which 1 were waited for; matrix products, arithmetic and copies ran while one was open for 0% of the time, Pallas kernels for 9%

profile of v24, /device:TPU:0, one launch (start us, length us, event | category | flops | bytes accessed | tf_op | source)
XLA Modules:
  0.0 31.9 jit_solution(1950660123225408941)
XLA Ops:
  0.0 1.0 %copy-done = bf16[2,32,32,128]{3,2,1,0:T(8,128)(2,1)S(1)} copy-done((bf16[2,32,32,128]{3,2,1,0:T(8,128)(2,1)S(1)}, bf16[2,32,32,128]{3,2,1,0:T(8,128)(2,1)}, u32[]{:S(2)}) %copy-start) | copy-done | bytes 524312
  1.0 0.1 chunks_of_bins.2.refs_0_
  1.1 4.1 %collective-permute-start.3 = (bf16[6,64,128]{2,1,0:T(8,128)(2,1)S(1)}, bf16[6,64,128]{2,1,0:T(8,128)(2,1)S(1)}, u32[]{:S(2)}, u32[]{:S(2)}) collective-permute-start(bf16[6,64,128]{2,1,0:T(8,128)(2,1)S(1)} %chunks_of_bins.2.refs_0_), channel_id=1, source_target_pairs={{0,16},{8,24},{16,0},{24,8},{1,17},{9,25},{17,1},{25,9},{2,18},{10... | collective-permute-start | bytes 294920 | tf_op jit(solution)/shard_map/ppermute | solution.py:296
  5.2 0.2 chunks_of_bins.3
  5.4 1.6 %collective-permute-start.4 = (bf16[6,64,128]{2,1,0:T(8,128)(2,1)S(1)}, bf16[6,64,128]{2,1,0:T(8,128)(2,1)S(1)}, u32[]{:S(2)}, u32[]{:S(2)}) collective-permute-start(bf16[6,64,128]{2,1,0:T(8,128)(2,1)S(1)} %get-tuple-element.22), channel_id=1, source_target_pairs={{0,8},{8,16},{16,24},{24,0},{1,9},{9,17},{17,25},{25,1},{2,10},{10... | collective-permute-start | bytes 294920 | tf_op jit(solution)/shard_map/ppermute | solution.py:296
  7.0 2.2 %collective-permute-start.5 = (bf16[6,64,128]{2,1,0:T(8,128)(2,1)S(1)}, bf16[6,64,128]{2,1,0:T(8,128)(2,1)S(1)}, u32[]{:S(2)}, u32[]{:S(2)}) collective-permute-start(bf16[6,64,128]{2,1,0:T(8,128)(2,1)S(1)} %get-tuple-element.23), channel_id=1, source_target_pairs={{0,24},{8,0},{16,8},{24,16},{1,25},{9,1},{17,9},{25,17},{2,26},{10... | collective-permute-start | bytes 294920 | tf_op jit(solution)/shard_map/ppermute | solution.py:296
  9.3 0.0 collective-permute-start
  9.3 0.6 %collective-permute-start.1 = (bf16[2,64,128]{2,1,0:T(8,128)(2,1)S(1)}, bf16[2,64,128]{2,1,0:T(8,128)(2,1)S(1)}, u32[]{:S(2)}, u32[]{:S(2)}) collective-permute-start(bf16[2,64,128]{2,1,0:T(8,128)(2,1)S(1)} %get-tuple-element.16), channel_id=1, source_target_pairs={{0,16},{8,24},{16,0},{24,8},{1,17},{9,25},{17,1},{25,9},{2,18},{10... | collective-permute-start | bytes 98312 | tf_op jit(solution)/shard_map/ppermute | solution.py:296
  9.9 3.5 %collective-permute-done.3.in_ref = bf16[6,64,128]{2,1,0:T(8,128)(2,1)S(1)} collective-permute-done((bf16[6,64,128]{2,1,0:T(8,128)(2,1)S(1)}, bf16[6,64,128]{2,1,0:T(8,128)(2,1)S(1)}, u32[]{:S(2)}, u32[]{:S(2)}) %collective-permute-start.3) | collective-permute-done | bytes 98336 | tf_op jit(solution)/shard_map/ppermute | solution.py:296
  13.3 1.2 %collective-permute-start.2 = (bf16[2,64,128]{2,1,0:T(8,128)(2,1)S(1)}, bf16[2,64,128]{2,1,0:T(8,128)(2,1)S(1)}, u32[]{:S(2)}, u32[]{:S(2)}) collective-permute-start(bf16[2,64,128]{2,1,0:T(8,128)(2,1)S(1)} %get-tuple-element.17), channel_id=1, source_target_pairs={{0,24},{8,0},{16,8},{24,16},{1,25},{9,1},{17,9},{25,17},{2,26},{10... | collective-permute-start | bytes 98312 | tf_op jit(solution)/shard_map/ppermute | solution.py:296
  14.5 0.0 copy-start.2
  14.5 0.7 %copy-done.2 = s32[4]{0:T(128)S(1)} copy-done((s32[4]{0:T(128)S(1)}, s32[4]{0:T(128)}, u32[]{:S(2)}) %copy-start.2) | copy-done | bytes 40
  15.2 1.2 %slant_tables.1 = (s32[4,128]{1,0:T(4,128)S(1)}, bf16[8,256,512]{2,1,0:T(8,128)(2,1)S(1)}, f32[8,2,8,256]{3,2,1,0:T(8,128)S(1)}) custom-call(s32[1,4]{1,0:T(1,128)S(1)} %bitcast.6), custom_call_target="tpu_custom_call" | custom-call | flops 10000000 | bytes 4000000 | tf_op jit(solution)/shard_map/slant_tables/pallas_call | solution.py:305
  16.4 0.0 collective-permute-done.4.refs_1_
  16.4 0.0 collective-permute-done.5.refs_2_
  16.4 0.0 copy-start.1
  16.4 1.5 %stack_and_slant.2.refs_7_ = f32[12,4,256]{2,1,0:T(4,128)S(1)} custom-call(bf16[6,64,128]{2,1,0:T(8,128)(2,1)S(1)} %first_arrived.1.refs_0_, bf16[6,64,128]{2,1,0:T(8,128)(2,1)S(1)} %collective-permute-done.4.refs_1_, bf16[6,64,128]{2,1,0:T(8,128)(2,1)S(1)} %collective-permute-done.5.refs_2_, bf16[6,64,128]{2,1,0:T(8,128)(2,1)S(1)} %get-tuple-element.24.refs_3_, ...), custom_call_target="tpu_custom_call" | custom-call | flops 200000000 | bytes 4000000 | tf_op jit(solution)/shard_map/stack_and_slant/pallas_call | solution.py:322
  17.9 0.0 collective-permute-done.refs_0_
  17.9 0.0 collective-permute-done.1.refs_1_
  17.9 0.0 collective-permute-done.2.refs_2_
  17.9 0.9 %stack_and_slant.3 = f32[4,8,4,128]{3,2,1,0:T(4,128)S(1)} custom-call(bf16[2,64,128]{2,1,0:T(8,128)(2,1)S(1)} %collective-permute-done.refs_0_, bf16[2,64,128]{2,1,0:T(8,128)(2,1)S(1)} %collective-permute-done.1.refs_1_, bf16[2,64,128]{2,1,0:T(8,128)(2,1)S(1)} %collective-permute-done.2.refs_2_, bf16[2,64,128]{2,1,0:T(8,128)(2,1)S(1)} %get-tuple-element.18.refs_3_, ...), custom_call_target="tpu_custom_call" | custom-call | flops 200000000 | bytes 4000000 | tf_op jit(solution)/shard_map/stack_and_slant/pallas_call | solution.py:322
  18.9 12.1 %all_to_all.5.term_ref = f32[32,4,128]{2,1,0:T(4,128)S(1)} all-to-all(f32[32,4,128]{2,1,0:T(4,128)S(1)} %bitcast.5), channel_id=1, replica_groups={{31,30,29,28,27,26,25,24,23,22,21,20,19,18,17,16,15,14,13,12,11,10,9,8,..., dimensions={0} | all-to-all | bytes 131072 | tf_op jit(solution)/shard_map/all_to_all | solution.py:346
  31.0 0.0 copy-done.1
  31.0 0.9 %sum_of_bins.1 = f32[1,32,512]{2,1,0:T(8,128)} custom-call(f32[32,4,128]{2,1,0:T(4,128)S(1)} %all_to_all.5.term_ref, bf16[2,2,256,256]{3,2,1,0:T(8,128)(2,1)S(1)} %copy-done.1), custom_call_target="tpu_custom_call" | custom-call | tf_op jit(solution)/shard_map/sum_of_bins/pallas_call | solution.py:355
  (2 shorter events, 0.0 us)
Async XLA Ops:
  0.0 1.0 %copy-start = (bf16[2,32,32,128]{3,2,1,0:T(8,128)(2,1)S(1)}, bf16[2,32,32,128]{3,2,1,0:T(8,128)(2,1)}, u32[]{:S(2)}) copy-start(bf16[2,32,32,128]{3,2,1,0:T(8,128)(2,1)} %param.3) | copy-start | bytes 1572868
  1.1 12.2 %collective-permute-start.3 = (bf16[6,64,128]{2,1,0:T(8,128)(2,1)S(1)}, bf16[6,64,128]{2,1,0:T(8,128)(2,1)S(1)}, u32[]{:S(2)}, u32[]{:S(2)}) collective-permute-start(bf16[6,64,128]{2,1,0:T(8,128)(2,1)S(1)} %chunks_of_bins.2.refs_0_), channel_id=1, source_target_pairs={{0,16},{8,24},{16,0},{24,8},{1,17},{9,25},{17,1},{25,9},{2,18},{10... | collective-permute-start | bytes 294920 | tf_op jit(solution)/shard_map/ppermute | solution.py:296
  5.4 11.0 %collective-permute-start.4 = (bf16[6,64,128]{2,1,0:T(8,128)(2,1)S(1)}, bf16[6,64,128]{2,1,0:T(8,128)(2,1)S(1)}, u32[]{:S(2)}, u32[]{:S(2)}) collective-permute-start(bf16[6,64,128]{2,1,0:T(8,128)(2,1)S(1)} %get-tuple-element.22), channel_id=1, source_target_pairs={{0,8},{8,16},{16,24},{24,0},{1,9},{9,17},{17,25},{25,1},{2,10},{10... | collective-permute-start | bytes 294920 | tf_op jit(solution)/shard_map/ppermute | solution.py:296
  7.0 9.4 %collective-permute-start.5 = (bf16[6,64,128]{2,1,0:T(8,128)(2,1)S(1)}, bf16[6,64,128]{2,1,0:T(8,128)(2,1)S(1)}, u32[]{:S(2)}, u32[]{:S(2)}) collective-permute-start(bf16[6,64,128]{2,1,0:T(8,128)(2,1)S(1)} %get-tuple-element.23), channel_id=1, source_target_pairs={{0,24},{8,0},{16,8},{24,16},{1,25},{9,1},{17,9},{25,17},{2,26},{10... | collective-permute-start | bytes 294920 | tf_op jit(solution)/shard_map/ppermute | solution.py:296
  9.3 8.6 %collective-permute-start = (bf16[2,64,128]{2,1,0:T(8,128)(2,1)S(1)}, bf16[2,64,128]{2,1,0:T(8,128)(2,1)S(1)}, u32[]{:S(2)}, u32[]{:S(2)}) collective-permute-start(bf16[2,64,128]{2,1,0:T(8,128)(2,1)S(1)} %get-tuple-element.15), channel_id=1, source_target_pairs={{0,8},{8,16},{16,24},{24,0},{1,9},{9,17},{17,25},{25,1},{2,10},{10... | collective-permute-start | bytes 98312 | tf_op jit(solution)/shard_map/ppermute | solution.py:296
  9.3 8.6 %collective-permute-start.1 = (bf16[2,64,128]{2,1,0:T(8,128)(2,1)S(1)}, bf16[2,64,128]{2,1,0:T(8,128)(2,1)S(1)}, u32[]{:S(2)}, u32[]{:S(2)}) collective-permute-start(bf16[2,64,128]{2,1,0:T(8,128)(2,1)S(1)} %get-tuple-element.16), channel_id=1, source_target_pairs={{0,16},{8,24},{16,0},{24,8},{1,17},{9,25},{17,1},{25,9},{2,18},{10... | collective-permute-start | bytes 98312 | tf_op jit(solution)/shard_map/ppermute | solution.py:296
  13.3 4.6 %collective-permute-start.2 = (bf16[2,64,128]{2,1,0:T(8,128)(2,1)S(1)}, bf16[2,64,128]{2,1,0:T(8,128)(2,1)S(1)}, u32[]{:S(2)}, u32[]{:S(2)}) collective-permute-start(bf16[2,64,128]{2,1,0:T(8,128)(2,1)S(1)} %get-tuple-element.17), channel_id=1, source_target_pairs={{0,24},{8,0},{16,8},{24,16},{1,25},{9,1},{17,9},{25,17},{2,26},{10... | collective-permute-start | bytes 98312 | tf_op jit(solution)/shard_map/ppermute | solution.py:296
  14.5 0.7 %copy-start.2 = (s32[4]{0:T(128)S(1)}, s32[4]{0:T(128)}, u32[]{:S(2)}) copy-start(s32[4]{0:T(128)} %param.4) | copy-start | bytes 52
  16.4 14.6 %copy-start.1 = (bf16[2,2,256,256]{3,2,1,0:T(8,128)(2,1)S(1)}, bf16[2,2,256,256]{3,2,1,0:T(8,128)(2,1)}, u32[]{:S(2)}) copy-start(bf16[2,2,256,256]{3,2,1,0:T(8,128)(2,1)} %constant.2.clone.table_ref) | copy-start | bytes 1572868

commit v25 on v23

--- a/solution.py
+++ b/solution.py
@@ -89,7 +89,8 @@
         if distance not in widened:
             group = lax.rem(own_group + distance, groups)
             index = len(widened)
-            wide_ref[index] = spec_ref[:, group].astype(jnp.float32).reshape(rows * bins, BLOCK)
+            value = spec_ref[:, group].astype(jnp.float32).reshape(rows * bins, BLOCK)
+            wide_ref[index, : rows * bins] = value
             widened.append(distance)
         for f in range(size):
             value = wide_ref[widened.index(distance), pl.ds(start + f, rows, stride=bins), :]
@@ -117,7 +118,8 @@
     windows = rows // 2
     places = place_ref[...]
     for distance, chunk_ref in zip(order, chunk_refs):
-        placed_ref[places[distance, 0]] = chunk_ref[...]
+        skip = start if chunk_ref.shape[0] > bins else 0
+        placed_ref[places[distance, 0]] = chunk_ref[skip : skip + bins]
 
     row_index = lax.broadcasted_iota(jnp.int32, (BLOCK, BLOCK), 0)
     lag_index = lax.broadcasted_iota(jnp.int32, (BLOCK, BLOCK), 1)
@@ -276,7 +278,7 @@
             ),
             in_specs=[vmem] + [anywhere] * len(earlier),
             out_specs=(vmem,) * len(cuts),
-            scratch_shapes=[pltpu.VMEM((len(distances), rows * bins, BLOCK), jnp.float32)],
+            scratch_shapes=[pltpu.VMEM((len(distances), (rows + 1) * bins, BLOCK), jnp.float32)],
             compiler_params=params,
             cost_estimate=pl.CostEstimate(flops=10**7, bytes_accessed=10**6, transcendentals=0),
             name="chunks_of_bins",
@@ -284,8 +286,15 @@
 
     late = max(1, 3 * bins // 8) if bins > 1 else 0
     pieces = [(0, bins - late), (bins - late, late)] if late else [(0, bins)]
-    order = sorted(range(1, groups), key=lambda steps: abs(2 * steps - groups)) + [0]
-    cuts = [(distance, *piece) for piece in pieces for distance in order]
+    far_first = sorted(range(1, groups), key=lambda steps: abs(2 * steps - groups))
+    kept, split = far_first[0], far_first[1:]
+    orders = [[kept] + split + [0], [kept] + split[::-1] + [0]][: len(pieces)]
+    parts_of = {
+        (distance, piece): (distance, *(piece if distance in split else (0, bins)))
+        for piece, order in zip(pieces, orders)
+        for distance in order
+    }
+    cuts = list(dict.fromkeys(parts_of.values()))
     (first_chunk,) = cut(cuts[:1])
     chunks = dict(zip(cuts, (first_chunk, *cut(cuts[1:], first_chunk))))
     for key in cuts:
@@ -314,7 +323,7 @@
         name="slant_tables",
     )(block_position.reshape(1, groups))
     earlier = []
-    for start, size in pieces:
+    for (start, size), order in zip(pieces, orders):
         last = start + size == bins
         shape = (groups, parts, message_rows, BLOCK) if last else (2 * size, groups, SLOWNESS)
         terms = pl.pallas_call(
@@ -325,7 +334,7 @@
             scratch_shapes=[
                 pltpu.VMEM((groups, size, rows, BLOCK), jnp.bfloat16),
                 pltpu.VMEM((size, BLOCK, groups * rows), jnp.bfloat16),
-                pltpu.VMEM((2, size * 2 * groups * 8, BLOCK), jnp.float32),
+                pltpu.VMEM((2, (size * 2 * groups + 1) * 8, BLOCK), jnp.float32),
             ],
             compiler_params=params,
             cost_estimate=pl.CostEstimate(
@@ -333,7 +342,7 @@
             ),
             name="stack_and_slant",
         )(
-            *[chunks[distance, start, size] for distance in order],
+            *[chunks[parts_of[distance, (start, size)]] for distance in order],
             places,
             lag_table,
             shift_table,

time: 31.4 us -> 31.8 us (1.013)
  waiting for transfers between devices: 0.81 us -> 2.58 us
  starting transfers between devices: 11.4 us -> 10 us
    ppermute x6 -> x5, waiting for transfers between devices: 0.81 us -> 2.58 us  [shards(): chunks[key] = lax.ppermute(chunks[key], 'chan', pairs)]
    ppermute x6 -> x5, starting transfers between devices: 11.4 us -> 10 us  [shards(): chunks[key] = lax.ppermute(chunks[key], 'chan', pairs)]
  transfers between devices with their start and end apart: 6 -> 5, of which waited for: 1 -> 2; matrix products, arithmetic and copies ran while one was open for 0% -> 0% of each run, Pallas kernels for 9% -> 9%
where the time goes in v25:
time: 31.8 us; the launch traced here: 31.6 us
  blocking collectives  12.5 us (39%)
  starting transfers between devices  10 us (31%)
  Pallas kernels  4.76 us (15%)
  waiting for transfers between devices  2.58 us (8%)
  local copies, waits for them, and re-layouts  1.7 us (5%)
    all_to_all x1, blocking collectives, shards(): lax.all_to_all(terms, ('chan', 'freq'), split_axis=0, concat_axis=0, axis...  12.5 us
    ppermute x5, starting transfers between devices, shards(): chunks[key] = lax.ppermute(chunks[key], 'chan', pairs)  10 us
    ppermute x5, waiting for transfers between devices, shards(): chunks[key] = lax.ppermute(chunks[key], 'chan', pairs)  2.58 us
    pallas_call x2, Pallas kernels, shards(): pl.pallas_call(functools.partial(stack_kernel, order, start, size, parts...  2.43 us
    unnamed x6, local copies, waits for them, and re-layouts  1.7 us
    pallas_call x1, Pallas kernels, shards(): pl.pallas_call(functools.partial(table_kernel, groups, bins, freq_dev), o...  1.19 us
    pallas_call x1, Pallas kernels, shards(): pl.pallas_call(functools.partial(image_kernel, slow_dev, spans), out_shap...  0.88 us
  transfers between devices with their start and end apart: 5, of which 2 were waited for; matrix products, arithmetic and copies ran while one was open for 0% of the time, Pallas kernels for 9%

profile of v25, /device:TPU:0, one launch (start us, length us, event | category | flops | bytes accessed | tf_op | source)
XLA Modules:
  0.0 31.6 jit_solution(3601935728663621424)
XLA Ops:
  0.0 0.0 copy-start
  0.0 1.0 %copy-done = bf16[2,32,32,128]{3,2,1,0:T(8,128)(2,1)S(1)} copy-done((bf16[2,32,32,128]{3,2,1,0:T(8,128)(2,1)S(1)}, bf16[2,32,32,128]{3,2,1,0:T(8,128)(2,1)}, u32[]{:S(2)}) %copy-start) | copy-done | bytes 524312
  1.0 0.1 chunks_of_bins.2.refs_0_
  1.1 4.1 %collective-permute-start = (bf16[8,64,128]{2,1,0:T(8,128)(2,1)S(1)}, bf16[8,64,128]{2,1,0:T(8,128)(2,1)S(1)}, u32[]{:S(2)}, u32[]{:S(2)}) collective-permute-start(bf16[8,64,128]{2,1,0:T(8,128)(2,1)S(1)} %chunks_of_bins.2.refs_0_), channel_id=1, source_target_pairs={{0,16},{8,24},{16,0},{24,8},{1,17},{9,25},{17,1},{25,9},{2,18},{10... | collective-permute-start | bytes 393224 | tf_op jit(solution)/shard_map/ppermute | solution.py:303
  5.2 0.2 chunks_of_bins.3
  5.4 1.6 %collective-permute-start.3 = (bf16[5,64,128]{2,1,0:T(8,128)(2,1)S(1)}, bf16[5,64,128]{2,1,0:T(8,128)(2,1)S(1)}, u32[]{:S(2)}, u32[]{:S(2)}) collective-permute-start(bf16[5,64,128]{2,1,0:T(8,128)(2,1)S(1)} %get-tuple-element.19), channel_id=1, source_target_pairs={{0,8},{8,16},{16,24},{24,0},{1,9},{9,17},{17,25},{25,1},{2,10},{10... | collective-permute-start | bytes 245768 | tf_op jit(solution)/shard_map/ppermute | solution.py:303
  7.0 2.2 %collective-permute-start.4 = (bf16[5,64,128]{2,1,0:T(8,128)(2,1)S(1)}, bf16[5,64,128]{2,1,0:T(8,128)(2,1)S(1)}, u32[]{:S(2)}, u32[]{:S(2)}) collective-permute-start(bf16[5,64,128]{2,1,0:T(8,128)(2,1)S(1)} %get-tuple-element.20), channel_id=1, source_target_pairs={{0,24},{8,0},{16,8},{24,16},{1,25},{9,1},{17,9},{25,17},{2,26},{10... | collective-permute-start | bytes 245768 | tf_op jit(solution)/shard_map/ppermute | solution.py:303
  9.3 0.0 collective-permute-start.1
  9.3 2.0 %collective-permute-start.2 = (bf16[3,64,128]{2,1,0:T(8,128)(2,1)S(1)}, bf16[3,64,128]{2,1,0:T(8,128)(2,1)S(1)}, u32[]{:S(2)}, u32[]{:S(2)}) collective-permute-start(bf16[3,64,128]{2,1,0:T(8,128)(2,1)S(1)} %get-tuple-element.14), channel_id=1, source_target_pairs={{0,8},{8,16},{16,24},{24,0},{1,9},{9,17},{17,25},{25,1},{2,10},{10... | collective-permute-start | bytes 147464 | tf_op jit(solution)/shard_map/ppermute | solution.py:303
  11.3 0.0 copy-start.2
  11.3 0.7 %copy-done.2 = s32[4]{0:T(128)S(1)} copy-done((s32[4]{0:T(128)S(1)}, s32[4]{0:T(128)}, u32[]{:S(2)}) %copy-start.2) | copy-done | bytes 40
  12.0 1.2 %slant_tables.1 = (s32[4,128]{1,0:T(4,128)S(1)}, bf16[8,256,512]{2,1,0:T(8,128)(2,1)S(1)}, f32[8,2,8,256]{3,2,1,0:T(8,128)S(1)}) custom-call(s32[1,4]{1,0:T(1,128)S(1)} %bitcast.6), custom_call_target="tpu_custom_call" | custom-call | flops 10000000 | bytes 4000000 | tf_op jit(solution)/shard_map/slant_tables/pallas_call | solution.py:312
  13.1 1.5 %collective-permute-done.in_ref = bf16[8,64,128]{2,1,0:T(8,128)(2,1)S(1)} collective-permute-done((bf16[8,64,128]{2,1,0:T(8,128)(2,1)S(1)}, bf16[8,64,128]{2,1,0:T(8,128)(2,1)S(1)}, u32[]{:S(2)}, u32[]{:S(2)}) %collective-permute-start) | collective-permute-done | bytes 131104 | tf_op jit(solution)/shard_map/ppermute | solution.py:303
  14.7 0.0 collective-permute-done.3.refs_1_
  14.7 1.1 %collective-permute-done.4.refs_2_ = bf16[5,64,128]{2,1,0:T(8,128)(2,1)S(1)} collective-permute-done((bf16[5,64,128]{2,1,0:T(8,128)(2,1)S(1)}, bf16[5,64,128]{2,1,0:T(8,128)(2,1)S(1)}, u32[]{:S(2)}, u32[]{:S(2)}) %collective-permute-start.4) | collective-permute-done | bytes 81952 | tf_op jit(solution)/shard_map/ppermute | solution.py:303
  15.7 0.0 copy-start.1
  15.7 1.3 %stack_and_slant.2.refs_7_ = f32[10,4,256]{2,1,0:T(4,128)S(1)} custom-call(bf16[8,64,128]{2,1,0:T(8,128)(2,1)S(1)} %first_arrived.1.refs_0_, bf16[5,64,128]{2,1,0:T(8,128)(2,1)S(1)} %collective-permute-done.3.refs_1_, bf16[5,64,128]{2,1,0:T(8,128)(2,1)S(1)} %collective-permute-done.4.refs_2_, bf16[8,64,128]{2,1,0:T(8,128)(2,1)S(1)} %get-tuple-element.15.refs_3_, ...), custom_call_target="tpu_custom_call" | custom-call | flops 200000000 | bytes 4000000 | tf_op jit(solution)/shard_map/stack_and_slant/pallas_call | solution.py:329
  17.1 0.0 collective-permute-done.1.refs_1_
  17.1 0.0 collective-permute-done.2.refs_2_
  17.1 1.1 %stack_and_slant.3 = f32[4,8,4,128]{3,2,1,0:T(4,128)S(1)} custom-call(bf16[8,64,128]{2,1,0:T(8,128)(2,1)S(1)} %first_arrived.1.refs_0_, bf16[3,64,128]{2,1,0:T(8,128)(2,1)S(1)} %collective-permute-done.1.refs_1_, bf16[3,64,128]{2,1,0:T(8,128)(2,1)S(1)} %collective-permute-done.2.refs_2_, bf16[8,64,128]{2,1,0:T(8,128)(2,1)S(1)} %get-tuple-element.15.refs_3_, ...), custom_call_target="tpu_custom_call" | custom-call | flops 200000000 | bytes 4000000 | tf_op jit(solution)/shard_map/stack_and_slant/pallas_call | solution.py:329
  18.2 12.5 %all_to_all.5.term_ref = f32[32,4,128]{2,1,0:T(4,128)S(1)} all-to-all(f32[32,4,128]{2,1,0:T(4,128)S(1)} %bitcast.5), channel_id=1, replica_groups={{31,30,29,28,27,26,25,24,23,22,21,20,19,18,17,16,15,14,13,12,11,10,9,8,..., dimensions={0} | all-to-all | bytes 131072 | tf_op jit(solution)/shard_map/all_to_all | solution.py:353
  30.7 0.0 copy-done.1
  30.7 0.9 %sum_of_bins.1 = f32[1,32,512]{2,1,0:T(8,128)} custom-call(f32[32,4,128]{2,1,0:T(4,128)S(1)} %all_to_all.5.term_ref, bf16[2,2,256,256]{3,2,1,0:T(8,128)(2,1)S(1)} %copy-done.1), custom_call_target="tpu_custom_call" | custom-call | tf_op jit(solution)/shard_map/sum_of_bins/pallas_call | solution.py:362
  (1 shorter events, 0.0 us)
Async XLA Ops:
  0.0 1.0 %copy-start = (bf16[2,32,32,128]{3,2,1,0:T(8,128)(2,1)S(1)}, bf16[2,32,32,128]{3,2,1,0:T(8,128)(2,1)}, u32[]{:S(2)}) copy-start(bf16[2,32,32,128]{3,2,1,0:T(8,128)(2,1)} %param.3) | copy-start | bytes 1572868
  1.1 13.5 %collective-permute-start = (bf16[8,64,128]{2,1,0:T(8,128)(2,1)S(1)}, bf16[8,64,128]{2,1,0:T(8,128)(2,1)S(1)}, u32[]{:S(2)}, u32[]{:S(2)}) collective-permute-start(bf16[8,64,128]{2,1,0:T(8,128)(2,1)S(1)} %chunks_of_bins.2.refs_0_), channel_id=1, source_target_pairs={{0,16},{8,24},{16,0},{24,8},{1,17},{9,25},{17,1},{25,9},{2,18},{10... | collective-permute-start | bytes 393224 | tf_op jit(solution)/shard_map/ppermute | solution.py:303
  5.4 9.3 %collective-permute-start.3 = (bf16[5,64,128]{2,1,0:T(8,128)(2,1)S(1)}, bf16[5,64,128]{2,1,0:T(8,128)(2,1)S(1)}, u32[]{:S(2)}, u32[]{:S(2)}) collective-permute-start(bf16[5,64,128]{2,1,0:T(8,128)(2,1)S(1)} %get-tuple-element.19), channel_id=1, source_target_pairs={{0,8},{8,16},{16,24},{24,0},{1,9},{9,17},{17,25},{25,1},{2,10},{10... | collective-permute-start | bytes 245768 | tf_op jit(solution)/shard_map/ppermute | solution.py:303
  7.0 8.7 %collective-permute-start.4 = (bf16[5,64,128]{2,1,0:T(8,128)(2,1)S(1)}, bf16[5,64,128]{2,1,0:T(8,128)(2,1)S(1)}, u32[]{:S(2)}, u32[]{:S(2)}) collective-permute-start(bf16[5,64,128]{2,1,0:T(8,128)(2,1)S(1)} %get-tuple-element.20), channel_id=1, source_target_pairs={{0,24},{8,0},{16,8},{24,16},{1,25},{9,1},{17,9},{25,17},{2,26},{10... | collective-permute-start | bytes 245768 | tf_op jit(solution)/shard_map/ppermute | solution.py:303
  9.3 7.8 %collective-permute-start.1 = (bf16[3,64,128]{2,1,0:T(8,128)(2,1)S(1)}, bf16[3,64,128]{2,1,0:T(8,128)(2,1)S(1)}, u32[]{:S(2)}, u32[]{:S(2)}) collective-permute-start(bf16[3,64,128]{2,1,0:T(8,128)(2,1)S(1)} %get-tuple-element.13), channel_id=1, source_target_pairs={{0,24},{8,0},{16,8},{24,16},{1,25},{9,1},{17,9},{25,17},{2,26},{10... | collective-permute-start | bytes 147464 | tf_op jit(solution)/shard_map/ppermute | solution.py:303
  9.3 7.8 %collective-permute-start.2 = (bf16[3,64,128]{2,1,0:T(8,128)(2,1)S(1)}, bf16[3,64,128]{2,1,0:T(8,128)(2,1)S(1)}, u32[]{:S(2)}, u32[]{:S(2)}) collective-permute-start(bf16[3,64,128]{2,1,0:T(8,128)(2,1)S(1)} %get-tuple-element.14), channel_id=1, source_target_pairs={{0,8},{8,16},{16,24},{24,0},{1,9},{9,17},{17,25},{25,1},{2,10},{10... | collective-permute-start | bytes 147464 | tf_op jit(solution)/shard_map/ppermute | solution.py:303
  11.3 0.7 %copy-start.2 = (s32[4]{0:T(128)S(1)}, s32[4]{0:T(128)}, u32[]{:S(2)}) copy-start(s32[4]{0:T(128)} %param.4) | copy-start | bytes 52
  15.7 15.0 %copy-start.1 = (bf16[2,2,256,256]{3,2,1,0:T(8,128)(2,1)S(1)}, bf16[2,2,256,256]{3,2,1,0:T(8,128)(2,1)}, u32[]{:S(2)}) copy-start(bf16[2,2,256,256]{3,2,1,0:T(8,128)(2,1)} %constant.2.clone.table_ref) | copy-start | bytes 1572868

commit v26 on v25

--- a/solution.py
+++ b/solution.py
@@ -112,8 +112,12 @@
     groups = len(order)
     chunk_refs = refs[:groups]
     place_ref, lag_ref, shift_ref = refs[groups : groups + 3]
-    earlier_refs = refs[groups + 3 : -4]
-    out_ref, placed_ref, left_ref, part_ref = refs[-4:]
+    placed_ref, left_ref, part_ref = refs[-3:]
+    if parts is None:
+        out_ref, rest_ref = refs[-5:-3]
+        rest_ref[...] = chunk_refs[-2][bins:]
+    else:
+        earlier_refs, out_ref = refs[groups + 3 : -4], refs[-4]
     rows = placed_ref.shape[2]
     windows = rows // 2
     places = place_ref[...]
@@ -287,14 +291,13 @@
     late = max(1, 3 * bins // 8) if bins > 1 else 0
     pieces = [(0, bins - late), (bins - late, late)] if late else [(0, bins)]
     far_first = sorted(range(1, groups), key=lambda steps: abs(2 * steps - groups))
-    kept, split = far_first[0], far_first[1:]
-    orders = [[kept] + split + [0], [kept] + split[::-1] + [0]][: len(pieces)]
+    order, kept = far_first + [0], far_first[-1]
     parts_of = {
-        (distance, piece): (distance, *(piece if distance in split else (0, bins)))
-        for piece, order in zip(pieces, orders)
+        (distance, piece): (distance, *((0, bins) if distance in (kept, 0) else piece))
+        for piece in pieces
         for distance in order
     }
-    cuts = list(dict.fromkeys(parts_of.values()))
+    cuts = sorted(dict.fromkeys(parts_of.values()), key=lambda key: key[0] != kept)
     (first_chunk,) = cut(cuts[:1])
     chunks = dict(zip(cuts, (first_chunk, *cut(cuts[1:], first_chunk))))
     for key in cuts:
@@ -323,14 +326,20 @@
         name="slant_tables",
     )(block_position.reshape(1, groups))
     earlier = []
-    for (start, size), order in zip(pieces, orders):
+    for start, size in pieces:
         last = start + size == bins
-        shape = (groups, parts, message_rows, BLOCK) if last else (2 * size, groups, SLOWNESS)
-        terms = pl.pallas_call(
+        if last:
+            shapes = (jax.ShapeDtypeStruct((groups, parts, message_rows, BLOCK), jnp.float32),)
+        else:
+            shapes = (
+                jax.ShapeDtypeStruct((2 * size, groups, SLOWNESS), jnp.float32),
+                jax.ShapeDtypeStruct((bins - size, rows, BLOCK), jnp.bfloat16),
+            )
+        terms, *rest = pl.pallas_call(
             functools.partial(stack_kernel, order, start, size, parts if last else None),
-            out_shape=jax.ShapeDtypeStruct(shape, jnp.float32),
+            out_shape=shapes,
             in_specs=[vmem] * (groups + 3 + len(earlier)),
-            out_specs=vmem,
+            out_specs=(vmem,) * len(shapes),
             scratch_shapes=[
                 pltpu.VMEM((groups, size, rows, BLOCK), jnp.bfloat16),
                 pltpu.VMEM((size, BLOCK, groups * rows), jnp.bfloat16),
@@ -349,6 +358,8 @@
             *earlier,
         )
         earlier.append(terms)
+        if not last:
+            chunks[parts_of[kept, (start, size)]] = rest[0]
     terms = terms.reshape(groups * parts, message_rows, BLOCK)
     arrived = lax.all_to_all(
         terms,

time: 31.8 us -> 32.2 us (1.013)
  waiting for transfers between devices: 2.58 us -> 4.24 us
  blocking collectives: 12.5 us -> 11.7 us
  starting transfers between devices: 10 us -> 9.61 us
    ppermute x5, waiting for transfers between devices: 2.58 us -> 4.24 us  [shards(): chunks[key] = lax.ppermute(chunks[key], 'chan', pairs)]
    all_to_all x1, blocking collectives: 12.5 us -> 11.7 us  [shards(): lax.all_to_all(terms, ('chan', 'freq'), split_axis=0, concat_axis=0, axis...]
    ppermute x5, starting transfers between devices: 10 us -> 9.61 us  [shards(): chunks[key] = lax.ppermute(chunks[key], 'chan', pairs)]
  transfers between devices with their start and end apart: 5 -> 5, of which waited for: 2 -> 1; matrix products, arithmetic and copies ran while one was open for 0% -> 0% of each run, Pallas kernels for 9% -> 8%
where the time goes in v26:
time: 32.2 us; the launch traced here: 32 us
  blocking collectives  11.7 us (36%)
  starting transfers between devices  9.61 us (30%)
  Pallas kernels  4.76 us (15%)
  waiting for transfers between devices  4.24 us (13%)
  local copies, waits for them, and re-layouts  1.7 us (5%)
    all_to_all x1, blocking collectives, shards(): lax.all_to_all(terms, ('chan', 'freq'), split_axis=0, concat_axis=0, axis...  11.7 us
    ppermute x5, starting transfers between devices, shards(): chunks[key] = lax.ppermute(chunks[key], 'chan', pairs)  9.61 us
    ppermute x5, waiting for transfers between devices, shards(): chunks[key] = lax.ppermute(chunks[key], 'chan', pairs)  4.24 us
    pallas_call x2, Pallas kernels, shards(): pl.pallas_call(functools.partial(stack_kernel, order, start, size, parts...  2.43 us
    unnamed x6, local copies, waits for them, and re-layouts  1.7 us
    pallas_call x1, Pallas kernels, shards(): pl.pallas_call(functools.partial(table_kernel, groups, bins, freq_dev), o...  1.19 us
    pallas_call x1, Pallas kernels, shards(): pl.pallas_call(functools.partial(image_kernel, slow_dev, spans), out_shap...  0.88 us
  transfers between devices with their start and end apart: 5, of which 1 were waited for; matrix products, arithmetic and copies ran while one was open for 0% of the time, Pallas kernels for 8%

profile of v26, /device:TPU:0, one launch (start us, length us, event | category | flops | bytes accessed | tf_op | source)
XLA Modules:
  0.0 32.0 jit_solution(4698066751988127791)
XLA Ops:
  0.0 0.0 copy-start
  0.0 1.0 %copy-done = bf16[2,32,32,128]{3,2,1,0:T(8,128)(2,1)S(1)} copy-done((bf16[2,32,32,128]{3,2,1,0:T(8,128)(2,1)S(1)}, bf16[2,32,32,128]{3,2,1,0:T(8,128)(2,1)}, u32[]{:S(2)}) %copy-start) | copy-done | bytes 524312
  1.0 0.1 chunks_of_bins.2.refs_0_
  1.1 5.1 %collective-permute-start.4 = (bf16[8,64,128]{2,1,0:T(8,128)(2,1)S(1)}, bf16[8,64,128]{2,1,0:T(8,128)(2,1)S(1)}, u32[]{:S(2)}, u32[]{:S(2)}) collective-permute-start(bf16[8,64,128]{2,1,0:T(8,128)(2,1)S(1)} %chunks_of_bins.2.refs_0_), channel_id=1, source_target_pairs={{0,24},{8,0},{16,8},{24,16},{1,25},{9,1},{17,9},{25,17},{2,26},{10... | collective-permute-start | bytes 393224 | tf_op jit(solution)/shard_map/ppermute | solution.py:306
  6.2 0.2 chunks_of_bins.3
  6.4 0.1 collective-permute-start.2
  6.5 1.0 %collective-permute-start.3 = (bf16[5,64,128]{2,1,0:T(8,128)(2,1)S(1)}, bf16[5,64,128]{2,1,0:T(8,128)(2,1)S(1)}, u32[]{:S(2)}, u32[]{:S(2)}) collective-permute-start(bf16[5,64,128]{2,1,0:T(8,128)(2,1)S(1)} %get-tuple-element.18), channel_id=1, source_target_pairs={{0,8},{8,16},{16,24},{24,0},{1,9},{9,17},{17,25},{25,1},{2,10},{10... | collective-permute-start | bytes 245768 | tf_op jit(solution)/shard_map/ppermute | solution.py:306
  7.5 1.9 %collective-permute-start = (bf16[3,64,128]{2,1,0:T(8,128)(2,1)S(1)}, bf16[3,64,128]{2,1,0:T(8,128)(2,1)S(1)}, u32[]{:S(2)}, u32[]{:S(2)}) collective-permute-start(bf16[3,64,128]{2,1,0:T(8,128)(2,1)S(1)} %get-tuple-element.15), channel_id=1, source_target_pairs={{0,16},{8,24},{16,0},{24,8},{1,17},{9,25},{17,1},{25,9},{2,18},{10... | collective-permute-start | bytes 147464 | tf_op jit(solution)/shard_map/ppermute | solution.py:306
  9.4 1.5 %collective-permute-start.1 = (bf16[3,64,128]{2,1,0:T(8,128)(2,1)S(1)}, bf16[3,64,128]{2,1,0:T(8,128)(2,1)S(1)}, u32[]{:S(2)}, u32[]{:S(2)}) collective-permute-start(bf16[3,64,128]{2,1,0:T(8,128)(2,1)S(1)} %get-tuple-element.16), channel_id=1, source_target_pairs={{0,8},{8,16},{16,24},{24,0},{1,9},{9,17},{17,25},{25,1},{2,10},{10... | collective-permute-start | bytes 147464 | tf_op jit(solution)/shard_map/ppermute | solution.py:306
  10.9 0.0 copy-start.2
  10.9 0.7 %copy-done.2 = s32[4]{0:T(128)S(1)} copy-done((s32[4]{0:T(128)S(1)}, s32[4]{0:T(128)}, u32[]{:S(2)}) %copy-start.2) | copy-done | bytes 40
  11.6 1.2 %slant_tables.1 = (s32[4,128]{1,0:T(4,128)S(1)}, bf16[8,256,512]{2,1,0:T(8,128)(2,1)S(1)}, f32[8,2,8,256]{3,2,1,0:T(8,128)S(1)}) custom-call(s32[1,4]{1,0:T(1,128)S(1)} %bitcast.6), custom_call_target="tpu_custom_call" | custom-call | flops 10000000 | bytes 4000000 | tf_op jit(solution)/shard_map/slant_tables/pallas_call | solution.py:315
  12.8 0.0 collective-permute-done.4.in_ref
  12.8 4.2 %collective-permute-done.2.refs_0_ = bf16[5,64,128]{2,1,0:T(8,128)(2,1)S(1)} collective-permute-done((bf16[5,64,128]{2,1,0:T(8,128)(2,1)S(1)}, bf16[5,64,128]{2,1,0:T(8,128)(2,1)S(1)}, u32[]{:S(2)}, u32[]{:S(2)}) %collective-permute-start.2) | collective-permute-done | bytes 81952 | tf_op jit(solution)/shard_map/ppermute | solution.py:306
  17.0 0.0 collective-permute-done.3.refs_1_
  17.0 0.0 copy-start.1
  17.0 1.3 %stack_and_slant.2 = (f32[10,4,256]{2,1,0:T(4,128)S(1)}, bf16[3,64,128]{2,1,0:T(8,128)(2,1)S(1)}) custom-call(bf16[5,64,128]{2,1,0:T(8,128)(2,1)S(1)} %collective-permute-done.2.refs_0_, bf16[5,64,128]{2,1,0:T(8,128)(2,1)S(1)} %collective-permute-done.3.refs_1_, bf16[8,64,128]{2,1,0:T(8,128)(2,1)S(1)} %first_arrived.1.refs_2_, ...), custom_call_target="tpu_custom_call" | custom-call | flops 200000000 | bytes 4000000 | tf_op jit(solution)/shard_map/stack_and_slant/pallas_call | solution.py:338
  18.3 0.0 collective-permute-done.refs_0_
  18.4 0.0 collective-permute-done.1.refs_1_
  18.4 1.1 %stack_and_slant.3 = f32[4,8,4,128]{3,2,1,0:T(4,128)S(1)} custom-call(bf16[3,64,128]{2,1,0:T(8,128)(2,1)S(1)} %collective-permute-done.refs_0_, bf16[3,64,128]{2,1,0:T(8,128)(2,1)S(1)} %collective-permute-done.1.refs_1_, bf16[3,64,128]{2,1,0:T(8,128)(2,1)S(1)} %get-tuple-element.23.refs_2_, bf16[8,64,128]{2,1,0:T(8,128)(2,1)S(1)} %get-tuple-element.19.refs_3_, ...), custom_call_target="tpu_custom_call" | custom-call | flops 200000000 | bytes 4000000 | tf_op jit(solution)/shard_map/stack_and_slant/pallas_call | solution.py:338
  19.5 11.7 %all_to_all.5.term_ref = f32[32,4,128]{2,1,0:T(4,128)S(1)} all-to-all(f32[32,4,128]{2,1,0:T(4,128)S(1)} %bitcast.5), channel_id=1, replica_groups={{31,30,29,28,27,26,25,24,23,22,21,20,19,18,17,16,15,14,13,12,11,10,9,8,..., dimensions={0} | all-to-all | bytes 131072 | tf_op jit(solution)/shard_map/all_to_all | solution.py:364
  31.2 0.0 copy-done.1
  31.2 0.9 %sum_of_bins.1 = f32[1,32,512]{2,1,0:T(8,128)} custom-call(f32[32,4,128]{2,1,0:T(4,128)S(1)} %all_to_all.5.term_ref, bf16[2,2,256,256]{3,2,1,0:T(8,128)(2,1)S(1)} %copy-done.1), custom_call_target="tpu_custom_call" | custom-call | tf_op jit(solution)/shard_map/sum_of_bins/pallas_call | solution.py:373
  (1 shorter events, 0.0 us)
Async XLA Ops:
  0.0 1.0 %copy-start = (bf16[2,32,32,128]{3,2,1,0:T(8,128)(2,1)S(1)}, bf16[2,32,32,128]{3,2,1,0:T(8,128)(2,1)}, u32[]{:S(2)}) copy-start(bf16[2,32,32,128]{3,2,1,0:T(8,128)(2,1)} %param.3) | copy-start | bytes 1572868
  1.1 11.7 %collective-permute-start.4 = (bf16[8,64,128]{2,1,0:T(8,128)(2,1)S(1)}, bf16[8,64,128]{2,1,0:T(8,128)(2,1)S(1)}, u32[]{:S(2)}, u32[]{:S(2)}) collective-permute-start(bf16[8,64,128]{2,1,0:T(8,128)(2,1)S(1)} %chunks_of_bins.2.refs_0_), channel_id=1, source_target_pairs={{0,24},{8,0},{16,8},{24,16},{1,25},{9,1},{17,9},{25,17},{2,26},{10... | collective-permute-start | bytes 393224 | tf_op jit(solution)/shard_map/ppermute | solution.py:306
  6.4 10.6 %collective-permute-start.2 = (bf16[5,64,128]{2,1,0:T(8,128)(2,1)S(1)}, bf16[5,64,128]{2,1,0:T(8,128)(2,1)S(1)}, u32[]{:S(2)}, u32[]{:S(2)}) collective-permute-start(bf16[5,64,128]{2,1,0:T(8,128)(2,1)S(1)} %get-tuple-element.17), channel_id=1, source_target_pairs={{0,16},{8,24},{16,0},{24,8},{1,17},{9,25},{17,1},{25,9},{2,18},{10... | collective-permute-start | bytes 245768 | tf_op jit(solution)/shard_map/ppermute | solution.py:306
  6.5 10.5 %collective-permute-start.3 = (bf16[5,64,128]{2,1,0:T(8,128)(2,1)S(1)}, bf16[5,64,128]{2,1,0:T(8,128)(2,1)S(1)}, u32[]{:S(2)}, u32[]{:S(2)}) collective-permute-start(bf16[5,64,128]{2,1,0:T(8,128)(2,1)S(1)} %get-tuple-element.18), channel_id=1, source_target_pairs={{0,8},{8,16},{16,24},{24,0},{1,9},{9,17},{17,25},{25,1},{2,10},{10... | collective-permute-start | bytes 245768 | tf_op jit(solution)/shard_map/ppermute | solution.py:306
  7.5 10.9 %collective-permute-start = (bf16[3,64,128]{2,1,0:T(8,128)(2,1)S(1)}, bf16[3,64,128]{2,1,0:T(8,128)(2,1)S(1)}, u32[]{:S(2)}, u32[]{:S(2)}) collective-permute-start(bf16[3,64,128]{2,1,0:T(8,128)(2,1)S(1)} %get-tuple-element.15), channel_id=1, source_target_pairs={{0,16},{8,24},{16,0},{24,8},{1,17},{9,25},{17,1},{25,9},{2,18},{10... | collective-permute-start | bytes 147464 | tf_op jit(solution)/shard_map/ppermute | solution.py:306
  9.4 9.0 %collective-permute-start.1 = (bf16[3,64,128]{2,1,0:T(8,128)(2,1)S(1)}, bf16[3,64,128]{2,1,0:T(8,128)(2,1)S(1)}, u32[]{:S(2)}, u32[]{:S(2)}) collective-permute-start(bf16[3,64,128]{2,1,0:T(8,128)(2,1)S(1)} %get-tuple-element.16), channel_id=1, source_target_pairs={{0,8},{8,16},{16,24},{24,0},{1,9},{9,17},{17,25},{25,1},{2,10},{10... | collective-permute-start | bytes 147464 | tf_op jit(solution)/shard_map/ppermute | solution.py:306
  10.9 0.7 %copy-start.2 = (s32[4]{0:T(128)S(1)}, s32[4]{0:T(128)}, u32[]{:S(2)}) copy-start(s32[4]{0:T(128)} %param.4) | copy-start | bytes 52
  17.0 14.1 %copy-start.1 = (bf16[2,2,256,256]{3,2,1,0:T(8,128)(2,1)S(1)}, bf16[2,2,256,256]{3,2,1,0:T(8,128)(2,1)}, u32[]{:S(2)}) copy-start(bf16[2,2,256,256]{3,2,1,0:T(8,128)(2,1)} %constant.2.clone.table_ref) | copy-start | bytes 1572868

commit v27 on v23

--- a/solution.py
+++ b/solution.py
@@ -89,7 +89,8 @@
         if distance not in widened:
             group = lax.rem(own_group + distance, groups)
             index = len(widened)
-            wide_ref[index] = spec_ref[:, group].astype(jnp.float32).reshape(rows * bins, BLOCK)
+            value = spec_ref[:, group].astype(jnp.float32).reshape(rows * bins, BLOCK)
+            wide_ref[index, : rows * bins] = value
             widened.append(distance)
         for f in range(size):
             value = wide_ref[widened.index(distance), pl.ds(start + f, rows, stride=bins), :]
@@ -276,7 +277,7 @@
             ),
             in_specs=[vmem] + [anywhere] * len(earlier),
             out_specs=(vmem,) * len(cuts),
-            scratch_shapes=[pltpu.VMEM((len(distances), rows * bins, BLOCK), jnp.float32)],
+            scratch_shapes=[pltpu.VMEM((len(distances), (rows + 1) * bins, BLOCK), jnp.float32)],
             compiler_params=params,
             cost_estimate=pl.CostEstimate(flops=10**7, bytes_accessed=10**6, transcendentals=0),
             name="chunks_of_bins",
@@ -325,7 +326,7 @@
             scratch_shapes=[
                 pltpu.VMEM((groups, size, rows, BLOCK), jnp.bfloat16),
                 pltpu.VMEM((size, BLOCK, groups * rows), jnp.bfloat16),
-                pltpu.VMEM((2, size * 2 * groups * 8, BLOCK), jnp.float32),
+                pltpu.VMEM((2, (size * 2 * groups + 1) * 8, BLOCK), jnp.float32),
             ],
             compiler_params=params,
             cost_estimate=pl.CostEstimate(

time: 31.4 us -> 31.4 us (level)
  no operation moved by 1% of the time
where the time goes in v27:
time: 31.4 us; the launch traced here: 31.2 us
  blocking collectives  12.5 us (40%)
  starting transfers between devices  11.4 us (36%)
  Pallas kernels  4.77 us (15%)
  local copies, waits for them, and re-layouts  1.7 us (5%)
  waiting for transfers between devices  0.81 us (3%)
    all_to_all x1, blocking collectives, shards(): lax.all_to_all(terms, ('chan', 'freq'), split_axis=0, concat_axis=0, axis...  12.5 us
    ppermute x6, starting transfers between devices, shards(): chunks[key] = lax.ppermute(chunks[key], 'chan', pairs)  11.4 us
    pallas_call x2, Pallas kernels, shards(): pl.pallas_call(functools.partial(stack_kernel, order, start, size, parts...  2.43 us
    unnamed x6, local copies, waits for them, and re-layouts  1.7 us
    pallas_call x1, Pallas kernels, shards(): pl.pallas_call(functools.partial(table_kernel, groups, bins, freq_dev), o...  1.19 us
    pallas_call x1, Pallas kernels, shards(): pl.pallas_call(functools.partial(image_kernel, slow_dev, spans), out_shap...  0.89 us
    ppermute x6, waiting for transfers between devices, shards(): chunks[key] = lax.ppermute(chunks[key], 'chan', pairs)  0.81 us
  transfers between devices with their start and end apart: 6, of which 1 were waited for; matrix products, arithmetic and copies ran while one was open for 0% of the time, Pallas kernels for 9%

profile of v27, /device:TPU:0, one launch (start us, length us, event | category | flops | bytes accessed | tf_op | source)
XLA Modules:
  0.0 31.2 jit_solution(11425590942947021756)
XLA Ops:
  0.0 0.0 copy-start
  0.0 1.0 %copy-done = bf16[2,32,32,128]{3,2,1,0:T(8,128)(2,1)S(1)} copy-done((bf16[2,32,32,128]{3,2,1,0:T(8,128)(2,1)S(1)}, bf16[2,32,32,128]{3,2,1,0:T(8,128)(2,1)}, u32[]{:S(2)}) %copy-start) | copy-done | bytes 524312
  1.1 4.1 %collective-permute-start.3 = (bf16[5,64,128]{2,1,0:T(8,128)(2,1)S(1)}, bf16[5,64,128]{2,1,0:T(8,128)(2,1)S(1)}, u32[]{:S(2)}, u32[]{:S(2)}) collective-permute-start(bf16[5,64,128]{2,1,0:T(8,128)(2,1)S(1)} %chunks_of_bins.2.refs_0_), channel_id=1, source_target_pairs={{0,16},{8,24},{16,0},{24,8},{1,17},{9,25},{17,1},{25,9},{2,18},{10... | collective-permute-start | bytes 245768 | tf_op jit(solution)/shard_map/ppermute | solution.py:295
  5.2 0.2 chunks_of_bins.3
  5.4 1.6 %collective-permute-start.4 = (bf16[5,64,128]{2,1,0:T(8,128)(2,1)S(1)}, bf16[5,64,128]{2,1,0:T(8,128)(2,1)S(1)}, u32[]{:S(2)}, u32[]{:S(2)}) collective-permute-start(bf16[5,64,128]{2,1,0:T(8,128)(2,1)S(1)} %get-tuple-element.22), channel_id=1, source_target_pairs={{0,8},{8,16},{16,24},{24,0},{1,9},{9,17},{17,25},{25,1},{2,10},{10... | collective-permute-start | bytes 245768 | tf_op jit(solution)/shard_map/ppermute | solution.py:295
  7.0 2.2 %collective-permute-start.5 = (bf16[5,64,128]{2,1,0:T(8,128)(2,1)S(1)}, bf16[5,64,128]{2,1,0:T(8,128)(2,1)S(1)}, u32[]{:S(2)}, u32[]{:S(2)}) collective-permute-start(bf16[5,64,128]{2,1,0:T(8,128)(2,1)S(1)} %get-tuple-element.23), channel_id=1, source_target_pairs={{0,24},{8,0},{16,8},{24,16},{1,25},{9,1},{17,9},{25,17},{2,26},{10... | collective-permute-start | bytes 245768 | tf_op jit(solution)/shard_map/ppermute | solution.py:295
  9.3 0.0 collective-permute-start
  9.3 0.6 %collective-permute-start.1 = (bf16[3,64,128]{2,1,0:T(8,128)(2,1)S(1)}, bf16[3,64,128]{2,1,0:T(8,128)(2,1)S(1)}, u32[]{:S(2)}, u32[]{:S(2)}) collective-permute-start(bf16[3,64,128]{2,1,0:T(8,128)(2,1)S(1)} %get-tuple-element.16), channel_id=1, source_target_pairs={{0,8},{8,16},{16,24},{24,0},{1,9},{9,17},{17,25},{25,1},{2,10},{10... | collective-permute-start | bytes 147464 | tf_op jit(solution)/shard_map/ppermute | solution.py:295
  9.9 0.8 %collective-permute-done.3.in_ref = bf16[5,64,128]{2,1,0:T(8,128)(2,1)S(1)} collective-permute-done((bf16[5,64,128]{2,1,0:T(8,128)(2,1)S(1)}, bf16[5,64,128]{2,1,0:T(8,128)(2,1)S(1)}, u32[]{:S(2)}, u32[]{:S(2)}) %collective-permute-start.3) | collective-permute-done | bytes 81952 | tf_op jit(solution)/shard_map/ppermute | solution.py:295
  10.6 2.8 %collective-permute-start.2 = (bf16[3,64,128]{2,1,0:T(8,128)(2,1)S(1)}, bf16[3,64,128]{2,1,0:T(8,128)(2,1)S(1)}, u32[]{:S(2)}, u32[]{:S(2)}) collective-permute-start(bf16[3,64,128]{2,1,0:T(8,128)(2,1)S(1)} %get-tuple-element.17), channel_id=1, source_target_pairs={{0,24},{8,0},{16,8},{24,16},{1,25},{9,1},{17,9},{25,17},{2,26},{10... | collective-permute-start | bytes 147464 | tf_op jit(solution)/shard_map/ppermute | solution.py:295
  13.5 0.0 copy-start.2
  13.5 0.7 %copy-done.2 = s32[4]{0:T(128)S(1)} copy-done((s32[4]{0:T(128)S(1)}, s32[4]{0:T(128)}, u32[]{:S(2)}) %copy-start.2) | copy-done | bytes 40
  14.1 1.2 %slant_tables.1 = (s32[4,128]{1,0:T(4,128)S(1)}, bf16[8,256,512]{2,1,0:T(8,128)(2,1)S(1)}, f32[8,2,8,256]{3,2,1,0:T(8,128)S(1)}) custom-call(s32[1,4]{1,0:T(1,128)S(1)} %bitcast.6), custom_call_target="tpu_custom_call" | custom-call | flops 10000000 | bytes 4000000 | tf_op jit(solution)/shard_map/slant_tables/pallas_call | solution.py:304
  15.3 0.0 collective-permute-done.4.refs_1_
  15.4 0.0 collective-permute-done.5.refs_2_
  15.4 0.0 copy-start.1
  15.4 1.3 %stack_and_slant.2.refs_7_ = f32[10,4,256]{2,1,0:T(4,128)S(1)} custom-call(bf16[5,64,128]{2,1,0:T(8,128)(2,1)S(1)} %first_arrived.1.refs_0_, bf16[5,64,128]{2,1,0:T(8,128)(2,1)S(1)} %collective-permute-done.4.refs_1_, bf16[5,64,128]{2,1,0:T(8,128)(2,1)S(1)} %collective-permute-done.5.refs_2_, bf16[5,64,128]{2,1,0:T(8,128)(2,1)S(1)} %get-tuple-element.24.refs_3_, ...), custom_call_target="tpu_custom_call" | custom-call | flops 200000000 | bytes 4000000 | tf_op jit(solution)/shard_map/stack_and_slant/pallas_call | solution.py:321
  16.7 0.0 collective-permute-done.refs_0_
  16.7 0.0 collective-permute-done.1.refs_1_
  16.7 0.0 collective-permute-done.2.refs_2_
  16.7 1.1 %stack_and_slant.3 = f32[4,8,4,128]{3,2,1,0:T(4,128)S(1)} custom-call(bf16[3,64,128]{2,1,0:T(8,128)(2,1)S(1)} %collective-permute-done.refs_0_, bf16[3,64,128]{2,1,0:T(8,128)(2,1)S(1)} %collective-permute-done.1.refs_1_, bf16[3,64,128]{2,1,0:T(8,128)(2,1)S(1)} %collective-permute-done.2.refs_2_, bf16[3,64,128]{2,1,0:T(8,128)(2,1)S(1)} %get-tuple-element.18.refs_3_, ...), custom_call_target="tpu_custom_call" | custom-call | flops 200000000 | bytes 4000000 | tf_op jit(solution)/shard_map/stack_and_slant/pallas_call | solution.py:321
  17.9 12.5 %all_to_all.5.term_ref = f32[32,4,128]{2,1,0:T(4,128)S(1)} all-to-all(f32[32,4,128]{2,1,0:T(4,128)S(1)} %bitcast.5), channel_id=1, replica_groups={{31,30,29,28,27,26,25,24,23,22,21,20,19,18,17,16,15,14,13,12,11,10,9,8,..., dimensions={0} | all-to-all | bytes 131072 | tf_op jit(solution)/shard_map/all_to_all | solution.py:345
  30.4 0.0 copy-done.1
  30.4 0.9 %sum_of_bins.1 = f32[1,32,512]{2,1,0:T(8,128)} custom-call(f32[32,4,128]{2,1,0:T(4,128)S(1)} %all_to_all.5.term_ref, bf16[2,2,256,256]{3,2,1,0:T(8,128)(2,1)S(1)} %copy-done.1), custom_call_target="tpu_custom_call" | custom-call | tf_op jit(solution)/shard_map/sum_of_bins/pallas_call | solution.py:354
  (2 shorter events, 0.1 us)
Async XLA Ops:
  0.0 1.0 %copy-start = (bf16[2,32,32,128]{3,2,1,0:T(8,128)(2,1)S(1)}, bf16[2,32,32,128]{3,2,1,0:T(8,128)(2,1)}, u32[]{:S(2)}) copy-start(bf16[2,32,32,128]{3,2,1,0:T(8,128)(2,1)} %param.3) | copy-start | bytes 1572868
  1.1 9.5 %collective-permute-start.3 = (bf16[5,64,128]{2,1,0:T(8,128)(2,1)S(1)}, bf16[5,64,128]{2,1,0:T(8,128)(2,1)S(1)}, u32[]{:S(2)}, u32[]{:S(2)}) collective-permute-start(bf16[5,64,128]{2,1,0:T(8,128)(2,1)S(1)} %chunks_of_bins.2.refs_0_), channel_id=1, source_target_pairs={{0,16},{8,24},{16,0},{24,8},{1,17},{9,25},{17,1},{25,9},{2,18},{10... | collective-permute-start | bytes 245768 | tf_op jit(solution)/shard_map/ppermute | solution.py:295
  5.4 9.9 %collective-permute-start.4 = (bf16[5,64,128]{2,1,0:T(8,128)(2,1)S(1)}, bf16[5,64,128]{2,1,0:T(8,128)(2,1)S(1)}, u32[]{:S(2)}, u32[]{:S(2)}) collective-permute-start(bf16[5,64,128]{2,1,0:T(8,128)(2,1)S(1)} %get-tuple-element.22), channel_id=1, source_target_pairs={{0,8},{8,16},{16,24},{24,0},{1,9},{9,17},{17,25},{25,1},{2,10},{10... | collective-permute-start | bytes 245768 | tf_op jit(solution)/shard_map/ppermute | solution.py:295
  7.0 8.3 %collective-permute-start.5 = (bf16[5,64,128]{2,1,0:T(8,128)(2,1)S(1)}, bf16[5,64,128]{2,1,0:T(8,128)(2,1)S(1)}, u32[]{:S(2)}, u32[]{:S(2)}) collective-permute-start(bf16[5,64,128]{2,1,0:T(8,128)(2,1)S(1)} %get-tuple-element.23), channel_id=1, source_target_pairs={{0,24},{8,0},{16,8},{24,16},{1,25},{9,1},{17,9},{25,17},{2,26},{10... | collective-permute-start | bytes 245768 | tf_op jit(solution)/shard_map/ppermute | solution.py:295
  9.3 7.4 %collective-permute-start = (bf16[3,64,128]{2,1,0:T(8,128)(2,1)S(1)}, bf16[3,64,128]{2,1,0:T(8,128)(2,1)S(1)}, u32[]{:S(2)}, u32[]{:S(2)}) collective-permute-start(bf16[3,64,128]{2,1,0:T(8,128)(2,1)S(1)} %get-tuple-element.15), channel_id=1, source_target_pairs={{0,16},{8,24},{16,0},{24,8},{1,17},{9,25},{17,1},{25,9},{2,18},{10... | collective-permute-start | bytes 147464 | tf_op jit(solution)/shard_map/ppermute | solution.py:295
  9.3 7.4 %collective-permute-start.1 = (bf16[3,64,128]{2,1,0:T(8,128)(2,1)S(1)}, bf16[3,64,128]{2,1,0:T(8,128)(2,1)S(1)}, u32[]{:S(2)}, u32[]{:S(2)}) collective-permute-start(bf16[3,64,128]{2,1,0:T(8,128)(2,1)S(1)} %get-tuple-element.16), channel_id=1, source_target_pairs={{0,8},{8,16},{16,24},{24,0},{1,9},{9,17},{17,25},{25,1},{2,10},{10... | collective-permute-start | bytes 147464 | tf_op jit(solution)/shard_map/ppermute | solution.py:295
  10.6 6.1 %collective-permute-start.2 = (bf16[3,64,128]{2,1,0:T(8,128)(2,1)S(1)}, bf16[3,64,128]{2,1,0:T(8,128)(2,1)S(1)}, u32[]{:S(2)}, u32[]{:S(2)}) collective-permute-start(bf16[3,64,128]{2,1,0:T(8,128)(2,1)S(1)} %get-tuple-element.17), channel_id=1, source_target_pairs={{0,24},{8,0},{16,8},{24,16},{1,25},{9,1},{17,9},{25,17},{2,26},{10... | collective-permute-start | bytes 147464 | tf_op jit(solution)/shard_map/ppermute | solution.py:295
  13.5 0.7 %copy-start.2 = (s32[4]{0:T(128)S(1)}, s32[4]{0:T(128)}, u32[]{:S(2)}) copy-start(s32[4]{0:T(128)} %param.4) | copy-start | bytes 52
  15.4 15.0 %copy-start.1 = (bf16[2,2,256,256]{3,2,1,0:T(8,128)(2,1)S(1)}, bf16[2,2,256,256]{3,2,1,0:T(8,128)(2,1)}, u32[]{:S(2)}) copy-start(bf16[2,2,256,256]{3,2,1,0:T(8,128)(2,1)} %constant.2.clone.table_ref) | copy-start | bytes 1572868

commit v28 on v27

--- a/solution.py
+++ b/solution.py
@@ -283,7 +283,7 @@
             name="chunks_of_bins",
         )(whole, *earlier)
 
-    late = max(1, 3 * bins // 8) if bins > 1 else 0
+    late = max(1, bins // 4) if bins > 1 else 0
     pieces = [(0, bins - late), (bins - late, late)] if late else [(0, bins)]
     order = sorted(range(1, groups), key=lambda steps: abs(2 * steps - groups)) + [0]
     cuts = [(distance, *piece) for piece in pieces for distance in order]

time: 31.4 us -> 31.7 us (level)
  waiting for transfers between devices: 0.81 us -> 3.9 us
  starting transfers between devices: 11.4 us -> 9.31 us
  blocking collectives: 12.5 us -> 11.8 us
    ppermute x6, waiting for transfers between devices: 0.81 us -> 3.9 us  [shards(): chunks[key] = lax.ppermute(chunks[key], 'chan', pairs)]
    ppermute x6, starting transfers between devices: 11.4 us -> 9.31 us  [shards(): chunks[key] = lax.ppermute(chunks[key], 'chan', pairs)]
    all_to_all x1, blocking collectives: 12.5 us -> 11.8 us  [shards(): lax.all_to_all(terms, ('chan', 'freq'), split_axis=0, concat_axis=0, axis...]
where the time goes in v28:
time: 31.7 us; the launch traced here: 31.5 us
  blocking collectives  11.8 us (37%)
  starting transfers between devices  9.31 us (29%)
  Pallas kernels  4.76 us (15%)
  waiting for transfers between devices  3.9 us (12%)
  local copies, waits for them, and re-layouts  1.7 us (5%)
    all_to_all x1, blocking collectives, shards(): lax.all_to_all(terms, ('chan', 'freq'), split_axis=0, concat_axis=0, axis...  11.8 us
    ppermute x6, starting transfers between devices, shards(): chunks[key] = lax.ppermute(chunks[key], 'chan', pairs)  9.31 us
    ppermute x6, waiting for transfers between devices, shards(): chunks[key] = lax.ppermute(chunks[key], 'chan', pairs)  3.9 us
    pallas_call x2, Pallas kernels, shards(): pl.pallas_call(functools.partial(stack_kernel, order, start, size, parts...  2.42 us
    unnamed x6, local copies, waits for them, and re-layouts  1.7 us
    pallas_call x1, Pallas kernels, shards(): pl.pallas_call(functools.partial(table_kernel, groups, bins, freq_dev), o...  1.19 us
    pallas_call x1, Pallas kernels, shards(): pl.pallas_call(functools.partial(image_kernel, slow_dev, spans), out_shap...  0.89 us
  transfers between devices with their start and end apart: 6, of which 1 were waited for; matrix products, arithmetic and copies ran while one was open for 0% of the time, Pallas kernels for 9%

profile of v28, /device:TPU:0, one launch (start us, length us, event | category | flops | bytes accessed | tf_op | source)
XLA Modules:
  0.0 31.5 jit_solution(1987621897504627338)
XLA Ops:
  0.0 1.0 %copy-done = bf16[2,32,32,128]{3,2,1,0:T(8,128)(2,1)S(1)} copy-done((bf16[2,32,32,128]{3,2,1,0:T(8,128)(2,1)S(1)}, bf16[2,32,32,128]{3,2,1,0:T(8,128)(2,1)}, u32[]{:S(2)}) %copy-start) | copy-done | bytes 524312
  1.0 0.1 chunks_of_bins.2.refs_0_
  1.1 4.1 %collective-permute-start.3 = (bf16[6,64,128]{2,1,0:T(8,128)(2,1)S(1)}, bf16[6,64,128]{2,1,0:T(8,128)(2,1)S(1)}, u32[]{:S(2)}, u32[]{:S(2)}) collective-permute-start(bf16[6,64,128]{2,1,0:T(8,128)(2,1)S(1)} %chunks_of_bins.2.refs_0_), channel_id=1, source_target_pairs={{0,16},{8,24},{16,0},{24,8},{1,17},{9,25},{17,1},{25,9},{2,18},{10... | collective-permute-start | bytes 294920 | tf_op jit(solution)/shard_map/ppermute | solution.py:295
  5.2 0.2 chunks_of_bins.3
  5.4 1.6 %collective-permute-start.4 = (bf16[6,64,128]{2,1,0:T(8,128)(2,1)S(1)}, bf16[6,64,128]{2,1,0:T(8,128)(2,1)S(1)}, u32[]{:S(2)}, u32[]{:S(2)}) collective-permute-start(bf16[6,64,128]{2,1,0:T(8,128)(2,1)S(1)} %get-tuple-element.22), channel_id=1, source_target_pairs={{0,8},{8,16},{16,24},{24,0},{1,9},{9,17},{17,25},{25,1},{2,10},{10... | collective-permute-start | bytes 294920 | tf_op jit(solution)/shard_map/ppermute | solution.py:295
  7.0 2.2 %collective-permute-start.5 = (bf16[6,64,128]{2,1,0:T(8,128)(2,1)S(1)}, bf16[6,64,128]{2,1,0:T(8,128)(2,1)S(1)}, u32[]{:S(2)}, u32[]{:S(2)}) collective-permute-start(bf16[6,64,128]{2,1,0:T(8,128)(2,1)S(1)} %get-tuple-element.23), channel_id=1, source_target_pairs={{0,24},{8,0},{16,8},{24,16},{1,25},{9,1},{17,9},{25,17},{2,26},{10... | collective-permute-start | bytes 294920 | tf_op jit(solution)/shard_map/ppermute | solution.py:295
  9.3 0.0 collective-permute-start
  9.3 0.6 %collective-permute-start.1 = (bf16[2,64,128]{2,1,0:T(8,128)(2,1)S(1)}, bf16[2,64,128]{2,1,0:T(8,128)(2,1)S(1)}, u32[]{:S(2)}, u32[]{:S(2)}) collective-permute-start(bf16[2,64,128]{2,1,0:T(8,128)(2,1)S(1)} %get-tuple-element.16), channel_id=1, source_target_pairs={{0,8},{8,16},{16,24},{24,0},{1,9},{9,17},{17,25},{25,1},{2,10},{10... | collective-permute-start | bytes 98312 | tf_op jit(solution)/shard_map/ppermute | solution.py:295
  9.9 3.9 %collective-permute-done.3.in_ref = bf16[6,64,128]{2,1,0:T(8,128)(2,1)S(1)} collective-permute-done((bf16[6,64,128]{2,1,0:T(8,128)(2,1)S(1)}, bf16[6,64,128]{2,1,0:T(8,128)(2,1)S(1)}, u32[]{:S(2)}, u32[]{:S(2)}) %collective-permute-start.3) | collective-permute-done | bytes 98336 | tf_op jit(solution)/shard_map/ppermute | solution.py:295
  13.7 0.8 %collective-permute-start.2 = (bf16[2,64,128]{2,1,0:T(8,128)(2,1)S(1)}, bf16[2,64,128]{2,1,0:T(8,128)(2,1)S(1)}, u32[]{:S(2)}, u32[]{:S(2)}) collective-permute-start(bf16[2,64,128]{2,1,0:T(8,128)(2,1)S(1)} %get-tuple-element.17), channel_id=1, source_target_pairs={{0,24},{8,0},{16,8},{24,16},{1,25},{9,1},{17,9},{25,17},{2,26},{10... | collective-permute-start | bytes 98312 | tf_op jit(solution)/shard_map/ppermute | solution.py:295
  14.5 0.0 copy-start.2
  14.5 0.7 %copy-done.2 = s32[4]{0:T(128)S(1)} copy-done((s32[4]{0:T(128)S(1)}, s32[4]{0:T(128)}, u32[]{:S(2)}) %copy-start.2) | copy-done | bytes 40
  15.2 1.2 %slant_tables.1 = (s32[4,128]{1,0:T(4,128)S(1)}, bf16[8,256,512]{2,1,0:T(8,128)(2,1)S(1)}, f32[8,2,8,256]{3,2,1,0:T(8,128)S(1)}) custom-call(s32[1,4]{1,0:T(1,128)S(1)} %bitcast.6), custom_call_target="tpu_custom_call" | custom-call | flops 10000000 | bytes 4000000 | tf_op jit(solution)/shard_map/slant_tables/pallas_call | solution.py:304
  16.4 0.0 collective-permute-done.4.refs_1_
  16.4 0.0 collective-permute-done.5.refs_2_
  16.4 0.0 copy-start.1
  16.4 1.5 %stack_and_slant.2.refs_7_ = f32[12,4,256]{2,1,0:T(4,128)S(1)} custom-call(bf16[6,64,128]{2,1,0:T(8,128)(2,1)S(1)} %first_arrived.1.refs_0_, bf16[6,64,128]{2,1,0:T(8,128)(2,1)S(1)} %collective-permute-done.4.refs_1_, bf16[6,64,128]{2,1,0:T(8,128)(2,1)S(1)} %collective-permute-done.5.refs_2_, bf16[6,64,128]{2,1,0:T(8,128)(2,1)S(1)} %get-tuple-element.24.refs_3_, ...), custom_call_target="tpu_custom_call" | custom-call | flops 200000000 | bytes 4000000 | tf_op jit(solution)/shard_map/stack_and_slant/pallas_call | solution.py:321
  17.9 0.0 collective-permute-done.refs_0_
  17.9 0.0 collective-permute-done.1.refs_1_
  17.9 0.0 collective-permute-done.2.refs_2_
  17.9 0.9 %stack_and_slant.3 = f32[4,8,4,128]{3,2,1,0:T(4,128)S(1)} custom-call(bf16[2,64,128]{2,1,0:T(8,128)(2,1)S(1)} %collective-permute-done.refs_0_, bf16[2,64,128]{2,1,0:T(8,128)(2,1)S(1)} %collective-permute-done.1.refs_1_, bf16[2,64,128]{2,1,0:T(8,128)(2,1)S(1)} %collective-permute-done.2.refs_2_, bf16[2,64,128]{2,1,0:T(8,128)(2,1)S(1)} %get-tuple-element.18.refs_3_, ...), custom_call_target="tpu_custom_call" | custom-call | flops 200000000 | bytes 4000000 | tf_op jit(solution)/shard_map/stack_and_slant/pallas_call | solution.py:321
  18.9 11.8 %all_to_all.5.term_ref = f32[32,4,128]{2,1,0:T(4,128)S(1)} all-to-all(f32[32,4,128]{2,1,0:T(4,128)S(1)} %bitcast.5), channel_id=1, replica_groups={{31,30,29,28,27,26,25,24,23,22,21,20,19,18,17,16,15,14,13,12,11,10,9,8,..., dimensions={0} | all-to-all | bytes 131072 | tf_op jit(solution)/shard_map/all_to_all | solution.py:345
  30.7 0.0 copy-done.1
  30.7 0.9 %sum_of_bins.1 = f32[1,32,512]{2,1,0:T(8,128)} custom-call(f32[32,4,128]{2,1,0:T(4,128)S(1)} %all_to_all.5.term_ref, bf16[2,2,256,256]{3,2,1,0:T(8,128)(2,1)S(1)} %copy-done.1), custom_call_target="tpu_custom_call" | custom-call | tf_op jit(solution)/shard_map/sum_of_bins/pallas_call | solution.py:354
  (2 shorter events, 0.0 us)
Async XLA Ops:
  0.0 1.0 %copy-start = (bf16[2,32,32,128]{3,2,1,0:T(8,128)(2,1)S(1)}, bf16[2,32,32,128]{3,2,1,0:T(8,128)(2,1)}, u32[]{:S(2)}) copy-start(bf16[2,32,32,128]{3,2,1,0:T(8,128)(2,1)} %param.3) | copy-start | bytes 1572868
  1.1 12.6 %collective-permute-start.3 = (bf16[6,64,128]{2,1,0:T(8,128)(2,1)S(1)}, bf16[6,64,128]{2,1,0:T(8,128)(2,1)S(1)}, u32[]{:S(2)}, u32[]{:S(2)}) collective-permute-start(bf16[6,64,128]{2,1,0:T(8,128)(2,1)S(1)} %chunks_of_bins.2.refs_0_), channel_id=1, source_target_pairs={{0,16},{8,24},{16,0},{24,8},{1,17},{9,25},{17,1},{25,9},{2,18},{10... | collective-permute-start | bytes 294920 | tf_op jit(solution)/shard_map/ppermute | solution.py:295
  5.4 11.0 %collective-permute-start.4 = (bf16[6,64,128]{2,1,0:T(8,128)(2,1)S(1)}, bf16[6,64,128]{2,1,0:T(8,128)(2,1)S(1)}, u32[]{:S(2)}, u32[]{:S(2)}) collective-permute-start(bf16[6,64,128]{2,1,0:T(8,128)(2,1)S(1)} %get-tuple-element.22), channel_id=1, source_target_pairs={{0,8},{8,16},{16,24},{24,0},{1,9},{9,17},{17,25},{25,1},{2,10},{10... | collective-permute-start | bytes 294920 | tf_op jit(solution)/shard_map/ppermute | solution.py:295
  7.0 9.3 %collective-permute-start.5 = (bf16[6,64,128]{2,1,0:T(8,128)(2,1)S(1)}, bf16[6,64,128]{2,1,0:T(8,128)(2,1)S(1)}, u32[]{:S(2)}, u32[]{:S(2)}) collective-permute-start(bf16[6,64,128]{2,1,0:T(8,128)(2,1)S(1)} %get-tuple-element.23), channel_id=1, source_target_pairs={{0,24},{8,0},{16,8},{24,16},{1,25},{9,1},{17,9},{25,17},{2,26},{10... | collective-permute-start | bytes 294920 | tf_op jit(solution)/shard_map/ppermute | solution.py:295
  9.3 8.6 %collective-permute-start = (bf16[2,64,128]{2,1,0:T(8,128)(2,1)S(1)}, bf16[2,64,128]{2,1,0:T(8,128)(2,1)S(1)}, u32[]{:S(2)}, u32[]{:S(2)}) collective-permute-start(bf16[2,64,128]{2,1,0:T(8,128)(2,1)S(1)} %get-tuple-element.15), channel_id=1, source_target_pairs={{0,16},{8,24},{16,0},{24,8},{1,17},{9,25},{17,1},{25,9},{2,18},{10... | collective-permute-start | bytes 98312 | tf_op jit(solution)/shard_map/ppermute | solution.py:295
  9.3 8.6 %collective-permute-start.1 = (bf16[2,64,128]{2,1,0:T(8,128)(2,1)S(1)}, bf16[2,64,128]{2,1,0:T(8,128)(2,1)S(1)}, u32[]{:S(2)}, u32[]{:S(2)}) collective-permute-start(bf16[2,64,128]{2,1,0:T(8,128)(2,1)S(1)} %get-tuple-element.16), channel_id=1, source_target_pairs={{0,8},{8,16},{16,24},{24,0},{1,9},{9,17},{17,25},{25,1},{2,10},{10... | collective-permute-start | bytes 98312 | tf_op jit(solution)/shard_map/ppermute | solution.py:295
  13.7 4.2 %collective-permute-start.2 = (bf16[2,64,128]{2,1,0:T(8,128)(2,1)S(1)}, bf16[2,64,128]{2,1,0:T(8,128)(2,1)S(1)}, u32[]{:S(2)}, u32[]{:S(2)}) collective-permute-start(bf16[2,64,128]{2,1,0:T(8,128)(2,1)S(1)} %get-tuple-element.17), channel_id=1, source_target_pairs={{0,24},{8,0},{16,8},{24,16},{1,25},{9,1},{17,9},{25,17},{2,26},{10... | collective-permute-start | bytes 98312 | tf_op jit(solution)/shard_map/ppermute | solution.py:295
  14.5 0.7 %copy-start.2 = (s32[4]{0:T(128)S(1)}, s32[4]{0:T(128)}, u32[]{:S(2)}) copy-start(s32[4]{0:T(128)} %param.4) | copy-start | bytes 52
  16.4 14.3 %copy-start.1 = (bf16[2,2,256,256]{3,2,1,0:T(8,128)(2,1)S(1)}, bf16[2,2,256,256]{3,2,1,0:T(8,128)(2,1)}, u32[]{:S(2)}) copy-start(bf16[2,2,256,256]{3,2,1,0:T(8,128)(2,1)} %constant.2.clone.table_ref) | copy-start | bytes 1572868

commit v29 on v27

--- a/solution.py
+++ b/solution.py
@@ -50,8 +50,8 @@
     own_group = lax.axis_index("chan")
     first_bin = lax.axis_index("freq") * freq_dev + own_group * bins
     sender = lax.broadcasted_iota(jnp.int32, (groups, groups), 1)
-    distance = lax.broadcasted_iota(jnp.int32, (groups, groups), 0)
-    sends = lax.rem(own_group + groups - distance, groups) == sender
+    mask = lax.broadcasted_iota(jnp.int32, (groups, groups), 0)
+    sends = lax.bitwise_xor(own_group, mask) == sender
     places = jnp.sum(jnp.where(sends, position_ref[...], 0), axis=1, keepdims=True)
     place_ref[...] = jnp.broadcast_to(places, place_ref.shape)
 
@@ -85,15 +85,15 @@
     out_refs, wide_ref = refs[-1 - len(cuts) : -1], refs[-1]
     own_group = lax.axis_index("chan")
     widened = []
-    for (distance, start, size), out_ref in zip(cuts, out_refs):
-        if distance not in widened:
-            group = lax.rem(own_group + distance, groups)
+    for (mask, start, size), out_ref in zip(cuts, out_refs):
+        if mask not in widened:
+            group = lax.bitwise_xor(own_group, mask)
             index = len(widened)
             value = spec_ref[:, group].astype(jnp.float32).reshape(rows * bins, BLOCK)
             wide_ref[index, : rows * bins] = value
-            widened.append(distance)
+            widened.append(mask)
         for f in range(size):
-            value = wide_ref[widened.index(distance), pl.ds(start + f, rows, stride=bins), :]
+            value = wide_ref[widened.index(mask), pl.ds(start + f, rows, stride=bins), :]
             out_ref[f] = value.astype(jnp.bfloat16)
 
 
@@ -117,8 +117,8 @@
     rows = placed_ref.shape[2]
     windows = rows // 2
     places = place_ref[...]
-    for distance, chunk_ref in zip(order, chunk_refs):
-        placed_ref[places[distance, 0]] = chunk_ref[...]
+    for mask, chunk_ref in zip(order, chunk_refs):
+        placed_ref[places[mask, 0]] = chunk_ref[...]
 
     row_index = lax.broadcasted_iota(jnp.int32, (BLOCK, BLOCK), 0)
     lag_index = lax.broadcasted_iota(jnp.int32, (BLOCK, BLOCK), 1)
@@ -269,7 +269,7 @@
     whole = spectra.reshape(rows, groups, bins, BLOCK)
 
     def cut(cuts, *earlier):
-        distances = {distance for distance, _, _ in cuts}
+        masks = {mask for mask, _, _ in cuts}
         return pl.pallas_call(
             functools.partial(chunk_kernel, cuts),
             out_shape=tuple(
@@ -277,7 +277,7 @@
             ),
             in_specs=[vmem] + [anywhere] * len(earlier),
             out_specs=(vmem,) * len(cuts),
-            scratch_shapes=[pltpu.VMEM((len(distances), (rows + 1) * bins, BLOCK), jnp.float32)],
+            scratch_shapes=[pltpu.VMEM((len(masks), (rows + 1) * bins, BLOCK), jnp.float32)],
             compiler_params=params,
             cost_estimate=pl.CostEstimate(flops=10**7, bytes_accessed=10**6, transcendentals=0),
             name="chunks_of_bins",
@@ -285,13 +285,13 @@
 
     late = max(1, 3 * bins // 8) if bins > 1 else 0
     pieces = [(0, bins - late), (bins - late, late)] if late else [(0, bins)]
-    order = sorted(range(1, groups), key=lambda steps: abs(2 * steps - groups)) + [0]
-    cuts = [(distance, *piece) for piece in pieces for distance in order]
+    order = list(range(groups // 2, groups)) + list(range(groups // 2 - 1, -1, -1))
+    cuts = [(mask, *piece) for piece in pieces for mask in order]
     (first_chunk,) = cut(cuts[:1])
     chunks = dict(zip(cuts, (first_chunk, *cut(cuts[1:], first_chunk))))
     for key in cuts:
         if key[0]:
-            pairs = [(source, (source + key[0]) % groups) for source in range(groups)]
+            pairs = [(source, source ^ key[0]) for source in range(groups)]
             chunks[key] = lax.ppermute(chunks[key], "chan", pairs)
     chunks[cuts[0]] = pl.pallas_call(
         copy_kernel,
@@ -334,7 +334,7 @@
             ),
             name="stack_and_slant",
         )(
-            *[chunks[distance, start, size] for distance in order],
+            *[chunks[mask, start, size] for mask in order],
             places,
             lag_table,
             shift_table,

time: 31.4 us -> 32 us (1.019)
  blocking collectives: 12.5 us -> 13.2 us
    all_to_all x1, blocking collectives: 12.5 us -> 13.2 us  [shards(): lax.all_to_all(terms, ('chan', 'freq'), split_axis=0, concat_axis=0, axis...]
  transfers between devices with their start and end apart: 6 -> 6, of which waited for: 1 -> 2; matrix products, arithmetic and copies ran while one was open for 0% -> 0% of each run, Pallas kernels for 9% -> 9%
where the time goes in v29:
time: 32 us; the launch traced here: 31.8 us
  blocking collectives  13.2 us (41%)
  starting transfers between devices  11.2 us (35%)
  Pallas kernels  4.75 us (15%)
  local copies, waits for them, and re-layouts  1.7 us (5%)
  waiting for transfers between devices  0.85 us (3%)
    all_to_all x1, blocking collectives, shards(): lax.all_to_all(terms, ('chan', 'freq'), split_axis=0, concat_axis=0, axis...  13.2 us
    ppermute x6, starting transfers between devices, shards(): chunks[key] = lax.ppermute(chunks[key], 'chan', pairs)  11.2 us
    pallas_call x2, Pallas kernels, shards(): pl.pallas_call(functools.partial(stack_kernel, order, start, size, parts...  2.41 us
    unnamed x6, local copies, waits for them, and re-layouts  1.7 us
    pallas_call x1, Pallas kernels, shards(): pl.pallas_call(functools.partial(table_kernel, groups, bins, freq_dev), o...  1.18 us
    pallas_call x1, Pallas kernels, shards(): pl.pallas_call(functools.partial(image_kernel, slow_dev, spans), out_shap...  0.89 us
    ppermute x6, waiting for transfers between devices, shards(): chunks[key] = lax.ppermute(chunks[key], 'chan', pairs)  0.85 us
  transfers between devices with their start and end apart: 6, of which 2 were waited for; matrix products, arithmetic and copies ran while one was open for 0% of the time, Pallas kernels for 9%

profile of v29, /device:TPU:0, one launch (start us, length us, event | category | flops | bytes accessed | tf_op | source)
XLA Modules:
  0.0 31.8 jit_solution(3849114292280983611)
XLA Ops:
  0.0 0.0 copy-start
  0.0 1.0 %copy-done = bf16[2,32,32,128]{3,2,1,0:T(8,128)(2,1)S(1)} copy-done((bf16[2,32,32,128]{3,2,1,0:T(8,128)(2,1)S(1)}, bf16[2,32,32,128]{3,2,1,0:T(8,128)(2,1)}, u32[]{:S(2)}) %copy-start) | copy-done | bytes 524312
  1.1 4.1 %collective-permute-start.3 = (bf16[5,64,128]{2,1,0:T(8,128)(2,1)S(1)}, bf16[5,64,128]{2,1,0:T(8,128)(2,1)S(1)}, u32[]{:S(2)}, u32[]{:S(2)}) collective-permute-start(bf16[5,64,128]{2,1,0:T(8,128)(2,1)S(1)} %chunks_of_bins.2.refs_0_), channel_id=1, source_target_pairs={{0,16},{8,24},{16,0},{24,8},{1,17},{9,25},{17,1},{25,9},{2,18},{10... | collective-permute-start | bytes 245768 | tf_op jit(solution)/shard_map/ppermute | solution.py:295
  5.2 0.2 chunks_of_bins.3
  5.4 1.4 %collective-permute-start.4 = (bf16[5,64,128]{2,1,0:T(8,128)(2,1)S(1)}, bf16[5,64,128]{2,1,0:T(8,128)(2,1)S(1)}, u32[]{:S(2)}, u32[]{:S(2)}) collective-permute-start(bf16[5,64,128]{2,1,0:T(8,128)(2,1)S(1)} %get-tuple-element.22), channel_id=1, source_target_pairs={{0,24},{8,16},{16,8},{24,0},{1,25},{9,17},{17,9},{25,1},{2,26},{10... | collective-permute-start | bytes 245768 | tf_op jit(solution)/shard_map/ppermute | solution.py:295
  6.8 0.3 collective-permute-start.5
  7.1 2.7 %collective-permute-start = (bf16[3,64,128]{2,1,0:T(8,128)(2,1)S(1)}, bf16[3,64,128]{2,1,0:T(8,128)(2,1)S(1)}, u32[]{:S(2)}, u32[]{:S(2)}) collective-permute-start(bf16[3,64,128]{2,1,0:T(8,128)(2,1)S(1)} %get-tuple-element.15), channel_id=1, source_target_pairs={{0,16},{8,24},{16,0},{24,8},{1,17},{9,25},{17,1},{25,9},{2,18},{10... | collective-permute-start | bytes 147464 | tf_op jit(solution)/shard_map/ppermute | solution.py:295
  9.9 1.4 %collective-permute-start.1 = (bf16[3,64,128]{2,1,0:T(8,128)(2,1)S(1)}, bf16[3,64,128]{2,1,0:T(8,128)(2,1)S(1)}, u32[]{:S(2)}, u32[]{:S(2)}) collective-permute-start(bf16[3,64,128]{2,1,0:T(8,128)(2,1)S(1)} %get-tuple-element.16), channel_id=1, source_target_pairs={{0,24},{8,16},{16,8},{24,0},{1,25},{9,17},{17,9},{25,1},{2,26},{10... | collective-permute-start | bytes 147464 | tf_op jit(solution)/shard_map/ppermute | solution.py:295
  11.2 0.0 collective-permute-done.3.in_ref
  11.2 1.3 %collective-permute-start.2 = (bf16[3,64,128]{2,1,0:T(8,128)(2,1)S(1)}, bf16[3,64,128]{2,1,0:T(8,128)(2,1)S(1)}, u32[]{:S(2)}, u32[]{:S(2)}) collective-permute-start(bf16[3,64,128]{2,1,0:T(8,128)(2,1)S(1)} %get-tuple-element.17), channel_id=1, source_target_pairs={{0,8},{8,0},{16,24},{24,16},{1,9},{9,1},{17,25},{25,17},{2,10},{10... | collective-permute-start | bytes 147464 | tf_op jit(solution)/shard_map/ppermute | solution.py:295
  12.5 0.0 copy-start.2
  12.5 0.7 %copy-done.2 = s32[4]{0:T(128)S(1)} copy-done((s32[4]{0:T(128)S(1)}, s32[4]{0:T(128)}, u32[]{:S(2)}) %copy-start.2) | copy-done | bytes 40
  13.2 1.2 %slant_tables.1 = (s32[4,128]{1,0:T(4,128)S(1)}, bf16[8,256,512]{2,1,0:T(8,128)(2,1)S(1)}, f32[8,2,8,256]{3,2,1,0:T(8,128)S(1)}) custom-call(s32[1,4]{1,0:T(1,128)S(1)} %bitcast.6), custom_call_target="tpu_custom_call" | custom-call | flops 10000000 | bytes 4000000 | tf_op jit(solution)/shard_map/slant_tables/pallas_call | solution.py:304
  14.4 0.0 collective-permute-done.4.refs_1_
  14.4 0.0 collective-permute-done.5.refs_2_
  14.4 0.0 copy-start.1
  14.4 1.3 %stack_and_slant.2.refs_7_ = f32[10,4,256]{2,1,0:T(4,128)S(1)} custom-call(bf16[5,64,128]{2,1,0:T(8,128)(2,1)S(1)} %first_arrived.1.refs_0_, bf16[5,64,128]{2,1,0:T(8,128)(2,1)S(1)} %collective-permute-done.4.refs_1_, bf16[5,64,128]{2,1,0:T(8,128)(2,1)S(1)} %collective-permute-done.5.refs_2_, bf16[5,64,128]{2,1,0:T(8,128)(2,1)S(1)} %get-tuple-element.24.refs_3_, ...), custom_call_target="tpu_custom_call" | custom-call | flops 200000000 | bytes 4000000 | tf_op jit(solution)/shard_map/stack_and_slant/pallas_call | solution.py:321
  15.7 0.7 %collective-permute-done.refs_0_ = bf16[3,64,128]{2,1,0:T(8,128)(2,1)S(1)} collective-permute-done((bf16[3,64,128]{2,1,0:T(8,128)(2,1)S(1)}, bf16[3,64,128]{2,1,0:T(8,128)(2,1)S(1)}, u32[]{:S(2)}, u32[]{:S(2)}) %collective-permute-start) | collective-permute-done | bytes 49184 | tf_op jit(solution)/shard_map/ppermute | solution.py:295
  16.4 0.0 collective-permute-done.1.refs_1_
  16.4 0.1 collective-permute-done.2.refs_2_
  16.6 1.1 %stack_and_slant.3 = f32[4,8,4,128]{3,2,1,0:T(4,128)S(1)} custom-call(bf16[3,64,128]{2,1,0:T(8,128)(2,1)S(1)} %collective-permute-done.refs_0_, bf16[3,64,128]{2,1,0:T(8,128)(2,1)S(1)} %collective-permute-done.1.refs_1_, bf16[3,64,128]{2,1,0:T(8,128)(2,1)S(1)} %collective-permute-done.2.refs_2_, bf16[3,64,128]{2,1,0:T(8,128)(2,1)S(1)} %get-tuple-element.18.refs_3_, ...), custom_call_target="tpu_custom_call" | custom-call | flops 200000000 | bytes 4000000 | tf_op jit(solution)/shard_map/stack_and_slant/pallas_call | solution.py:321
  17.7 13.2 %all_to_all.5.term_ref = f32[32,4,128]{2,1,0:T(4,128)S(1)} all-to-all(f32[32,4,128]{2,1,0:T(4,128)S(1)} %bitcast.5), channel_id=1, replica_groups={{31,30,29,28,27,26,25,24,23,22,21,20,19,18,17,16,15,14,13,12,11,10,9,8,..., dimensions={0} | all-to-all | bytes 131072 | tf_op jit(solution)/shard_map/all_to_all | solution.py:345
  30.9 0.0 copy-done.1
  30.9 0.9 %sum_of_bins.1 = f32[1,32,512]{2,1,0:T(8,128)} custom-call(f32[32,4,128]{2,1,0:T(4,128)S(1)} %all_to_all.5.term_ref, bf16[2,2,256,256]{3,2,1,0:T(8,128)(2,1)S(1)} %copy-done.1), custom_call_target="tpu_custom_call" | custom-call | tf_op jit(solution)/shard_map/sum_of_bins/pallas_call | solution.py:354
  (2 shorter events, 0.1 us)
Async XLA Ops:
  0.0 1.0 %copy-start = (bf16[2,32,32,128]{3,2,1,0:T(8,128)(2,1)S(1)}, bf16[2,32,32,128]{3,2,1,0:T(8,128)(2,1)}, u32[]{:S(2)}) copy-start(bf16[2,32,32,128]{3,2,1,0:T(8,128)(2,1)} %param.3) | copy-start | bytes 1572868
  1.1 10.1 %collective-permute-start.3 = (bf16[5,64,128]{2,1,0:T(8,128)(2,1)S(1)}, bf16[5,64,128]{2,1,0:T(8,128)(2,1)S(1)}, u32[]{:S(2)}, u32[]{:S(2)}) collective-permute-start(bf16[5,64,128]{2,1,0:T(8,128)(2,1)S(1)} %chunks_of_bins.2.refs_0_), channel_id=1, source_target_pairs={{0,16},{8,24},{16,0},{24,8},{1,17},{9,25},{17,1},{25,9},{2,18},{10... | collective-permute-start | bytes 245768 | tf_op jit(solution)/shard_map/ppermute | solution.py:295
  5.4 9.0 %collective-permute-start.4 = (bf16[5,64,128]{2,1,0:T(8,128)(2,1)S(1)}, bf16[5,64,128]{2,1,0:T(8,128)(2,1)S(1)}, u32[]{:S(2)}, u32[]{:S(2)}) collective-permute-start(bf16[5,64,128]{2,1,0:T(8,128)(2,1)S(1)} %get-tuple-element.22), channel_id=1, source_target_pairs={{0,24},{8,16},{16,8},{24,0},{1,25},{9,17},{17,9},{25,1},{2,26},{10... | collective-permute-start | bytes 245768 | tf_op jit(solution)/shard_map/ppermute | solution.py:295
  6.8 7.6 %collective-permute-start.5 = (bf16[5,64,128]{2,1,0:T(8,128)(2,1)S(1)}, bf16[5,64,128]{2,1,0:T(8,128)(2,1)S(1)}, u32[]{:S(2)}, u32[]{:S(2)}) collective-permute-start(bf16[5,64,128]{2,1,0:T(8,128)(2,1)S(1)} %get-tuple-element.23), channel_id=1, source_target_pairs={{0,8},{8,0},{16,24},{24,16},{1,9},{9,1},{17,25},{25,17},{2,10},{10... | collective-permute-start | bytes 245768 | tf_op jit(solution)/shard_map/ppermute | solution.py:295
  7.1 9.3 %collective-permute-start = (bf16[3,64,128]{2,1,0:T(8,128)(2,1)S(1)}, bf16[3,64,128]{2,1,0:T(8,128)(2,1)S(1)}, u32[]{:S(2)}, u32[]{:S(2)}) collective-permute-start(bf16[3,64,128]{2,1,0:T(8,128)(2,1)S(1)} %get-tuple-element.15), channel_id=1, source_target_pairs={{0,16},{8,24},{16,0},{24,8},{1,17},{9,25},{17,1},{25,9},{2,18},{10... | collective-permute-start | bytes 147464 | tf_op jit(solution)/shard_map/ppermute | solution.py:295
  9.9 6.6 %collective-permute-start.1 = (bf16[3,64,128]{2,1,0:T(8,128)(2,1)S(1)}, bf16[3,64,128]{2,1,0:T(8,128)(2,1)S(1)}, u32[]{:S(2)}, u32[]{:S(2)}) collective-permute-start(bf16[3,64,128]{2,1,0:T(8,128)(2,1)S(1)} %get-tuple-element.16), channel_id=1, source_target_pairs={{0,24},{8,16},{16,8},{24,0},{1,25},{9,17},{17,9},{25,1},{2,26},{10... | collective-permute-start | bytes 147464 | tf_op jit(solution)/shard_map/ppermute | solution.py:295
  11.2 5.3 %collective-permute-start.2 = (bf16[3,64,128]{2,1,0:T(8,128)(2,1)S(1)}, bf16[3,64,128]{2,1,0:T(8,128)(2,1)S(1)}, u32[]{:S(2)}, u32[]{:S(2)}) collective-permute-start(bf16[3,64,128]{2,1,0:T(8,128)(2,1)S(1)} %get-tuple-element.17), channel_id=1, source_target_pairs={{0,8},{8,0},{16,24},{24,16},{1,9},{9,1},{17,25},{25,17},{2,10},{10... | collective-permute-start | bytes 147464 | tf_op jit(solution)/shard_map/ppermute | solution.py:295
  12.5 0.7 %copy-start.2 = (s32[4]{0:T(128)S(1)}, s32[4]{0:T(128)}, u32[]{:S(2)}) copy-start(s32[4]{0:T(128)} %param.4) | copy-start | bytes 52
  14.4 16.5 %copy-start.1 = (bf16[2,2,256,256]{3,2,1,0:T(8,128)(2,1)S(1)}, bf16[2,2,256,256]{3,2,1,0:T(8,128)(2,1)}, u32[]{:S(2)}) copy-start(bf16[2,2,256,256]{3,2,1,0:T(8,128)(2,1)} %constant.2.clone.table_ref) | copy-start | bytes 1572868

commit v30 on v28

--- a/solution.py
+++ b/solution.py
@@ -283,7 +283,7 @@
             name="chunks_of_bins",
         )(whole, *earlier)
 
-    late = max(1, bins // 4) if bins > 1 else 0
+    late = bins // 2
     pieces = [(0, bins - late), (bins - late, late)] if late else [(0, bins)]
     order = sorted(range(1, groups), key=lambda steps: abs(2 * steps - groups)) + [0]
     cuts = [(distance, *piece) for piece in pieces for distance in order]

time: 31.7 us -> 31.5 us (level)
  waiting for transfers between devices: 3.9 us -> 0.37 us
  starting transfers between devices: 9.31 us -> 11.8 us
  blocking collectives: 11.8 us -> 12.6 us
    ppermute x6, waiting for transfers between devices: 3.9 us -> 0.37 us  [shards(): chunks[key] = lax.ppermute(chunks[key], 'chan', pairs)]
    ppermute x6, starting transfers between devices: 9.31 us -> 11.8 us  [shards(): chunks[key] = lax.ppermute(chunks[key], 'chan', pairs)]
    all_to_all x1, blocking collectives: 11.8 us -> 12.6 us  [shards(): lax.all_to_all(terms, ('chan', 'freq'), split_axis=0, concat_axis=0, axis...]
  transfers between devices with their start and end apart: 6 -> 6, of which waited for: 1 -> 1; matrix products, arithmetic and copies ran while one was open for 0% -> 0% of each run, Pallas kernels for 9% -> 8%
where the time goes in v30:
time: 31.5 us; the launch traced here: 31.3 us
  blocking collectives  12.6 us (40%)
  starting transfers between devices  11.8 us (37%)
  Pallas kernels  4.79 us (15%)
  local copies, waits for them, and re-layouts  1.7 us (5%)
  waiting for transfers between devices  0.37 us (1%)
    all_to_all x1, blocking collectives, shards(): lax.all_to_all(terms, ('chan', 'freq'), split_axis=0, concat_axis=0, axis...  12.6 us
    ppermute x6, starting transfers between devices, shards(): chunks[key] = lax.ppermute(chunks[key], 'chan', pairs)  11.8 us
    pallas_call x2, Pallas kernels, shards(): pl.pallas_call(functools.partial(stack_kernel, order, start, size, parts...  2.45 us
    unnamed x6, local copies, waits for them, and re-layouts  1.7 us
    pallas_call x1, Pallas kernels, shards(): pl.pallas_call(functools.partial(table_kernel, groups, bins, freq_dev), o...  1.19 us
    pallas_call x1, Pallas kernels, shards(): pl.pallas_call(functools.partial(image_kernel, slow_dev, spans), out_shap...  0.88 us
  transfers between devices with their start and end apart: 6, of which 1 were waited for; matrix products, arithmetic and copies ran while one was open for 0% of the time, Pallas kernels for 8%

profile of v30, /device:TPU:0, one launch (start us, length us, event | category | flops | bytes accessed | tf_op | source)
XLA Modules:
  0.0 31.3 jit_solution(5323738896776210185)
XLA Ops:
  0.0 0.0 copy-start
  0.0 1.0 %copy-done = bf16[2,32,32,128]{3,2,1,0:T(8,128)(2,1)S(1)} copy-done((bf16[2,32,32,128]{3,2,1,0:T(8,128)(2,1)S(1)}, bf16[2,32,32,128]{3,2,1,0:T(8,128)(2,1)}, u32[]{:S(2)}) %copy-start) | copy-done | bytes 524312
  1.1 4.1 %collective-permute-start.3 = (bf16[4,64,128]{2,1,0:T(8,128)(2,1)S(1)}, bf16[4,64,128]{2,1,0:T(8,128)(2,1)S(1)}, u32[]{:S(2)}, u32[]{:S(2)}) collective-permute-start(bf16[4,64,128]{2,1,0:T(8,128)(2,1)S(1)} %chunks_of_bins.2.refs_0_), channel_id=1, source_target_pairs={{0,16},{8,24},{16,0},{24,8},{1,17},{9,25},{17,1},{25,9},{2,18},{10... | collective-permute-start | bytes 196616 | tf_op jit(solution)/shard_map/ppermute | solution.py:295
  5.2 0.2 chunks_of_bins.3
  5.4 1.6 %collective-permute-start.4 = (bf16[4,64,128]{2,1,0:T(8,128)(2,1)S(1)}, bf16[4,64,128]{2,1,0:T(8,128)(2,1)S(1)}, u32[]{:S(2)}, u32[]{:S(2)}) collective-permute-start(bf16[4,64,128]{2,1,0:T(8,128)(2,1)S(1)} %get-tuple-element.22), channel_id=1, source_target_pairs={{0,8},{8,16},{16,24},{24,0},{1,9},{9,17},{17,25},{25,1},{2,10},{10... | collective-permute-start | bytes 196616 | tf_op jit(solution)/shard_map/ppermute | solution.py:295
  7.0 2.2 %collective-permute-start.5 = (bf16[4,64,128]{2,1,0:T(8,128)(2,1)S(1)}, bf16[4,64,128]{2,1,0:T(8,128)(2,1)S(1)}, u32[]{:S(2)}, u32[]{:S(2)}) collective-permute-start(bf16[4,64,128]{2,1,0:T(8,128)(2,1)S(1)} %get-tuple-element.23), channel_id=1, source_target_pairs={{0,24},{8,0},{16,8},{24,16},{1,25},{9,1},{17,9},{25,17},{2,26},{10... | collective-permute-start | bytes 196616 | tf_op jit(solution)/shard_map/ppermute | solution.py:295
  9.3 0.0 collective-permute-start
  9.3 0.6 %collective-permute-start.1 = (bf16[4,64,128]{2,1,0:T(8,128)(2,1)S(1)}, bf16[4,64,128]{2,1,0:T(8,128)(2,1)S(1)}, u32[]{:S(2)}, u32[]{:S(2)}) collective-permute-start(bf16[4,64,128]{2,1,0:T(8,128)(2,1)S(1)} %get-tuple-element.16), channel_id=1, source_target_pairs={{0,8},{8,16},{16,24},{24,0},{1,9},{9,17},{17,25},{25,1},{2,10},{10... | collective-permute-start | bytes 196616 | tf_op jit(solution)/shard_map/ppermute | solution.py:295
  9.9 0.0 collective-permute-done.3.in_ref
  9.9 3.3 %collective-permute-start.2 = (bf16[4,64,128]{2,1,0:T(8,128)(2,1)S(1)}, bf16[4,64,128]{2,1,0:T(8,128)(2,1)S(1)}, u32[]{:S(2)}, u32[]{:S(2)}) collective-permute-start(bf16[4,64,128]{2,1,0:T(8,128)(2,1)S(1)} %get-tuple-element.17), channel_id=1, source_target_pairs={{0,24},{8,0},{16,8},{24,16},{1,25},{9,1},{17,9},{25,17},{2,26},{10... | collective-permute-start | bytes 196616 | tf_op jit(solution)/shard_map/ppermute | solution.py:295
  13.1 0.0 copy-start.2
  13.1 0.7 %copy-done.2 = s32[4]{0:T(128)S(1)} copy-done((s32[4]{0:T(128)S(1)}, s32[4]{0:T(128)}, u32[]{:S(2)}) %copy-start.2) | copy-done | bytes 40
  13.8 1.2 %slant_tables.1 = (s32[4,128]{1,0:T(4,128)S(1)}, bf16[8,256,512]{2,1,0:T(8,128)(2,1)S(1)}, f32[8,2,8,256]{3,2,1,0:T(8,128)S(1)}) custom-call(s32[1,4]{1,0:T(1,128)S(1)} %bitcast.6), custom_call_target="tpu_custom_call" | custom-call | flops 10000000 | bytes 4000000 | tf_op jit(solution)/shard_map/slant_tables/pallas_call | solution.py:304
  15.0 0.0 collective-permute-done.4.refs_1_
  15.0 0.0 collective-permute-done.5.refs_2_
  15.0 0.0 copy-start.1
  15.0 1.2 %stack_and_slant.2.refs_7_ = f32[8,4,256]{2,1,0:T(4,128)S(1)} custom-call(bf16[4,64,128]{2,1,0:T(8,128)(2,1)S(1)} %first_arrived.1.refs_0_, bf16[4,64,128]{2,1,0:T(8,128)(2,1)S(1)} %collective-permute-done.4.refs_1_, bf16[4,64,128]{2,1,0:T(8,128)(2,1)S(1)} %collective-permute-done.5.refs_2_, bf16[4,64,128]{2,1,0:T(8,128)(2,1)S(1)} %get-tuple-element.24.refs_3_, ...), custom_call_target="tpu_custom_call" | custom-call | flops 200000000 | bytes 4000000 | tf_op jit(solution)/shard_map/stack_and_slant/pallas_call | solution.py:321
  16.2 0.4 %collective-permute-done.refs_0_ = bf16[4,64,128]{2,1,0:T(8,128)(2,1)S(1)} collective-permute-done((bf16[4,64,128]{2,1,0:T(8,128)(2,1)S(1)}, bf16[4,64,128]{2,1,0:T(8,128)(2,1)S(1)}, u32[]{:S(2)}, u32[]{:S(2)}) %collective-permute-start) | collective-permute-done | bytes 65568 | tf_op jit(solution)/shard_map/ppermute | solution.py:295
  16.5 0.0 collective-permute-done.1.refs_1_
  16.6 0.0 collective-permute-done.2.refs_2_
  16.6 1.3 %stack_and_slant.3 = f32[4,8,4,128]{3,2,1,0:T(4,128)S(1)} custom-call(bf16[4,64,128]{2,1,0:T(8,128)(2,1)S(1)} %collective-permute-done.refs_0_, bf16[4,64,128]{2,1,0:T(8,128)(2,1)S(1)} %collective-permute-done.1.refs_1_, bf16[4,64,128]{2,1,0:T(8,128)(2,1)S(1)} %collective-permute-done.2.refs_2_, bf16[4,64,128]{2,1,0:T(8,128)(2,1)S(1)} %get-tuple-element.18.refs_3_, ...), custom_call_target="tpu_custom_call" | custom-call | flops 200000000 | bytes 4000000 | tf_op jit(solution)/shard_map/stack_and_slant/pallas_call | solution.py:321
  17.8 12.6 %all_to_all.5.term_ref = f32[32,4,128]{2,1,0:T(4,128)S(1)} all-to-all(f32[32,4,128]{2,1,0:T(4,128)S(1)} %bitcast.5), channel_id=1, replica_groups={{31,30,29,28,27,26,25,24,23,22,21,20,19,18,17,16,15,14,13,12,11,10,9,8,..., dimensions={0} | all-to-all | bytes 131072 | tf_op jit(solution)/shard_map/all_to_all | solution.py:345
  30.4 0.0 copy-done.1
  30.4 0.9 %sum_of_bins.1 = f32[1,32,512]{2,1,0:T(8,128)} custom-call(f32[32,4,128]{2,1,0:T(4,128)S(1)} %all_to_all.5.term_ref, bf16[2,2,256,256]{3,2,1,0:T(8,128)(2,1)S(1)} %copy-done.1), custom_call_target="tpu_custom_call" | custom-call | tf_op jit(solution)/shard_map/sum_of_bins/pallas_call | solution.py:354
  (2 shorter events, 0.0 us)
Async XLA Ops:
  0.0 1.0 %copy-start = (bf16[2,32,32,128]{3,2,1,0:T(8,128)(2,1)S(1)}, bf16[2,32,32,128]{3,2,1,0:T(8,128)(2,1)}, u32[]{:S(2)}) copy-start(bf16[2,32,32,128]{3,2,1,0:T(8,128)(2,1)} %param.3) | copy-start | bytes 1572868
  1.1 8.8 %collective-permute-start.3 = (bf16[4,64,128]{2,1,0:T(8,128)(2,1)S(1)}, bf16[4,64,128]{2,1,0:T(8,128)(2,1)S(1)}, u32[]{:S(2)}, u32[]{:S(2)}) collective-permute-start(bf16[4,64,128]{2,1,0:T(8,128)(2,1)S(1)} %chunks_of_bins.2.refs_0_), channel_id=1, source_target_pairs={{0,16},{8,24},{16,0},{24,8},{1,17},{9,25},{17,1},{25,9},{2,18},{10... | collective-permute-start | bytes 196616 | tf_op jit(solution)/shard_map/ppermute | solution.py:295
  5.4 9.6 %collective-permute-start.4 = (bf16[4,64,128]{2,1,0:T(8,128)(2,1)S(1)}, bf16[4,64,128]{2,1,0:T(8,128)(2,1)S(1)}, u32[]{:S(2)}, u32[]{:S(2)}) collective-permute-start(bf16[4,64,128]{2,1,0:T(8,128)(2,1)S(1)} %get-tuple-element.22), channel_id=1, source_target_pairs={{0,8},{8,16},{16,24},{24,0},{1,9},{9,17},{17,25},{25,1},{2,10},{10... | collective-permute-start | bytes 196616 | tf_op jit(solution)/shard_map/ppermute | solution.py:295
  7.0 7.9 %collective-permute-start.5 = (bf16[4,64,128]{2,1,0:T(8,128)(2,1)S(1)}, bf16[4,64,128]{2,1,0:T(8,128)(2,1)S(1)}, u32[]{:S(2)}, u32[]{:S(2)}) collective-permute-start(bf16[4,64,128]{2,1,0:T(8,128)(2,1)S(1)} %get-tuple-element.23), channel_id=1, source_target_pairs={{0,24},{8,0},{16,8},{24,16},{1,25},{9,1},{17,9},{25,17},{2,26},{10... | collective-permute-start | bytes 196616 | tf_op jit(solution)/shard_map/ppermute | solution.py:295
  9.3 7.3 %collective-permute-start = (bf16[4,64,128]{2,1,0:T(8,128)(2,1)S(1)}, bf16[4,64,128]{2,1,0:T(8,128)(2,1)S(1)}, u32[]{:S(2)}, u32[]{:S(2)}) collective-permute-start(bf16[4,64,128]{2,1,0:T(8,128)(2,1)S(1)} %get-tuple-element.15), channel_id=1, source_target_pairs={{0,16},{8,24},{16,0},{24,8},{1,17},{9,25},{17,1},{25,9},{2,18},{10... | collective-permute-start | bytes 196616 | tf_op jit(solution)/shard_map/ppermute | solution.py:295
  9.3 7.3 %collective-permute-start.1 = (bf16[4,64,128]{2,1,0:T(8,128)(2,1)S(1)}, bf16[4,64,128]{2,1,0:T(8,128)(2,1)S(1)}, u32[]{:S(2)}, u32[]{:S(2)}) collective-permute-start(bf16[4,64,128]{2,1,0:T(8,128)(2,1)S(1)} %get-tuple-element.16), channel_id=1, source_target_pairs={{0,8},{8,16},{16,24},{24,0},{1,9},{9,17},{17,25},{25,1},{2,10},{10... | collective-permute-start | bytes 196616 | tf_op jit(solution)/shard_map/ppermute | solution.py:295
  9.9 6.7 %collective-permute-start.2 = (bf16[4,64,128]{2,1,0:T(8,128)(2,1)S(1)}, bf16[4,64,128]{2,1,0:T(8,128)(2,1)S(1)}, u32[]{:S(2)}, u32[]{:S(2)}) collective-permute-start(bf16[4,64,128]{2,1,0:T(8,128)(2,1)S(1)} %get-tuple-element.17), channel_id=1, source_target_pairs={{0,24},{8,0},{16,8},{24,16},{1,25},{9,1},{17,9},{25,17},{2,26},{10... | collective-permute-start | bytes 196616 | tf_op jit(solution)/shard_map/ppermute | solution.py:295
  13.1 0.7 %copy-start.2 = (s32[4]{0:T(128)S(1)}, s32[4]{0:T(128)}, u32[]{:S(2)}) copy-start(s32[4]{0:T(128)} %param.4) | copy-start | bytes 52
  15.0 15.4 %copy-start.1 = (bf16[2,2,256,256]{3,2,1,0:T(8,128)(2,1)S(1)}, bf16[2,2,256,256]{3,2,1,0:T(8,128)(2,1)}, u32[]{:S(2)}) copy-start(bf16[2,2,256,256]{3,2,1,0:T(8,128)(2,1)} %constant.2.clone.table_ref) | copy-start | bytes 1572868

commit v31 on v30

--- a/solution.py
+++ b/solution.py
@@ -108,7 +108,7 @@
     return jnp.where(usable, scale / jnp.maximum(count, 1).astype(jnp.float32), 0.0)
 
 
-def stack_kernel(order, start, bins, parts, *refs):
+def stack_kernel(order, start, bins, parts, last, *refs):
     groups = len(order)
     chunk_refs = refs[:groups]
     place_ref, lag_ref, shift_ref = refs[groups : groups + 3]
@@ -190,25 +190,31 @@
         terms.append(turned_re[:groups] + turned_re[groups:])
         terms.append(turned_im[:groups] + turned_im[groups:])
 
-    if parts is None:
+    slow_dev = SLOWNESS // parts
+    spans = BLOCK // slow_dev
+    packed_rows = 0
+    if last:
+        for earlier_ref in reversed(earlier_refs):
+            if len(earlier_ref.shape) == 3:
+                terms = [earlier_ref[entry] for entry in range(earlier_ref.shape[0])] + terms
+            else:
+                packed_rows = earlier_ref.shape[2]
+                out_ref[:, :, :packed_rows] = earlier_ref[...]
+    elif len(out_ref.shape) == 3:
         for entry, term in enumerate(terms):
             out_ref[entry] = term
         return
-    for earlier_ref in reversed(earlier_refs):
-        terms = [earlier_ref[entry] for entry in range(earlier_ref.shape[0])] + terms
-    slow_dev = SLOWNESS // parts
-    spans = BLOCK // slow_dev
     span_index = lax.broadcasted_iota(jnp.int32, (groups, BLOCK), 1) // slow_dev
     for part in range(parts):
         source = (part % spans) * slow_dev
         lanes = slice(part // spans * BLOCK, (part // spans + 1) * BLOCK)
-        for row in range(out_ref.shape[2]):
+        for row in range(out_ref.shape[2] - packed_rows):
             packed = jnp.zeros((groups, BLOCK), jnp.float32)
             for span, term in enumerate(terms[row * spans : (row + 1) * spans]):
                 moved = pltpu.roll(term[:, lanes], (span * slow_dev - source) % BLOCK, 1)
                 packed = jnp.where(span_index == span, moved, packed)
             for delta in range(groups):
-                out_ref[groups - 1 - delta, parts - 1 - part, row] = packed[delta]
+                out_ref[groups - 1 - delta, parts - 1 - part, packed_rows + row] = packed[delta]
 
 
 def image_kernel(slow_dev, spans, term_ref, table_ref, out_ref):
@@ -317,9 +323,15 @@
     earlier = []
     for start, size in pieces:
         last = start + size == bins
-        shape = (groups, parts, message_rows, BLOCK) if last else (2 * size, groups, SLOWNESS)
+        own_rows, loose = divmod(2 * size * slow_dev, BLOCK)
+        if last:
+            shape = (groups, parts, message_rows, BLOCK)
+        elif loose:
+            shape = (2 * size, groups, SLOWNESS)
+        else:
+            shape = (groups, parts, own_rows, BLOCK)
         terms = pl.pallas_call(
-            functools.partial(stack_kernel, order, start, size, parts if last else None),
+            functools.partial(stack_kernel, order, start, size, parts, last),
             out_shape=jax.ShapeDtypeStruct(shape, jnp.float32),
             in_specs=[vmem] * (groups + 3 + len(earlier)),
             out_specs=vmem,

time: 31.5 us -> 31.5 us (level)
  transfers between devices with their start and end apart: 6 -> 6, of which waited for: 1 -> 1; matrix products, arithmetic and copies ran while one was open for 0% -> 0% of each run, Pallas kernels for 8% -> 9%
where the time goes in v31:
time: 31.5 us; the launch traced here: 31.3 us
  blocking collectives  12.6 us (40%)
  starting transfers between devices  11.8 us (37%)
  Pallas kernels  4.88 us (15%)
  local copies, waits for them, and re-layouts  1.7 us (5%)
    all_to_all x1, blocking collectives, shards(): lax.all_to_all(terms, ('chan', 'freq'), split_axis=0, concat_axis=0, axis...  12.6 us
    ppermute x6, starting transfers between devices, shards(): chunks[key] = lax.ppermute(chunks[key], 'chan', pairs)  11.8 us
    pallas_call x2, Pallas kernels, shards(): pl.pallas_call(functools.partial(stack_kernel, order, start, size, parts,...  2.54 us
    unnamed x6, local copies, waits for them, and re-layouts  1.7 us
    pallas_call x1, Pallas kernels, shards(): pl.pallas_call(functools.partial(table_kernel, groups, bins, freq_dev), o...  1.19 us
    pallas_call x1, Pallas kernels, shards(): pl.pallas_call(functools.partial(image_kernel, slow_dev, spans), out_shap...  0.88 us
  transfers between devices with their start and end apart: 6, of which 1 were waited for; matrix products, arithmetic and copies ran while one was open for 0% of the time, Pallas kernels for 9%

profile of v31, /device:TPU:0, one launch (start us, length us, event | category | flops | bytes accessed | tf_op | source)
XLA Modules:
  0.0 31.3 jit_solution(9101345817271432387)
XLA Ops:
  0.0 0.0 copy-start
  0.0 1.0 %copy-done = bf16[2,32,32,128]{3,2,1,0:T(8,128)(2,1)S(1)} copy-done((bf16[2,32,32,128]{3,2,1,0:T(8,128)(2,1)S(1)}, bf16[2,32,32,128]{3,2,1,0:T(8,128)(2,1)}, u32[]{:S(2)}) %copy-start) | copy-done | bytes 524312
  1.1 4.1 %collective-permute-start.3 = (bf16[4,64,128]{2,1,0:T(8,128)(2,1)S(1)}, bf16[4,64,128]{2,1,0:T(8,128)(2,1)S(1)}, u32[]{:S(2)}, u32[]{:S(2)}) collective-permute-start(bf16[4,64,128]{2,1,0:T(8,128)(2,1)S(1)} %chunks_of_bins.2.refs_0_), channel_id=1, source_target_pairs={{0,16},{8,24},{16,0},{24,8},{1,17},{9,25},{17,1},{25,9},{2,18},{10... | collective-permute-start | bytes 196616 | tf_op jit(solution)/shard_map/ppermute | solution.py:301
  5.2 0.2 chunks_of_bins.3
  5.4 1.6 %collective-permute-start.4 = (bf16[4,64,128]{2,1,0:T(8,128)(2,1)S(1)}, bf16[4,64,128]{2,1,0:T(8,128)(2,1)S(1)}, u32[]{:S(2)}, u32[]{:S(2)}) collective-permute-start(bf16[4,64,128]{2,1,0:T(8,128)(2,1)S(1)} %get-tuple-element.22), channel_id=1, source_target_pairs={{0,8},{8,16},{16,24},{24,0},{1,9},{9,17},{17,25},{25,1},{2,10},{10... | collective-permute-start | bytes 196616 | tf_op jit(solution)/shard_map/ppermute | solution.py:301
  7.0 2.2 %collective-permute-start.5 = (bf16[4,64,128]{2,1,0:T(8,128)(2,1)S(1)}, bf16[4,64,128]{2,1,0:T(8,128)(2,1)S(1)}, u32[]{:S(2)}, u32[]{:S(2)}) collective-permute-start(bf16[4,64,128]{2,1,0:T(8,128)(2,1)S(1)} %get-tuple-element.23), channel_id=1, source_target_pairs={{0,24},{8,0},{16,8},{24,16},{1,25},{9,1},{17,9},{25,17},{2,26},{10... | collective-permute-start | bytes 196616 | tf_op jit(solution)/shard_map/ppermute | solution.py:301
  9.3 0.0 collective-permute-start
  9.3 0.6 %collective-permute-start.1 = (bf16[4,64,128]{2,1,0:T(8,128)(2,1)S(1)}, bf16[4,64,128]{2,1,0:T(8,128)(2,1)S(1)}, u32[]{:S(2)}, u32[]{:S(2)}) collective-permute-start(bf16[4,64,128]{2,1,0:T(8,128)(2,1)S(1)} %get-tuple-element.16), channel_id=1, source_target_pairs={{0,8},{8,16},{16,24},{24,0},{1,9},{9,17},{17,25},{25,1},{2,10},{10... | collective-permute-start | bytes 196616 | tf_op jit(solution)/shard_map/ppermute | solution.py:301
  9.9 0.0 collective-permute-done.3.in_ref
  9.9 3.3 %collective-permute-start.2 = (bf16[4,64,128]{2,1,0:T(8,128)(2,1)S(1)}, bf16[4,64,128]{2,1,0:T(8,128)(2,1)S(1)}, u32[]{:S(2)}, u32[]{:S(2)}) collective-permute-start(bf16[4,64,128]{2,1,0:T(8,128)(2,1)S(1)} %get-tuple-element.17), channel_id=1, source_target_pairs={{0,24},{8,0},{16,8},{24,16},{1,25},{9,1},{17,9},{25,17},{2,26},{10... | collective-permute-start | bytes 196616 | tf_op jit(solution)/shard_map/ppermute | solution.py:301
  13.1 0.0 copy-start.2
  13.1 0.7 %copy-done.2 = s32[4]{0:T(128)S(1)} copy-done((s32[4]{0:T(128)S(1)}, s32[4]{0:T(128)}, u32[]{:S(2)}) %copy-start.2) | copy-done | bytes 40
  13.8 1.2 %slant_tables.1 = (s32[4,128]{1,0:T(4,128)S(1)}, bf16[8,256,512]{2,1,0:T(8,128)(2,1)S(1)}, f32[8,2,8,256]{3,2,1,0:T(8,128)S(1)}) custom-call(s32[1,4]{1,0:T(1,128)S(1)} %bitcast.6), custom_call_target="tpu_custom_call" | custom-call | flops 10000000 | bytes 4000000 | tf_op jit(solution)/shard_map/slant_tables/pallas_call | solution.py:310
  15.0 0.0 collective-permute-done.4.refs_1_
  15.0 0.0 collective-permute-done.5.refs_2_
  15.0 0.0 copy-start.1
  15.0 1.3 %stack_and_slant.2.refs_7_ = f32[4,8,2,128]{3,2,1,0:T(2,128)S(1)} custom-call(bf16[4,64,128]{2,1,0:T(8,128)(2,1)S(1)} %first_arrived.1.refs_0_, bf16[4,64,128]{2,1,0:T(8,128)(2,1)S(1)} %collective-permute-done.4.refs_1_, bf16[4,64,128]{2,1,0:T(8,128)(2,1)S(1)} %collective-permute-done.5.refs_2_, bf16[4,64,128]{2,1,0:T(8,128)(2,1)S(1)} %get-tuple-element.24.refs_3_, ...), custom_call_target="tpu_custom_call" | custom-call | flops 200000000 | bytes 4000000 | tf_op jit(solution)/shard_map/stack_and_slant/pallas_call | solution.py:333
  16.3 0.3 collective-permute-done.refs_0_
  16.5 0.0 collective-permute-done.1.refs_1_
  16.6 0.0 collective-permute-done.2.refs_2_
  16.6 1.3 %stack_and_slant.3 = f32[4,8,4,128]{3,2,1,0:T(4,128)S(1)} custom-call(bf16[4,64,128]{2,1,0:T(8,128)(2,1)S(1)} %collective-permute-done.refs_0_, bf16[4,64,128]{2,1,0:T(8,128)(2,1)S(1)} %collective-permute-done.1.refs_1_, bf16[4,64,128]{2,1,0:T(8,128)(2,1)S(1)} %collective-permute-done.2.refs_2_, bf16[4,64,128]{2,1,0:T(8,128)(2,1)S(1)} %get-tuple-element.18.refs_3_, ...), custom_call_target="tpu_custom_call" | custom-call | flops 200000000 | bytes 4000000 | tf_op jit(solution)/shard_map/stack_and_slant/pallas_call | solution.py:333
  17.8 12.6 %all_to_all.5.term_ref = f32[32,4,128]{2,1,0:T(4,128)S(1)} all-to-all(f32[32,4,128]{2,1,0:T(4,128)S(1)} %bitcast.5), channel_id=1, replica_groups={{31,30,29,28,27,26,25,24,23,22,21,20,19,18,17,16,15,14,13,12,11,10,9,8,..., dimensions={0} | all-to-all | bytes 131072 | tf_op jit(solution)/shard_map/all_to_all | solution.py:357
  30.4 0.0 copy-done.1
  30.4 0.9 %sum_of_bins.1 = f32[1,32,512]{2,1,0:T(8,128)} custom-call(f32[32,4,128]{2,1,0:T(4,128)S(1)} %all_to_all.5.term_ref, bf16[2,2,256,256]{3,2,1,0:T(8,128)(2,1)S(1)} %copy-done.1), custom_call_target="tpu_custom_call" | custom-call | tf_op jit(solution)/shard_map/sum_of_bins/pallas_call | solution.py:366
  (2 shorter events, 0.0 us)
Async XLA Ops:
  0.0 1.0 %copy-start = (bf16[2,32,32,128]{3,2,1,0:T(8,128)(2,1)S(1)}, bf16[2,32,32,128]{3,2,1,0:T(8,128)(2,1)}, u32[]{:S(2)}) copy-start(bf16[2,32,32,128]{3,2,1,0:T(8,128)(2,1)} %param.3) | copy-start | bytes 1572868
  1.1 8.8 %collective-permute-start.3 = (bf16[4,64,128]{2,1,0:T(8,128)(2,1)S(1)}, bf16[4,64,128]{2,1,0:T(8,128)(2,1)S(1)}, u32[]{:S(2)}, u32[]{:S(2)}) collective-permute-start(bf16[4,64,128]{2,1,0:T(8,128)(2,1)S(1)} %chunks_of_bins.2.refs_0_), channel_id=1, source_target_pairs={{0,16},{8,24},{16,0},{24,8},{1,17},{9,25},{17,1},{25,9},{2,18},{10... | collective-permute-start | bytes 196616 | tf_op jit(solution)/shard_map/ppermute | solution.py:301
  5.4 9.6 %collective-permute-start.4 = (bf16[4,64,128]{2,1,0:T(8,128)(2,1)S(1)}, bf16[4,64,128]{2,1,0:T(8,128)(2,1)S(1)}, u32[]{:S(2)}, u32[]{:S(2)}) collective-permute-start(bf16[4,64,128]{2,1,0:T(8,128)(2,1)S(1)} %get-tuple-element.22), channel_id=1, source_target_pairs={{0,8},{8,16},{16,24},{24,0},{1,9},{9,17},{17,25},{25,1},{2,10},{10... | collective-permute-start | bytes 196616 | tf_op jit(solution)/shard_map/ppermute | solution.py:301
  7.0 7.9 %collective-permute-start.5 = (bf16[4,64,128]{2,1,0:T(8,128)(2,1)S(1)}, bf16[4,64,128]{2,1,0:T(8,128)(2,1)S(1)}, u32[]{:S(2)}, u32[]{:S(2)}) collective-permute-start(bf16[4,64,128]{2,1,0:T(8,128)(2,1)S(1)} %get-tuple-element.23), channel_id=1, source_target_pairs={{0,24},{8,0},{16,8},{24,16},{1,25},{9,1},{17,9},{25,17},{2,26},{10... | collective-permute-start | bytes 196616 | tf_op jit(solution)/shard_map/ppermute | solution.py:301
  9.3 7.3 %collective-permute-start = (bf16[4,64,128]{2,1,0:T(8,128)(2,1)S(1)}, bf16[4,64,128]{2,1,0:T(8,128)(2,1)S(1)}, u32[]{:S(2)}, u32[]{:S(2)}) collective-permute-start(bf16[4,64,128]{2,1,0:T(8,128)(2,1)S(1)} %get-tuple-element.15), channel_id=1, source_target_pairs={{0,16},{8,24},{16,0},{24,8},{1,17},{9,25},{17,1},{25,9},{2,18},{10... | collective-permute-start | bytes 196616 | tf_op jit(solution)/shard_map/ppermute | solution.py:301
  9.3 7.3 %collective-permute-start.1 = (bf16[4,64,128]{2,1,0:T(8,128)(2,1)S(1)}, bf16[4,64,128]{2,1,0:T(8,128)(2,1)S(1)}, u32[]{:S(2)}, u32[]{:S(2)}) collective-permute-start(bf16[4,64,128]{2,1,0:T(8,128)(2,1)S(1)} %get-tuple-element.16), channel_id=1, source_target_pairs={{0,8},{8,16},{16,24},{24,0},{1,9},{9,17},{17,25},{25,1},{2,10},{10... | collective-permute-start | bytes 196616 | tf_op jit(solution)/shard_map/ppermute | solution.py:301
  9.9 6.7 %collective-permute-start.2 = (bf16[4,64,128]{2,1,0:T(8,128)(2,1)S(1)}, bf16[4,64,128]{2,1,0:T(8,128)(2,1)S(1)}, u32[]{:S(2)}, u32[]{:S(2)}) collective-permute-start(bf16[4,64,128]{2,1,0:T(8,128)(2,1)S(1)} %get-tuple-element.17), channel_id=1, source_target_pairs={{0,24},{8,0},{16,8},{24,16},{1,25},{9,1},{17,9},{25,17},{2,26},{10... | collective-permute-start | bytes 196616 | tf_op jit(solution)/shard_map/ppermute | solution.py:301
  13.1 0.7 %copy-start.2 = (s32[4]{0:T(128)S(1)}, s32[4]{0:T(128)}, u32[]{:S(2)}) copy-start(s32[4]{0:T(128)} %param.4) | copy-start | bytes 52
  15.0 15.4 %copy-start.1 = (bf16[2,2,256,256]{3,2,1,0:T(8,128)(2,1)S(1)}, bf16[2,2,256,256]{3,2,1,0:T(8,128)(2,1)}, u32[]{:S(2)}) copy-start(bf16[2,2,256,256]{3,2,1,0:T(8,128)(2,1)} %constant.2.clone.table_ref) | copy-start | bytes 1572868

commit v32 on v27

--- a/solution.py
+++ b/solution.py
@@ -288,7 +288,8 @@
     order = sorted(range(1, groups), key=lambda steps: abs(2 * steps - groups)) + [0]
     cuts = [(distance, *piece) for piece in pieces for distance in order]
     (first_chunk,) = cut(cuts[:1])
-    chunks = dict(zip(cuts, (first_chunk, *cut(cuts[1:], first_chunk))))
+    near = cut(cuts[1 : groups - 1], first_chunk)
+    chunks = dict(zip(cuts, (first_chunk, *near, *cut(cuts[groups - 1 :], near[0]))))
     for key in cuts:
         if key[0]:
             pairs = [(source, (source + key[0]) % groups) for source in range(groups)]

time: 31.4 us -> 32.9 us (1.048)
  starting transfers between devices: 11.4 us -> 14.1 us
  waiting for transfers between devices: 0.81 us -> 0.03 us
  blocking collectives: 12.5 us -> 12 us
    ppermute x6, starting transfers between devices: 11.4 us -> 14.1 us  [shards(): chunks[key] = lax.ppermute(chunks[key], 'chan', pairs)]
    ppermute x6, waiting for transfers between devices: 0.81 us -> 0.03 us  [shards(): chunks[key] = lax.ppermute(chunks[key], 'chan', pairs)]
    all_to_all x1, blocking collectives: 12.5 us -> 12 us  [shards(): lax.all_to_all(terms, ('chan', 'freq'), split_axis=0, concat_axis=0, axis...]
  transfers between devices with their start and end apart: 6 -> 6, of which waited for: 1 -> 0; matrix products, arithmetic and copies ran while one was open for 0% -> 0% of each run, Pallas kernels for 9% -> 8%
where the time goes in v32:
time: 32.9 us; the launch traced here: 32.7 us
  starting transfers between devices  14.1 us (43%)
  blocking collectives  12 us (36%)
  Pallas kernels  4.82 us (15%)
  local copies, waits for them, and re-layouts  1.7 us (5%)
    ppermute x6, starting transfers between devices, shards(): chunks[key] = lax.ppermute(chunks[key], 'chan', pairs)  14.1 us
    all_to_all x1, blocking collectives, shards(): lax.all_to_all(terms, ('chan', 'freq'), split_axis=0, concat_axis=0, axis...  12 us
    pallas_call x2, Pallas kernels, shards(): pl.pallas_call(functools.partial(stack_kernel, order, start, size, parts...  2.42 us
    unnamed x6, local copies, waits for them, and re-layouts  1.7 us
    pallas_call x1, Pallas kernels, shards(): pl.pallas_call(functools.partial(table_kernel, groups, bins, freq_dev), o...  1.19 us
    pallas_call x1, Pallas kernels, shards(): pl.pallas_call(functools.partial(image_kernel, slow_dev, spans), out_shap...  0.89 us
  transfers between devices with their start and end apart: 6, of which 0 were waited for; matrix products, arithmetic and copies ran while one was open for 0% of the time, Pallas kernels for 8%

profile of v32, /device:TPU:0, one launch (start us, length us, event | category | flops | bytes accessed | tf_op | source)
XLA Modules:
  0.0 32.7 jit_solution(13889259733143497375)
XLA Ops:
  0.0 0.0 copy-start
  0.0 1.0 %copy-done = bf16[2,32,32,128]{3,2,1,0:T(8,128)(2,1)S(1)} copy-done((bf16[2,32,32,128]{3,2,1,0:T(8,128)(2,1)S(1)}, bf16[2,32,32,128]{3,2,1,0:T(8,128)(2,1)}, u32[]{:S(2)}) %copy-start) | copy-done | bytes 524312
  1.1 4.1 %collective-permute-start.3 = (bf16[5,64,128]{2,1,0:T(8,128)(2,1)S(1)}, bf16[5,64,128]{2,1,0:T(8,128)(2,1)S(1)}, u32[]{:S(2)}, u32[]{:S(2)}) collective-permute-start(bf16[5,64,128]{2,1,0:T(8,128)(2,1)S(1)} %chunks_of_bins.3.refs_0_), channel_id=1, source_target_pairs={{0,16},{8,24},{16,0},{24,8},{1,17},{9,25},{17,1},{25,9},{2,18},{10... | collective-permute-start | bytes 245768 | tf_op jit(solution)/shard_map/ppermute | solution.py:296
  5.2 0.1 chunks_of_bins.4
  5.3 1.4 %collective-permute-start.5 = (bf16[5,64,128]{2,1,0:T(8,128)(2,1)S(1)}, bf16[5,64,128]{2,1,0:T(8,128)(2,1)S(1)}, u32[]{:S(2)}, u32[]{:S(2)}) collective-permute-start(bf16[5,64,128]{2,1,0:T(8,128)(2,1)S(1)} %get-tuple-element.23), channel_id=1, source_target_pairs={{0,24},{8,0},{16,8},{24,16},{1,25},{9,1},{17,9},{25,17},{2,26},{10... | collective-permute-start | bytes 245768 | tf_op jit(solution)/shard_map/ppermute | solution.py:296
  6.7 0.7 %collective-permute-start.4 = (bf16[5,64,128]{2,1,0:T(8,128)(2,1)S(1)}, bf16[5,64,128]{2,1,0:T(8,128)(2,1)S(1)}, u32[]{:S(2)}, u32[]{:S(2)}) collective-permute-start(bf16[5,64,128]{2,1,0:T(8,128)(2,1)S(1)} %get-tuple-element.15.refs_0_), channel_id=1, source_target_pairs={{0,8},{8,16},{16,24},{24,0},{1,9},{9,17},{17,25},{25,1},{2,10},{10... | collective-permute-start | bytes 245768 | tf_op jit(solution)/shard_map/ppermute | solution.py:296
  7.4 0.2 chunks_of_bins.5
  7.5 1.1 %collective-permute-start = (bf16[3,64,128]{2,1,0:T(8,128)(2,1)S(1)}, bf16[3,64,128]{2,1,0:T(8,128)(2,1)S(1)}, u32[]{:S(2)}, u32[]{:S(2)}) collective-permute-start(bf16[3,64,128]{2,1,0:T(8,128)(2,1)S(1)} %get-tuple-element.16), channel_id=1, source_target_pairs={{0,16},{8,24},{16,0},{24,8},{1,17},{9,25},{17,1},{25,9},{2,18},{10... | collective-permute-start | bytes 147464 | tf_op jit(solution)/shard_map/ppermute | solution.py:296
  8.6 2.7 %collective-permute-start.1 = (bf16[3,64,128]{2,1,0:T(8,128)(2,1)S(1)}, bf16[3,64,128]{2,1,0:T(8,128)(2,1)S(1)}, u32[]{:S(2)}, u32[]{:S(2)}) collective-permute-start(bf16[3,64,128]{2,1,0:T(8,128)(2,1)S(1)} %get-tuple-element.17), channel_id=1, source_target_pairs={{0,8},{8,16},{16,24},{24,0},{1,9},{9,17},{17,25},{25,1},{2,10},{10... | collective-permute-start | bytes 147464 | tf_op jit(solution)/shard_map/ppermute | solution.py:296
  11.3 0.0 collective-permute-done.3.in_ref
  11.3 4.2 %collective-permute-start.2 = (bf16[3,64,128]{2,1,0:T(8,128)(2,1)S(1)}, bf16[3,64,128]{2,1,0:T(8,128)(2,1)S(1)}, u32[]{:S(2)}, u32[]{:S(2)}) collective-permute-start(bf16[3,64,128]{2,1,0:T(8,128)(2,1)S(1)} %get-tuple-element.18), channel_id=1, source_target_pairs={{0,24},{8,0},{16,8},{24,16},{1,25},{9,1},{17,9},{25,17},{2,26},{10... | collective-permute-start | bytes 147464 | tf_op jit(solution)/shard_map/ppermute | solution.py:296
  15.5 0.7 %copy-done.2 = s32[4]{0:T(128)S(1)} copy-done((s32[4]{0:T(128)S(1)}, s32[4]{0:T(128)}, u32[]{:S(2)}) %copy-start.2) | copy-done | bytes 40
  16.1 1.2 %slant_tables.1 = (s32[4,128]{1,0:T(4,128)S(1)}, bf16[8,256,512]{2,1,0:T(8,128)(2,1)S(1)}, f32[8,2,8,256]{3,2,1,0:T(8,128)S(1)}) custom-call(s32[1,4]{1,0:T(1,128)S(1)} %bitcast.7), custom_call_target="tpu_custom_call" | custom-call | flops 10000000 | bytes 4000000 | tf_op jit(solution)/shard_map/slant_tables/pallas_call | solution.py:305
  17.3 0.0 collective-permute-done.5.refs_2_
  17.3 0.0 collective-permute-done.4.refs_1_
  17.4 0.0 copy-start.1
  17.4 1.3 %stack_and_slant.2.refs_7_ = f32[10,4,256]{2,1,0:T(4,128)S(1)} custom-call(bf16[5,64,128]{2,1,0:T(8,128)(2,1)S(1)} %first_arrived.1.refs_0_, bf16[5,64,128]{2,1,0:T(8,128)(2,1)S(1)} %collective-permute-done.4.refs_1_, bf16[5,64,128]{2,1,0:T(8,128)(2,1)S(1)} %collective-permute-done.5.refs_2_, bf16[5,64,128]{2,1,0:T(8,128)(2,1)S(1)} %get-tuple-element.24.refs_3_, ...), custom_call_target="tpu_custom_call" | custom-call | flops 200000000 | bytes 4000000 | tf_op jit(solution)/shard_map/stack_and_slant/pallas_call | solution.py:322
  18.7 0.0 collective-permute-done.refs_0_
  18.7 0.0 collective-permute-done.1.refs_1_
  18.7 0.0 collective-permute-done.2.refs_2_
  18.7 1.1 %stack_and_slant.3 = f32[4,8,4,128]{3,2,1,0:T(4,128)S(1)} custom-call(bf16[3,64,128]{2,1,0:T(8,128)(2,1)S(1)} %collective-permute-done.refs_0_, bf16[3,64,128]{2,1,0:T(8,128)(2,1)S(1)} %collective-permute-done.1.refs_1_, bf16[3,64,128]{2,1,0:T(8,128)(2,1)S(1)} %collective-permute-done.2.refs_2_, bf16[3,64,128]{2,1,0:T(8,128)(2,1)S(1)} %get-tuple-element.19.refs_3_, ...), custom_call_target="tpu_custom_call" | custom-call | flops 200000000 | bytes 4000000 | tf_op jit(solution)/shard_map/stack_and_slant/pallas_call | solution.py:322
  19.8 12.0 %all_to_all.5.term_ref = f32[32,4,128]{2,1,0:T(4,128)S(1)} all-to-all(f32[32,4,128]{2,1,0:T(4,128)S(1)} %bitcast.6), channel_id=1, replica_groups={{31,30,29,28,27,26,25,24,23,22,21,20,19,18,17,16,15,14,13,12,11,10,9,8,..., dimensions={0} | all-to-all | bytes 131072 | tf_op jit(solution)/shard_map/all_to_all | solution.py:346
  31.8 0.0 copy-done.1
  31.8 0.9 %sum_of_bins.1 = f32[1,32,512]{2,1,0:T(8,128)} custom-call(f32[32,4,128]{2,1,0:T(4,128)S(1)} %all_to_all.5.term_ref, bf16[2,2,256,256]{3,2,1,0:T(8,128)(2,1)S(1)} %copy-done.1), custom_call_target="tpu_custom_call" | custom-call | tf_op jit(solution)/shard_map/sum_of_bins/pallas_call | solution.py:355
  (3 shorter events, 0.1 us)
Async XLA Ops:
  0.0 1.0 %copy-start = (bf16[2,32,32,128]{3,2,1,0:T(8,128)(2,1)S(1)}, bf16[2,32,32,128]{3,2,1,0:T(8,128)(2,1)}, u32[]{:S(2)}) copy-start(bf16[2,32,32,128]{3,2,1,0:T(8,128)(2,1)} %param.3) | copy-start | bytes 1572868
  1.1 10.2 %collective-permute-start.3 = (bf16[5,64,128]{2,1,0:T(8,128)(2,1)S(1)}, bf16[5,64,128]{2,1,0:T(8,128)(2,1)S(1)}, u32[]{:S(2)}, u32[]{:S(2)}) collective-permute-start(bf16[5,64,128]{2,1,0:T(8,128)(2,1)S(1)} %chunks_of_bins.3.refs_0_), channel_id=1, source_target_pairs={{0,16},{8,24},{16,0},{24,8},{1,17},{9,25},{17,1},{25,9},{2,18},{10... | collective-permute-start | bytes 245768 | tf_op jit(solution)/shard_map/ppermute | solution.py:296
  5.3 12.0 %collective-permute-start.5 = (bf16[5,64,128]{2,1,0:T(8,128)(2,1)S(1)}, bf16[5,64,128]{2,1,0:T(8,128)(2,1)S(1)}, u32[]{:S(2)}, u32[]{:S(2)}) collective-permute-start(bf16[5,64,128]{2,1,0:T(8,128)(2,1)S(1)} %get-tuple-element.23), channel_id=1, source_target_pairs={{0,24},{8,0},{16,8},{24,16},{1,25},{9,1},{17,9},{25,17},{2,26},{10... | collective-permute-start | bytes 245768 | tf_op jit(solution)/shard_map/ppermute | solution.py:296
  6.7 10.7 %collective-permute-start.4 = (bf16[5,64,128]{2,1,0:T(8,128)(2,1)S(1)}, bf16[5,64,128]{2,1,0:T(8,128)(2,1)S(1)}, u32[]{:S(2)}, u32[]{:S(2)}) collective-permute-start(bf16[5,64,128]{2,1,0:T(8,128)(2,1)S(1)} %get-tuple-element.15.refs_0_), channel_id=1, source_target_pairs={{0,8},{8,16},{16,24},{24,0},{1,9},{9,17},{17,25},{25,1},{2,10},{10... | collective-permute-start | bytes 245768 | tf_op jit(solution)/shard_map/ppermute | solution.py:296
  7.5 11.2 %collective-permute-start = (bf16[3,64,128]{2,1,0:T(8,128)(2,1)S(1)}, bf16[3,64,128]{2,1,0:T(8,128)(2,1)S(1)}, u32[]{:S(2)}, u32[]{:S(2)}) collective-permute-start(bf16[3,64,128]{2,1,0:T(8,128)(2,1)S(1)} %get-tuple-element.16), channel_id=1, source_target_pairs={{0,16},{8,24},{16,0},{24,8},{1,17},{9,25},{17,1},{25,9},{2,18},{10... | collective-permute-start | bytes 147464 | tf_op jit(solution)/shard_map/ppermute | solution.py:296
  8.6 10.1 %collective-permute-start.1 = (bf16[3,64,128]{2,1,0:T(8,128)(2,1)S(1)}, bf16[3,64,128]{2,1,0:T(8,128)(2,1)S(1)}, u32[]{:S(2)}, u32[]{:S(2)}) collective-permute-start(bf16[3,64,128]{2,1,0:T(8,128)(2,1)S(1)} %get-tuple-element.17), channel_id=1, source_target_pairs={{0,8},{8,16},{16,24},{24,0},{1,9},{9,17},{17,25},{25,1},{2,10},{10... | collective-permute-start | bytes 147464 | tf_op jit(solution)/shard_map/ppermute | solution.py:296
  11.3 7.4 %collective-permute-start.2 = (bf16[3,64,128]{2,1,0:T(8,128)(2,1)S(1)}, bf16[3,64,128]{2,1,0:T(8,128)(2,1)S(1)}, u32[]{:S(2)}, u32[]{:S(2)}) collective-permute-start(bf16[3,64,128]{2,1,0:T(8,128)(2,1)S(1)} %get-tuple-element.18), channel_id=1, source_target_pairs={{0,24},{8,0},{16,8},{24,16},{1,25},{9,1},{17,9},{25,17},{2,26},{10... | collective-permute-start | bytes 147464 | tf_op jit(solution)/shard_map/ppermute | solution.py:296
  15.5 0.7 %copy-start.2 = (s32[4]{0:T(128)S(1)}, s32[4]{0:T(128)}, u32[]{:S(2)}) copy-start(s32[4]{0:T(128)} %param.4) | copy-start | bytes 52
  17.4 14.5 %copy-start.1 = (bf16[2,2,256,256]{3,2,1,0:T(8,128)(2,1)S(1)}, bf16[2,2,256,256]{3,2,1,0:T(8,128)(2,1)}, u32[]{:S(2)}) copy-start(bf16[2,2,256,256]{3,2,1,0:T(8,128)(2,1)} %constant.2.clone.table_ref) | copy-start | bytes 1572868

commit v33 on v27

--- a/solution.py
+++ b/solution.py
@@ -285,7 +285,7 @@
 
     late = max(1, 3 * bins // 8) if bins > 1 else 0
     pieces = [(0, bins - late), (bins - late, late)] if late else [(0, bins)]
-    order = sorted(range(1, groups), key=lambda steps: abs(2 * steps - groups)) + [0]
+    order = sorted(range(1, groups), key=lambda steps: (abs(2 * steps - groups), -steps)) + [0]
     cuts = [(distance, *piece) for piece in pieces for distance in order]
     (first_chunk,) = cut(cuts[:1])
     chunks = dict(zip(cuts, (first_chunk, *cut(cuts[1:], first_chunk))))

time: 31.4 us -> 31.7 us (level)
  waiting for transfers between devices: 0.81 us -> 2.17 us
  blocking collectives: 12.5 us -> 11.7 us
    ppermute x6, waiting for transfers between devices: 0.81 us -> 2.17 us  [shards(): chunks[key] = lax.ppermute(chunks[key], 'chan', pairs)]
    all_to_all x1, blocking collectives: 12.5 us -> 11.7 us  [shards(): lax.all_to_all(terms, ('chan', 'freq'), split_axis=0, concat_axis=0, axis...]
where the time goes in v33:
time: 31.7 us; the launch traced here: 31.5 us
  blocking collectives  11.7 us (37%)
  starting transfers between devices  11.1 us (35%)
  Pallas kernels  4.75 us (15%)
  waiting for transfers between devices  2.17 us (7%)
  local copies, waits for them, and re-layouts  1.7 us (5%)
    all_to_all x1, blocking collectives, shards(): lax.all_to_all(terms, ('chan', 'freq'), split_axis=0, concat_axis=0, axis...  11.7 us
    ppermute x6, starting transfers between devices, shards(): chunks[key] = lax.ppermute(chunks[key], 'chan', pairs)  11.1 us
    pallas_call x2, Pallas kernels, shards(): pl.pallas_call(functools.partial(stack_kernel, order, start, size, parts...  2.41 us
    ppermute x6, waiting for transfers between devices, shards(): chunks[key] = lax.ppermute(chunks[key], 'chan', pairs)  2.17 us
    unnamed x6, local copies, waits for them, and re-layouts  1.7 us
    pallas_call x1, Pallas kernels, shards(): pl.pallas_call(functools.partial(table_kernel, groups, bins, freq_dev), o...  1.19 us
    pallas_call x1, Pallas kernels, shards(): pl.pallas_call(functools.partial(image_kernel, slow_dev, spans), out_shap...  0.89 us
  transfers between devices with their start and end apart: 6, of which 1 were waited for; matrix products, arithmetic and copies ran while one was open for 0% of the time, Pallas kernels for 9%

profile of v33, /device:TPU:0, one launch (start us, length us, event | category | flops | bytes accessed | tf_op | source)
XLA Modules:
  0.0 31.5 jit_solution(828465024867242594)
XLA Ops:
  0.0 0.0 copy-start
  0.0 1.0 %copy-done = bf16[2,32,32,128]{3,2,1,0:T(8,128)(2,1)S(1)} copy-done((bf16[2,32,32,128]{3,2,1,0:T(8,128)(2,1)S(1)}, bf16[2,32,32,128]{3,2,1,0:T(8,128)(2,1)}, u32[]{:S(2)}) %copy-start) | copy-done | bytes 524312
  1.1 4.1 %collective-permute-start.3 = (bf16[5,64,128]{2,1,0:T(8,128)(2,1)S(1)}, bf16[5,64,128]{2,1,0:T(8,128)(2,1)S(1)}, u32[]{:S(2)}, u32[]{:S(2)}) collective-permute-start(bf16[5,64,128]{2,1,0:T(8,128)(2,1)S(1)} %chunks_of_bins.2.refs_0_), channel_id=1, source_target_pairs={{0,16},{8,24},{16,0},{24,8},{1,17},{9,25},{17,1},{25,9},{2,18},{10... | collective-permute-start | bytes 245768 | tf_op jit(solution)/shard_map/ppermute | solution.py:295
  5.2 0.2 chunks_of_bins.3
  5.4 1.4 %collective-permute-start.4 = (bf16[5,64,128]{2,1,0:T(8,128)(2,1)S(1)}, bf16[5,64,128]{2,1,0:T(8,128)(2,1)S(1)}, u32[]{:S(2)}, u32[]{:S(2)}) collective-permute-start(bf16[5,64,128]{2,1,0:T(8,128)(2,1)S(1)} %get-tuple-element.22), channel_id=1, source_target_pairs={{0,24},{8,0},{16,8},{24,16},{1,25},{9,1},{17,9},{25,17},{2,26},{10... | collective-permute-start | bytes 245768 | tf_op jit(solution)/shard_map/ppermute | solution.py:295
  6.8 0.7 %collective-permute-start.5 = (bf16[5,64,128]{2,1,0:T(8,128)(2,1)S(1)}, bf16[5,64,128]{2,1,0:T(8,128)(2,1)S(1)}, u32[]{:S(2)}, u32[]{:S(2)}) collective-permute-start(bf16[5,64,128]{2,1,0:T(8,128)(2,1)S(1)} %get-tuple-element.23), channel_id=1, source_target_pairs={{0,8},{8,16},{16,24},{24,0},{1,9},{9,17},{17,25},{25,1},{2,10},{10... | collective-permute-start | bytes 245768 | tf_op jit(solution)/shard_map/ppermute | solution.py:295
  7.5 1.0 %collective-permute-start = (bf16[3,64,128]{2,1,0:T(8,128)(2,1)S(1)}, bf16[3,64,128]{2,1,0:T(8,128)(2,1)S(1)}, u32[]{:S(2)}, u32[]{:S(2)}) collective-permute-start(bf16[3,64,128]{2,1,0:T(8,128)(2,1)S(1)} %get-tuple-element.15), channel_id=1, source_target_pairs={{0,16},{8,24},{16,0},{24,8},{1,17},{9,25},{17,1},{25,9},{2,18},{10... | collective-permute-start | bytes 147464 | tf_op jit(solution)/shard_map/ppermute | solution.py:295
  8.5 2.9 %collective-permute-start.1 = (bf16[3,64,128]{2,1,0:T(8,128)(2,1)S(1)}, bf16[3,64,128]{2,1,0:T(8,128)(2,1)S(1)}, u32[]{:S(2)}, u32[]{:S(2)}) collective-permute-start(bf16[3,64,128]{2,1,0:T(8,128)(2,1)S(1)} %get-tuple-element.16), channel_id=1, source_target_pairs={{0,24},{8,0},{16,8},{24,16},{1,25},{9,1},{17,9},{25,17},{2,26},{10... | collective-permute-start | bytes 147464 | tf_op jit(solution)/shard_map/ppermute | solution.py:295
  11.4 0.0 collective-permute-done.3.in_ref
  11.4 1.0 %collective-permute-start.2 = (bf16[3,64,128]{2,1,0:T(8,128)(2,1)S(1)}, bf16[3,64,128]{2,1,0:T(8,128)(2,1)S(1)}, u32[]{:S(2)}, u32[]{:S(2)}) collective-permute-start(bf16[3,64,128]{2,1,0:T(8,128)(2,1)S(1)} %get-tuple-element.17), channel_id=1, source_target_pairs={{0,8},{8,16},{16,24},{24,0},{1,9},{9,17},{17,25},{25,1},{2,10},{10... | collective-permute-start | bytes 147464 | tf_op jit(solution)/shard_map/ppermute | solution.py:295
  12.4 0.0 copy-start.2
  12.4 0.7 %copy-done.2 = s32[4]{0:T(128)S(1)} copy-done((s32[4]{0:T(128)S(1)}, s32[4]{0:T(128)}, u32[]{:S(2)}) %copy-start.2) | copy-done | bytes 40
  13.1 1.2 %slant_tables.1 = (s32[4,128]{1,0:T(4,128)S(1)}, bf16[8,256,512]{2,1,0:T(8,128)(2,1)S(1)}, f32[8,2,8,256]{3,2,1,0:T(8,128)S(1)}) custom-call(s32[1,4]{1,0:T(1,128)S(1)} %bitcast.6), custom_call_target="tpu_custom_call" | custom-call | flops 10000000 | bytes 4000000 | tf_op jit(solution)/shard_map/slant_tables/pallas_call | solution.py:304
  14.3 0.0 collective-permute-done.4.refs_1_
  14.3 0.0 collective-permute-done.5.refs_2_
  14.3 0.0 copy-start.1
  14.3 1.3 %stack_and_slant.2.refs_7_ = f32[10,4,256]{2,1,0:T(4,128)S(1)} custom-call(bf16[5,64,128]{2,1,0:T(8,128)(2,1)S(1)} %first_arrived.1.refs_0_, bf16[5,64,128]{2,1,0:T(8,128)(2,1)S(1)} %collective-permute-done.4.refs_1_, bf16[5,64,128]{2,1,0:T(8,128)(2,1)S(1)} %collective-permute-done.5.refs_2_, bf16[5,64,128]{2,1,0:T(8,128)(2,1)S(1)} %get-tuple-element.24.refs_3_, ...), custom_call_target="tpu_custom_call" | custom-call | flops 200000000 | bytes 4000000 | tf_op jit(solution)/shard_map/stack_and_slant/pallas_call | solution.py:321
  15.6 0.0 collective-permute-done.refs_0_
  15.6 0.0 collective-permute-done.1.refs_1_
  15.7 2.1 %collective-permute-done.2.refs_2_ = bf16[3,64,128]{2,1,0:T(8,128)(2,1)S(1)} collective-permute-done((bf16[3,64,128]{2,1,0:T(8,128)(2,1)S(1)}, bf16[3,64,128]{2,1,0:T(8,128)(2,1)S(1)}, u32[]{:S(2)}, u32[]{:S(2)}) %collective-permute-start.2) | collective-permute-done | bytes 49184 | tf_op jit(solution)/shard_map/ppermute | solution.py:295
  17.8 1.1 %stack_and_slant.3 = f32[4,8,4,128]{3,2,1,0:T(4,128)S(1)} custom-call(bf16[3,64,128]{2,1,0:T(8,128)(2,1)S(1)} %collective-permute-done.refs_0_, bf16[3,64,128]{2,1,0:T(8,128)(2,1)S(1)} %collective-permute-done.1.refs_1_, bf16[3,64,128]{2,1,0:T(8,128)(2,1)S(1)} %collective-permute-done.2.refs_2_, bf16[3,64,128]{2,1,0:T(8,128)(2,1)S(1)} %get-tuple-element.18.refs_3_, ...), custom_call_target="tpu_custom_call" | custom-call | flops 200000000 | bytes 4000000 | tf_op jit(solution)/shard_map/stack_and_slant/pallas_call | solution.py:321
  18.9 11.7 %all_to_all.5.term_ref = f32[32,4,128]{2,1,0:T(4,128)S(1)} all-to-all(f32[32,4,128]{2,1,0:T(4,128)S(1)} %bitcast.5), channel_id=1, replica_groups={{31,30,29,28,27,26,25,24,23,22,21,20,19,18,17,16,15,14,13,12,11,10,9,8,..., dimensions={0} | all-to-all | bytes 131072 | tf_op jit(solution)/shard_map/all_to_all | solution.py:345
  30.6 0.0 copy-done.1
  30.6 0.9 %sum_of_bins.1 = f32[1,32,512]{2,1,0:T(8,128)} custom-call(f32[32,4,128]{2,1,0:T(4,128)S(1)} %all_to_all.5.term_ref, bf16[2,2,256,256]{3,2,1,0:T(8,128)(2,1)S(1)} %copy-done.1), custom_call_target="tpu_custom_call" | custom-call | tf_op jit(solution)/shard_map/sum_of_bins/pallas_call | solution.py:354
  (2 shorter events, 0.1 us)
Async XLA Ops:
  0.0 1.0 %copy-start = (bf16[2,32,32,128]{3,2,1,0:T(8,128)(2,1)S(1)}, bf16[2,32,32,128]{3,2,1,0:T(8,128)(2,1)}, u32[]{:S(2)}) copy-start(bf16[2,32,32,128]{3,2,1,0:T(8,128)(2,1)} %param.3) | copy-start | bytes 1572868
  1.1 10.3 %collective-permute-start.3 = (bf16[5,64,128]{2,1,0:T(8,128)(2,1)S(1)}, bf16[5,64,128]{2,1,0:T(8,128)(2,1)S(1)}, u32[]{:S(2)}, u32[]{:S(2)}) collective-permute-start(bf16[5,64,128]{2,1,0:T(8,128)(2,1)S(1)} %chunks_of_bins.2.refs_0_), channel_id=1, source_target_pairs={{0,16},{8,24},{16,0},{24,8},{1,17},{9,25},{17,1},{25,9},{2,18},{10... | collective-permute-start | bytes 245768 | tf_op jit(solution)/shard_map/ppermute | solution.py:295
  5.4 8.9 %collective-permute-start.4 = (bf16[5,64,128]{2,1,0:T(8,128)(2,1)S(1)}, bf16[5,64,128]{2,1,0:T(8,128)(2,1)S(1)}, u32[]{:S(2)}, u32[]{:S(2)}) collective-permute-start(bf16[5,64,128]{2,1,0:T(8,128)(2,1)S(1)} %get-tuple-element.22), channel_id=1, source_target_pairs={{0,24},{8,0},{16,8},{24,16},{1,25},{9,1},{17,9},{25,17},{2,26},{10... | collective-permute-start | bytes 245768 | tf_op jit(solution)/shard_map/ppermute | solution.py:295
  6.8 7.5 %collective-permute-start.5 = (bf16[5,64,128]{2,1,0:T(8,128)(2,1)S(1)}, bf16[5,64,128]{2,1,0:T(8,128)(2,1)S(1)}, u32[]{:S(2)}, u32[]{:S(2)}) collective-permute-start(bf16[5,64,128]{2,1,0:T(8,128)(2,1)S(1)} %get-tuple-element.23), channel_id=1, source_target_pairs={{0,8},{8,16},{16,24},{24,0},{1,9},{9,17},{17,25},{25,1},{2,10},{10... | collective-permute-start | bytes 245768 | tf_op jit(solution)/shard_map/ppermute | solution.py:295
  7.5 8.1 %collective-permute-start = (bf16[3,64,128]{2,1,0:T(8,128)(2,1)S(1)}, bf16[3,64,128]{2,1,0:T(8,128)(2,1)S(1)}, u32[]{:S(2)}, u32[]{:S(2)}) collective-permute-start(bf16[3,64,128]{2,1,0:T(8,128)(2,1)S(1)} %get-tuple-element.15), channel_id=1, source_target_pairs={{0,16},{8,24},{16,0},{24,8},{1,17},{9,25},{17,1},{25,9},{2,18},{10... | collective-permute-start | bytes 147464 | tf_op jit(solution)/shard_map/ppermute | solution.py:295
  8.5 7.1 %collective-permute-start.1 = (bf16[3,64,128]{2,1,0:T(8,128)(2,1)S(1)}, bf16[3,64,128]{2,1,0:T(8,128)(2,1)S(1)}, u32[]{:S(2)}, u32[]{:S(2)}) collective-permute-start(bf16[3,64,128]{2,1,0:T(8,128)(2,1)S(1)} %get-tuple-element.16), channel_id=1, source_target_pairs={{0,24},{8,0},{16,8},{24,16},{1,25},{9,1},{17,9},{25,17},{2,26},{10... | collective-permute-start | bytes 147464 | tf_op jit(solution)/shard_map/ppermute | solution.py:295
  11.4 6.4 %collective-permute-start.2 = (bf16[3,64,128]{2,1,0:T(8,128)(2,1)S(1)}, bf16[3,64,128]{2,1,0:T(8,128)(2,1)S(1)}, u32[]{:S(2)}, u32[]{:S(2)}) collective-permute-start(bf16[3,64,128]{2,1,0:T(8,128)(2,1)S(1)} %get-tuple-element.17), channel_id=1, source_target_pairs={{0,8},{8,16},{16,24},{24,0},{1,9},{9,17},{17,25},{25,1},{2,10},{10... | collective-permute-start | bytes 147464 | tf_op jit(solution)/shard_map/ppermute | solution.py:295
  12.4 0.7 %copy-start.2 = (s32[4]{0:T(128)S(1)}, s32[4]{0:T(128)}, u32[]{:S(2)}) copy-start(s32[4]{0:T(128)} %param.4) | copy-start | bytes 52
  14.3 16.3 %copy-start.1 = (bf16[2,2,256,256]{3,2,1,0:T(8,128)(2,1)S(1)}, bf16[2,2,256,256]{3,2,1,0:T(8,128)(2,1)}, u32[]{:S(2)}) copy-start(bf16[2,2,256,256]{3,2,1,0:T(8,128)(2,1)} %constant.2.clone.table_ref) | copy-start | bytes 1572868

commit v34 on v24

--- a/solution.py
+++ b/solution.py
@@ -282,7 +282,7 @@
             name="chunks_of_bins",
         )(whole, *earlier)
 
-    late = max(1, bins // 4) if bins > 1 else 0
+    late = max(1, 3 * bins // 8) if bins > 1 else 0
     pieces = [(0, bins - late), (bins - late, late)] if late else [(0, bins)]
     far_first = sorted(range(1, groups), key=lambda steps: abs(2 * steps - groups)) + [0]
     near_first = list(range(1, groups)) + [0]

time: 32.1 us -> 32.2 us (level)
  waiting for transfers between devices: 3.49 us -> 0.81 us
  starting transfers between devices: 9.73 us -> 11.4 us
  blocking collectives: 12.1 us -> 13.3 us
    ppermute x6, waiting for transfers between devices: 3.49 us -> 0.81 us  [shards(): chunks[key] = lax.ppermute(chunks[key], 'chan', pairs)]
    ppermute x6, starting transfers between devices: 9.73 us -> 11.4 us  [shards(): chunks[key] = lax.ppermute(chunks[key], 'chan', pairs)]
    all_to_all x1, blocking collectives: 12.1 us -> 13.3 us  [shards(): lax.all_to_all(terms, ('chan', 'freq'), split_axis=0, concat_axis=0, axis...]
  transfers between devices with their start and end apart: 6 -> 6, of which waited for: 1 -> 1; matrix products, arithmetic and copies ran while one was open for 0% -> 0% of each run, Pallas kernels for 9% -> 8%
where the time goes in v34:
time: 32.2 us; the launch traced here: 32 us
  blocking collectives  13.3 us (41%)
  starting transfers between devices  11.4 us (35%)
  Pallas kernels  4.76 us (15%)
  local copies, waits for them, and re-layouts  1.7 us (5%)
  waiting for transfers between devices  0.81 us (3%)
    all_to_all x1, blocking collectives, shards(): lax.all_to_all(terms, ('chan', 'freq'), split_axis=0, concat_axis=0, axis...  13.3 us
    ppermute x6, starting transfers between devices, shards(): chunks[key] = lax.ppermute(chunks[key], 'chan', pairs)  11.4 us
    pallas_call x2, Pallas kernels, shards(): pl.pallas_call(functools.partial(stack_kernel, order, start, size, parts...  2.41 us
    unnamed x6, local copies, waits for them, and re-layouts  1.7 us
    pallas_call x1, Pallas kernels, shards(): pl.pallas_call(functools.partial(table_kernel, groups, bins, freq_dev), o...  1.19 us
    pallas_call x1, Pallas kernels, shards(): pl.pallas_call(functools.partial(image_kernel, slow_dev, spans), out_shap...  0.89 us
    ppermute x6, waiting for transfers between devices, shards(): chunks[key] = lax.ppermute(chunks[key], 'chan', pairs)  0.81 us
  transfers between devices with their start and end apart: 6, of which 1 were waited for; matrix products, arithmetic and copies ran while one was open for 0% of the time, Pallas kernels for 8%

profile of v34, /device:TPU:0, one launch (start us, length us, event | category | flops | bytes accessed | tf_op | source)
XLA Modules:
  0.0 32.0 jit_solution(12582778213497537466)
XLA Ops:
  0.0 0.0 copy-start
  0.0 1.0 %copy-done = bf16[2,32,32,128]{3,2,1,0:T(8,128)(2,1)S(1)} copy-done((bf16[2,32,32,128]{3,2,1,0:T(8,128)(2,1)S(1)}, bf16[2,32,32,128]{3,2,1,0:T(8,128)(2,1)}, u32[]{:S(2)}) %copy-start) | copy-done | bytes 524312
  1.1 4.1 %collective-permute-start.3 = (bf16[5,64,128]{2,1,0:T(8,128)(2,1)S(1)}, bf16[5,64,128]{2,1,0:T(8,128)(2,1)S(1)}, u32[]{:S(2)}, u32[]{:S(2)}) collective-permute-start(bf16[5,64,128]{2,1,0:T(8,128)(2,1)S(1)} %chunks_of_bins.2.refs_0_), channel_id=1, source_target_pairs={{0,16},{8,24},{16,0},{24,8},{1,17},{9,25},{17,1},{25,9},{2,18},{10... | collective-permute-start | bytes 245768 | tf_op jit(solution)/shard_map/ppermute | solution.py:296
  5.2 0.2 chunks_of_bins.3
  5.4 1.6 %collective-permute-start.4 = (bf16[5,64,128]{2,1,0:T(8,128)(2,1)S(1)}, bf16[5,64,128]{2,1,0:T(8,128)(2,1)S(1)}, u32[]{:S(2)}, u32[]{:S(2)}) collective-permute-start(bf16[5,64,128]{2,1,0:T(8,128)(2,1)S(1)} %get-tuple-element.22), channel_id=1, source_target_pairs={{0,8},{8,16},{16,24},{24,0},{1,9},{9,17},{17,25},{25,1},{2,10},{10... | collective-permute-start | bytes 245768 | tf_op jit(solution)/shard_map/ppermute | solution.py:296
  7.0 2.2 %collective-permute-start.5 = (bf16[5,64,128]{2,1,0:T(8,128)(2,1)S(1)}, bf16[5,64,128]{2,1,0:T(8,128)(2,1)S(1)}, u32[]{:S(2)}, u32[]{:S(2)}) collective-permute-start(bf16[5,64,128]{2,1,0:T(8,128)(2,1)S(1)} %get-tuple-element.23), channel_id=1, source_target_pairs={{0,24},{8,0},{16,8},{24,16},{1,25},{9,1},{17,9},{25,17},{2,26},{10... | collective-permute-start | bytes 245768 | tf_op jit(solution)/shard_map/ppermute | solution.py:296
  9.3 0.0 collective-permute-start
  9.3 0.6 %collective-permute-start.1 = (bf16[3,64,128]{2,1,0:T(8,128)(2,1)S(1)}, bf16[3,64,128]{2,1,0:T(8,128)(2,1)S(1)}, u32[]{:S(2)}, u32[]{:S(2)}) collective-permute-start(bf16[3,64,128]{2,1,0:T(8,128)(2,1)S(1)} %get-tuple-element.16), channel_id=1, source_target_pairs={{0,16},{8,24},{16,0},{24,8},{1,17},{9,25},{17,1},{25,9},{2,18},{10... | collective-permute-start | bytes 147464 | tf_op jit(solution)/shard_map/ppermute | solution.py:296
  9.9 0.8 %collective-permute-done.3.in_ref = bf16[5,64,128]{2,1,0:T(8,128)(2,1)S(1)} collective-permute-done((bf16[5,64,128]{2,1,0:T(8,128)(2,1)S(1)}, bf16[5,64,128]{2,1,0:T(8,128)(2,1)S(1)}, u32[]{:S(2)}, u32[]{:S(2)}) %collective-permute-start.3) | collective-permute-done | bytes 81952 | tf_op jit(solution)/shard_map/ppermute | solution.py:296
  10.6 2.8 %collective-permute-start.2 = (bf16[3,64,128]{2,1,0:T(8,128)(2,1)S(1)}, bf16[3,64,128]{2,1,0:T(8,128)(2,1)S(1)}, u32[]{:S(2)}, u32[]{:S(2)}) collective-permute-start(bf16[3,64,128]{2,1,0:T(8,128)(2,1)S(1)} %get-tuple-element.17), channel_id=1, source_target_pairs={{0,24},{8,0},{16,8},{24,16},{1,25},{9,1},{17,9},{25,17},{2,26},{10... | collective-permute-start | bytes 147464 | tf_op jit(solution)/shard_map/ppermute | solution.py:296
  13.5 0.0 copy-start.2
  13.5 0.7 %copy-done.2 = s32[4]{0:T(128)S(1)} copy-done((s32[4]{0:T(128)S(1)}, s32[4]{0:T(128)}, u32[]{:S(2)}) %copy-start.2) | copy-done | bytes 40
  14.1 1.2 %slant_tables.1 = (s32[4,128]{1,0:T(4,128)S(1)}, bf16[8,256,512]{2,1,0:T(8,128)(2,1)S(1)}, f32[8,2,8,256]{3,2,1,0:T(8,128)S(1)}) custom-call(s32[1,4]{1,0:T(1,128)S(1)} %bitcast.6), custom_call_target="tpu_custom_call" | custom-call | flops 10000000 | bytes 4000000 | tf_op jit(solution)/shard_map/slant_tables/pallas_call | solution.py:305
  15.3 0.0 collective-permute-done.4.refs_1_
  15.4 0.0 collective-permute-done.5.refs_2_
  15.4 0.0 copy-start.1
  15.4 1.3 %stack_and_slant.2.refs_7_ = f32[10,4,256]{2,1,0:T(4,128)S(1)} custom-call(bf16[5,64,128]{2,1,0:T(8,128)(2,1)S(1)} %first_arrived.1.refs_0_, bf16[5,64,128]{2,1,0:T(8,128)(2,1)S(1)} %collective-permute-done.4.refs_1_, bf16[5,64,128]{2,1,0:T(8,128)(2,1)S(1)} %collective-permute-done.5.refs_2_, bf16[5,64,128]{2,1,0:T(8,128)(2,1)S(1)} %get-tuple-element.24.refs_3_, ...), custom_call_target="tpu_custom_call" | custom-call | flops 200000000 | bytes 4000000 | tf_op jit(solution)/shard_map/stack_and_slant/pallas_call | solution.py:322
  16.7 0.0 collective-permute-done.refs_0_
  16.7 0.0 collective-permute-done.1.refs_1_
  16.7 0.0 collective-permute-done.2.refs_2_
  16.7 1.1 %stack_and_slant.3 = f32[4,8,4,128]{3,2,1,0:T(4,128)S(1)} custom-call(bf16[3,64,128]{2,1,0:T(8,128)(2,1)S(1)} %collective-permute-done.refs_0_, bf16[3,64,128]{2,1,0:T(8,128)(2,1)S(1)} %collective-permute-done.1.refs_1_, bf16[3,64,128]{2,1,0:T(8,128)(2,1)S(1)} %collective-permute-done.2.refs_2_, bf16[3,64,128]{2,1,0:T(8,128)(2,1)S(1)} %get-tuple-element.18.refs_3_, ...), custom_call_target="tpu_custom_call" | custom-call | flops 200000000 | bytes 4000000 | tf_op jit(solution)/shard_map/stack_and_slant/pallas_call | solution.py:322
  17.8 13.3 %all_to_all.5.term_ref = f32[32,4,128]{2,1,0:T(4,128)S(1)} all-to-all(f32[32,4,128]{2,1,0:T(4,128)S(1)} %bitcast.5), channel_id=1, replica_groups={{31,30,29,28,27,26,25,24,23,22,21,20,19,18,17,16,15,14,13,12,11,10,9,8,..., dimensions={0} | all-to-all | bytes 131072 | tf_op jit(solution)/shard_map/all_to_all | solution.py:346
  31.1 0.0 copy-done.1
  31.1 0.9 %sum_of_bins.1 = f32[1,32,512]{2,1,0:T(8,128)} custom-call(f32[32,4,128]{2,1,0:T(4,128)S(1)} %all_to_all.5.term_ref, bf16[2,2,256,256]{3,2,1,0:T(8,128)(2,1)S(1)} %copy-done.1), custom_call_target="tpu_custom_call" | custom-call | tf_op jit(solution)/shard_map/sum_of_bins/pallas_call | solution.py:355
  (2 shorter events, 0.1 us)
Async XLA Ops:
  0.0 1.0 %copy-start = (bf16[2,32,32,128]{3,2,1,0:T(8,128)(2,1)S(1)}, bf16[2,32,32,128]{3,2,1,0:T(8,128)(2,1)}, u32[]{:S(2)}) copy-start(bf16[2,32,32,128]{3,2,1,0:T(8,128)(2,1)} %param.3) | copy-start | bytes 1572868
  1.1 9.6 %collective-permute-start.3 = (bf16[5,64,128]{2,1,0:T(8,128)(2,1)S(1)}, bf16[5,64,128]{2,1,0:T(8,128)(2,1)S(1)}, u32[]{:S(2)}, u32[]{:S(2)}) collective-permute-start(bf16[5,64,128]{2,1,0:T(8,128)(2,1)S(1)} %chunks_of_bins.2.refs_0_), channel_id=1, source_target_pairs={{0,16},{8,24},{16,0},{24,8},{1,17},{9,25},{17,1},{25,9},{2,18},{10... | collective-permute-start | bytes 245768 | tf_op jit(solution)/shard_map/ppermute | solution.py:296
  5.4 9.9 %collective-permute-start.4 = (bf16[5,64,128]{2,1,0:T(8,128)(2,1)S(1)}, bf16[5,64,128]{2,1,0:T(8,128)(2,1)S(1)}, u32[]{:S(2)}, u32[]{:S(2)}) collective-permute-start(bf16[5,64,128]{2,1,0:T(8,128)(2,1)S(1)} %get-tuple-element.22), channel_id=1, source_target_pairs={{0,8},{8,16},{16,24},{24,0},{1,9},{9,17},{17,25},{25,1},{2,10},{10... | collective-permute-start | bytes 245768 | tf_op jit(solution)/shard_map/ppermute | solution.py:296
  7.0 8.3 %collective-permute-start.5 = (bf16[5,64,128]{2,1,0:T(8,128)(2,1)S(1)}, bf16[5,64,128]{2,1,0:T(8,128)(2,1)S(1)}, u32[]{:S(2)}, u32[]{:S(2)}) collective-permute-start(bf16[5,64,128]{2,1,0:T(8,128)(2,1)S(1)} %get-tuple-element.23), channel_id=1, source_target_pairs={{0,24},{8,0},{16,8},{24,16},{1,25},{9,1},{17,9},{25,17},{2,26},{10... | collective-permute-start | bytes 245768 | tf_op jit(solution)/shard_map/ppermute | solution.py:296
  9.3 7.4 %collective-permute-start = (bf16[3,64,128]{2,1,0:T(8,128)(2,1)S(1)}, bf16[3,64,128]{2,1,0:T(8,128)(2,1)S(1)}, u32[]{:S(2)}, u32[]{:S(2)}) collective-permute-start(bf16[3,64,128]{2,1,0:T(8,128)(2,1)S(1)} %get-tuple-element.15), channel_id=1, source_target_pairs={{0,8},{8,16},{16,24},{24,0},{1,9},{9,17},{17,25},{25,1},{2,10},{10... | collective-permute-start | bytes 147464 | tf_op jit(solution)/shard_map/ppermute | solution.py:296
  9.3 7.4 %collective-permute-start.1 = (bf16[3,64,128]{2,1,0:T(8,128)(2,1)S(1)}, bf16[3,64,128]{2,1,0:T(8,128)(2,1)S(1)}, u32[]{:S(2)}, u32[]{:S(2)}) collective-permute-start(bf16[3,64,128]{2,1,0:T(8,128)(2,1)S(1)} %get-tuple-element.16), channel_id=1, source_target_pairs={{0,16},{8,24},{16,0},{24,8},{1,17},{9,25},{17,1},{25,9},{2,18},{10... | collective-permute-start | bytes 147464 | tf_op jit(solution)/shard_map/ppermute | solution.py:296
  10.6 6.1 %collective-permute-start.2 = (bf16[3,64,128]{2,1,0:T(8,128)(2,1)S(1)}, bf16[3,64,128]{2,1,0:T(8,128)(2,1)S(1)}, u32[]{:S(2)}, u32[]{:S(2)}) collective-permute-start(bf16[3,64,128]{2,1,0:T(8,128)(2,1)S(1)} %get-tuple-element.17), channel_id=1, source_target_pairs={{0,24},{8,0},{16,8},{24,16},{1,25},{9,1},{17,9},{25,17},{2,26},{10... | collective-permute-start | bytes 147464 | tf_op jit(solution)/shard_map/ppermute | solution.py:296
  13.5 0.7 %copy-start.2 = (s32[4]{0:T(128)S(1)}, s32[4]{0:T(128)}, u32[]{:S(2)}) copy-start(s32[4]{0:T(128)} %param.4) | copy-start | bytes 52
  15.4 15.8 %copy-start.1 = (bf16[2,2,256,256]{3,2,1,0:T(8,128)(2,1)S(1)}, bf16[2,2,256,256]{3,2,1,0:T(8,128)(2,1)}, u32[]{:S(2)}) copy-start(bf16[2,2,256,256]{3,2,1,0:T(8,128)(2,1)} %constant.2.clone.table_ref) | copy-start | bytes 1572868
